TPU v7x, 128 devices: a whole 4x4x4 slice. The times are simulated.
128 devices in a mesh: row: 16 (over y, x_lo, core), col: 8 (over z, x_hi).
Axes of the slice: x: 4 (x_hi: 2, x_lo: 2; x = x_hi * 2 + x_lo), y: 4, z: 4, core: 2. Of those that a mesh axis runs over, the one named last changes fastest.
Arguments:
- inputs: bfloat16 [2048, 14848], P('col', 'row'), may hold values from -6 to 6
- cotangent: bfloat16 [2048, 30720], P('col', 'row'), may hold values from -0.29882812 to 0.29882812
- weight: bfloat16 [14848, 30720], P('col', 'row'), may hold values from -0.046875 to 0.046875
- adapter_down_factor: bfloat16 [14848, 16], replicated, may hold values from -0.046875 to 0.046875
- adapter_up_factor: bfloat16 [16, 30720], replicated, may hold values from -1.5 to 1.5
Outputs:
- grad_input: bfloat16 [2048, 14848], P('row', 'col')
- grad_a: float32 [14848, 16], P('row')
- grad_b: float32 [16, 30720], P(None, 'row')
All inputs are finite; a program needn't handle non-finite values.
Results may differ from a plain program's by a relative error of at most 0.001.
Values may be sent and summed in bfloat16 or wider, within the bound.
No kernel may reach another device: no remote copies, remote signals or barrier semaphores. Data moves between devices by JAX's collectives and lax.ppermute only.
A program may use at most 128 MiB of HBM per device.

v0:
```python
import jax
import jax.numpy as jnp
from jax import lax
from jax.sharding import PartitionSpec as P

scaling = 2.0


def contract_trailing_axis(left, right):
    return jnp.dot(left, right.T, preferred_element_type=jnp.float32)


def partial_rows(block_rows, weight, up_weight_slice, down_slice):
    partial_value = contract_trailing_axis(block_rows, weight)
    low_rank = contract_trailing_axis(block_rows, up_weight_slice)
    return partial_value + scaling * jnp.dot(
        low_rank, down_slice.astype(jnp.float32).T, precision=lax.Precision.HIGHEST
    )


def on_device(inputs, cotangent, weight, adapter_down_factor, adapter_up_factor):
    row_position = lax.axis_index("row")
    column_position = lax.axis_index("col")
    width_row_block = inputs.shape[1]
    width_columns = weight.shape[0]
    hidden_columns = cotangent.shape[1]
    down_factor_rows = lax.dynamic_slice_in_dim(
        adapter_down_factor, row_position * width_row_block, width_row_block, 0
    )
    down_factor_columns = lax.dynamic_slice_in_dim(
        adapter_down_factor, column_position * width_columns, width_columns, 0
    )
    up_weight_slice = lax.dynamic_slice_in_dim(
        adapter_up_factor, row_position * hidden_columns, hidden_columns, 1
    )
    low_part = contract_trailing_axis(cotangent, up_weight_slice)
    proj_part = jnp.dot(inputs, down_factor_rows, preferred_element_type=jnp.float32)
    gradient_lowrank, projected_rows = lax.psum((low_part, proj_part), "row")
    gathered = lax.all_gather(cotangent, "col", axis=0, tiled=True)
    summed = lax.psum_scatter(
        partial_rows(gathered, weight, up_weight_slice, down_factor_columns),
        "row",
        scatter_dimension=0,
        tiled=True,
    )
    grad_input = summed.astype(jnp.bfloat16)
    part_a = scaling * jnp.dot(
        inputs.astype(jnp.float32).T, gradient_lowrank, precision=lax.Precision.HIGHEST
    )
    part_b = scaling * jnp.dot(
        projected_rows.T, cotangent.astype(jnp.float32), precision=lax.Precision.HIGHEST
    )
    grad_a, grad_b = lax.psum((part_a, part_b), "col")
    return (grad_input, grad_a, grad_b)


def solution(mesh):
    in_specs = (P("col", "row"), P("col", "row"), P("col", "row"), P(), P())
    out_specs = (P("row", "col"), P("row", None), P(None, "row"))
    return jax.shard_map(
        on_device, mesh=mesh, in_specs=in_specs, out_specs=out_specs, check_vma=False
    )
```

profile of v0, /device:TPU:0, one launch (start us, length us, event | category | flops | bytes accessed | tf_op | source)
XLA Modules:
  0.0 412.6 jit_solution(9289828329038741423)
XLA Ops:
  7.2 0.0 copy-start
  7.2 0.0 all-gather.2.cloned.1.call-start
  7.2 0.7 all-gather.2.cloned.1.call-update
  7.9 0.0 reduce-scatter.2.cloned.1.call-start
  8.0 107.4 %all-gather.2.cloned.1.call-done = bf16[2048,1920]{1,0:T(8,128)(2,1)} async-done(((bf16[256,1920]{1,0:T(8,128)(2,1)}), bf16[2048,1920]{1,0:T(8,128)(2,1)}) %all-gather.2.cloned.1.call-update) | async-done | bytes 7864336 | tf_op jit(solution)/shard_map/all_gather | solution.py:39
  115.4 0.0 copy-done
  115.4 5.4 %fusion.4 = f32[16,2048]{1,0:T(8,128)S(1)} fusion(bf16[2048,1920]{1,0:T(8,128)(2,1)} %all-gather.2.cloned.1.call-done, bf16[16,30720]{1,0:T(8,128)(2,1)S(1)} %copy-done, s32[]{:T(128)S(6)} %select_n.9), kind=kOutput, calls=%fused_computation.9 | convolution fusion | flops 125829120 | bytes 8056836 | tf_op jit(solution)/shard_map/dot_general | solution.py:10
  120.7 7.6 %fusion.1 = f32[2048,1856]{0,1:T(8,128)S(1)} fusion(f32[16,2048]{1,0:T(8,128)S(1)} %fusion.4, bf16[14848,16]{0,1:T(8,128)(2,1)} %param.8, s32[]{:T(128)S(6)} %select_n.10), kind=kOutput, calls=%fused_computation.6 | convolution fusion | flops 729808896 | bytes 15396868 | tf_op jit(solution)/shard_map/dot_general | solution.py:16
  128.3 22.5 %multiply_add_fusion = f32[2048,1856]{0,1:T(8,128)} fusion(f32[2048,1856]{0,1:T(8,128)S(1)} %fusion.1, bf16[2048,1920]{1,0:T(8,128)(2,1)} %all-gather.2.cloned.1.call-done, bf16[1856,1920]{1,0:T(8,128)(2,1)} %param.7), kind=kOutput, calls=%fused_computation | convolution fusion | flops 14603780096 | bytes 45400064 | tf_op jit(solution)/shard_map/dot_general | solution.py:10
  150.8 0.0 copy-start.2
  150.8 0.0 copy-start.1
  150.8 0.0 reduce-scatter.2.cloned.1.call-update
  150.8 0.0 all-reduce.3.cloned.1.call-start
  150.8 0.9 copy-done.2
  151.8 1.0 convolution_bitcast_fusion.1
  152.8 0.0 copy-done.1
  152.8 0.3 convolution_bitcast_fusion
  153.1 57.7 %all-reduce = (f32[256,16]{0,1:T(8,128)S(1)}, f32[256,16]{0,1:T(8,128)S(1)}) all-reduce(f32[256,16]{0,1:T(8,128)S(1)} %convolution_bitcast_fusion, f32[256,16]{0,1:T(8,128)S(1)} %convolution_bitcast_fusion.1), channel_id=1, replica_groups=mesh['row'=16,'col'=8] {'row'}, use_global_device_ids=true, to_apply=%region_1.0 | all-reduce | flops 8192 | bytes 65536 | tf_op jit(solution)/shard_map/psum | solution.py:38
  210.8 1.2 convolution_multiply_fusion
  212.0 0.0 all-reduce.3.cloned.1.call-update
  212.0 0.5 fusion
  212.5 43.0 %psum.29 = f32[928,16]{0,1:T(8,128)} all-reduce(f32[928,16]{0,1:T(8,128)S(1)} %fusion), channel_id=1, replica_groups=mesh['row'=16,'col'=8] {'col'}, use_global_device_ids=true, to_apply=%region_2.0 | all-reduce | flops 14848 | bytes 118784 | tf_op jit(solution)/shard_map/psum | solution.py:53
  255.5 63.4 %reduce-scatter.2.cloned.1.call-done = f32[128,1856]{0,1:T(8,128)} async-done(((f32[2048,1856]{0,1:T(8,128)}), f32[128,1856]{0,1:T(8,128)}) %reduce-scatter.2.cloned.1.call-update) | async-done | bytes 950288 | tf_op jit(solution)/shard_map/reduce_scatter | solution.py:40
  318.9 2.0 convert_element_type.2
  320.9 83.6 %all-reduce.3.cloned.1.call-done = f32[16,1920]{1,0:T(8,128)} async-done(((f32[16,1920]{1,0:T(8,128)}), f32[16,1920]{1,0:T(8,128)}) %all-reduce.3.cloned.1.call-update) | async-done | bytes 122896 | tf_op jit(solution)/shard_map/psum | solution.py:53
  404.5 1.6 copy.9
Async XLA Ops:
  7.2 108.2 %copy-start = (bf16[16,30720]{1,0:T(8,128)(2,1)S(1)}, bf16[16,30720]{1,0:T(8,128)(2,1)}, u32[]{:S(2)}) copy-start(bf16[16,30720]{1,0:T(8,128)(2,1)} %param.9) | copy-start | bytes 2949124
  7.2 108.2 %all-gather.2.cloned.1.call-start = ((), (), s32[]{:S(2)}) async-start(), calls=%async_computation.1 | async-start | bytes 8847360 | tf_op jit(solution)/shard_map/all_gather | solution.py:39
  7.9 310.9 %reduce-scatter.2.cloned.1.call-start = ((), (), s32[]{:S(2)}) async-start(), calls=%async_computation.2 | async-start | bytes 16154624 | tf_op jit(solution)/shard_map/reduce_scatter | solution.py:40
  150.8 1.0 copy-start.2
  150.8 2.0 copy-start.1
  150.8 253.7 %all-reduce.3.cloned.1.call-start = ((), (), s32[]{:S(2)}) async-start(), calls=%async_computation.3 | async-start | bytes 245760 | tf_op jit(solution)/shard_map/psum | solution.py:53
Sparse Core Ops, SparseCore 0:
  10.3 104.9 all-gather.1
  150.9 167.9 reduce-scatter.1
  321.9 82.5 all-reduce.2
where the time goes:
time: 413 us
  waiting for transfers between devices  255 us (62%)
  blocking collectives  101 us (24%)
  matrix products  38.3 us (9%)
  between operations  13.8 us (3%)
    all_gather x1, waiting for transfers between devices, on_device(): gathered = lax.all_gather(cotangent, 'col', axis=0, tiled=True)  107 us
    psum x1, waiting for transfers between devices, on_device(): grad_a, grad_b = lax.psum((part_a, part_b), 'col')  83.6 us
    reduce_scatter x1, waiting for transfers between devices, on_device(): lax.psum_scatter(partial_rows(gathered, weight, up_weight_slice, down_fac...  63.4 us
    psum x1, blocking collectives, on_device(): gradient_lowrank, projected_rows = lax.psum((low_part, proj_part), 'row')  57.7 us
    psum x1, blocking collectives, on_device(): grad_a, grad_b = lax.psum((part_a, part_b), 'col')  43 us
    dot_general x3, matrix products, contract_trailing_axis(): return jnp.dot(left, right.T, preferred_element_type=jnp.float32)  28.2 us
  transfers between devices with their start and end apart: 3, of which 3 were waited for; matrix products, arithmetic and copies ran while one was open for 1% of the time, Pallas kernels for 0%

commit v1 on v0

v1 whole, which is shorter than its diff:
```python
import functools

import jax
import jax.numpy as jnp
from jax import lax
from jax.experimental import pallas as pl
from jax.experimental.pallas import tpu as pltpu
from jax.sharding import Mesh, PartitionSpec as P

scaling = 2.0
AXES = ("y", "xl", "core", "z", "xh")
SIZES = (4, 2, 2, 4, 2)
ROW = ("y", "xl", "core")
COL = ("z", "xh")
CHUNKS = 4

POWER = 17
REACH = 170.0
SMALLEST = 1e-35


def encode(value, width, padded):
    column = lax.broadcasted_iota(jnp.int32, value.shape, 1)
    value = jnp.where(column < width, value, 0.0)
    largest = jnp.max(jnp.abs(value), axis=1, keepdims=True)
    scale = jnp.maximum((largest * 1.01).astype(jnp.bfloat16).astype(jnp.float32), SMALLEST)
    scale = scale.astype(jnp.bfloat16).astype(jnp.float32)
    a = value * (REACH / scale)
    a2 = a * a
    a4 = a2 * a2
    a8 = a4 * a4
    coded = a8 * a8 * a
    return jnp.where(column == width, scale, coded).astype(jnp.bfloat16)


def decode(coded, width):
    coded = coded.astype(jnp.float32)
    scale = coded[:, width : width + 1] * (1.0 / REACH)
    size = jnp.abs(coded)
    root = jnp.exp2(jnp.log2(jnp.maximum(size, 1e-38)) * (1.0 / POWER))
    root = jnp.where(size > 0.0, root, 0.0)
    return jnp.where(coded < 0.0, -root, root) * scale


def split3(value):
    high = value.astype(jnp.bfloat16)
    rest = value - high.astype(jnp.float32)
    middle = rest.astype(jnp.bfloat16)
    low = (rest - middle.astype(jnp.float32)).astype(jnp.bfloat16)
    return high, middle, low


def pieces3(value):
    high = lax.reduce_precision(value, 8, 7)
    middle = lax.reduce_precision(value - high, 8, 7)
    return [p.astype(jnp.bfloat16) for p in (high, middle, value - high - middle)]


def dot_t(left, right):
    return lax.dot_general(
        left, right, (((1,), (1,)), ((), ())), preferred_element_type=jnp.float32
    )


def partial_kernel(width, base, c0, c1, c2, c3, wo, wr, uo, ur, down, own, o1, o2, o3, held, low, acc):
    j = pl.program_id(0)
    rows = c0.shape[0]
    half = wo.shape[1]
    tile = wo.shape[0]

    @pl.when(j == 0)
    def _():
        for p, c in enumerate((c0, c1, c2, c3)):
            held[p * rows : (p + 1) * rows, :] = c[...]
        total = dot_t(held[:, :half], uo[...]) + dot_t(held[:, half:], ur[...])
        low[...] = jnp.concatenate(split3(total), axis=1)

    acc[:, pl.ds(pl.multiple_of(j * tile, tile), tile)] = (
        dot_t(held[:, :half], wo[...]) + dot_t(held[:, half:], wr[...]) + dot_t(low[...], down[...])
    )

    @pl.when(j == pl.num_programs(0) - 1)
    def _():
        padded = o1.shape[1]
        for p, ahead in enumerate((0, 3, 1, 2)):
            value = acc[p * rows : (p + 1) * rows, :padded]
            target = lax.rem(base[0] + ahead, 4)
            coded = encode(value, width, padded)

            @pl.when(target == 0)
            def _():
                own[...] = value

            for d, o in ((1, o1), (2, o2), (3, o3)):

                @pl.when(target == d)
                def _(o=o):
                    o[...] = coded


def partial(base, pieces, wo, wr, uo, ur, down):
    width, half = wo.shape
    rows = pieces[0].shape[0]
    tile = 256
    steps = pl.cdiv(width, tile)
    padded = (width // 128 + 1) * 128
    whole = lambda a: pl.BlockSpec(a.shape, lambda j, b: (0, 0))
    strip = lambda a: pl.BlockSpec((tile, a.shape[1]), lambda j, b: (j, 0))
    out = pl.BlockSpec((rows, padded), lambda j, b: (0, 0))
    return pl.pallas_call(
        functools.partial(partial_kernel, width),
        grid_spec=pltpu.PrefetchScalarGridSpec(
            num_scalar_prefetch=1,
            grid=(steps,),
            in_specs=[*(whole(p) for p in pieces), strip(wo), strip(wr), whole(uo), whole(ur), strip(down)],
            out_specs=[out] * 4,
            scratch_shapes=[
                pltpu.VMEM((4 * rows, 2 * half), jnp.bfloat16),
                pltpu.VMEM((4 * rows, 48), jnp.bfloat16),
                pltpu.VMEM((4 * rows, steps * tile), jnp.float32),
            ],
        ),
        out_shape=[jax.ShapeDtypeStruct((rows, padded), jnp.float32)]
        + [jax.ShapeDtypeStruct((rows, padded), jnp.bfloat16)] * 3,
        compiler_params=pltpu.CompilerParams(vmem_limit_bytes=40 << 20),
        cost_estimate=pl.CostEstimate(
            flops=2 * 4 * rows * 2 * half * width, bytes_accessed=4 * width * half + 16 * rows * half, transcendentals=0
        ),
        name="partial",
    )(base, *pieces, wo, wr, uo, ur, down)


def fold_kernel(width, swap, own, a, b, c, keep, send):
    rows = keep.shape[0]
    total = own[...]
    for r in (a, b, c):
        total = total + decode(r[...], width)
    first, second = total[:rows], total[rows:]
    swapped = swap[0] == 1
    keep[...] = jnp.where(swapped, second, first)
    send[...] = encode(jnp.where(swapped, first, second), width, total.shape[1])


def fold(swap, own, received, width):
    rows, padded = own.shape
    vmem = pl.BlockSpec(memory_space=pltpu.VMEM)
    return pl.pallas_call(
        functools.partial(fold_kernel, width),
        in_specs=[pl.BlockSpec(memory_space=pltpu.SMEM)] + [vmem] * 4,
        out_specs=[vmem] * 2,
        out_shape=[
            jax.ShapeDtypeStruct((rows // 2, padded), jnp.float32),
            jax.ShapeDtypeStruct((rows // 2, padded), jnp.bfloat16),
        ],
        cost_estimate=pl.CostEstimate(flops=20 * rows * padded, bytes_accessed=16 * rows * padded, transcendentals=6 * rows * padded),
        name="fold",
    )(swap, own, *received)


def finish_kernel(width, *refs):
    n = (len(refs) - 1) // 2
    out = refs[-1]
    at = 0
    for keep, got in zip(refs[:n], refs[n : 2 * n]):
        rows = keep.shape[0]
        total = keep[...] + decode(got[...], width)
        out[at : at + rows, :] = total[:, :width].astype(out.dtype)
        at += rows


def finish(keeps, gots, width):
    vmem = pl.BlockSpec(memory_space=pltpu.VMEM)
    rows = sum(k.shape[0] for k in keeps)
    return pl.pallas_call(
        functools.partial(finish_kernel, width),
        in_specs=[vmem] * (2 * len(keeps)),
        out_specs=vmem,
        out_shape=jax.ShapeDtypeStruct((rows, width), jnp.bfloat16),
        name="finish",
    )(*keeps, *gots)


def ahead(array, axis, step):
    n = SIZES[AXES.index(axis)]
    return lax.ppermute(array, axis, [(i, (i + step) % n) for i in range(n)])


def across(array, axis, bit):
    n = SIZES[AXES.index(axis)]
    return lax.ppermute(array, axis, [(i, i ^ bit) for i in range(n)])


def on_device(inputs, cotangent, weight, adapter_down_factor, adapter_up_factor):
    y, xl, core, z, xh = (lax.axis_index(a) for a in AXES)
    row_position = (y * 2 + xl) * 2 + core
    column_position = z * 2 + xh
    tokens, hidden = cotangent.shape
    width_row_block = inputs.shape[1]
    width = weight.shape[0]
    rows = tokens // 2

    mine = lax.dynamic_slice_in_dim(cotangent, core * rows, rows, 0)
    theirs = lax.dynamic_slice_in_dim(cotangent, (1 - core) * rows, rows, 0)
    other = across(theirs, "core", 1)
    weight_other = across(weight, "core", 1)
    block = jnp.concatenate([mine, other], axis=1)

    up_own = lax.dynamic_slice_in_dim(adapter_up_factor, row_position * hidden, hidden, 1)
    up_other = lax.dynamic_slice_in_dim(adapter_up_factor, (row_position ^ 1) * hidden, hidden, 1)
    down_columns = scaling * lax.dynamic_slice_in_dim(adapter_down_factor, column_position * width, width, 0)
    down3 = jnp.concatenate([down_columns] * 3, axis=1)
    down_rows = lax.dynamic_slice_in_dim(adapter_down_factor, row_position * width_row_block, width_row_block, 0)

    low_part = dot_t(up_own, cotangent)
    proj_part = lax.dot_general(down_rows, inputs, (((0,), (1,)), ((), ())), preferred_element_type=jnp.float32)
    small = jnp.concatenate([low_part, proj_part], axis=0)
    for axis, bit in (("core", 1), ("xl", 1), ("y", 1), ("y", 2)):
        small = small + across(small, axis, bit)
    rank = low_part.shape[0]
    low48 = jnp.concatenate(pieces3(scaling * small[:rank]), axis=0)
    proj48 = jnp.concatenate(pieces3(scaling * small[rank:]), axis=0)

    def three(left, right):
        out = jnp.dot(left, right, preferred_element_type=jnp.float32)
        return out[:rank] + (out[rank : 2 * rank] + out[2 * rank :])

    parts = jnp.concatenate([three(low48, inputs), three(proj48, cotangent)], axis=1)

    base = jnp.reshape(lax.rem(z - y + 4, 4), (1,)).astype(jnp.int32)
    swap = jnp.reshape(xl ^ xh, (1,)).astype(jnp.int32)

    m = rows // CHUNKS
    keeps, gots = [], []
    for s in range(CHUNKS):
        own = block[s * m : (s + 1) * m]
        pair = jnp.concatenate([own, across(own, "xh", 1)], axis=0)
        below = ahead(pair, "z", 1)
        above = ahead(pair, "z", 3)
        far = ahead(below, "z", 1) if s % 2 == 0 else ahead(above, "z", 3)
        kept, o1, o2, o3 = partial(base, (pair, below, above, far), weight, weight_other, up_own, up_other, down3)
        received = (ahead(o1, "y", 1), ahead(o3, "y", 3), ahead(o2, "y", 2))
        keep, send = fold(swap, kept, received, width)
        keeps.append(keep)
        gots.append(across(send, "xl", 1))
    grad_input = finish(keeps, gots, width)

    for axis, bit in (("xh", 1), ("z", 1), ("z", 2)):
        parts = parts + across(parts, axis, bit)
    grad_a = parts[:, :width_row_block].T
    grad_b = parts[:, width_row_block:]
    return grad_input, grad_a, grad_b


def solution(mesh):
    fine = Mesh(mesh.devices.reshape(SIZES), AXES)
    in_specs = (P(COL, ROW), P(COL, ROW), P(COL, ROW), P(), P())
    out_specs = (P(ROW, COL), P(ROW, None), P(None, ROW))
    return jax.shard_map(on_device, mesh=fine, in_specs=in_specs, out_specs=out_specs, check_vma=False)
```

time: 413 us -> 193 us (0.47)
  waiting for transfers between devices: 255 us -> 39.2 us
  blocking collectives: 101 us -> 0 us
  starting transfers between devices: 0.12 us -> 66.6 us
  Pallas kernels: 0 us -> 57.4 us
  matrix products: 38.3 us -> 4.28 us
  local copies, waits for them, and re-layouts: 2.51 us -> 19.2 us
  between operations: 13.8 us -> 1.08 us
    all_gather x1 -> x0, waiting for transfers between devices: 107 us -> none  [on_device(): gathered = lax.all_gather(cotangent, 'col', axis=0, tiled=True)]
    psum x2 -> x0, blocking collectives: 101 us -> none  [the longest x1 57.7 us: on_device(): gradient_lowrank, projected_rows = lax.psum((low_part, proj_part), 'row')]
    psum x1 -> x0, waiting for transfers between devices: 83.6 us -> none  [on_device(): grad_a, grad_b = lax.psum((part_a, part_b), 'col')]
    ppermute x0 -> x41, starting transfers between devices: none -> 66.6 us  [the longest x24 40.7 us: ahead(): return lax.ppermute(array, axis, [(i, (i + step) % n) for i in range(n)])]
    reduce_scatter x1 -> x0, waiting for transfers between devices: 63.4 us -> none  [on_device(): lax.psum_scatter(partial_rows(gathered, weight, up_weight_slice, down_fac...]
    pallas_call x0 -> x9, Pallas kernels: none -> 57.4 us  [the longest x4 43.5 us: partial(): pl.pallas_call(functools.partial(partial_kernel, width), grid_spec=pltpu....]
    ppermute x0 -> x41, waiting for transfers between devices: none -> 39.2 us  [the longest x17 24.8 us: across(): return lax.ppermute(array, axis, [(i, i ^ bit) for i in range(n)])]
    dot_general x7 -> x4, matrix products: 38.3 us -> 4.28 us  [the longest x2 1.76 us: three(): out = jnp.dot(left, right, preferred_element_type=jnp.float32)]
  transfers between devices with their start and end apart: 3 -> 41, of which waited for: 3 -> 12; matrix products, arithmetic and copies ran while one was open for 1% -> 7% of each run, Pallas kernels for 0% -> 29%
where the time goes in v1:
time: 193 us; the launch traced here: 191 us
  starting transfers between devices  66.6 us (35%)
  Pallas kernels  57.4 us (30%)
  waiting for transfers between devices  39.2 us (20%)
  local copies, waits for them, and re-layouts  19.2 us (10%)
  matrix products  4.28 us (2%)
  other arithmetic  3.81 us (2%)
    pallas_call x4, Pallas kernels, partial(): pl.pallas_call(functools.partial(partial_kernel, width), grid_spec=pltpu....  43.5 us
    ppermute x24, starting transfers between devices, ahead(): return lax.ppermute(array, axis, [(i, (i + step) % n) for i in range(n)])  40.7 us
    ppermute x17, starting transfers between devices, across(): return lax.ppermute(array, axis, [(i, i ^ bit) for i in range(n)])  25.8 us
    ppermute x17, waiting for transfers between devices, across(): return lax.ppermute(array, axis, [(i, i ^ bit) for i in range(n)])  24.8 us
    unnamed x61, local copies, waits for them, and re-layouts  14.4 us
    ppermute x24, waiting for transfers between devices, ahead(): return lax.ppermute(array, axis, [(i, (i + step) % n) for i in range(n)])  14.3 us
    pallas_call x4, Pallas kernels, fold(): pl.pallas_call(functools.partial(fold_kernel, width), in_specs=[pl.BlockS...  11.1 us
  transfers between devices with their start and end apart: 41, of which 12 were waited for; matrix products, arithmetic and copies ran while one was open for 7% of the time, Pallas kernels for 29%

profile of v1, /device:TPU:0, one launch (start us, length us, event | category | flops | bytes accessed | tf_op | source)
XLA Modules:
  0.0 191.5 jit_solution(2567077022630740614)
XLA Ops:
  0.8 0.9 constant_dynamic-slice_fusion
  1.7 1.0 fusion.5
  2.7 1.5 fusion.26
  4.8 7.4 %collective-permute-done.34 = f32[32,256]{1,0:T(8,128)S(1)} collective-permute-done((f32[32,256]{1,0:T(8,128)S(1)}, f32[32,256]{1,0:T(8,128)S(1)}, u32[]{:S(2)}, u32[]{:S(2)}) %collective-permute-start.34) | collective-permute-done | bytes 32800 | tf_op jit(solution)/shard_map/ppermute | solution.py:190
  12.1 1.6 collective-permute-start.35
  13.7 2.3 %collective-permute-done.35 = f32[32,256]{1,0:T(8,128)S(1)} collective-permute-done((f32[32,256]{1,0:T(8,128)S(1)}, f32[32,256]{1,0:T(8,128)S(1)}, u32[]{:S(2)}, u32[]{:S(2)}) %collective-permute-start.35) | collective-permute-done | bytes 32800 | tf_op jit(solution)/shard_map/ppermute | solution.py:190
  16.1 1.7 collective-permute-start.36
  17.7 1.2 constant_dynamic-slice_fusion.2
  19.1 0.9 collective-permute-done.36
  20.0 3.3 %collective-permute-start.37 = (f32[32,256]{1,0:T(8,128)S(1)}, f32[32,256]{1,0:T(8,128)S(1)}, u32[]{:S(2)}, u32[]{:S(2)}) collective-permute-start(f32[32,256]{1,0:T(8,128)S(1)} %add.75), channel_id=1, source_target_pairs={{0,64},{32,96},{64,0},{96,32},{1,65},{33,97},{65,1},{97,33},{2,66}... | collective-permute-start | bytes 98312 | tf_op jit(solution)/shard_map/ppermute | solution.py:190
  23.3 1.6 dynamic-slice_multiply_fusion
  25.7 1.5 fusion.13
  27.3 3.2 %collective-permute-start.38 = (f32[16,2848]{1,0:T(8,128)S(1)}, f32[16,2848]{1,0:T(8,128)S(1)}, u32[]{:S(2)}, u32[]{:S(2)}) collective-permute-start(f32[16,2848]{1,0:T(8,128)S(1)} %pad_maximum_fusion.5), channel_id=1, source_target_pairs={{0,1},{1,0},{2,3},{3,2},{4,5},{5,4},{6,7},{7,6},{8,9},{9,8},{10,11... | collective-permute-start | bytes 546824 | tf_op jit(solution)/shard_map/ppermute | solution.py:190
  31.1 5.0 %collective-permute-done.38 = f32[16,2848]{1,0:T(8,128)S(1)} collective-permute-done((f32[16,2848]{1,0:T(8,128)S(1)}, f32[16,2848]{1,0:T(8,128)S(1)}, u32[]{:S(2)}, u32[]{:S(2)}) %collective-permute-start.38) | collective-permute-done | bytes 182304 | tf_op jit(solution)/shard_map/ppermute | solution.py:190
  36.3 2.2 %collective-permute-start.39 = (f32[16,2848]{1,0:T(8,128)S(1)}, f32[16,2848]{1,0:T(8,128)S(1)}, u32[]{:S(2)}, u32[]{:S(2)}) collective-permute-start(f32[16,2848]{1,0:T(8,128)S(1)} %fusion.25), channel_id=1, source_target_pairs={{0,2},{2,0},{4,6},{6,4},{1,3},{3,1},{5,7},{7,5},{8,10},{10,8},{12,... | collective-permute-start | bytes 546824 | tf_op jit(solution)/shard_map/ppermute | solution.py:190
  38.4 3.4 %collective-permute-start.9 = (bf16[32,3840]{1,0:T(8,128)(2,1)S(1)}, bf16[32,3840]{1,0:T(8,128)(2,1)S(1)}, u32[]{:S(2)}, u32[]{:S(2)}) collective-permute-start(bf16[32,3840]{1,0:T(8,128)(2,1)S(1)} %get-tuple-element.59), channel_id=1, source_target_pairs={{0,1},{1,0},{2,3},{3,2},{4,5},{5,4},{6,7},{7,6},{8,9},{9,8},{10,11... | collective-permute-start | bytes 737288 | tf_op jit(solution)/shard_map/ppermute | solution.py:190
  42.0 3.4 %collective-permute-start.23 = (bf16[32,3840]{1,0:T(8,128)(2,1)S(1)}, bf16[32,3840]{1,0:T(8,128)(2,1)S(1)}, u32[]{:S(2)}, u32[]{:S(2)}) collective-permute-start(bf16[32,3840]{1,0:T(8,128)(2,1)S(1)} %get-tuple-element.57), channel_id=1, source_target_pairs={{0,1},{1,0},{2,3},{3,2},{4,5},{5,4},{6,7},{7,6},{8,9},{9,8},{10,11... | collective-permute-start | bytes 737288 | tf_op jit(solution)/shard_map/ppermute | solution.py:190
  45.4 1.6 collective-permute-start.2
  47.0 1.8 collective-permute-done.9
  48.8 2.5 %collective-permute-start.3 = (bf16[64,3840]{1,0:T(8,128)(2,1)S(1)}, bf16[64,3840]{1,0:T(8,128)(2,1)S(1)}, u32[]{:S(2)}, u32[]{:S(2)}) collective-permute-start(bf16[64,3840]{1,0:T(8,128)(2,1)S(1)} %pad_maximum_fusion.c0), channel_id=1, source_target_pairs={{0,6},{2,0},{4,2},{6,4},{1,7},{3,1},{5,3},{7,5},{8,14},{10,8},{12,... | collective-permute-start | bytes 1474568 | tf_op jit(solution)/shard_map/ppermute | solution.py:185
  51.4 1.5 collective-permute-done.16
  52.9 1.3 collective-permute-start.10
  54.2 1.4 collective-permute-done.23
  55.6 4.1 %collective-permute-start.11 = (bf16[64,3840]{1,0:T(8,128)(2,1)S(1)}, bf16[64,3840]{1,0:T(8,128)(2,1)}, u32[]{:S(2)}, u32[]{:S(2)}) collective-permute-start(bf16[64,3840]{1,0:T(8,128)(2,1)S(1)} %pad_maximum_fusion.1.c0), channel_id=1, source_target_pairs={{0,6},{2,0},{4,2},{6,4},{1,7},{3,1},{5,3},{7,5},{8,14},{10,8},{12,... | collective-permute-start | bytes 1474568 | tf_op jit(solution)/shard_map/ppermute | solution.py:185
  59.8 0.8 copy-done.5
  60.6 2.5 %collective-permute-start.4 = (bf16[64,3840]{1,0:T(8,128)(2,1)}, bf16[64,3840]{1,0:T(8,128)(2,1)}, u32[]{:S(2)}, u32[]{:S(2)}) collective-permute-start(bf16[64,3840]{1,0:T(8,128)(2,1)} %collective-permute-done.2.c1), channel_id=1, source_target_pairs={{0,2},{2,4},{4,6},{6,0},{1,3},{3,5},{5,7},{7,1},{8,10},{10,12},{12... | collective-permute-start | bytes 1474568 | tf_op jit(solution)/shard_map/ppermute | solution.py:185
  63.1 6.0 %collective-permute-done.10.c1 = bf16[64,3840]{1,0:T(8,128)(2,1)S(1)} collective-permute-done((bf16[64,3840]{1,0:T(8,128)(2,1)S(1)}, bf16[64,3840]{1,0:T(8,128)(2,1)S(1)}, u32[]{:S(2)}, u32[]{:S(2)}) %collective-permute-start.10) | collective-permute-done | bytes 491552 | tf_op jit(solution)/shard_map/ppermute | solution.py:185
  69.1 0.8 copy-done.3
  69.9 2.3 %collective-permute-start.25 = (bf16[64,3840]{1,0:T(8,128)(2,1)S(1)}, bf16[64,3840]{1,0:T(8,128)(2,1)S(1)}, u32[]{:S(2)}, u32[]{:S(2)}) collective-permute-start(bf16[64,3840]{1,0:T(8,128)(2,1)S(1)} %pad_maximum_fusion.3.c0), channel_id=1, source_target_pairs={{0,6},{2,0},{4,2},{6,4},{1,7},{3,1},{5,3},{7,5},{8,14},{10,8},{12,... | collective-permute-start | bytes 1474568 | tf_op jit(solution)/shard_map/ppermute | solution.py:185
  72.2 1.9 collective-permute-start.12
  74.8 1.2 copy.10.down
  76.0 1.0 add.82
  77.1 2.7 %collective-permute-done.17.c1 = bf16[64,3840]{1,0:T(8,128)(2,1)} collective-permute-done((bf16[64,3840]{1,0:T(8,128)(2,1)S(1)}, bf16[64,3840]{1,0:T(8,128)(2,1)}, u32[]{:S(2)}, u32[]{:S(2)}) %collective-permute-start.17) | collective-permute-done | bytes 491552 | tf_op jit(solution)/shard_map/ppermute | solution.py:185
  79.8 2.3 %collective-permute-start.18 = (bf16[64,3840]{1,0:T(8,128)(2,1)S(1)}, bf16[64,3840]{1,0:T(8,128)(2,1)S(1)}, u32[]{:S(2)}, u32[]{:S(2)}) collective-permute-start(bf16[64,3840]{1,0:T(8,128)(2,1)S(1)} %pad_maximum_fusion.2.c0), channel_id=1, source_target_pairs={{0,6},{2,0},{4,2},{6,4},{1,7},{3,1},{5,3},{7,5},{8,14},{10,8},{12,... | collective-permute-start | bytes 1474568 | tf_op jit(solution)/shard_map/ppermute | solution.py:185
  82.1 5.6 %collective-permute-done.4.c3 = bf16[64,3840]{1,0:T(8,128)(2,1)} collective-permute-done((bf16[64,3840]{1,0:T(8,128)(2,1)}, bf16[64,3840]{1,0:T(8,128)(2,1)}, u32[]{:S(2)}, u32[]{:S(2)}) %collective-permute-start.4) | collective-permute-done | bytes 491552 | tf_op jit(solution)/shard_map/ppermute | solution.py:185
  88.1 2.5 %collective-permute-start.19 = (bf16[64,3840]{1,0:T(8,128)(2,1)}, bf16[64,3840]{1,0:T(8,128)(2,1)S(1)}, u32[]{:S(2)}, u32[]{:S(2)}) collective-permute-start(bf16[64,3840]{1,0:T(8,128)(2,1)} %collective-permute-done.17.c1), channel_id=1, source_target_pairs={{0,2},{2,4},{4,6},{6,0},{1,3},{3,5},{5,7},{7,1},{8,10},{10,12},{12... | collective-permute-start | bytes 1474568 | tf_op jit(solution)/shard_map/ppermute | solution.py:185
  90.6 3.0 %copy-done.1 = bf16[1856,1920]{1,0:T(8,128)(2,1)S(1)} copy-done((bf16[1856,1920]{1,0:T(8,128)(2,1)S(1)}, bf16[1856,1920]{1,0:T(8,128)(2,1)}, u32[]{:S(2)}) %copy-start.1) | copy-done | bytes 7127064
  93.6 1.0 copy-done.6
  94.6 10.8 %partial.4 = (f32[64,1920]{1,0:T(8,128)S(1)}, bf16[64,1920]{1,0:T(8,128)(2,1)S(1)}, bf16[64,1920]{1,0:T(8,128)(2,1)S(1)}, bf16[64,1920]{1,0:T(8,128)(2,1)S(1)}) custom-call(s32[1]{0:T(128)} %bitcast.1.base, bf16[64,3840]{1,0:T(8,128)(2,1)S(1)} %pad_maximum_fusion.c0, bf16[64,3840]{1,0:T(8,128)(2,1)} %collective-permute-done.2.c1, ...), custom_call_target="tpu_custom_call" | custom-call | flops 3649044480 | bytes 16220160 | tf_op jit(solution)/shard_map/partial/pallas_call | solution.py:110
  105.4 0.8 copy-done.7
  106.3 1.8 collective-permute-start.40
  108.0 1.5 collective-permute-start.26
  109.5 3.0 %copy-done.2 = bf16[1856,1920]{1,0:T(8,128)(2,1)S(1)} copy-done((bf16[1856,1920]{1,0:T(8,128)(2,1)S(1)}, bf16[1856,1920]{1,0:T(8,128)(2,1)}, u32[]{:S(2)}) %copy-start.2) | copy-done | bytes 7127064
  112.6 10.8 %partial.5 = (f32[64,1920]{1,0:T(8,128)S(1)}, bf16[64,1920]{1,0:T(8,128)(2,1)S(1)}, bf16[64,1920]{1,0:T(8,128)(2,1)S(1)}, bf16[64,1920]{1,0:T(8,128)(2,1)S(1)}) custom-call(s32[1]{0:T(128)} %bitcast.1.base, bf16[64,3840]{1,0:T(8,128)(2,1)S(1)} %pad_maximum_fusion.1.c0, bf16[64,3840]{1,0:T(8,128)(2,1)S(1)} %copy-done.4, ...), custom_call_target="tpu_custom_call" | custom-call | flops 3649044480 | bytes 16220160 | tf_op jit(solution)/shard_map/partial/pallas_call | solution.py:110
  123.3 0.8 copy-done.8
  124.1 1.8 collective-permute-start.6
  126.0 1.5 collective-permute-start.7
  127.4 2.1 %collective-permute-start.8 = (bf16[64,1920]{1,0:T(8,128)(2,1)S(1)}, bf16[64,1920]{1,0:T(8,128)(2,1)S(1)}, u32[]{:S(2)}, u32[]{:S(2)}) collective-permute-start(bf16[64,1920]{1,0:T(8,128)(2,1)S(1)} %get-tuple-element.30), channel_id=1, source_target_pairs={{0,64},{32,96},{64,0},{96,32},{1,65},{33,97},{65,1},{97,33},{2,66}... | collective-permute-start | bytes 737288 | tf_op jit(solution)/shard_map/ppermute | solution.py:185
  130.3 10.6 %partial.6 = (f32[64,1920]{1,0:T(8,128)S(1)}, bf16[64,1920]{1,0:T(8,128)(2,1)S(1)}, bf16[64,1920]{1,0:T(8,128)(2,1)S(1)}, bf16[64,1920]{1,0:T(8,128)(2,1)S(1)}) custom-call(s32[1]{0:T(128)} %bitcast.1.base, bf16[64,3840]{1,0:T(8,128)(2,1)S(1)} %pad_maximum_fusion.2.c0, bf16[64,3840]{1,0:T(8,128)(2,1)} %collective-permute-done.17.c1, ...), custom_call_target="tpu_custom_call" | custom-call | flops 3649044480 | bytes 16220160 | tf_op jit(solution)/shard_map/partial/pallas_call | solution.py:110
  140.9 2.6 %collective-permute-start.14 = (bf16[64,1920]{1,0:T(8,128)(2,1)S(1)}, bf16[64,1920]{1,0:T(8,128)(2,1)S(1)}, u32[]{:S(2)}, u32[]{:S(2)}) collective-permute-start(bf16[64,1920]{1,0:T(8,128)(2,1)S(1)} %get-tuple-element.34), channel_id=1, source_target_pairs={{0,96},{32,0},{64,32},{96,64},{1,97},{33,1},{65,33},{97,65},{2,98}... | collective-permute-start | bytes 737288 | tf_op jit(solution)/shard_map/ppermute | solution.py:185
  143.7 0.8 collective-permute-start.20
  144.5 2.5 %collective-permute-start.21 = (bf16[64,1920]{1,0:T(8,128)(2,1)S(1)}, bf16[64,1920]{1,0:T(8,128)(2,1)}, u32[]{:S(2)}, u32[]{:S(2)}) collective-permute-start(bf16[64,1920]{1,0:T(8,128)(2,1)S(1)} %get-tuple-element.39), channel_id=1, source_target_pairs={{0,96},{32,0},{64,32},{96,64},{1,97},{33,1},{65,33},{97,65},{2,98}... | collective-permute-start | bytes 737288 | tf_op jit(solution)/shard_map/ppermute | solution.py:185
  147.0 2.1 %collective-permute-start.22 = (bf16[64,1920]{1,0:T(8,128)(2,1)S(1)}, bf16[64,1920]{1,0:T(8,128)(2,1)}, u32[]{:S(2)}, u32[]{:S(2)}) collective-permute-start(bf16[64,1920]{1,0:T(8,128)(2,1)S(1)} %get-tuple-element.40), channel_id=1, source_target_pairs={{0,64},{32,96},{64,0},{96,32},{1,65},{33,97},{65,1},{97,33},{2,66}... | collective-permute-start | bytes 737288 | tf_op jit(solution)/shard_map/ppermute | solution.py:185
  149.1 11.4 %partial.7 = (f32[64,1920]{1,0:T(8,128)S(1)}, bf16[64,1920]{1,0:T(8,128)(2,1)}, bf16[64,1920]{1,0:T(8,128)(2,1)}, bf16[64,1920]{1,0:T(8,128)(2,1)}) custom-call(s32[1]{0:T(128)} %bitcast.1.base, bf16[64,3840]{1,0:T(8,128)(2,1)S(1)} %pad_maximum_fusion.3.c0, bf16[64,3840]{1,0:T(8,128)(2,1)S(1)} %collective-permute-done.24.c1, ...), custom_call_target="tpu_custom_call" | custom-call | flops 3649044480 | bytes 16220160 | tf_op jit(solution)/shard_map/partial/pallas_call | solution.py:110
  160.6 3.2 %collective-permute-start.28 = (bf16[64,1920]{1,0:T(8,128)(2,1)}, bf16[64,1920]{1,0:T(8,128)(2,1)S(1)}, u32[]{:S(2)}, u32[]{:S(2)}) collective-permute-start(bf16[64,1920]{1,0:T(8,128)(2,1)} %get-tuple-element.44), channel_id=1, source_target_pairs={{0,96},{32,0},{64,32},{96,64},{1,97},{33,1},{65,33},{97,65},{2,98}... | collective-permute-start | bytes 737288 | tf_op jit(solution)/shard_map/ppermute | solution.py:185
  165.5 2.8 %fold.4 = (f32[32,1920]{1,0:T(8,128)}, bf16[32,1920]{1,0:T(8,128)(2,1)}) custom-call(s32[1]{0:T(128)} %bitcast.swap, f32[64,1920]{1,0:T(8,128)} %copy-done.7, bf16[64,1920]{1,0:T(8,128)(2,1)} %copy-done.20, bf16[64,1920]{1,0:T(8,128)(2,1)} %copy-done.21, bf16[64,1920]{1,0:T(8,128)(2,1)} %copy-done.22), custom_call_target="tpu_custom_call" | custom-call | flops 2457600 | bytes 1966080 | tf_op jit(solution)/shard_map/fold/pallas_call | solution.py:147
  168.3 2.8 %fold.5 = (f32[32,1920]{1,0:T(8,128)}, bf16[32,1920]{1,0:T(8,128)(2,1)}) custom-call(s32[1]{0:T(128)} %bitcast.swap, f32[64,1920]{1,0:T(8,128)} %copy-done.8, bf16[64,1920]{1,0:T(8,128)(2,1)} %copy-done.23, bf16[64,1920]{1,0:T(8,128)(2,1)} %copy-done.25, bf16[64,1920]{1,0:T(8,128)(2,1)} %copy-done.26), custom_call_target="tpu_custom_call" | custom-call | flops 2457600 | bytes 1966080 | tf_op jit(solution)/shard_map/fold/pallas_call | solution.py:147
  171.0 1.5 collective-permute-start.30
  173.0 2.8 %fold.6 = (f32[32,1920]{1,0:T(8,128)}, bf16[32,1920]{1,0:T(8,128)(2,1)}) custom-call(s32[1]{0:T(128)} %bitcast.swap, f32[64,1920]{1,0:T(8,128)} %copy-done.9, bf16[64,1920]{1,0:T(8,128)(2,1)} %copy-done.24, bf16[64,1920]{1,0:T(8,128)(2,1)} %collective-permute-done.21.b, bf16[64,1920]{1,0:T(8,128)(2,1)} %collective-permute-done.22.c), custom_call_target="tpu_custom_call" | custom-call | flops 2457600 | bytes 1966080 | tf_op jit(solution)/shard_map/fold/pallas_call | solution.py:147
  175.8 1.5 collective-permute-start.32
  178.1 2.8 %fold.7 = (f32[32,1920]{1,0:T(8,128)}, bf16[32,1920]{1,0:T(8,128)(2,1)}) custom-call(s32[1]{0:T(128)} %bitcast.swap, f32[64,1920]{1,0:T(8,128)} %copy-done.10, bf16[64,1920]{1,0:T(8,128)(2,1)} %copy-done.27, bf16[64,1920]{1,0:T(8,128)(2,1)} %copy-done.28, bf16[64,1920]{1,0:T(8,128)(2,1)} %copy-done.29), custom_call_target="tpu_custom_call" | custom-call | flops 2457600 | bytes 1966080 | tf_op jit(solution)/shard_map/fold/pallas_call | solution.py:147
  182.1 3.9 %collective-permute-done.33.refs_7_ = bf16[32,1920]{1,0:T(8,128)(2,1)S(1)} collective-permute-done((bf16[32,1920]{1,0:T(8,128)(2,1)}, bf16[32,1920]{1,0:T(8,128)(2,1)S(1)}, u32[]{:S(2)}, u32[]{:S(2)}) %collective-permute-start.33) | collective-permute-done | bytes 122912 | tf_op jit(solution)/shard_map/ppermute | solution.py:190
  186.7 2.8 %finish.1 = bf16[128,1856]{1,0:T(8,128)(2,1)} custom-call(f32[32,1920]{1,0:T(8,128)} %get-tuple-element.31.refs_0_, f32[32,1920]{1,0:T(8,128)} %get-tuple-element.36.refs_1_, f32[32,1920]{1,0:T(8,128)} %get-tuple-element.41.refs_2_, f32[32,1920]{1,0:T(8,128)} %get-tuple-element.46.refs_3_, bf16[32,1920]{1,0:T(8,128)(2,1)} %copy-done.16, ...), custom_call_target="tpu_custom_call" | custom-call | tf_op jit(solution)/shard_map/finish/pallas_call | solution.py:174
  189.5 2.0 %copy.14 = bf16[128,1856]{0,1:T(8,128)(2,1)} copy(bf16[128,1856]{1,0:T(8,128)(2,1)} %finish.1) | data formatting | bytes 950272
  (116 shorter events, 9.9 us)
Async XLA Ops:
  0.6 1.0 copy-start
  0.6 87.4 %collective-permute-start.5 = (bf16[1856,1920]{1,0:T(8,128)(2,1)}, bf16[1856,1920]{1,0:T(8,128)(2,1)}, u32[]{:S(2)}, u32[]{:S(2)}) collective-permute-start(bf16[1856,1920]{1,0:T(8,128)(2,1)} %wo.7), channel_id=1, source_target_pairs={{0,8},{8,0},{1,9},{9,1},{2,10},{10,2},{3,11},{11,3},{4,12},{12,4},... | collective-permute-start | bytes 21381128 | tf_op jit(solution)/shard_map/ppermute | solution.py:190
  4.2 7.9 %collective-permute-start.34 = (f32[32,256]{1,0:T(8,128)S(1)}, f32[32,256]{1,0:T(8,128)S(1)}, u32[]{:S(2)}, u32[]{:S(2)}) collective-permute-start(f32[32,256]{1,0:T(8,128)S(1)} %pad_maximum_fusion.7), channel_id=1, source_target_pairs={{0,8},{8,0},{1,9},{9,1},{2,10},{10,2},{3,11},{11,3},{4,12},{12,4},... | collective-permute-start | bytes 98312 | tf_op jit(solution)/shard_map/ppermute | solution.py:190
  12.1 3.9 %collective-permute-start.35 = (f32[32,256]{1,0:T(8,128)S(1)}, f32[32,256]{1,0:T(8,128)S(1)}, u32[]{:S(2)}, u32[]{:S(2)}) collective-permute-start(f32[32,256]{1,0:T(8,128)S(1)} %fusion.24), channel_id=1, source_target_pairs={{0,16},{16,0},{1,17},{17,1},{2,18},{18,2},{3,19},{19,3},{4,20},{20... | collective-permute-start | bytes 98312 | tf_op jit(solution)/shard_map/ppermute | solution.py:190
  16.1 3.9 %collective-permute-start.36 = (f32[32,256]{1,0:T(8,128)S(1)}, f32[32,256]{1,0:T(8,128)S(1)}, u32[]{:S(2)}, u32[]{:S(2)}) collective-permute-start(f32[32,256]{1,0:T(8,128)S(1)} %add.74), channel_id=1, source_target_pairs={{0,32},{32,0},{64,96},{96,64},{1,33},{33,1},{65,97},{97,65},{2,34}... | collective-permute-start | bytes 98312 | tf_op jit(solution)/shard_map/ppermute | solution.py:190
  19.0 11.6 %collective-permute-start = (bf16[128,1920]{1,0:T(8,128)(2,1)S(1)}, bf16[128,1920]{1,0:T(8,128)(2,1)S(1)}, u32[]{:S(2)}, u32[]{:S(2)}) collective-permute-start(bf16[128,1920]{1,0:T(8,128)(2,1)S(1)} %get-tuple-element.63), channel_id=1, source_target_pairs={{0,8},{8,0},{1,9},{9,1},{2,10},{10,2},{3,11},{11,3},{4,12},{12,4},... | collective-permute-start | bytes 1474568 | tf_op jit(solution)/shard_map/ppermute | solution.py:190
  20.0 5.4 %collective-permute-start.37 = (f32[32,256]{1,0:T(8,128)S(1)}, f32[32,256]{1,0:T(8,128)S(1)}, u32[]{:S(2)}, u32[]{:S(2)}) collective-permute-start(f32[32,256]{1,0:T(8,128)S(1)} %add.75), channel_id=1, source_target_pairs={{0,64},{32,96},{64,0},{96,32},{1,65},{33,97},{65,1},{97,33},{2,66}... | collective-permute-start | bytes 98312 | tf_op jit(solution)/shard_map/ppermute | solution.py:190
  24.8 49.3 %copy-start.14 = (bf16[1856,16]{0,1:T(8,128)(2,1)S(1)}, bf16[1856,16]{0,1:T(8,128)(2,1)}, u32[]{:S(2)}) copy-start(bf16[1856,16]{0,1:T(8,128)(2,1)} %dynamic-slice_multiply_fusion) | copy-start | bytes 178180
  27.3 8.8 %collective-permute-start.38 = (f32[16,2848]{1,0:T(8,128)S(1)}, f32[16,2848]{1,0:T(8,128)S(1)}, u32[]{:S(2)}, u32[]{:S(2)}) collective-permute-start(f32[16,2848]{1,0:T(8,128)S(1)} %pad_maximum_fusion.5), channel_id=1, source_target_pairs={{0,1},{1,0},{2,3},{3,2},{4,5},{5,4},{6,7},{7,6},{8,9},{9,8},{10,11... | collective-permute-start | bytes 546824 | tf_op jit(solution)/shard_map/ppermute | solution.py:190
  30.6 11.4 %collective-permute-start.1 = (bf16[32,3840]{1,0:T(8,128)(2,1)S(1)}, bf16[32,3840]{1,0:T(8,128)(2,1)S(1)}, u32[]{:S(2)}, u32[]{:S(2)}) collective-permute-start(bf16[32,3840]{1,0:T(8,128)(2,1)S(1)} %get-tuple-element.58), channel_id=1, source_target_pairs={{0,1},{1,0},{2,3},{3,2},{4,5},{5,4},{6,7},{7,6},{8,9},{9,8},{10,11... | collective-permute-start | bytes 737288 | tf_op jit(solution)/shard_map/ppermute | solution.py:190
  36.2 10.8 %copy-start.13 = (f32[16,2848]{1,0:T(8,128)}, f32[16,2848]{1,0:T(8,128)S(1)}, u32[]{:S(2)}) copy-start(f32[16,2848]{1,0:T(8,128)S(1)} %fusion.25) | copy-start | bytes 546820
  36.3 9.1 %collective-permute-start.39 = (f32[16,2848]{1,0:T(8,128)S(1)}, f32[16,2848]{1,0:T(8,128)S(1)}, u32[]{:S(2)}, u32[]{:S(2)}) collective-permute-start(f32[16,2848]{1,0:T(8,128)S(1)} %fusion.25), channel_id=1, source_target_pairs={{0,2},{2,0},{4,6},{6,4},{1,3},{3,1},{5,7},{7,5},{8,10},{10,8},{12,... | collective-permute-start | bytes 546824 | tf_op jit(solution)/shard_map/ppermute | solution.py:190
  38.4 10.4 %collective-permute-start.9 = (bf16[32,3840]{1,0:T(8,128)(2,1)S(1)}, bf16[32,3840]{1,0:T(8,128)(2,1)S(1)}, u32[]{:S(2)}, u32[]{:S(2)}) collective-permute-start(bf16[32,3840]{1,0:T(8,128)(2,1)S(1)} %get-tuple-element.59), channel_id=1, source_target_pairs={{0,1},{1,0},{2,3},{3,2},{4,5},{5,4},{6,7},{7,6},{8,9},{9,8},{10,11... | collective-permute-start | bytes 737288 | tf_op jit(solution)/shard_map/ppermute | solution.py:190
  41.8 11.1 %collective-permute-start.16 = (bf16[32,3840]{1,0:T(8,128)(2,1)S(1)}, bf16[32,3840]{1,0:T(8,128)(2,1)S(1)}, u32[]{:S(2)}, u32[]{:S(2)}) collective-permute-start(bf16[32,3840]{1,0:T(8,128)(2,1)S(1)} %get-tuple-element.60), channel_id=1, source_target_pairs={{0,1},{1,0},{2,3},{3,2},{4,5},{5,4},{6,7},{7,6},{8,9},{9,8},{10,11... | collective-permute-start | bytes 737288 | tf_op jit(solution)/shard_map/ppermute | solution.py:190
  42.0 13.6 %collective-permute-start.23 = (bf16[32,3840]{1,0:T(8,128)(2,1)S(1)}, bf16[32,3840]{1,0:T(8,128)(2,1)S(1)}, u32[]{:S(2)}, u32[]{:S(2)}) collective-permute-start(bf16[32,3840]{1,0:T(8,128)(2,1)S(1)} %get-tuple-element.57), channel_id=1, source_target_pairs={{0,1},{1,0},{2,3},{3,2},{4,5},{5,4},{6,7},{7,6},{8,9},{9,8},{10,11... | collective-permute-start | bytes 737288 | tf_op jit(solution)/shard_map/ppermute | solution.py:190
  45.4 6.0 %copy-start.15 = (f32[16,2848]{1,0:T(8,128)}, f32[16,2848]{1,0:T(8,128)S(1)}, u32[]{:S(2)}) copy-start(f32[16,2848]{1,0:T(8,128)S(1)} %collective-permute-done.39) | copy-start | bytes 546820
  45.4 14.3 %collective-permute-start.2 = (bf16[64,3840]{1,0:T(8,128)(2,1)S(1)}, bf16[64,3840]{1,0:T(8,128)(2,1)}, u32[]{:S(2)}, u32[]{:S(2)}) collective-permute-start(bf16[64,3840]{1,0:T(8,128)(2,1)S(1)} %pad_maximum_fusion.c0), channel_id=1, source_target_pairs={{0,2},{2,4},{4,6},{6,0},{1,3},{3,5},{5,7},{7,1},{8,10},{10,12},{12... | collective-permute-start | bytes 1474568 | tf_op jit(solution)/shard_map/ppermute | solution.py:185
  48.8 11.0 %collective-permute-start.3 = (bf16[64,3840]{1,0:T(8,128)(2,1)S(1)}, bf16[64,3840]{1,0:T(8,128)(2,1)S(1)}, u32[]{:S(2)}, u32[]{:S(2)}) collective-permute-start(bf16[64,3840]{1,0:T(8,128)(2,1)S(1)} %pad_maximum_fusion.c0), channel_id=1, source_target_pairs={{0,6},{2,0},{4,2},{6,4},{1,7},{3,1},{5,3},{7,5},{8,14},{10,8},{12,... | collective-permute-start | bytes 1474568 | tf_op jit(solution)/shard_map/ppermute | solution.py:185
  52.9 16.2 %collective-permute-start.10 = (bf16[64,3840]{1,0:T(8,128)(2,1)S(1)}, bf16[64,3840]{1,0:T(8,128)(2,1)S(1)}, u32[]{:S(2)}, u32[]{:S(2)}) collective-permute-start(bf16[64,3840]{1,0:T(8,128)(2,1)S(1)} %pad_maximum_fusion.1.c0), channel_id=1, source_target_pairs={{0,2},{2,4},{4,6},{6,0},{1,3},{3,5},{5,7},{7,1},{8,10},{10,12},{12... | collective-permute-start | bytes 1474568 | tf_op jit(solution)/shard_map/ppermute | solution.py:185
  55.6 16.7 %collective-permute-start.11 = (bf16[64,3840]{1,0:T(8,128)(2,1)S(1)}, bf16[64,3840]{1,0:T(8,128)(2,1)}, u32[]{:S(2)}, u32[]{:S(2)}) collective-permute-start(bf16[64,3840]{1,0:T(8,128)(2,1)S(1)} %pad_maximum_fusion.1.c0), channel_id=1, source_target_pairs={{0,6},{2,0},{4,2},{6,4},{1,7},{3,1},{5,3},{7,5},{8,14},{10,8},{12,... | collective-permute-start | bytes 1474568 | tf_op jit(solution)/shard_map/ppermute | solution.py:185
  59.7 20.1 %collective-permute-start.17 = (bf16[64,3840]{1,0:T(8,128)(2,1)S(1)}, bf16[64,3840]{1,0:T(8,128)(2,1)}, u32[]{:S(2)}, u32[]{:S(2)}) collective-permute-start(bf16[64,3840]{1,0:T(8,128)(2,1)S(1)} %pad_maximum_fusion.2.c0), channel_id=1, source_target_pairs={{0,2},{2,4},{4,6},{6,0},{1,3},{3,5},{5,7},{7,1},{8,10},{10,12},{12... | collective-permute-start | bytes 1474568 | tf_op jit(solution)/shard_map/ppermute | solution.py:185
  60.6 27.0 %collective-permute-start.4 = (bf16[64,3840]{1,0:T(8,128)(2,1)}, bf16[64,3840]{1,0:T(8,128)(2,1)}, u32[]{:S(2)}, u32[]{:S(2)}) collective-permute-start(bf16[64,3840]{1,0:T(8,128)(2,1)} %collective-permute-done.2.c1), channel_id=1, source_target_pairs={{0,2},{2,4},{4,6},{6,0},{1,3},{3,5},{5,7},{7,1},{8,10},{10,12},{12... | collective-permute-start | bytes 1474568 | tf_op jit(solution)/shard_map/ppermute | solution.py:185
  69.9 36.3 %collective-permute-start.25 = (bf16[64,3840]{1,0:T(8,128)(2,1)S(1)}, bf16[64,3840]{1,0:T(8,128)(2,1)S(1)}, u32[]{:S(2)}, u32[]{:S(2)}) collective-permute-start(bf16[64,3840]{1,0:T(8,128)(2,1)S(1)} %pad_maximum_fusion.3.c0), channel_id=1, source_target_pairs={{0,6},{2,0},{4,2},{6,4},{1,7},{3,1},{5,3},{7,5},{8,14},{10,8},{12,... | collective-permute-start | bytes 1474568 | tf_op jit(solution)/shard_map/ppermute | solution.py:185
  72.2 35.8 %collective-permute-start.12 = (bf16[64,3840]{1,0:T(8,128)(2,1)}, bf16[64,3840]{1,0:T(8,128)(2,1)}, u32[]{:S(2)}, u32[]{:S(2)}) collective-permute-start(bf16[64,3840]{1,0:T(8,128)(2,1)} %collective-permute-done.11.c2), channel_id=1, source_target_pairs={{0,6},{2,0},{4,2},{6,4},{1,7},{3,1},{5,3},{7,5},{8,14},{10,8},{12,... | collective-permute-start | bytes 1474568 | tf_op jit(solution)/shard_map/ppermute | solution.py:185
  77.1 29.2 %copy-start.11 = (f32[16,2848]{1,0:T(8,128)}, f32[16,2848]{1,0:T(8,128)S(1)}, u32[]{:S(2)}) copy-start(f32[16,2848]{1,0:T(8,128)S(1)} %add.82) | copy-start | bytes 546820
  79.8 46.2 %collective-permute-start.18 = (bf16[64,3840]{1,0:T(8,128)(2,1)S(1)}, bf16[64,3840]{1,0:T(8,128)(2,1)S(1)}, u32[]{:S(2)}, u32[]{:S(2)}) collective-permute-start(bf16[64,3840]{1,0:T(8,128)(2,1)S(1)} %pad_maximum_fusion.2.c0), channel_id=1, source_target_pairs={{0,6},{2,0},{4,2},{6,4},{1,7},{3,1},{5,3},{7,5},{8,14},{10,8},{12,... | collective-permute-start | bytes 1474568 | tf_op jit(solution)/shard_map/ppermute | solution.py:185
  87.6 39.8 %collective-permute-start.24 = (bf16[64,3840]{1,0:T(8,128)(2,1)S(1)}, bf16[64,3840]{1,0:T(8,128)(2,1)S(1)}, u32[]{:S(2)}, u32[]{:S(2)}) collective-permute-start(bf16[64,3840]{1,0:T(8,128)(2,1)S(1)} %pad_maximum_fusion.3.c0), channel_id=1, source_target_pairs={{0,2},{2,4},{4,6},{6,0},{1,3},{3,5},{5,7},{7,1},{8,10},{10,12},{12... | collective-permute-start | bytes 1474568 | tf_op jit(solution)/shard_map/ppermute | solution.py:185
  88.1 41.5 %collective-permute-start.19 = (bf16[64,3840]{1,0:T(8,128)(2,1)}, bf16[64,3840]{1,0:T(8,128)(2,1)S(1)}, u32[]{:S(2)}, u32[]{:S(2)}) collective-permute-start(bf16[64,3840]{1,0:T(8,128)(2,1)} %collective-permute-done.17.c1), channel_id=1, source_target_pairs={{0,2},{2,4},{4,6},{6,0},{1,3},{3,5},{5,7},{7,1},{8,10},{10,12},{12... | collective-permute-start | bytes 1474568 | tf_op jit(solution)/shard_map/ppermute | solution.py:185
  90.6 3.0 %copy-start.1 = (bf16[1856,1920]{1,0:T(8,128)(2,1)S(1)}, bf16[1856,1920]{1,0:T(8,128)(2,1)}, u32[]{:S(2)}) copy-start(bf16[1856,1920]{1,0:T(8,128)(2,1)} %wo.7) | copy-start | bytes 21381124
  93.6 1.0 copy-start.6
  94.6 14.9 %copy-start.4 = (bf16[64,3840]{1,0:T(8,128)(2,1)S(1)}, bf16[64,3840]{1,0:T(8,128)(2,1)}, u32[]{:S(2)}) copy-start(bf16[64,3840]{1,0:T(8,128)(2,1)} %copy-done.3) | copy-start | bytes 1474564
  105.4 0.8 copy-start.7
  106.3 17.8 %collective-permute-start.40 = (f32[16,2848]{1,0:T(8,128)S(1)}, f32[16,2848]{1,0:T(8,128)S(1)}, u32[]{:S(2)}, u32[]{:S(2)}) collective-permute-start(f32[16,2848]{1,0:T(8,128)S(1)} %add.82), channel_id=1, source_target_pairs={{0,4},{2,6},{4,0},{6,2},{1,5},{3,7},{5,1},{7,3},{8,12},{10,14},{12... | collective-permute-start | bytes 546824 | tf_op jit(solution)/shard_map/ppermute | solution.py:190
  108.0 32.8 %collective-permute-start.26 = (bf16[64,3840]{1,0:T(8,128)(2,1)S(1)}, bf16[64,3840]{1,0:T(8,128)(2,1)S(1)}, u32[]{:S(2)}, u32[]{:S(2)}) collective-permute-start(bf16[64,3840]{1,0:T(8,128)(2,1)S(1)} %collective-permute-done.25.c2), channel_id=1, source_target_pairs={{0,6},{2,0},{4,2},{6,4},{1,7},{3,1},{5,3},{7,5},{8,14},{10,8},{12,... | collective-permute-start | bytes 1474568 | tf_op jit(solution)/shard_map/ppermute | solution.py:185
  109.5 3.0 %copy-start.2 = (bf16[1856,1920]{1,0:T(8,128)(2,1)S(1)}, bf16[1856,1920]{1,0:T(8,128)(2,1)}, u32[]{:S(2)}) copy-start(bf16[1856,1920]{1,0:T(8,128)(2,1)} %wo.7) | copy-start | bytes 21381124
  124.1 19.4 %collective-permute-start.6 = (bf16[64,1920]{1,0:T(8,128)(2,1)S(1)}, bf16[64,1920]{1,0:T(8,128)(2,1)S(1)}, u32[]{:S(2)}, u32[]{:S(2)}) collective-permute-start(bf16[64,1920]{1,0:T(8,128)(2,1)S(1)} %get-tuple-element.28), channel_id=1, source_target_pairs={{0,32},{32,64},{64,96},{96,0},{1,33},{33,65},{65,97},{97,1},{2,34}... | collective-permute-start | bytes 737288 | tf_op jit(solution)/shard_map/ppermute | solution.py:185
  126.0 17.7 %collective-permute-start.7 = (bf16[64,1920]{1,0:T(8,128)(2,1)S(1)}, bf16[64,1920]{1,0:T(8,128)(2,1)S(1)}, u32[]{:S(2)}, u32[]{:S(2)}) collective-permute-start(bf16[64,1920]{1,0:T(8,128)(2,1)S(1)} %get-tuple-element.29), channel_id=1, source_target_pairs={{0,96},{32,0},{64,32},{96,64},{1,97},{33,1},{65,33},{97,65},{2,98}... | collective-permute-start | bytes 737288 | tf_op jit(solution)/shard_map/ppermute | solution.py:185
  127.4 17.0 %collective-permute-start.8 = (bf16[64,1920]{1,0:T(8,128)(2,1)S(1)}, bf16[64,1920]{1,0:T(8,128)(2,1)S(1)}, u32[]{:S(2)}, u32[]{:S(2)}) collective-permute-start(bf16[64,1920]{1,0:T(8,128)(2,1)S(1)} %get-tuple-element.30), channel_id=1, source_target_pairs={{0,64},{32,96},{64,0},{96,32},{1,65},{33,97},{65,1},{97,33},{2,66}... | collective-permute-start | bytes 737288 | tf_op jit(solution)/shard_map/ppermute | solution.py:185
  129.5 17.4 %collective-permute-start.13 = (bf16[64,1920]{1,0:T(8,128)(2,1)S(1)}, bf16[64,1920]{1,0:T(8,128)(2,1)S(1)}, u32[]{:S(2)}, u32[]{:S(2)}) collective-permute-start(bf16[64,1920]{1,0:T(8,128)(2,1)S(1)} %get-tuple-element.33), channel_id=1, source_target_pairs={{0,32},{32,64},{64,96},{96,0},{1,33},{33,65},{65,97},{97,1},{2,34}... | collective-permute-start | bytes 737288 | tf_op jit(solution)/shard_map/ppermute | solution.py:185
  140.9 19.6 %copy-start.9 = (f32[64,1920]{1,0:T(8,128)}, f32[64,1920]{1,0:T(8,128)S(1)}, u32[]{:S(2)}) copy-start(f32[64,1920]{1,0:T(8,128)S(1)} %get-tuple-element.37.own) | copy-start | bytes 1474564
  140.9 19.6 %collective-permute-start.14 = (bf16[64,1920]{1,0:T(8,128)(2,1)S(1)}, bf16[64,1920]{1,0:T(8,128)(2,1)S(1)}, u32[]{:S(2)}, u32[]{:S(2)}) collective-permute-start(bf16[64,1920]{1,0:T(8,128)(2,1)S(1)} %get-tuple-element.34), channel_id=1, source_target_pairs={{0,96},{32,0},{64,32},{96,64},{1,97},{33,1},{65,33},{97,65},{2,98}... | collective-permute-start | bytes 737288 | tf_op jit(solution)/shard_map/ppermute | solution.py:185
  143.5 16.9 %copy-start.20 = (bf16[64,1920]{1,0:T(8,128)(2,1)}, bf16[64,1920]{1,0:T(8,128)(2,1)S(1)}, u32[]{:S(2)}) copy-start(bf16[64,1920]{1,0:T(8,128)(2,1)S(1)} %collective-permute-done.6.a) | copy-start | bytes 737284
  143.5 17.1 %collective-permute-start.15 = (bf16[64,1920]{1,0:T(8,128)(2,1)S(1)}, bf16[64,1920]{1,0:T(8,128)(2,1)S(1)}, u32[]{:S(2)}, u32[]{:S(2)}) collective-permute-start(bf16[64,1920]{1,0:T(8,128)(2,1)S(1)} %get-tuple-element.35), channel_id=1, source_target_pairs={{0,64},{32,96},{64,0},{96,32},{1,65},{33,97},{65,1},{97,33},{2,66}... | collective-permute-start | bytes 737288 | tf_op jit(solution)/shard_map/ppermute | solution.py:185
  143.7 16.7 %copy-start.21 = (bf16[64,1920]{1,0:T(8,128)(2,1)}, bf16[64,1920]{1,0:T(8,128)(2,1)S(1)}, u32[]{:S(2)}) copy-start(bf16[64,1920]{1,0:T(8,128)(2,1)S(1)} %collective-permute-done.7.b) | copy-start | bytes 737284
  143.7 20.1 %collective-permute-start.20 = (bf16[64,1920]{1,0:T(8,128)(2,1)S(1)}, bf16[64,1920]{1,0:T(8,128)(2,1)S(1)}, u32[]{:S(2)}, u32[]{:S(2)}) collective-permute-start(bf16[64,1920]{1,0:T(8,128)(2,1)S(1)} %get-tuple-element.38), channel_id=1, source_target_pairs={{0,32},{32,64},{64,96},{96,0},{1,33},{33,65},{65,97},{97,1},{2,34}... | collective-permute-start | bytes 737288 | tf_op jit(solution)/shard_map/ppermute | solution.py:185
  144.5 16.0 %copy-start.22 = (bf16[64,1920]{1,0:T(8,128)(2,1)}, bf16[64,1920]{1,0:T(8,128)(2,1)S(1)}, u32[]{:S(2)}) copy-start(bf16[64,1920]{1,0:T(8,128)(2,1)S(1)} %collective-permute-done.8.c) | copy-start | bytes 737284
  144.5 26.6 %collective-permute-start.21 = (bf16[64,1920]{1,0:T(8,128)(2,1)S(1)}, bf16[64,1920]{1,0:T(8,128)(2,1)}, u32[]{:S(2)}, u32[]{:S(2)}) collective-permute-start(bf16[64,1920]{1,0:T(8,128)(2,1)S(1)} %get-tuple-element.39), channel_id=1, source_target_pairs={{0,96},{32,0},{64,32},{96,64},{1,97},{33,1},{65,33},{97,65},{2,98}... | collective-permute-start | bytes 737288 | tf_op jit(solution)/shard_map/ppermute | solution.py:185
  147.0 13.5 %copy-start.23 = (bf16[64,1920]{1,0:T(8,128)(2,1)}, bf16[64,1920]{1,0:T(8,128)(2,1)S(1)}, u32[]{:S(2)}) copy-start(bf16[64,1920]{1,0:T(8,128)(2,1)S(1)} %collective-permute-done.13.a) | copy-start | bytes 737284
  147.0 17.8 %copy-start.12 = (f32[16,2848]{1,0:T(8,128)S(1)}, f32[16,2848]{1,0:T(8,128)}, u32[]{:S(2)}) copy-start(f32[16,2848]{1,0:T(8,128)} %copy-done.11) | copy-start | bytes 546820
  147.0 25.5 %collective-permute-start.22 = (bf16[64,1920]{1,0:T(8,128)(2,1)S(1)}, bf16[64,1920]{1,0:T(8,128)(2,1)}, u32[]{:S(2)}, u32[]{:S(2)}) collective-permute-start(bf16[64,1920]{1,0:T(8,128)(2,1)S(1)} %get-tuple-element.40), channel_id=1, source_target_pairs={{0,64},{32,96},{64,0},{96,32},{1,65},{33,97},{65,1},{97,33},{2,66}... | collective-permute-start | bytes 737288 | tf_op jit(solution)/shard_map/ppermute | solution.py:185
  160.4 16.9 %copy-start.10 = (f32[64,1920]{1,0:T(8,128)}, f32[64,1920]{1,0:T(8,128)S(1)}, u32[]{:S(2)}) copy-start(f32[64,1920]{1,0:T(8,128)S(1)} %get-tuple-element.42.own) | copy-start | bytes 1474564
  160.5 4.0 %copy-start.25 = (bf16[64,1920]{1,0:T(8,128)(2,1)}, bf16[64,1920]{1,0:T(8,128)(2,1)S(1)}, u32[]{:S(2)}) copy-start(bf16[64,1920]{1,0:T(8,128)(2,1)S(1)} %collective-permute-done.14.b) | copy-start | bytes 737284
  160.5 15.3 %collective-permute-start.27 = (bf16[64,1920]{1,0:T(8,128)(2,1)}, bf16[64,1920]{1,0:T(8,128)(2,1)S(1)}, u32[]{:S(2)}, u32[]{:S(2)}) collective-permute-start(bf16[64,1920]{1,0:T(8,128)(2,1)} %get-tuple-element.43), channel_id=1, source_target_pairs={{0,32},{32,64},{64,96},{96,0},{1,33},{33,65},{65,97},{97,1},{2,34}... | collective-permute-start | bytes 737288 | tf_op jit(solution)/shard_map/ppermute | solution.py:185
  160.6 3.9 %copy-start.26 = (bf16[64,1920]{1,0:T(8,128)(2,1)}, bf16[64,1920]{1,0:T(8,128)(2,1)S(1)}, u32[]{:S(2)}) copy-start(bf16[64,1920]{1,0:T(8,128)(2,1)S(1)} %collective-permute-done.15.c) | copy-start | bytes 737284
  160.6 16.8 %collective-permute-start.28 = (bf16[64,1920]{1,0:T(8,128)(2,1)}, bf16[64,1920]{1,0:T(8,128)(2,1)S(1)}, u32[]{:S(2)}, u32[]{:S(2)}) collective-permute-start(bf16[64,1920]{1,0:T(8,128)(2,1)} %get-tuple-element.44), channel_id=1, source_target_pairs={{0,96},{32,0},{64,32},{96,64},{1,97},{33,1},{65,33},{97,65},{2,98}... | collective-permute-start | bytes 737288 | tf_op jit(solution)/shard_map/ppermute | solution.py:185
  164.5 12.9 %collective-permute-start.29 = (bf16[64,1920]{1,0:T(8,128)(2,1)}, bf16[64,1920]{1,0:T(8,128)(2,1)S(1)}, u32[]{:S(2)}, u32[]{:S(2)}) collective-permute-start(bf16[64,1920]{1,0:T(8,128)(2,1)} %get-tuple-element.45), channel_id=1, source_target_pairs={{0,64},{32,96},{64,0},{96,32},{1,65},{33,97},{65,1},{97,33},{2,66}... | collective-permute-start | bytes 737288 | tf_op jit(solution)/shard_map/ppermute | solution.py:185
  171.0 11.1 %collective-permute-start.30 = (bf16[32,1920]{1,0:T(8,128)(2,1)}, bf16[32,1920]{1,0:T(8,128)(2,1)S(1)}, u32[]{:S(2)}, u32[]{:S(2)}) collective-permute-start(bf16[32,1920]{1,0:T(8,128)(2,1)} %get-tuple-element.47), channel_id=1, source_target_pairs={{0,16},{16,0},{1,17},{17,1},{2,18},{18,2},{3,19},{19,3},{4,20},{20... | collective-permute-start | bytes 368648 | tf_op jit(solution)/shard_map/ppermute | solution.py:190
  172.5 9.6 %collective-permute-start.31 = (bf16[32,1920]{1,0:T(8,128)(2,1)}, bf16[32,1920]{1,0:T(8,128)(2,1)S(1)}, u32[]{:S(2)}, u32[]{:S(2)}) collective-permute-start(bf16[32,1920]{1,0:T(8,128)(2,1)} %get-tuple-element.48), channel_id=1, source_target_pairs={{0,16},{16,0},{1,17},{17,1},{2,18},{18,2},{3,19},{19,3},{4,20},{20... | collective-permute-start | bytes 368648 | tf_op jit(solution)/shard_map/ppermute | solution.py:190
  175.8 1.6 copy-start.27
  175.8 6.3 %collective-permute-start.32 = (bf16[32,1920]{1,0:T(8,128)(2,1)}, bf16[32,1920]{1,0:T(8,128)(2,1)S(1)}, u32[]{:S(2)}, u32[]{:S(2)}) collective-permute-start(bf16[32,1920]{1,0:T(8,128)(2,1)} %get-tuple-element.49), channel_id=1, source_target_pairs={{0,16},{16,0},{1,17},{17,1},{2,18},{18,2},{3,19},{19,3},{4,20},{20... | collective-permute-start | bytes 368648 | tf_op jit(solution)/shard_map/ppermute | solution.py:190
  180.9 5.1 %collective-permute-start.33 = (bf16[32,1920]{1,0:T(8,128)(2,1)}, bf16[32,1920]{1,0:T(8,128)(2,1)S(1)}, u32[]{:S(2)}, u32[]{:S(2)}) collective-permute-start(bf16[32,1920]{1,0:T(8,128)(2,1)} %get-tuple-element.50), channel_id=1, source_target_pairs={{0,16},{16,0},{1,17},{17,1},{2,18},{18,2},{3,19},{19,3},{4,20},{20... | collective-permute-start | bytes 368648 | tf_op jit(solution)/shard_map/ppermute | solution.py:190
  182.1 3.9 %copy-start.16 = (bf16[32,1920]{1,0:T(8,128)(2,1)}, bf16[32,1920]{1,0:T(8,128)(2,1)S(1)}, u32[]{:S(2)}) copy-start(bf16[32,1920]{1,0:T(8,128)(2,1)S(1)} %collective-permute-done.30.refs_4_) | copy-start | bytes 368644
  182.1 3.9 %copy-start.17 = (bf16[32,1920]{1,0:T(8,128)(2,1)}, bf16[32,1920]{1,0:T(8,128)(2,1)S(1)}, u32[]{:S(2)}) copy-start(bf16[32,1920]{1,0:T(8,128)(2,1)S(1)} %collective-permute-done.31.refs_5_) | copy-start | bytes 368644
  182.1 3.9 %copy-start.18 = (bf16[32,1920]{1,0:T(8,128)(2,1)}, bf16[32,1920]{1,0:T(8,128)(2,1)S(1)}, u32[]{:S(2)}) copy-start(bf16[32,1920]{1,0:T(8,128)(2,1)S(1)} %collective-permute-done.32.refs_6_) | copy-start | bytes 368644
  (7 other events, 5.2 us)

commit v2 on v1

v2 whole, which is shorter than its diff:
```python
import functools

import jax
import jax.numpy as jnp
from jax import lax
from jax.experimental import pallas as pl
from jax.experimental.pallas import tpu as pltpu
from jax.sharding import Mesh, PartitionSpec as P

scaling = 2.0
AXES = ("y", "xl", "core", "z", "xh")
SIZES = (4, 2, 2, 4, 2)
ROW = ("y", "xl", "core")
COL = ("z", "xh")

POWER = 17
REACH = 170.0
SMALLEST = 1e-35
TILE = 512
KERNEL_BYTES = 58 << 20
PRETEND = 1


def tiles(width):
    return [(j, slice(at, min(at + TILE, width))) for j, at in enumerate(range(0, width, TILE))]


def encode(value):
    largest = jnp.max(jnp.abs(value), axis=1, keepdims=True)
    scale = jnp.maximum(largest * 1.01, SMALLEST).astype(jnp.bfloat16).astype(jnp.float32)
    a = value * (REACH / scale)
    a2 = a * a
    a4 = a2 * a2
    a8 = a4 * a4
    return a8 * a8 * a, scale


def put(out, here, coded, scales, width):
    if here.stop < width:
        out[:, here] = coded.astype(jnp.bfloat16)
        return
    coded = jnp.concatenate([coded, jnp.zeros((coded.shape[0], out.shape[1] - width), jnp.float32)], axis=1)
    column = lax.broadcasted_iota(jnp.int32, coded.shape, 1) + here.start
    for j, scale in enumerate(scales):
        coded = jnp.where(column == width + j, scale, coded)
    out[:, here.start :] = coded.astype(jnp.bfloat16)


def decode(ref, j, here, width, rows=slice(None)):
    coded = ref[rows, here].astype(jnp.float32)
    scale = ref[rows, width + j : width + j + 1].astype(jnp.float32) * (1.0 / REACH)
    size = jnp.abs(coded)
    root = jnp.exp2(jnp.log2(jnp.maximum(size, 1e-38)) * (1.0 / POWER))
    root = jnp.where(size > 0.0, root, 0.0)
    return jnp.where(coded < 0.0, -root, root) * scale


def split3(value):
    high = value.astype(jnp.bfloat16)
    rest = value - high.astype(jnp.float32)
    middle = rest.astype(jnp.bfloat16)
    low = (rest - middle.astype(jnp.float32)).astype(jnp.bfloat16)
    return high, middle, low


def pieces3(value):
    high = lax.reduce_precision(value, 8, 7)
    middle = lax.reduce_precision(value - high, 8, 7)
    return [p.astype(jnp.bfloat16) for p in (high, middle, value - high - middle)]


def dot_t(left, right):
    return lax.dot_general(
        left, right, (((1,), (1,)), ((), ())), preferred_element_type=jnp.float32
    )


def partial_kernel(width, layout, n, base, *refs):
    pieces, (wo, wr, uo, ur, down, own, *outs, held, low, kept_scales, sems) = refs[:n], refs[n:]
    j = pl.program_id(0)
    rows = own.shape[0]
    half = wo.shape[1]
    full = width // TILE
    rest = width - full * TILE
    tail = own.shape[1] // 128 * 128
    column = lax.broadcasted_iota(jnp.int32, (rows, 128), 1)

    @pl.when(j == 0)
    def _():
        gathers = []
        for i, (which, start, size, step, offset) in enumerate(layout):
            at = pl.multiple_of(lax.rem(base[0] + step, 4) * rows + offset, 16)
            gathers.append(pltpu.make_async_copy(pieces[which].at[pl.ds(start, size)], held.at[pl.ds(at, size)], sems.at[i]))
            gathers[-1].start()
        for copy in gathers:
            copy.wait()
        total = dot_t(held[:, :half], uo[...]) + dot_t(held[:, half:], ur[...])
        low[...] = jnp.concatenate(split3(total), axis=1)
        kept_scales[...] = jnp.zeros_like(kept_scales)

    def sums(size):
        value = dot_t(held[:, :half], wo[:size, :]) + dot_t(held[:, half:], wr[:size, :]) + dot_t(low[...], down[:size, :])
        for d in range(3):
            coded, scale = encode(value[(d + 1) * rows : (d + 2) * rows])
            kept_scales[d] = jnp.where(column == width % 128 + j, scale, kept_scales[d])
            yield value, d, coded

    @pl.when(j < full)
    def _():
        here = pl.ds(pl.multiple_of(j * TILE, TILE), TILE)
        for value, d, coded in sums(TILE):
            outs[d][:, here] = coded.astype(jnp.bfloat16)
        own[:, here] = value[:rows]

    @pl.when(j == full)
    def _():
        for value, d, coded in sums(rest):
            before = tail - full * TILE
            outs[d][:, full * TILE : tail] = coded[:, :before].astype(jnp.bfloat16)
            last = jnp.concatenate([coded[:, before:], jnp.zeros((rows, 128 - (width - tail)), jnp.float32)], axis=1)
            outs[d][:, tail:] = jnp.where(column < width - tail, last, kept_scales[d]).astype(jnp.bfloat16)
        own[:, full * TILE :] = value[:rows]


def partial(base, pieces, layout, wo, wr, uo, ur, down):
    width, half = wo.shape
    rows = sum(size for _, _, size, _, _ in layout) // 4
    padded = (width // 128 + 1) * 128
    hbm = pl.BlockSpec(memory_space=pltpu.HBM)
    strip = lambda a: pl.BlockSpec((TILE, a.shape[1]), lambda j, b: (j, 0))
    whole = lambda a: pl.BlockSpec(a.shape, lambda j, b: (0, 0))
    return pl.pallas_call(
        functools.partial(partial_kernel, width, layout, len(pieces)),
        grid_spec=pltpu.PrefetchScalarGridSpec(
            num_scalar_prefetch=1,
            grid=(width // TILE + 1,),
            in_specs=[hbm] * len(pieces) + [strip(wo), strip(wr), whole(uo), whole(ur), strip(down)],
            out_specs=[pl.BlockSpec((rows, width), lambda j, b: (0, 0))]
            + [pl.BlockSpec((rows, padded), lambda j, b: (0, 0))] * 3,
            scratch_shapes=[
                pltpu.VMEM((4 * rows, 2 * half), jnp.bfloat16),
                pltpu.VMEM((4 * rows, 48), jnp.bfloat16),
                pltpu.VMEM((3, rows, 128), jnp.float32),
                pltpu.SemaphoreType.DMA((len(layout),)),
            ],
        ),
        out_shape=[jax.ShapeDtypeStruct((rows, width), jnp.float32)]
        + [jax.ShapeDtypeStruct((rows, padded), jnp.bfloat16)] * 3,
        compiler_params=pltpu.CompilerParams(vmem_limit_bytes=KERNEL_BYTES),
        cost_estimate=pl.CostEstimate(flops=PRETEND, bytes_accessed=1, transcendentals=0),
        name="partial",
    )(base, *pieces, wo, wr, uo, ur, down)


def half_kernel(width, layout, n, base, *refs):
    pieces, (wo, wr, uo, ur, down, own, *outs, held, low, sems) = refs[:n], refs[n:]
    rows = own.shape[0]
    half = wo.shape[1]
    gathers = []
    for i, (which, start, size, step, offset) in enumerate(layout):
        at = pl.multiple_of(lax.rem(base[0] + step, 4) * rows + offset, 16)
        gathers.append(pltpu.make_async_copy(pieces[which].at[pl.ds(start, size)], held.at[pl.ds(at, size)], sems.at[i]))
        gathers[-1].start()
    for copy in gathers:
        copy.wait()
    total = dot_t(held[:, :half], uo[...]) + dot_t(held[:, half:], ur[...])
    low[...] = jnp.concatenate(split3(total), axis=1)
    scales = [[], [], []]
    for j, here in tiles(width):
        value = dot_t(held[:, :half], wo[here, :]) + dot_t(held[:, half:], wr[here, :]) + dot_t(low[...], down[here, :])
        own[:, here] = value[:rows]
        for d, out in enumerate(outs):
            coded, scale = encode(value[(d + 1) * rows : (d + 2) * rows])
            scales[d].append(scale)
            put(out, here, coded, scales[d], width)


def partial_half(which, base, pieces, layout, wo, wr, uo, ur, down):
    width, half = wo.shape[0] // 2, wo.shape[1]
    rows = sum(size for _, _, size, _, _ in layout) // 4
    padded = (width // 128 + 1) * 128
    hbm = pl.BlockSpec(memory_space=pltpu.HBM)
    strip = lambda a: pl.BlockSpec((width, a.shape[1]), lambda j, b: (which, 0))
    whole = lambda a: pl.BlockSpec(a.shape, lambda j, b: (0, 0))
    return pl.pallas_call(
        functools.partial(half_kernel, width, layout, len(pieces)),
        grid_spec=pltpu.PrefetchScalarGridSpec(
            num_scalar_prefetch=1,
            grid=(1,),
            in_specs=[hbm] * len(pieces) + [strip(wo), strip(wr), whole(uo), whole(ur), strip(down)],
            out_specs=[pl.BlockSpec((rows, width), lambda j, b: (0, 0))]
            + [pl.BlockSpec((rows, padded), lambda j, b: (0, 0))] * 3,
            scratch_shapes=[
                pltpu.VMEM((4 * rows, 2 * half), jnp.bfloat16),
                pltpu.VMEM((4 * rows, 48), jnp.bfloat16),
                pltpu.SemaphoreType.DMA((len(layout),)),
            ],
        ),
        out_shape=[jax.ShapeDtypeStruct((rows, width), jnp.float32)]
        + [jax.ShapeDtypeStruct((rows, padded), jnp.bfloat16)] * 3,
        compiler_params=pltpu.CompilerParams(vmem_limit_bytes=KERNEL_BYTES),
        cost_estimate=pl.CostEstimate(flops=PRETEND, bytes_accessed=1, transcendentals=0),
        name="partial_half",
    )(base, *pieces, wo, wr, uo, ur, down)


def fold_kernel(width, swap, own, a, b, c, keep, send):
    rows = keep.shape[0]
    swapped = swap[0] == 1
    scales = []
    for j, here in tiles(width):
        total = own[:, here]
        for r in (a, b, c):
            total = total + decode(r, j, here, width)
        first, second = total[:rows], total[rows:]
        keep[:, here] = jnp.where(swapped, second, first)
        coded, scale = encode(jnp.where(swapped, first, second))
        scales.append(scale)
        put(send, here, coded, scales, width)


def fold(swap, own, received, width):
    rows = own.shape[0]
    padded = received[0].shape[1]
    vmem = pl.BlockSpec()
    return pl.pallas_call(
        functools.partial(fold_kernel, width),
        in_specs=[pl.BlockSpec(memory_space=pltpu.SMEM)] + [vmem] * 4,
        out_specs=[vmem] * 2,
        out_shape=[
            jax.ShapeDtypeStruct((rows // 2, width), jnp.float32),
            jax.ShapeDtypeStruct((rows // 2, padded), jnp.bfloat16),
        ],
        cost_estimate=pl.CostEstimate(flops=1, bytes_accessed=1, transcendentals=0),
        name="fold",
    )(swap, own, *received)


def finish_kernel(keep0, got0, keep1, got1, keep2, got2, out):
    rows, width = keep0.shape
    for j, here in tiles(width):
        out[:rows, here] = (keep0[:, here] + decode(got0, j, here, width)).astype(out.dtype)
    halves = []
    for keep, got in ((keep1, got1), (keep2, got2)):
        for j, here in tiles(keep.shape[1]):
            halves.append(keep[:, here] + decode(got, j, here, keep.shape[1]))
    out[rows:, :] = jnp.concatenate(halves, axis=1).astype(out.dtype)


def finish(*keeps_and_gots):
    vmem = pl.BlockSpec()
    keep0, _, keep1 = keeps_and_gots[:3]
    return pl.pallas_call(
        finish_kernel,
        in_specs=[vmem] * 6,
        out_specs=vmem,
        out_shape=jax.ShapeDtypeStruct((keep0.shape[0] + keep1.shape[0], keep0.shape[1]), jnp.bfloat16),
        name="finish",
    )(*keeps_and_gots)


def ahead(array, axis, step):
    n = SIZES[AXES.index(axis)]
    return lax.ppermute(array, axis, [(i, (i + step) % n) for i in range(n)])


def across(array, axis, bit):
    n = SIZES[AXES.index(axis)]
    return lax.ppermute(array, axis, [(i, i ^ bit) for i in range(n)])


def after(array, *others):
    return lax.optimization_barrier((array, *others))[0]


def phase(*arrays):
    return lax.optimization_barrier(arrays)


PARTS = (64, 64)


def on_device(inputs, cotangent, weight, adapter_down_factor, adapter_up_factor):
    y, xl, core, z, xh = (lax.axis_index(a) for a in AXES)
    row_position = (y * 2 + xl) * 2 + core
    column_position = z * 2 + xh
    tokens, hidden = cotangent.shape
    width_row_block = inputs.shape[1]
    width = weight.shape[0]
    rows = tokens // 2
    p = rows * PARTS[0] // sum(PARTS)
    q = rows - p
    h = p // 2
    base = jnp.reshape(lax.rem(z - y + 4, 4), (1,)).astype(jnp.int32)
    swap = jnp.reshape(xl ^ xh, (1,)).astype(jnp.int32)

    mine = lax.dynamic_slice_in_dim(cotangent, core * rows, rows, 0)
    theirs = lax.dynamic_slice_in_dim(cotangent, (1 - core) * rows, rows, 0)
    other = across(theirs, "core", 1)
    block = jnp.concatenate([mine, other], axis=1)

    up_own = lax.dynamic_slice_in_dim(adapter_up_factor, row_position * hidden, hidden, 1)
    up_other = lax.dynamic_slice_in_dim(adapter_up_factor, (row_position ^ 1) * hidden, hidden, 1)
    down_columns = scaling * lax.dynamic_slice_in_dim(adapter_down_factor, column_position * width, width, 0)
    down3 = jnp.concatenate([down_columns] * 3, axis=1)
    down_rows = lax.dynamic_slice_in_dim(adapter_down_factor, row_position * width_row_block, width_row_block, 0)

    low_part = dot_t(up_own, after(cotangent, other))
    proj_part = lax.dot_general(down_rows, inputs, (((0,), (1,)), ((), ())), preferred_element_type=jnp.float32)
    rank = low_part.shape[0]
    small = jnp.concatenate([low_part, proj_part], axis=0)

    up1, down1 = ahead(block[:p], "z", 1), ahead(block[:p], "z", 3)
    x0 = across(block[:p], "xh", 1)
    small_other = across(small, "core", 1)
    block, weight, up1, down1, x0, small, small_other = phase(block, weight, up1, down1, x0, small, small_other)
    small = small + small_other

    up2 = ahead(jnp.concatenate([up1[:h], x0], axis=0), "z", 1)
    down2 = ahead(jnp.concatenate([down1[h:], x0], axis=0), "z", 3)
    x1 = across(block[p:], "xh", 1)
    weight_other = across(weight, "core", 1)
    small_other = across(small, "xl", 1)
    block, up2, down2, x1, weight_other, small_other, up_other, down3 = phase(
        block, up2, down2, x1, weight_other, small_other, up_other, down3
    )
    small = small + small_other

    up3, down3z = ahead(up2[h : 2 * h], "z", 1), ahead(down2[2 * h :], "z", 3)
    small_other = across(small, "y", 1)
    pair1 = jnp.concatenate([block[p:], x1], axis=0)
    pair1, up3, down3z, small_other = phase(pair1, up3, down3z, small_other)
    small = small + small_other

    up4, down4 = ahead(pair1, "z", 1), ahead(pair1, "z", 3)
    layout0 = [
        (0, 0, p, 0, 0),
        (1, 0, p, 0, p),
        (2, 0, p, 3, 0),
        (3, 0, p, 1, 0),
        (4, h, p, 3, p),
        (5, h, p, 1, p),
        (4, 0, h, 2, 0),
        (5, 0, h, 2, h),
        (6, 0, h, 2, p),
        (7, 0, h, 2, p + h),
    ]
    kept0, a0, b0, c0 = partial(
        base, (block, x0, up1, down1, up2, down2, up3, down3z), layout0, weight, weight_other, up_own, up_other, down3
    )
    small_other = across(small, "y", 2)
    up4, down4, kept0, a0, b0, c0, small_other = phase(up4, down4, kept0, a0, b0, c0, small_other)
    small = small + small_other

    up5, down5 = ahead(up4[:q], "z", 1), ahead(down4[q:], "z", 3)
    a0, c0 = ahead(a0, "y", 1), ahead(c0, "y", 3)
    low48 = jnp.concatenate(pieces3(scaling * small[:rank]), axis=0)
    proj48 = jnp.concatenate(pieces3(scaling * small[rank:]), axis=0)

    def three(left, right):
        out = jnp.dot(left, right, preferred_element_type=jnp.float32)
        return out[:rank] + (out[rank : 2 * rank] + out[2 * rank :])

    parts = jnp.concatenate([three(low48, inputs), three(proj48, cotangent)], axis=1)
    up5, down5, a0, c0, b0, parts = phase(up5, down5, a0, c0, b0, parts)

    layout1 = [
        (0, p, q, 0, 0),
        (1, 0, q, 0, q),
        (2, 0, 2 * q, 3, 0),
        (3, 0, 2 * q, 1, 0),
        (4, 0, q, 2, 0),
        (5, 0, q, 2, q),
    ]

    def half_of_sums(which):
        return partial_half(
            which, base, (block, x1, up4, down4, up5, down5), layout1, weight, weight_other, up_own, up_other, down3
        )

    b0 = ahead(b0, "y", 2)
    parts_other = across(parts, "xh", 1)
    kept1, a1, b1, c1 = half_of_sums(0)
    kept1, a1, b1, c1, b0, parts_other, block = phase(kept1, a1, b1, c1, b0, parts_other, block)
    parts = parts + parts_other

    a1, c1, b1 = ahead(a1, "y", 1), ahead(c1, "y", 3), ahead(b1, "y", 2)
    parts_other = across(parts, "z", 1)
    kept2, a2, b2, c2 = half_of_sums(1)
    keep0, send0 = fold(swap, kept0, (a0, c0, b0), width)
    kept2, a2, b2, c2, a1, c1, b1, keep0, send0, parts_other = phase(
        kept2, a2, b2, c2, a1, c1, b1, keep0, send0, parts_other
    )
    parts = parts + parts_other

    a2, c2, b2 = ahead(a2, "y", 1), ahead(c2, "y", 3), ahead(b2, "y", 2)
    got0 = across(send0, "xl", 1)
    parts_other = across(parts, "z", 2)
    keep1, send1 = fold(swap, kept1, (a1, c1, b1), width // 2)
    a2, c2, b2, got0, keep1, send1, parts_other = phase(a2, c2, b2, got0, keep1, send1, parts_other)
    parts = parts + parts_other
    grad_a = parts[:, :width_row_block].T
    grad_b = parts[:, width_row_block:]

    got1 = across(send1, "xl", 1)
    keep2, send2 = fold(swap, kept2, (a2, c2, b2), width // 2)
    got2 = across(send2, "xl", 1)
    grad_input = finish(keep0, got0, keep1, got1, keep2, got2)
    return grad_input, grad_a, grad_b


def solution(mesh):
    fine = Mesh(mesh.devices.reshape(SIZES), AXES)
    in_specs = (P(COL, ROW), P(COL, ROW), P(COL, ROW), P(), P())
    out_specs = (P(ROW, COL), P(ROW, None), P(None, ROW))
    return jax.shard_map(on_device, mesh=fine, in_specs=in_specs, out_specs=out_specs, check_vma=False)
```

time: 193 us -> 169 us (0.88)
  starting transfers between devices: 66.6 us -> 45 us
  waiting for transfers between devices: 39.2 us -> 48.9 us
  local copies, waits for them, and re-layouts: 19.2 us -> 12 us
  matrix products: 4.28 us -> 1.86 us
    ppermute x24 -> x19, starting transfers between devices: 40.7 us -> 26 us  [ahead(): return lax.ppermute(array, axis, [(i, (i + step) % n) for i in range(n)])]
    unnamed x61, local copies, waits for them, and re-layouts: 14.4 us -> 3.56 us
    ppermute x24 -> x19, waiting for transfers between devices: 14.3 us -> 23.1 us  [ahead(): return lax.ppermute(array, axis, [(i, (i + step) % n) for i in range(n)])]
    ppermute x17 -> x14, starting transfers between devices: 25.8 us -> 18.9 us  [across(): return lax.ppermute(array, axis, [(i, i ^ bit) for i in range(n)])]
    concatenate x4 -> x2, other arithmetic: 0.13 us -> 2.29 us  [the longest x1 1.27 us: on_device(): down2 = ahead(jnp.concatenate([down1[h:], x0], axis=0), 'z', 3)]
    slice x0 -> x8, local copies, waits for them, and re-layouts: none -> 2.09 us  [the longest x2 1.92 us: on_device(): up3, down3z = (ahead(up2[h:2 * h], 'z', 1), ahead(down2[2 * h:], 'z', 3))]
    pallas_call x4 -> x3, Pallas kernels: 11.1 us -> 10 us  [fold(): pl.pallas_call(functools.partial(fold_kernel, width), in_specs=[pl.BlockS...]
    ppermute x17 -> x14, waiting for transfers between devices: 24.8 us -> 25.9 us  [across(): return lax.ppermute(array, axis, [(i, i ^ bit) for i in range(n)])]
  transfers between devices with their start and end apart: 41 -> 33, of which waited for: 12 -> 15; matrix products, arithmetic and copies ran while one was open for 7% -> 7% of each run, Pallas kernels for 29% -> 31%
where the time goes in v2:
time: 169 us
  Pallas kernels  55.5 us (33%)
  waiting for transfers between devices  48.9 us (29%)
  starting transfers between devices  45 us (27%)
  local copies, waits for them, and re-layouts  12 us (7%)
  other arithmetic  4.27 us (3%)
  matrix products  1.86 us (1%)
    ppermute x19, starting transfers between devices, ahead(): return lax.ppermute(array, axis, [(i, (i + step) % n) for i in range(n)])  26 us
    ppermute x14, waiting for transfers between devices, across(): return lax.ppermute(array, axis, [(i, i ^ bit) for i in range(n)])  25.9 us
    pallas_call x2, Pallas kernels, partial_half(): pl.pallas_call(functools.partial(half_kernel, width, layout, len(pieces))...  24.5 us
    ppermute x19, waiting for transfers between devices, ahead(): return lax.ppermute(array, axis, [(i, (i + step) % n) for i in range(n)])  23.1 us
    ppermute x14, starting transfers between devices, across(): return lax.ppermute(array, axis, [(i, i ^ bit) for i in range(n)])  18.9 us
    pallas_call x1, Pallas kernels, partial(): pl.pallas_call(functools.partial(partial_kernel, width, layout, len(piece...  18.3 us
    pallas_call x3, Pallas kernels, fold(): pl.pallas_call(functools.partial(fold_kernel, width), in_specs=[pl.BlockS...  10 us
    unnamed x61, local copies, waits for them, and re-layouts  3.56 us
  transfers between devices with their start and end apart: 33, of which 15 were waited for; matrix products, arithmetic and copies ran while one was open for 7% of the time, Pallas kernels for 31%

profile of v2, /device:TPU:0, one launch (start us, length us, event | category | flops | bytes accessed | tf_op | source)
XLA Modules:
  0.0 168.7 jit_solution(13879393365088570365)
XLA Ops:
  0.7 1.4 constant_dynamic-slice_fusion.3
  2.1 1.5 constant_dynamic-slice_fusion
  3.6 1.0 fusion.3
  4.7 3.2 %collective-permute-start.3 = (bf16[64,3840]{1,0:T(8,128)(2,1)S(1)}, bf16[64,3840]{1,0:T(8,128)(2,1)S(1)}, u32[]{:S(2)}, u32[]{:S(2)}) collective-permute-start(bf16[64,3840]{1,0:T(8,128)(2,1)S(1)} %fusion), channel_id=1, source_target_pairs={{0,1},{1,0},{2,3},{3,2},{4,5},{5,4},{6,7},{7,6},{8,9},{9,8},{10,11... | collective-permute-start | bytes 1474568 | tf_op jit(solution)/shard_map/ppermute | solution.py:269
  7.9 4.0 %collective-permute-start.2 = (bf16[64,3840]{1,0:T(8,128)(2,1)S(1)}, bf16[64,3840]{1,0:T(8,128)(2,1)S(1)}, u32[]{:S(2)}, u32[]{:S(2)}) collective-permute-start(bf16[64,3840]{1,0:T(8,128)(2,1)S(1)} %fusion), channel_id=1, source_target_pairs={{0,6},{2,0},{4,2},{6,4},{1,7},{3,1},{5,3},{7,5},{8,14},{10,8},{12,... | collective-permute-start | bytes 1474568 | tf_op jit(solution)/shard_map/ppermute | solution.py:264
  11.9 0.3 fusion.22
  12.5 1.1 collective-permute-done.4
  13.6 6.3 %collective-permute-done.3.refs_1_ = bf16[64,3840]{1,0:T(8,128)(2,1)S(1)} collective-permute-done((bf16[64,3840]{1,0:T(8,128)(2,1)S(1)}, bf16[64,3840]{1,0:T(8,128)(2,1)S(1)}, u32[]{:S(2)}, u32[]{:S(2)}) %collective-permute-start.3) | collective-permute-done | bytes 491552 | tf_op jit(solution)/shard_map/ppermute | solution.py:269
  19.9 2.9 %collective-permute-done.2.refs_3_ = bf16[64,3840]{1,0:T(8,128)(2,1)S(1)} collective-permute-done((bf16[64,3840]{1,0:T(8,128)(2,1)S(1)}, bf16[64,3840]{1,0:T(8,128)(2,1)S(1)}, u32[]{:S(2)}, u32[]{:S(2)}) %collective-permute-start.2) | collective-permute-done | bytes 491552 | tf_op jit(solution)/shard_map/ppermute | solution.py:264
  22.8 3.4 %collective-permute-done.1.refs_2_ = bf16[64,3840]{1,0:T(8,128)(2,1)S(1)} collective-permute-done((bf16[64,3840]{1,0:T(8,128)(2,1)S(1)}, bf16[64,3840]{1,0:T(8,128)(2,1)S(1)}, u32[]{:S(2)}, u32[]{:S(2)}) %collective-permute-start.1) | collective-permute-done | bytes 491552 | tf_op jit(solution)/shard_map/ppermute | solution.py:264
  26.2 1.3 pad_maximum_fusion.2
  27.5 0.4 collective-permute-start.6
  27.9 1.6 collective-permute-start.5
  29.6 0.6 collective-permute-start.7
  30.2 0.9 dynamic-slice_multiply_fusion
  31.1 1.6 collective-permute-start.9
  32.7 0.7 pad_maximum_fusion.5
  33.4 10.0 %collective-permute-done.9 = f32[32,256]{1,0:T(8,128)S(1)} collective-permute-done((f32[32,256]{1,0:T(8,128)S(1)}, f32[32,256]{1,0:T(8,128)S(1)}, u32[]{:S(2)}, u32[]{:S(2)}) %collective-permute-start.9) | collective-permute-done | bytes 32800 | tf_op jit(solution)/shard_map/ppermute | solution.py:269
  43.4 1.2 collective-permute-done.7.refs_1_
  44.6 2.1 %collective-permute-done.6.refs_5_ = bf16[96,3840]{1,0:T(8,128)(2,1)} collective-permute-done((bf16[96,3840]{1,0:T(8,128)(2,1)}, bf16[96,3840]{1,0:T(8,128)(2,1)}, u32[]{:S(2)}, u32[]{:S(2)}) %collective-permute-start.6) | collective-permute-done | bytes 737312 | tf_op jit(solution)/shard_map/ppermute | solution.py:264
  46.7 1.3 collective-permute-done.5.refs_4_
  48.0 1.7 collective-permute-start.12
  49.7 1.0 slice.64
  50.6 1.0 slice.65
  51.6 0.4 collective-permute-start.11
  52.0 1.7 %collective-permute-start.10 = (bf16[32,3840]{1,0:T(8,128)(2,1)S(1)}, bf16[32,3840]{1,0:T(8,128)(2,1)S(1)}, u32[]{:S(2)}, u32[]{:S(2)}) collective-permute-start(bf16[32,3840]{1,0:T(8,128)(2,1)S(1)} %slice.64), channel_id=1, source_target_pairs={{0,2},{2,4},{4,6},{6,0},{1,3},{3,5},{5,7},{7,1},{8,10},{10,12},{12... | collective-permute-start | bytes 737288 | tf_op jit(solution)/shard_map/ppermute | solution.py:264
  53.7 1.0 pad_maximum_fusion.1
  54.8 3.8 %collective-permute-done.11.refs_7_ = bf16[32,3840]{1,0:T(8,128)(2,1)S(1)} collective-permute-done((bf16[32,3840]{1,0:T(8,128)(2,1)S(1)}, bf16[32,3840]{1,0:T(8,128)(2,1)S(1)}, u32[]{:S(2)}, u32[]{:S(2)}) %collective-permute-start.11) | collective-permute-done | bytes 245792 | tf_op jit(solution)/shard_map/ppermute | solution.py:264
  58.6 1.5 collective-permute-done.10.refs_6_
  60.1 1.0 collective-permute-start.14
  61.1 1.0 collective-permute-start.13
  62.2 2.9 %collective-permute-start.15 = (f32[32,256]{1,0:T(8,128)S(1)}, f32[32,256]{1,0:T(8,128)S(1)}, u32[]{:S(2)}, u32[]{:S(2)}) collective-permute-start(f32[32,256]{1,0:T(8,128)S(1)} %add.75), channel_id=1, source_target_pairs={{0,64},{32,96},{64,0},{96,32},{1,65},{33,97},{65,1},{97,33},{2,66}... | collective-permute-start | bytes 98312 | tf_op jit(solution)/shard_map/ppermute | solution.py:269
  65.1 1.9 %copy.10.refs_12_.refs_10_ = bf16[1856,48]{1,0:T(8,128)(2,1)} copy(bf16[1856,48]{0,1:T(8,128)(2,1)} %pad_maximum_fusion.5) | data formatting | bytes 356352 | tf_op jit(solution)/shard_map/optimization_barrier | solution.py:277
  67.0 18.3 %partial.1 = (f32[128,1856]{1,0:T(8,128)}, bf16[128,1920]{1,0:T(8,128)(2,1)}, bf16[128,1920]{1,0:T(8,128)(2,1)}, bf16[128,1920]{1,0:T(8,128)(2,1)}) custom-call(s32[1]{0:T(128)} %bitcast.base, bf16[128,3840]{1,0:T(8,128)(2,1)} %copy-done.1, bf16[64,3840]{1,0:T(8,128)(2,1)} %copy-done.6, bf16[64,3840]{1,0:T(8,128)(2,1)} %copy-done.11, ...), custom_call_target="tpu_custom_call" | custom-call | flops 1 | bytes 1 | tf_op jit(solution)/shard_map/partial/pallas_call | solution.py:132
  85.8 0.5 copy-done.3
  86.2 0.3 copy-done.4
  86.6 2.2 %collective-permute-start.17 = (bf16[64,3840]{1,0:T(8,128)(2,1)S(1)}, bf16[64,3840]{1,0:T(8,128)(2,1)S(1)}, u32[]{:S(2)}, u32[]{:S(2)}) collective-permute-start(bf16[64,3840]{1,0:T(8,128)(2,1)S(1)} %slice.67), channel_id=1, source_target_pairs={{0,6},{2,0},{4,2},{6,4},{1,7},{3,1},{5,3},{7,5},{8,14},{10,8},{12,... | collective-permute-start | bytes 1474568 | tf_op jit(solution)/shard_map/ppermute | solution.py:264
  88.9 3.1 %collective-permute-start.19 = (bf16[128,1920]{1,0:T(8,128)(2,1)S(1)}, bf16[128,1920]{1,0:T(8,128)(2,1)S(1)}, u32[]{:S(2)}, u32[]{:S(2)}) collective-permute-start(bf16[128,1920]{1,0:T(8,128)(2,1)S(1)} %copy-done.26), channel_id=1, source_target_pairs={{0,96},{32,0},{64,32},{96,64},{1,97},{33,1},{65,33},{97,65},{2,98}... | collective-permute-start | bytes 1474568 | tf_op jit(solution)/shard_map/ppermute | solution.py:264
  92.4 4.6 %collective-permute-done.17.refs_5_ = bf16[64,3840]{1,0:T(8,128)(2,1)S(1)} collective-permute-done((bf16[64,3840]{1,0:T(8,128)(2,1)S(1)}, bf16[64,3840]{1,0:T(8,128)(2,1)S(1)}, u32[]{:S(2)}, u32[]{:S(2)}) %collective-permute-start.17) | collective-permute-done | bytes 491552 | tf_op jit(solution)/shard_map/ppermute | solution.py:264
  97.0 3.4 %collective-permute-done.16.refs_4_ = bf16[64,3840]{1,0:T(8,128)(2,1)S(1)} collective-permute-done((bf16[64,3840]{1,0:T(8,128)(2,1)S(1)}, bf16[64,3840]{1,0:T(8,128)(2,1)S(1)}, u32[]{:S(2)}, u32[]{:S(2)}) %collective-permute-start.16) | collective-permute-done | bytes 491552 | tf_op jit(solution)/shard_map/ppermute | solution.py:264
  100.5 1.5 collective-permute-start.20
  101.9 0.3 collective-permute-start.21
  102.2 12.2 %partial_half.2 = (f32[128,928]{1,0:T(8,128)}, bf16[128,1024]{1,0:T(8,128)(2,1)}, bf16[128,1024]{1,0:T(8,128)(2,1)}, bf16[128,1024]{1,0:T(8,128)(2,1)}) custom-call(s32[1]{0:T(128)} %bitcast.base, bf16[128,3840]{1,0:T(8,128)(2,1)} %copy-done.1, bf16[64,3840]{1,0:T(8,128)(2,1)} %copy-done.5, bf16[128,3840]{1,0:T(8,128)(2,1)} %copy-done.4, ...), custom_call_target="tpu_custom_call" | custom-call | flops 1 | bytes 1 | tf_op jit(solution)/shard_map/partial_half/pallas_call | solution.py:185
  114.5 2.4 %collective-permute-start.22 = (bf16[128,1024]{1,0:T(8,128)(2,1)}, bf16[128,1024]{1,0:T(8,128)(2,1)S(1)}, u32[]{:S(2)}, u32[]{:S(2)}) collective-permute-start(bf16[128,1024]{1,0:T(8,128)(2,1)} %get-tuple-element.121), channel_id=1, source_target_pairs={{0,32},{32,64},{64,96},{96,0},{1,33},{33,65},{65,97},{97,1},{2,34}... | collective-permute-start | bytes 786440 | tf_op jit(solution)/shard_map/ppermute | solution.py:264
  117.0 0.9 collective-permute-start.23
  117.8 1.3 collective-permute-start.24
  119.1 5.0 %collective-permute-start.25 = (f32[16,2848]{1,0:T(8,128)S(1)}, f32[16,2848]{1,0:T(8,128)S(1)}, u32[]{:S(2)}, u32[]{:S(2)}) collective-permute-start(f32[16,2848]{1,0:T(8,128)S(1)} %add.81), channel_id=1, source_target_pairs={{0,2},{2,0},{4,6},{6,4},{1,3},{3,1},{5,7},{7,5},{8,10},{10,8},{12,... | collective-permute-start | bytes 546824 | tf_op jit(solution)/shard_map/ppermute | solution.py:269
  124.1 12.2 %partial_half.3 = (f32[128,928]{1,0:T(8,128)}, bf16[128,1024]{1,0:T(8,128)(2,1)}, bf16[128,1024]{1,0:T(8,128)(2,1)}, bf16[128,1024]{1,0:T(8,128)(2,1)}) custom-call(s32[1]{0:T(128)} %bitcast.base, bf16[128,3840]{1,0:T(8,128)(2,1)} %copy-done.1, bf16[64,3840]{1,0:T(8,128)(2,1)} %copy-done.5, bf16[128,3840]{1,0:T(8,128)(2,1)} %copy-done.4, ...), custom_call_target="tpu_custom_call" | custom-call | flops 1 | bytes 1 | tf_op jit(solution)/shard_map/partial_half/pallas_call | solution.py:185
  136.4 4.2 %fold.3 = (f32[64,1856]{1,0:T(8,128)}, bf16[64,1920]{1,0:T(8,128)(2,1)}) custom-call(s32[1]{0:T(128)} %bitcast.1.swap, f32[128,1856]{1,0:T(8,128)} %get-tuple-element.124.own, bf16[128,1920]{1,0:T(8,128)(2,1)} %copy-done.12, bf16[128,1920]{1,0:T(8,128)(2,1)} %copy-done.13, bf16[128,1920]{1,0:T(8,128)(2,1)} %copy-done.14), custom_call_target="tpu_custom_call" | custom-call | flops 1 | bytes 1 | tf_op jit(solution)/shard_map/fold/pallas_call | solution.py:226
  141.0 3.2 %collective-permute-start.27 = (bf16[128,1024]{1,0:T(8,128)(2,1)S(1)}, bf16[128,1024]{1,0:T(8,128)(2,1)S(1)}, u32[]{:S(2)}, u32[]{:S(2)}) collective-permute-start(bf16[128,1024]{1,0:T(8,128)(2,1)S(1)} %copy-done.29), channel_id=1, source_target_pairs={{0,96},{32,0},{64,32},{96,64},{1,97},{33,1},{65,33},{97,65},{2,98}... | collective-permute-start | bytes 786440 | tf_op jit(solution)/shard_map/ppermute | solution.py:264
  144.2 0.9 collective-permute-start.28
  145.1 1.5 collective-permute-start.30
  146.6 2.9 %fold.4 = (f32[64,928]{1,0:T(8,128)}, bf16[64,1024]{1,0:T(8,128)(2,1)}) custom-call(s32[1]{0:T(128)} %bitcast.1.swap, f32[128,928]{1,0:T(8,128)} %get-tuple-element.136.own, bf16[128,1024]{1,0:T(8,128)(2,1)} %copy-done.15, bf16[128,1024]{1,0:T(8,128)(2,1)} %copy-done.16, bf16[128,1024]{1,0:T(8,128)(2,1)} %copy-done.17), custom_call_target="tpu_custom_call" | custom-call | flops 1 | bytes 1 | tf_op jit(solution)/shard_map/fold/pallas_call | solution.py:226
  149.5 2.7 %collective-permute-done.30 = f32[16,2848]{1,0:T(8,128)S(1)} collective-permute-done((f32[16,2848]{1,0:T(8,128)S(1)}, f32[16,2848]{1,0:T(8,128)S(1)}, u32[]{:S(2)}, u32[]{:S(2)}) %collective-permute-start.30) | collective-permute-done | bytes 182304 | tf_op jit(solution)/shard_map/ppermute | solution.py:269
  152.2 0.6 collective-permute-done.29.got0
  152.9 0.9 slice.89
  153.9 1.4 collective-permute-start.31
  155.3 2.9 %fold.5 = (f32[64,928]{1,0:T(8,128)}, bf16[64,1024]{1,0:T(8,128)(2,1)}) custom-call(s32[1]{0:T(128)} %bitcast.1.swap, f32[128,928]{1,0:T(8,128)} %get-tuple-element.146.own, bf16[128,1024]{1,0:T(8,128)(2,1)} %copy-done.18, bf16[128,1024]{1,0:T(8,128)(2,1)} %copy-done.19, bf16[128,1024]{1,0:T(8,128)(2,1)} %copy-done.20), custom_call_target="tpu_custom_call" | custom-call | flops 1 | bytes 1 | tf_op jit(solution)/shard_map/fold/pallas_call | solution.py:226
  158.1 0.6 collective-permute-start.32
  158.8 0.6 slice_bitcast_fusion
  159.4 3.9 %collective-permute-done.32.got2 = bf16[64,1024]{1,0:T(8,128)(2,1)S(1)} collective-permute-done((bf16[64,1024]{1,0:T(8,128)(2,1)}, bf16[64,1024]{1,0:T(8,128)(2,1)S(1)}, u32[]{:S(2)}, u32[]{:S(2)}) %collective-permute-start.32) | collective-permute-done | bytes 131104 | tf_op jit(solution)/shard_map/ppermute | solution.py:269
  163.3 0.6 copy-done.25
  164.0 2.7 %finish.1 = bf16[128,1856]{1,0:T(8,128)(2,1)} custom-call(f32[64,1856]{1,0:T(8,128)} %get-tuple-element.131.keep0, bf16[64,1920]{1,0:T(8,128)(2,1)} %copy-done.23, f32[64,928]{1,0:T(8,128)} %get-tuple-element.144.keep1, bf16[64,1024]{1,0:T(8,128)(2,1)} %copy-done.24, f32[64,928]{1,0:T(8,128)} %get-tuple-element.150.keep2, bf16[64,1024]{1,0:T(8,128)(2,1)} %copy-done.25), custom_call_target="tpu_custom_call" | custom-call | tf_op jit(solution)/shard_map/finish/pallas_call | solution.py:253
  166.7 2.0 %copy.13 = bf16[128,1856]{0,1:T(8,128)(2,1)} copy(bf16[128,1856]{1,0:T(8,128)(2,1)} %finish.1) | data formatting | bytes 950272
  (105 shorter events, 1.9 us)
Async XLA Ops:
  0.6 3.0 %copy-start = (bf16[256,928]{0,1:T(8,128)(2,1)S(1)}, bf16[256,928]{0,1:T(8,128)(2,1)}, u32[]{:S(2)}) copy-start(bf16[256,928]{0,1:T(8,128)(2,1)} %param.5) | copy-start | bytes 1425412
  0.7 11.3 %copy-start.2 = (bf16[256,1920]{1,0:T(8,128)(2,1)S(1)}, bf16[256,1920]{1,0:T(8,128)(2,1)}, u32[]{:S(2)}) copy-start(bf16[256,1920]{1,0:T(8,128)(2,1)} %param.6) | copy-start | bytes 2949124
  2.0 2.6 %collective-permute-start = (bf16[128,1920]{1,0:T(8,128)(2,1)S(1)}, bf16[128,1920]{1,0:T(8,128)(2,1)S(1)}, u32[]{:S(2)}, u32[]{:S(2)}) collective-permute-start(bf16[128,1920]{1,0:T(8,128)(2,1)S(1)} %get-tuple-element.162), channel_id=1, source_target_pairs={{0,8},{8,0},{1,9},{9,1},{2,10},{10,2},{3,11},{11,3},{4,12},{12,4},... | collective-permute-start | bytes 1474568 | tf_op jit(solution)/shard_map/ppermute | solution.py:269
  3.6 8.8 %copy-start.9 = (bf16[16,1920]{1,0:T(8,128)(2,1)}, bf16[16,1920]{1,0:T(8,128)(2,1)S(1)}, u32[]{:S(2)}) copy-start(bf16[16,1920]{1,0:T(8,128)(2,1)S(1)} %get-tuple-element.160.refs_10_.refs_8_) | copy-start | bytes 184324
  4.7 15.2 %collective-permute-start.3 = (bf16[64,3840]{1,0:T(8,128)(2,1)S(1)}, bf16[64,3840]{1,0:T(8,128)(2,1)S(1)}, u32[]{:S(2)}, u32[]{:S(2)}) collective-permute-start(bf16[64,3840]{1,0:T(8,128)(2,1)S(1)} %fusion), channel_id=1, source_target_pairs={{0,1},{1,0},{2,3},{3,2},{4,5},{5,4},{6,7},{7,6},{8,9},{9,8},{10,11... | collective-permute-start | bytes 1474568 | tf_op jit(solution)/shard_map/ppermute | solution.py:269
  7.9 14.9 %collective-permute-start.2 = (bf16[64,3840]{1,0:T(8,128)(2,1)S(1)}, bf16[64,3840]{1,0:T(8,128)(2,1)S(1)}, u32[]{:S(2)}, u32[]{:S(2)}) collective-permute-start(bf16[64,3840]{1,0:T(8,128)(2,1)S(1)} %fusion), channel_id=1, source_target_pairs={{0,6},{2,0},{4,2},{6,4},{1,7},{3,1},{5,3},{7,5},{8,14},{10,8},{12,... | collective-permute-start | bytes 1474568 | tf_op jit(solution)/shard_map/ppermute | solution.py:264
  11.9 14.2 %collective-permute-start.1 = (bf16[64,3840]{1,0:T(8,128)(2,1)S(1)}, bf16[64,3840]{1,0:T(8,128)(2,1)S(1)}, u32[]{:S(2)}, u32[]{:S(2)}) collective-permute-start(bf16[64,3840]{1,0:T(8,128)(2,1)S(1)} %fusion), channel_id=1, source_target_pairs={{0,2},{2,4},{4,6},{6,0},{1,3},{3,5},{5,7},{7,1},{8,10},{10,12},{12... | collective-permute-start | bytes 1474568 | tf_op jit(solution)/shard_map/ppermute | solution.py:264
  12.3 1.3 collective-permute-start.4
  12.5 41.2 %copy-start.1 = (bf16[128,3840]{1,0:T(8,128)(2,1)}, bf16[128,3840]{1,0:T(8,128)(2,1)S(1)}, u32[]{:S(2)}) copy-start(bf16[128,3840]{1,0:T(8,128)(2,1)S(1)} %pad_maximum_fusion.refs_0_) | copy-start | bytes 2949124
  19.9 9.7 %copy-start.6 = (bf16[64,3840]{1,0:T(8,128)(2,1)}, bf16[64,3840]{1,0:T(8,128)(2,1)S(1)}, u32[]{:S(2)}) copy-start(bf16[64,3840]{1,0:T(8,128)(2,1)S(1)} %collective-permute-done.3.refs_1_) | copy-start | bytes 1474564
  22.8 6.8 %copy-start.10 = (bf16[64,3840]{1,0:T(8,128)(2,1)}, bf16[64,3840]{1,0:T(8,128)(2,1)S(1)}, u32[]{:S(2)}) copy-start(bf16[64,3840]{1,0:T(8,128)(2,1)S(1)} %collective-permute-done.2.refs_3_) | copy-start | bytes 1474564
  26.2 3.4 %copy-start.11 = (bf16[64,3840]{1,0:T(8,128)(2,1)}, bf16[64,3840]{1,0:T(8,128)(2,1)S(1)}, u32[]{:S(2)}) copy-start(bf16[64,3840]{1,0:T(8,128)(2,1)S(1)} %collective-permute-done.1.refs_2_) | copy-start | bytes 1474564
  26.2 21.8 %collective-permute-start.8 = (bf16[1856,1920]{1,0:T(8,128)(2,1)}, bf16[1856,1920]{1,0:T(8,128)(2,1)}, u32[]{:S(2)}, u32[]{:S(2)}) collective-permute-start(bf16[1856,1920]{1,0:T(8,128)(2,1)} %refs_6_.1), channel_id=1, source_target_pairs={{0,8},{8,0},{1,9},{9,1},{2,10},{10,2},{3,11},{11,3},{4,12},{12,4},... | collective-permute-start | bytes 21381128 | tf_op jit(solution)/shard_map/ppermute | solution.py:269
  27.5 19.2 %collective-permute-start.6 = (bf16[96,3840]{1,0:T(8,128)(2,1)}, bf16[96,3840]{1,0:T(8,128)(2,1)}, u32[]{:S(2)}, u32[]{:S(2)}) collective-permute-start(bf16[96,3840]{1,0:T(8,128)(2,1)} %get-tuple-element.163), channel_id=1, source_target_pairs={{0,6},{2,0},{4,2},{6,4},{1,7},{3,1},{5,3},{7,5},{8,14},{10,8},{12,... | collective-permute-start | bytes 2211848 | tf_op jit(solution)/shard_map/ppermute | solution.py:264
  27.9 20.1 %collective-permute-start.5 = (bf16[96,3840]{1,0:T(8,128)(2,1)}, bf16[96,3840]{1,0:T(8,128)(2,1)}, u32[]{:S(2)}, u32[]{:S(2)}) collective-permute-start(bf16[96,3840]{1,0:T(8,128)(2,1)} %get-tuple-element.164), channel_id=1, source_target_pairs={{0,2},{2,4},{4,6},{6,0},{1,3},{3,5},{5,7},{7,1},{8,10},{10,12},{12... | collective-permute-start | bytes 2211848 | tf_op jit(solution)/shard_map/ppermute | solution.py:264
  29.6 15.0 %collective-permute-start.7 = (bf16[64,3840]{1,0:T(8,128)(2,1)S(1)}, bf16[64,3840]{1,0:T(8,128)(2,1)S(1)}, u32[]{:S(2)}, u32[]{:S(2)}) collective-permute-start(bf16[64,3840]{1,0:T(8,128)(2,1)S(1)} %slice.62), channel_id=1, source_target_pairs={{0,1},{1,0},{2,3},{3,2},{4,5},{5,4},{6,7},{7,6},{8,9},{9,8},{10,11... | collective-permute-start | bytes 1474568 | tf_op jit(solution)/shard_map/ppermute | solution.py:269
  31.1 12.3 %collective-permute-start.9 = (f32[32,256]{1,0:T(8,128)S(1)}, f32[32,256]{1,0:T(8,128)S(1)}, u32[]{:S(2)}, u32[]{:S(2)}) collective-permute-start(f32[32,256]{1,0:T(8,128)S(1)} %add.70), channel_id=1, source_target_pairs={{0,16},{16,0},{1,17},{17,1},{2,18},{18,2},{3,19},{19,3},{4,20},{20... | collective-permute-start | bytes 98312 | tf_op jit(solution)/shard_map/ppermute | solution.py:269
  44.6 10.2 %copy-start.5 = (bf16[64,3840]{1,0:T(8,128)(2,1)}, bf16[64,3840]{1,0:T(8,128)(2,1)S(1)}, u32[]{:S(2)}) copy-start(bf16[64,3840]{1,0:T(8,128)(2,1)S(1)} %collective-permute-done.7.refs_1_) | copy-start | bytes 1474564
  48.0 6.7 %collective-permute-start.12 = (f32[32,256]{1,0:T(8,128)S(1)}, f32[32,256]{1,0:T(8,128)S(1)}, u32[]{:S(2)}, u32[]{:S(2)}) collective-permute-start(f32[32,256]{1,0:T(8,128)S(1)} %add.74), channel_id=1, source_target_pairs={{0,32},{32,0},{64,96},{96,64},{1,33},{33,1},{65,97},{97,65},{2,34}... | collective-permute-start | bytes 98312 | tf_op jit(solution)/shard_map/ppermute | solution.py:269
  51.6 7.0 %collective-permute-start.11 = (bf16[32,3840]{1,0:T(8,128)(2,1)S(1)}, bf16[32,3840]{1,0:T(8,128)(2,1)S(1)}, u32[]{:S(2)}, u32[]{:S(2)}) collective-permute-start(bf16[32,3840]{1,0:T(8,128)(2,1)S(1)} %slice.65), channel_id=1, source_target_pairs={{0,6},{2,0},{4,2},{6,4},{1,7},{3,1},{5,3},{7,5},{8,14},{10,8},{12,... | collective-permute-start | bytes 737288 | tf_op jit(solution)/shard_map/ppermute | solution.py:264
  52.0 8.2 %collective-permute-start.10 = (bf16[32,3840]{1,0:T(8,128)(2,1)S(1)}, bf16[32,3840]{1,0:T(8,128)(2,1)S(1)}, u32[]{:S(2)}, u32[]{:S(2)}) collective-permute-start(bf16[32,3840]{1,0:T(8,128)(2,1)S(1)} %slice.64), channel_id=1, source_target_pairs={{0,2},{2,4},{4,6},{6,0},{1,3},{3,5},{5,7},{7,1},{8,10},{10,12},{12... | collective-permute-start | bytes 737288 | tf_op jit(solution)/shard_map/ppermute | solution.py:264
  58.6 1.5 copy-start.21
  60.1 1.0 copy-start.22
  60.1 25.2 %collective-permute-start.14 = (bf16[128,3840]{1,0:T(8,128)(2,1)}, bf16[128,3840]{1,0:T(8,128)(2,1)S(1)}, u32[]{:S(2)}, u32[]{:S(2)}) collective-permute-start(bf16[128,3840]{1,0:T(8,128)(2,1)} %pad_maximum_fusion.1), channel_id=1, source_target_pairs={{0,6},{2,0},{4,2},{6,4},{1,7},{3,1},{5,3},{7,5},{8,14},{10,8},{12,... | collective-permute-start | bytes 2949128 | tf_op jit(solution)/shard_map/ppermute | solution.py:264
  61.1 24.2 %collective-permute-start.13 = (bf16[128,3840]{1,0:T(8,128)(2,1)}, bf16[128,3840]{1,0:T(8,128)(2,1)S(1)}, u32[]{:S(2)}, u32[]{:S(2)}) collective-permute-start(bf16[128,3840]{1,0:T(8,128)(2,1)} %pad_maximum_fusion.1), channel_id=1, source_target_pairs={{0,2},{2,4},{4,6},{6,0},{1,3},{3,5},{5,7},{7,1},{8,10},{10,12},{12... | collective-permute-start | bytes 2949128 | tf_op jit(solution)/shard_map/ppermute | solution.py:264
  62.2 23.1 %collective-permute-start.15 = (f32[32,256]{1,0:T(8,128)S(1)}, f32[32,256]{1,0:T(8,128)S(1)}, u32[]{:S(2)}, u32[]{:S(2)}) collective-permute-start(f32[32,256]{1,0:T(8,128)S(1)} %add.75), channel_id=1, source_target_pairs={{0,64},{32,96},{64,0},{96,32},{1,65},{33,97},{65,1},{97,33},{2,66}... | collective-permute-start | bytes 98312 | tf_op jit(solution)/shard_map/ppermute | solution.py:269
  85.3 0.9 copy-start.3
  85.3 1.3 copy-start.4
  85.3 3.5 %copy-start.27 = (bf16[128,1920]{1,0:T(8,128)(2,1)S(1)}, bf16[128,1920]{1,0:T(8,128)(2,1)}, u32[]{:S(2)}) copy-start(bf16[128,1920]{1,0:T(8,128)(2,1)} %get-tuple-element.104) | copy-start | bytes 1474564
  85.4 3.6 %copy-start.26 = (bf16[128,1920]{1,0:T(8,128)(2,1)S(1)}, bf16[128,1920]{1,0:T(8,128)(2,1)}, u32[]{:S(2)}) copy-start(bf16[128,1920]{1,0:T(8,128)(2,1)} %get-tuple-element.105) | copy-start | bytes 1474564
  86.6 10.5 %collective-permute-start.17 = (bf16[64,3840]{1,0:T(8,128)(2,1)S(1)}, bf16[64,3840]{1,0:T(8,128)(2,1)S(1)}, u32[]{:S(2)}, u32[]{:S(2)}) collective-permute-start(bf16[64,3840]{1,0:T(8,128)(2,1)S(1)} %slice.67), channel_id=1, source_target_pairs={{0,6},{2,0},{4,2},{6,4},{1,7},{3,1},{5,3},{7,5},{8,14},{10,8},{12,... | collective-permute-start | bytes 1474568 | tf_op jit(solution)/shard_map/ppermute | solution.py:264
  88.8 11.7 %collective-permute-start.16 = (bf16[64,3840]{1,0:T(8,128)(2,1)S(1)}, bf16[64,3840]{1,0:T(8,128)(2,1)S(1)}, u32[]{:S(2)}, u32[]{:S(2)}) collective-permute-start(bf16[64,3840]{1,0:T(8,128)(2,1)S(1)} %slice.66), channel_id=1, source_target_pairs={{0,2},{2,4},{4,6},{6,0},{1,3},{3,5},{5,7},{7,1},{8,10},{10,12},{12... | collective-permute-start | bytes 1474568 | tf_op jit(solution)/shard_map/ppermute | solution.py:264
  88.8 11.7 %collective-permute-start.18 = (bf16[128,1920]{1,0:T(8,128)(2,1)S(1)}, bf16[128,1920]{1,0:T(8,128)(2,1)S(1)}, u32[]{:S(2)}, u32[]{:S(2)}) collective-permute-start(bf16[128,1920]{1,0:T(8,128)(2,1)S(1)} %copy-done.27), channel_id=1, source_target_pairs={{0,32},{32,64},{64,96},{96,0},{1,33},{33,65},{65,97},{97,1},{2,34}... | collective-permute-start | bytes 1474568 | tf_op jit(solution)/shard_map/ppermute | solution.py:264
  88.9 11.5 %collective-permute-start.19 = (bf16[128,1920]{1,0:T(8,128)(2,1)S(1)}, bf16[128,1920]{1,0:T(8,128)(2,1)S(1)}, u32[]{:S(2)}, u32[]{:S(2)}) collective-permute-start(bf16[128,1920]{1,0:T(8,128)(2,1)S(1)} %copy-done.26), channel_id=1, source_target_pairs={{0,96},{32,0},{64,32},{96,64},{1,97},{33,1},{65,33},{97,65},{2,98}... | collective-permute-start | bytes 1474568 | tf_op jit(solution)/shard_map/ppermute | solution.py:264
  97.0 5.2 %copy-start.7 = (bf16[64,3840]{1,0:T(8,128)(2,1)}, bf16[64,3840]{1,0:T(8,128)(2,1)S(1)}, u32[]{:S(2)}) copy-start(bf16[64,3840]{1,0:T(8,128)(2,1)S(1)} %collective-permute-done.17.refs_5_) | copy-start | bytes 1474564
  100.4 1.8 %copy-start.8 = (bf16[64,3840]{1,0:T(8,128)(2,1)}, bf16[64,3840]{1,0:T(8,128)(2,1)S(1)}, u32[]{:S(2)}) copy-start(bf16[64,3840]{1,0:T(8,128)(2,1)S(1)} %collective-permute-done.16.refs_4_) | copy-start | bytes 1474564
  100.5 14.0 %copy-start.12 = (bf16[128,1920]{1,0:T(8,128)(2,1)}, bf16[128,1920]{1,0:T(8,128)(2,1)S(1)}, u32[]{:S(2)}) copy-start(bf16[128,1920]{1,0:T(8,128)(2,1)S(1)} %collective-permute-done.18.a) | copy-start | bytes 1474564
  100.5 14.0 %copy-start.13 = (bf16[128,1920]{1,0:T(8,128)(2,1)}, bf16[128,1920]{1,0:T(8,128)(2,1)S(1)}, u32[]{:S(2)}) copy-start(bf16[128,1920]{1,0:T(8,128)(2,1)S(1)} %collective-permute-done.19.b) | copy-start | bytes 1474564
  100.5 14.1 %collective-permute-start.20 = (bf16[128,1920]{1,0:T(8,128)(2,1)}, bf16[128,1920]{1,0:T(8,128)(2,1)S(1)}, u32[]{:S(2)}, u32[]{:S(2)}) collective-permute-start(bf16[128,1920]{1,0:T(8,128)(2,1)} %get-tuple-element.114), channel_id=1, source_target_pairs={{0,64},{32,96},{64,0},{96,32},{1,65},{33,97},{65,1},{97,33},{2,66}... | collective-permute-start | bytes 1474568 | tf_op jit(solution)/shard_map/ppermute | solution.py:264
  101.9 12.6 %collective-permute-start.21 = (f32[16,2848]{1,0:T(8,128)S(1)}, f32[16,2848]{1,0:T(8,128)S(1)}, u32[]{:S(2)}, u32[]{:S(2)}) collective-permute-start(f32[16,2848]{1,0:T(8,128)S(1)} %pad_maximum_fusion.4), channel_id=1, source_target_pairs={{0,1},{1,0},{2,3},{3,2},{4,5},{5,4},{6,7},{7,6},{8,9},{9,8},{10,11... | collective-permute-start | bytes 546824 | tf_op jit(solution)/shard_map/ppermute | solution.py:269
  114.5 21.8 %copy-start.14 = (bf16[128,1920]{1,0:T(8,128)(2,1)}, bf16[128,1920]{1,0:T(8,128)(2,1)S(1)}, u32[]{:S(2)}) copy-start(bf16[128,1920]{1,0:T(8,128)(2,1)S(1)} %collective-permute-done.20.c) | copy-start | bytes 1474564
  114.5 26.1 %collective-permute-start.22 = (bf16[128,1024]{1,0:T(8,128)(2,1)}, bf16[128,1024]{1,0:T(8,128)(2,1)S(1)}, u32[]{:S(2)}, u32[]{:S(2)}) collective-permute-start(bf16[128,1024]{1,0:T(8,128)(2,1)} %get-tuple-element.121), channel_id=1, source_target_pairs={{0,32},{32,64},{64,96},{96,0},{1,33},{33,65},{65,97},{97,1},{2,34}... | collective-permute-start | bytes 786440 | tf_op jit(solution)/shard_map/ppermute | solution.py:264
  117.0 23.6 %collective-permute-start.23 = (bf16[128,1024]{1,0:T(8,128)(2,1)}, bf16[128,1024]{1,0:T(8,128)(2,1)S(1)}, u32[]{:S(2)}, u32[]{:S(2)}) collective-permute-start(bf16[128,1024]{1,0:T(8,128)(2,1)} %get-tuple-element.122), channel_id=1, source_target_pairs={{0,96},{32,0},{64,32},{96,64},{1,97},{33,1},{65,33},{97,65},{2,98}... | collective-permute-start | bytes 786440 | tf_op jit(solution)/shard_map/ppermute | solution.py:264
  117.8 22.8 %collective-permute-start.24 = (bf16[128,1024]{1,0:T(8,128)(2,1)}, bf16[128,1024]{1,0:T(8,128)(2,1)S(1)}, u32[]{:S(2)}, u32[]{:S(2)}) collective-permute-start(bf16[128,1024]{1,0:T(8,128)(2,1)} %get-tuple-element.123), channel_id=1, source_target_pairs={{0,64},{32,96},{64,0},{96,32},{1,65},{33,97},{65,1},{97,33},{2,66}... | collective-permute-start | bytes 786440 | tf_op jit(solution)/shard_map/ppermute | solution.py:264
  119.1 21.5 %collective-permute-start.25 = (f32[16,2848]{1,0:T(8,128)S(1)}, f32[16,2848]{1,0:T(8,128)S(1)}, u32[]{:S(2)}, u32[]{:S(2)}) collective-permute-start(f32[16,2848]{1,0:T(8,128)S(1)} %add.81), channel_id=1, source_target_pairs={{0,2},{2,0},{4,6},{6,4},{1,3},{3,1},{5,7},{7,5},{8,10},{10,8},{12,... | collective-permute-start | bytes 546824 | tf_op jit(solution)/shard_map/ppermute | solution.py:269
  136.3 4.6 %copy-start.29 = (bf16[128,1024]{1,0:T(8,128)(2,1)S(1)}, bf16[128,1024]{1,0:T(8,128)(2,1)}, u32[]{:S(2)}) copy-start(bf16[128,1024]{1,0:T(8,128)(2,1)} %get-tuple-element.133) | copy-start | bytes 786436
  136.4 7.8 %copy-start.28 = (bf16[128,1024]{1,0:T(8,128)(2,1)S(1)}, bf16[128,1024]{1,0:T(8,128)(2,1)}, u32[]{:S(2)}) copy-start(bf16[128,1024]{1,0:T(8,128)(2,1)} %get-tuple-element.134) | copy-start | bytes 786436
  140.6 6.0 %copy-start.15 = (bf16[128,1024]{1,0:T(8,128)(2,1)}, bf16[128,1024]{1,0:T(8,128)(2,1)S(1)}, u32[]{:S(2)}) copy-start(bf16[128,1024]{1,0:T(8,128)(2,1)S(1)} %collective-permute-done.22.a) | copy-start | bytes 786436
  140.6 6.0 %copy-start.16 = (bf16[128,1024]{1,0:T(8,128)(2,1)}, bf16[128,1024]{1,0:T(8,128)(2,1)S(1)}, u32[]{:S(2)}) copy-start(bf16[128,1024]{1,0:T(8,128)(2,1)S(1)} %collective-permute-done.23.b) | copy-start | bytes 786436
  140.6 6.0 %copy-start.17 = (bf16[128,1024]{1,0:T(8,128)(2,1)}, bf16[128,1024]{1,0:T(8,128)(2,1)S(1)}, u32[]{:S(2)}) copy-start(bf16[128,1024]{1,0:T(8,128)(2,1)S(1)} %collective-permute-done.24.c) | copy-start | bytes 786436
  140.7 12.2 %collective-permute-start.26 = (bf16[128,1024]{1,0:T(8,128)(2,1)}, bf16[128,1024]{1,0:T(8,128)(2,1)S(1)}, u32[]{:S(2)}, u32[]{:S(2)}) collective-permute-start(bf16[128,1024]{1,0:T(8,128)(2,1)} %get-tuple-element.132), channel_id=1, source_target_pairs={{0,32},{32,64},{64,96},{96,0},{1,33},{33,65},{65,97},{97,1},{2,34}... | collective-permute-start | bytes 786440 | tf_op jit(solution)/shard_map/ppermute | solution.py:264
  141.0 11.9 %collective-permute-start.27 = (bf16[128,1024]{1,0:T(8,128)(2,1)S(1)}, bf16[128,1024]{1,0:T(8,128)(2,1)S(1)}, u32[]{:S(2)}, u32[]{:S(2)}) collective-permute-start(bf16[128,1024]{1,0:T(8,128)(2,1)S(1)} %copy-done.29), channel_id=1, source_target_pairs={{0,96},{32,0},{64,32},{96,64},{1,97},{33,1},{65,33},{97,65},{2,98}... | collective-permute-start | bytes 786440 | tf_op jit(solution)/shard_map/ppermute | solution.py:264
  144.2 8.7 %collective-permute-start.28 = (bf16[128,1024]{1,0:T(8,128)(2,1)S(1)}, bf16[128,1024]{1,0:T(8,128)(2,1)S(1)}, u32[]{:S(2)}, u32[]{:S(2)}) collective-permute-start(bf16[128,1024]{1,0:T(8,128)(2,1)S(1)} %copy-done.28), channel_id=1, source_target_pairs={{0,64},{32,96},{64,0},{96,32},{1,65},{33,97},{65,1},{97,33},{2,66}... | collective-permute-start | bytes 786440 | tf_op jit(solution)/shard_map/ppermute | solution.py:264
  145.0 7.8 %collective-permute-start.29 = (bf16[64,1920]{1,0:T(8,128)(2,1)}, bf16[64,1920]{1,0:T(8,128)(2,1)S(1)}, u32[]{:S(2)}, u32[]{:S(2)}) collective-permute-start(bf16[64,1920]{1,0:T(8,128)(2,1)} %get-tuple-element.135), channel_id=1, source_target_pairs={{0,16},{16,0},{1,17},{17,1},{2,18},{18,2},{3,19},{19,3},{4,20},{20... | collective-permute-start | bytes 737288 | tf_op jit(solution)/shard_map/ppermute | solution.py:269
  145.1 7.2 %collective-permute-start.30 = (f32[16,2848]{1,0:T(8,128)S(1)}, f32[16,2848]{1,0:T(8,128)S(1)}, u32[]{:S(2)}, u32[]{:S(2)}) collective-permute-start(f32[16,2848]{1,0:T(8,128)S(1)} %add.82), channel_id=1, source_target_pairs={{0,4},{2,6},{4,0},{6,2},{1,5},{3,7},{5,1},{7,3},{8,12},{10,14},{12... | collective-permute-start | bytes 546824 | tf_op jit(solution)/shard_map/ppermute | solution.py:269
  152.9 10.5 %copy-start.23 = (bf16[64,1920]{1,0:T(8,128)(2,1)}, bf16[64,1920]{1,0:T(8,128)(2,1)S(1)}, u32[]{:S(2)}) copy-start(bf16[64,1920]{1,0:T(8,128)(2,1)S(1)} %collective-permute-done.29.got0) | copy-start | bytes 737284
  152.9 2.4 %copy-start.18 = (bf16[128,1024]{1,0:T(8,128)(2,1)}, bf16[128,1024]{1,0:T(8,128)(2,1)S(1)}, u32[]{:S(2)}) copy-start(bf16[128,1024]{1,0:T(8,128)(2,1)S(1)} %collective-permute-done.26.a) | copy-start | bytes 786436
  152.9 2.4 %copy-start.19 = (bf16[128,1024]{1,0:T(8,128)(2,1)}, bf16[128,1024]{1,0:T(8,128)(2,1)S(1)}, u32[]{:S(2)}) copy-start(bf16[128,1024]{1,0:T(8,128)(2,1)S(1)} %collective-permute-done.27.b) | copy-start | bytes 786436
  152.9 2.4 %copy-start.20 = (bf16[128,1024]{1,0:T(8,128)(2,1)}, bf16[128,1024]{1,0:T(8,128)(2,1)S(1)}, u32[]{:S(2)}) copy-start(bf16[128,1024]{1,0:T(8,128)(2,1)S(1)} %collective-permute-done.28.c) | copy-start | bytes 786436
  153.9 5.6 %collective-permute-start.31 = (bf16[64,1024]{1,0:T(8,128)(2,1)}, bf16[64,1024]{1,0:T(8,128)(2,1)S(1)}, u32[]{:S(2)}, u32[]{:S(2)}) collective-permute-start(bf16[64,1024]{1,0:T(8,128)(2,1)} %get-tuple-element.145), channel_id=1, source_target_pairs={{0,16},{16,0},{1,17},{17,1},{2,18},{18,2},{3,19},{19,3},{4,20},{20... | collective-permute-start | bytes 393224 | tf_op jit(solution)/shard_map/ppermute | solution.py:269
  158.1 5.2 %collective-permute-start.32 = (bf16[64,1024]{1,0:T(8,128)(2,1)}, bf16[64,1024]{1,0:T(8,128)(2,1)S(1)}, u32[]{:S(2)}, u32[]{:S(2)}) collective-permute-start(bf16[64,1024]{1,0:T(8,128)(2,1)} %get-tuple-element.151), channel_id=1, source_target_pairs={{0,16},{16,0},{1,17},{17,1},{2,18},{18,2},{3,19},{19,3},{4,20},{20... | collective-permute-start | bytes 393224 | tf_op jit(solution)/shard_map/ppermute | solution.py:269
  159.4 3.9 %copy-start.24 = (bf16[64,1024]{1,0:T(8,128)(2,1)}, bf16[64,1024]{1,0:T(8,128)(2,1)S(1)}, u32[]{:S(2)}) copy-start(bf16[64,1024]{1,0:T(8,128)(2,1)S(1)} %collective-permute-done.31.got1) | copy-start | bytes 393220
  163.3 0.6 copy-start.25

commit v3 on v2

--- a/solution.py
+++ b/solution.py
@@ -50,8 +50,7 @@
     coded = ref[rows, here].astype(jnp.float32)
     scale = ref[rows, width + j : width + j + 1].astype(jnp.float32) * (1.0 / REACH)
     size = jnp.abs(coded)
-    root = jnp.exp2(jnp.log2(jnp.maximum(size, 1e-38)) * (1.0 / POWER))
-    root = jnp.where(size > 0.0, root, 0.0)
+    root = jnp.where(size > 0.0, jnp.exp(jnp.log(size) * (1.0 / POWER)), 0.0)
     return jnp.where(coded < 0.0, -root, root) * scale
 
 
@@ -67,6 +66,10 @@
     high = lax.reduce_precision(value, 8, 7)
     middle = lax.reduce_precision(value - high, 8, 7)
     return [p.astype(jnp.bfloat16) for p in (high, middle, value - high - middle)]
+
+
+def dot(left, right):
+    return jnp.dot(left, right, preferred_element_type=jnp.float32)
 
 
 def dot_t(left, right):
@@ -99,7 +102,7 @@
         kept_scales[...] = jnp.zeros_like(kept_scales)
 
     def sums(size):
-        value = dot_t(held[:, :half], wo[:size, :]) + dot_t(held[:, half:], wr[:size, :]) + dot_t(low[...], down[:size, :])
+        value = dot_t(held[:, :half], wo[:size, :]) + dot_t(held[:, half:], wr[:size, :]) + dot(low[...], down[:, :size])
         for d in range(3):
             coded, scale = encode(value[(d + 1) * rows : (d + 2) * rows])
             kept_scales[d] = jnp.where(column == width % 128 + j, scale, kept_scales[d])
@@ -134,7 +137,13 @@
         grid_spec=pltpu.PrefetchScalarGridSpec(
             num_scalar_prefetch=1,
             grid=(width // TILE + 1,),
-            in_specs=[hbm] * len(pieces) + [strip(wo), strip(wr), whole(uo), whole(ur), strip(down)],
+            in_specs=[hbm] * len(pieces) + [
+                strip(wo),
+                strip(wr),
+                whole(uo),
+                whole(ur),
+                pl.BlockSpec((down.shape[0], TILE), lambda j, b: (0, j)),
+            ],
             out_specs=[pl.BlockSpec((rows, width), lambda j, b: (0, 0))]
             + [pl.BlockSpec((rows, padded), lambda j, b: (0, 0))] * 3,
             scratch_shapes=[
@@ -152,27 +161,47 @@
     )(base, *pieces, wo, wr, uo, ur, down)
 
 
-def half_kernel(width, layout, n, base, *refs):
-    pieces, (wo, wr, uo, ur, down, own, *outs, held, low, sems) = refs[:n], refs[n:]
+def half_kernel(which, width, layout, n, base, *refs):
+    pieces, (wo, wr, uo, ur, down, own, *outs, held, held_wo, held_wr, low, total, sems, w_sems) = refs[:n], refs[n:]
     rows = own.shape[0]
     half = wo.shape[1]
+    always = base[0] >= 0
+    strip = pl.ds(which * width, width)
+    first = pltpu.make_async_copy(wo.at[strip], held_wo, w_sems.at[0])
+    second = pltpu.make_async_copy(wr.at[strip], held_wr, w_sems.at[1])
     gathers = []
-    for i, (which, start, size, step, offset) in enumerate(layout):
+    for i, (piece, start, size, step, offset) in enumerate(layout):
         at = pl.multiple_of(lax.rem(base[0] + step, 4) * rows + offset, 16)
-        gathers.append(pltpu.make_async_copy(pieces[which].at[pl.ds(start, size)], held.at[pl.ds(at, size)], sems.at[i]))
+        gathers.append(pltpu.make_async_copy(pieces[piece].at[pl.ds(start, size)], held.at[pl.ds(at, size)], sems.at[i]))
         gathers[-1].start()
-    for copy in gathers:
-        copy.wait()
-    total = dot_t(held[:, :half], uo[...]) + dot_t(held[:, half:], ur[...])
-    low[...] = jnp.concatenate(split3(total), axis=1)
-    scales = [[], [], []]
-    for j, here in tiles(width):
-        value = dot_t(held[:, :half], wo[here, :]) + dot_t(held[:, half:], wr[here, :]) + dot_t(low[...], down[here, :])
-        own[:, here] = value[:rows]
-        for d, out in enumerate(outs):
-            coded, scale = encode(value[(d + 1) * rows : (d + 2) * rows])
-            scales[d].append(scale)
-            put(out, here, coded, scales[d], width)
+    first.start()
+    second.start()
+
+    @pl.when(always)
+    def _():
+        for copy in gathers:
+            copy.wait()
+        factors = dot_t(held[:, :half], uo[...]) + dot_t(held[:, half:], ur[...])
+        low[...] = jnp.concatenate(split3(factors), axis=1)
+
+    @pl.when(always)
+    def _():
+        first.wait()
+        for _, here in tiles(width):
+            shift = slice(which * width + here.start, which * width + here.stop)
+            total[:, here] = dot_t(held[:, :half], held_wo[here, :]) + dot(low[...], down[:, shift])
+
+    @pl.when(always)
+    def _():
+        second.wait()
+        scales = [[], [], []]
+        for j, here in tiles(width):
+            value = total[:, here] + dot_t(held[:, half:], held_wr[here, :])
+            own[:, here] = value[:rows]
+            for d, out in enumerate(outs):
+                coded, scale = encode(value[(d + 1) * rows : (d + 2) * rows])
+                scales[d].append(scale)
+                put(out, here, coded, scales[d], width)
 
 
 def partial_half(which, base, pieces, layout, wo, wr, uo, ur, down):
@@ -180,20 +209,23 @@
     rows = sum(size for _, _, size, _, _ in layout) // 4
     padded = (width // 128 + 1) * 128
     hbm = pl.BlockSpec(memory_space=pltpu.HBM)
-    strip = lambda a: pl.BlockSpec((width, a.shape[1]), lambda j, b: (which, 0))
     whole = lambda a: pl.BlockSpec(a.shape, lambda j, b: (0, 0))
     return pl.pallas_call(
-        functools.partial(half_kernel, width, layout, len(pieces)),
+        functools.partial(half_kernel, which, width, layout, len(pieces)),
         grid_spec=pltpu.PrefetchScalarGridSpec(
             num_scalar_prefetch=1,
             grid=(1,),
-            in_specs=[hbm] * len(pieces) + [strip(wo), strip(wr), whole(uo), whole(ur), strip(down)],
+            in_specs=[hbm] * (len(pieces) + 2) + [whole(uo), whole(ur), whole(down)],
             out_specs=[pl.BlockSpec((rows, width), lambda j, b: (0, 0))]
             + [pl.BlockSpec((rows, padded), lambda j, b: (0, 0))] * 3,
             scratch_shapes=[
                 pltpu.VMEM((4 * rows, 2 * half), jnp.bfloat16),
+                pltpu.VMEM((width, half), jnp.bfloat16),
+                pltpu.VMEM((width, half), jnp.bfloat16),
                 pltpu.VMEM((4 * rows, 48), jnp.bfloat16),
+                pltpu.VMEM((4 * rows, width), jnp.float32),
                 pltpu.SemaphoreType.DMA((len(layout),)),
+                pltpu.SemaphoreType.DMA((2,)),
             ],
         ),
         out_shape=[jax.ShapeDtypeStruct((rows, width), jnp.float32)]
@@ -222,7 +254,7 @@
 def fold(swap, own, received, width):
     rows = own.shape[0]
     padded = received[0].shape[1]
-    vmem = pl.BlockSpec()
+    vmem = pl.BlockSpec(memory_space=pltpu.VMEM)
     return pl.pallas_call(
         functools.partial(fold_kernel, width),
         in_specs=[pl.BlockSpec(memory_space=pltpu.SMEM)] + [vmem] * 4,
@@ -236,25 +268,30 @@
     )(swap, own, *received)
 
 
-def finish_kernel(keep0, got0, keep1, got1, keep2, got2, out):
+def finish_kernel(keep0, got0, keep1, got1, keep2, got2, out, total):
     rows, width = keep0.shape
     for j, here in tiles(width):
-        out[:rows, here] = (keep0[:, here] + decode(got0, j, here, width)).astype(out.dtype)
+        total[:rows, here] = keep0[:, here] + decode(got0, j, here, width)
     halves = []
     for keep, got in ((keep1, got1), (keep2, got2)):
         for j, here in tiles(keep.shape[1]):
             halves.append(keep[:, here] + decode(got, j, here, keep.shape[1]))
-    out[rows:, :] = jnp.concatenate(halves, axis=1).astype(out.dtype)
+    total[rows:, :] = jnp.concatenate(halves, axis=1)
+    for at in range(0, width, 256):
+        here = slice(at, min(at + 256, width))
+        out[here, :] = total[:, here].T.astype(out.dtype)
 
 
 def finish(*keeps_and_gots):
-    vmem = pl.BlockSpec()
+    vmem = pl.BlockSpec(memory_space=pltpu.VMEM)
     keep0, _, keep1 = keeps_and_gots[:3]
+    shape = (keep0.shape[0] + keep1.shape[0], keep0.shape[1])
     return pl.pallas_call(
         finish_kernel,
         in_specs=[vmem] * 6,
         out_specs=vmem,
-        out_shape=jax.ShapeDtypeStruct((keep0.shape[0] + keep1.shape[0], keep0.shape[1]), jnp.bfloat16),
+        out_shape=jax.ShapeDtypeStruct(shape[::-1], jnp.bfloat16),
+        scratch_shapes=[pltpu.VMEM(shape, jnp.float32)],
         name="finish",
     )(*keeps_and_gots)
 
@@ -301,8 +338,8 @@
 
     up_own = lax.dynamic_slice_in_dim(adapter_up_factor, row_position * hidden, hidden, 1)
     up_other = lax.dynamic_slice_in_dim(adapter_up_factor, (row_position ^ 1) * hidden, hidden, 1)
-    down_columns = scaling * lax.dynamic_slice_in_dim(adapter_down_factor, column_position * width, width, 0)
-    down3 = jnp.concatenate([down_columns] * 3, axis=1)
+    down_columns = scaling * lax.dynamic_slice_in_dim(adapter_down_factor.T, column_position * width, width, 1)
+    down3 = jnp.concatenate([down_columns] * 3, axis=0)
     down_rows = lax.dynamic_slice_in_dim(adapter_down_factor, row_position * width_row_block, width_row_block, 0)
 
     low_part = dot_t(up_own, after(cotangent, other))
@@ -362,7 +399,9 @@
         return out[:rank] + (out[rank : 2 * rank] + out[2 * rank :])
 
     parts = jnp.concatenate([three(low48, inputs), three(proj48, cotangent)], axis=1)
-    up5, down5, a0, c0, b0, parts = phase(up5, down5, a0, c0, b0, parts)
+    parts_other = across(parts, "xh", 1)
+    up5, down5, a0, c0, b0, parts, parts_other = phase(up5, down5, a0, c0, b0, parts, parts_other)
+    parts = parts + parts_other
 
     layout1 = [
         (0, p, q, 0, 0),
@@ -379,33 +418,29 @@
         )
 
     b0 = ahead(b0, "y", 2)
-    parts_other = across(parts, "xh", 1)
     kept1, a1, b1, c1 = half_of_sums(0)
-    kept1, a1, b1, c1, b0, parts_other, block = phase(kept1, a1, b1, c1, b0, parts_other, block)
-    parts = parts + parts_other
+    kept1, a1, b1, c1, b0, parts, block = phase(kept1, a1, b1, c1, b0, parts, block)
 
     a1, c1, b1 = ahead(a1, "y", 1), ahead(c1, "y", 3), ahead(b1, "y", 2)
     parts_other = across(parts, "z", 1)
     kept2, a2, b2, c2 = half_of_sums(1)
+    kept2, a2, b2, c2, a1, c1, b1, b0, parts_other = phase(kept2, a2, b2, c2, a1, c1, b1, b0, parts_other)
+    parts = parts + parts_other
+
+    a2, c2, b2 = ahead(a2, "y", 1), ahead(c2, "y", 3), ahead(b2, "y", 2)
+    parts_other = across(parts, "z", 2)
     keep0, send0 = fold(swap, kept0, (a0, c0, b0), width)
-    kept2, a2, b2, c2, a1, c1, b1, keep0, send0, parts_other = phase(
-        kept2, a2, b2, c2, a1, c1, b1, keep0, send0, parts_other
-    )
-    parts = parts + parts_other
-
-    a2, c2, b2 = ahead(a2, "y", 1), ahead(c2, "y", 3), ahead(b2, "y", 2)
-    got0 = across(send0, "xl", 1)
-    parts_other = across(parts, "z", 2)
     keep1, send1 = fold(swap, kept1, (a1, c1, b1), width // 2)
-    a2, c2, b2, got0, keep1, send1, parts_other = phase(a2, c2, b2, got0, keep1, send1, parts_other)
-    parts = parts + parts_other
+    a2, c2, b2, keep0, send0, keep1, send1, parts_other = phase(a2, c2, b2, keep0, send0, keep1, send1, parts_other)
+
+    got0, got1 = across(send0, "xl", 1), across(send1, "xl", 1)
+    keep2, send2 = fold(swap, kept2, (a2, c2, b2), width // 2)
+    got2 = across(send2, "xl", 1)
+    parts = after(parts, send2) + parts_other
     grad_a = parts[:, :width_row_block].T
     grad_b = parts[:, width_row_block:]
-
-    got1 = across(send1, "xl", 1)
-    keep2, send2 = fold(swap, kept2, (a2, c2, b2), width // 2)
-    got2 = across(send2, "xl", 1)
-    grad_input = finish(keep0, got0, keep1, got1, keep2, got2)
+    got0, got1, got2, grad_a, grad_b = phase(got0, got1, got2, grad_a, grad_b)
+    grad_input = finish(keep0, got0, keep1, got1, keep2, got2).T
     return grad_input, grad_a, grad_b
 
 

time: 169 us -> 160 us (0.947)
  local copies, waits for them, and re-layouts: 12 us -> 7.62 us
  waiting for transfers between devices: 48.9 us -> 45.8 us
    ppermute x19, waiting for transfers between devices: 23.1 us -> 16.7 us  [ahead(): return lax.ppermute(array, axis, [(i, (i + step) % n) for i in range(n)])]
    ppermute x14, waiting for transfers between devices: 25.9 us -> 29.1 us  [across(): return lax.ppermute(array, axis, [(i, i ^ bit) for i in range(n)])]
    unnamed x61 -> x58, local copies, waits for them, and re-layouts: 3.56 us -> 1.29 us
    ppermute x14, starting transfers between devices: 18.9 us -> 16.9 us  [across(): return lax.ppermute(array, axis, [(i, i ^ bit) for i in range(n)])]
    optimization_barrier x1 -> x0, local copies, waits for them, and re-layouts: 1.9 us -> none  [phase(): return lax.optimization_barrier(arrays)]
  transfers between devices with their start and end apart: 33 -> 33, of which waited for: 15 -> 14; matrix products, arithmetic and copies ran while one was open for 7% -> 6% of each run, Pallas kernels for 31% -> 33%
where the time goes in v3:
time: 160 us; the launch traced here: 159 us
  Pallas kernels  54.9 us (34%)
  waiting for transfers between devices  45.8 us (29%)
  starting transfers between devices  43.5 us (27%)
  local copies, waits for them, and re-layouts  7.62 us (5%)
  other arithmetic  4.22 us (3%)
  matrix products  1.86 us (1%)
    ppermute x14, waiting for transfers between devices, across(): return lax.ppermute(array, axis, [(i, i ^ bit) for i in range(n)])  29.1 us
    ppermute x19, starting transfers between devices, ahead(): return lax.ppermute(array, axis, [(i, (i + step) % n) for i in range(n)])  26.6 us
    pallas_call x2, Pallas kernels, partial_half(): pl.pallas_call(functools.partial(half_kernel, which, width, layout, len(p...  23.5 us
    pallas_call x1, Pallas kernels, partial(): pl.pallas_call(functools.partial(partial_kernel, width, layout, len(piece...  18.4 us
    ppermute x14, starting transfers between devices, across(): return lax.ppermute(array, axis, [(i, i ^ bit) for i in range(n)])  16.9 us
    ppermute x19, waiting for transfers between devices, ahead(): return lax.ppermute(array, axis, [(i, (i + step) % n) for i in range(n)])  16.7 us
    pallas_call x3, Pallas kernels, fold(): pl.pallas_call(functools.partial(fold_kernel, width), in_specs=[pl.BlockS...  10.2 us
  transfers between devices with their start and end apart: 33, of which 14 were waited for; matrix products, arithmetic and copies ran while one was open for 6% of the time, Pallas kernels for 33%

profile of v3, /device:TPU:0, one launch (start us, length us, event | category | flops | bytes accessed | tf_op | source)
XLA Modules:
  0.0 159.1 jit_solution(8977260773127415975)
XLA Ops:
  0.7 1.4 constant_dynamic-slice_fusion.3
  2.1 1.5 constant_dynamic-slice_fusion
  3.6 1.0 fusion.3
  4.7 3.2 %collective-permute-start.3 = (bf16[64,3840]{1,0:T(8,128)(2,1)S(1)}, bf16[64,3840]{1,0:T(8,128)(2,1)S(1)}, u32[]{:S(2)}, u32[]{:S(2)}) collective-permute-start(bf16[64,3840]{1,0:T(8,128)(2,1)S(1)} %fusion), channel_id=1, source_target_pairs={{0,1},{1,0},{2,3},{3,2},{4,5},{5,4},{6,7},{7,6},{8,9},{9,8},{10,11... | collective-permute-start | bytes 1474568 | tf_op jit(solution)/shard_map/ppermute | solution.py:306
  7.9 4.0 %collective-permute-start.2 = (bf16[64,3840]{1,0:T(8,128)(2,1)S(1)}, bf16[64,3840]{1,0:T(8,128)(2,1)S(1)}, u32[]{:S(2)}, u32[]{:S(2)}) collective-permute-start(bf16[64,3840]{1,0:T(8,128)(2,1)S(1)} %fusion), channel_id=1, source_target_pairs={{0,6},{2,0},{4,2},{6,4},{1,7},{3,1},{5,3},{7,5},{8,14},{10,8},{12,... | collective-permute-start | bytes 1474568 | tf_op jit(solution)/shard_map/ppermute | solution.py:301
  11.9 0.3 fusion.22
  12.5 1.1 collective-permute-done.4
  13.6 6.3 %collective-permute-done.3.refs_1_ = bf16[64,3840]{1,0:T(8,128)(2,1)S(1)} collective-permute-done((bf16[64,3840]{1,0:T(8,128)(2,1)S(1)}, bf16[64,3840]{1,0:T(8,128)(2,1)S(1)}, u32[]{:S(2)}, u32[]{:S(2)}) %collective-permute-start.3) | collective-permute-done | bytes 491552 | tf_op jit(solution)/shard_map/ppermute | solution.py:306
  19.9 2.9 %collective-permute-done.2.refs_3_ = bf16[64,3840]{1,0:T(8,128)(2,1)S(1)} collective-permute-done((bf16[64,3840]{1,0:T(8,128)(2,1)S(1)}, bf16[64,3840]{1,0:T(8,128)(2,1)S(1)}, u32[]{:S(2)}, u32[]{:S(2)}) %collective-permute-start.2) | collective-permute-done | bytes 491552 | tf_op jit(solution)/shard_map/ppermute | solution.py:301
  22.8 3.4 %collective-permute-done.1.refs_2_ = bf16[64,3840]{1,0:T(8,128)(2,1)S(1)} collective-permute-done((bf16[64,3840]{1,0:T(8,128)(2,1)S(1)}, bf16[64,3840]{1,0:T(8,128)(2,1)S(1)}, u32[]{:S(2)}, u32[]{:S(2)}) %collective-permute-start.1) | collective-permute-done | bytes 491552 | tf_op jit(solution)/shard_map/ppermute | solution.py:301
  26.2 1.2 pad_maximum_fusion.2
  27.5 0.4 collective-permute-start.6
  27.9 1.6 %collective-permute-start.5 = (bf16[96,3840]{1,0:T(8,128)(2,1)}, bf16[96,3840]{1,0:T(8,128)(2,1)}, u32[]{:S(2)}, u32[]{:S(2)}) collective-permute-start(bf16[96,3840]{1,0:T(8,128)(2,1)} %get-tuple-element.172), channel_id=1, source_target_pairs={{0,2},{2,4},{4,6},{6,0},{1,3},{3,5},{5,7},{7,1},{8,10},{10,12},{12... | collective-permute-start | bytes 2211848 | tf_op jit(solution)/shard_map/ppermute | solution.py:301
  29.6 0.6 collective-permute-start.7
  30.1 0.9 multiply_bitcast_fusion
  31.1 1.6 collective-permute-start.9
  32.7 0.7 pad_maximum_fusion.5.refs_12_.refs_10_
  33.3 10.0 %collective-permute-done.9 = f32[32,256]{1,0:T(8,128)S(1)} collective-permute-done((f32[32,256]{1,0:T(8,128)S(1)}, f32[32,256]{1,0:T(8,128)S(1)}, u32[]{:S(2)}, u32[]{:S(2)}) %collective-permute-start.9) | collective-permute-done | bytes 32800 | tf_op jit(solution)/shard_map/ppermute | solution.py:306
  43.4 1.2 collective-permute-done.7.refs_1_
  44.6 2.1 %collective-permute-done.6.refs_5_ = bf16[96,3840]{1,0:T(8,128)(2,1)} collective-permute-done((bf16[96,3840]{1,0:T(8,128)(2,1)}, bf16[96,3840]{1,0:T(8,128)(2,1)}, u32[]{:S(2)}, u32[]{:S(2)}) %collective-permute-start.6) | collective-permute-done | bytes 737312 | tf_op jit(solution)/shard_map/ppermute | solution.py:301
  46.7 1.3 collective-permute-done.5.refs_4_
  48.0 1.7 %collective-permute-start.12 = (f32[32,256]{1,0:T(8,128)S(1)}, f32[32,256]{1,0:T(8,128)S(1)}, u32[]{:S(2)}, u32[]{:S(2)}) collective-permute-start(f32[32,256]{1,0:T(8,128)S(1)} %add.74), channel_id=1, source_target_pairs={{0,32},{32,0},{64,96},{96,64},{1,33},{33,1},{65,97},{97,65},{2,34}... | collective-permute-start | bytes 98312 | tf_op jit(solution)/shard_map/ppermute | solution.py:306
  49.6 1.0 slice.64
  50.6 1.0 slice.65
  51.6 0.4 collective-permute-start.11
  51.9 1.7 %collective-permute-start.10 = (bf16[32,3840]{1,0:T(8,128)(2,1)S(1)}, bf16[32,3840]{1,0:T(8,128)(2,1)S(1)}, u32[]{:S(2)}, u32[]{:S(2)}) collective-permute-start(bf16[32,3840]{1,0:T(8,128)(2,1)S(1)} %slice.64), channel_id=1, source_target_pairs={{0,2},{2,4},{4,6},{6,0},{1,3},{3,5},{5,7},{7,1},{8,10},{10,12},{12... | collective-permute-start | bytes 737288 | tf_op jit(solution)/shard_map/ppermute | solution.py:301
  53.7 1.0 pad_maximum_fusion.1
  54.7 3.8 %collective-permute-done.11.refs_7_ = bf16[32,3840]{1,0:T(8,128)(2,1)S(1)} collective-permute-done((bf16[32,3840]{1,0:T(8,128)(2,1)S(1)}, bf16[32,3840]{1,0:T(8,128)(2,1)S(1)}, u32[]{:S(2)}, u32[]{:S(2)}) %collective-permute-start.11) | collective-permute-done | bytes 245792 | tf_op jit(solution)/shard_map/ppermute | solution.py:301
  58.6 1.5 collective-permute-done.10.refs_6_
  60.1 1.0 collective-permute-start.14
  61.1 1.0 collective-permute-start.13
  62.1 2.9 %collective-permute-start.15 = (f32[32,256]{1,0:T(8,128)S(1)}, f32[32,256]{1,0:T(8,128)S(1)}, u32[]{:S(2)}, u32[]{:S(2)}) collective-permute-start(f32[32,256]{1,0:T(8,128)S(1)} %add.75), channel_id=1, source_target_pairs={{0,64},{32,96},{64,0},{96,32},{1,65},{33,97},{65,1},{97,33},{2,66}... | collective-permute-start | bytes 98312 | tf_op jit(solution)/shard_map/ppermute | solution.py:306
  65.0 18.4 %partial.1 = (f32[128,1856]{1,0:T(8,128)}, bf16[128,1920]{1,0:T(8,128)(2,1)}, bf16[128,1920]{1,0:T(8,128)(2,1)}, bf16[128,1920]{1,0:T(8,128)(2,1)}) custom-call(s32[1]{0:T(128)} %bitcast.base, bf16[128,3840]{1,0:T(8,128)(2,1)} %copy-done.1, bf16[64,3840]{1,0:T(8,128)(2,1)} %copy-done.6, bf16[64,3840]{1,0:T(8,128)(2,1)} %copy-done.11, ...), custom_call_target="tpu_custom_call" | custom-call | flops 1 | bytes 1 | tf_op jit(solution)/shard_map/partial/pallas_call | solution.py:135
  83.5 0.9 collective-permute-done.13.refs_2_
  84.4 0.3 fusion.5
  84.7 0.3 fusion.11
  85.3 1.7 %collective-permute-start.17 = (bf16[64,3840]{1,0:T(8,128)(2,1)S(1)}, bf16[64,3840]{1,0:T(8,128)(2,1)S(1)}, u32[]{:S(2)}, u32[]{:S(2)}) collective-permute-start(bf16[64,3840]{1,0:T(8,128)(2,1)S(1)} %slice.67), channel_id=1, source_target_pairs={{0,6},{2,0},{4,2},{6,4},{1,7},{3,1},{5,3},{7,5},{8,14},{10,8},{12,... | collective-permute-start | bytes 1474568 | tf_op jit(solution)/shard_map/ppermute | solution.py:301
  87.0 0.4 collective-permute-start.16
  87.4 0.4 collective-permute-start.18
  87.9 2.8 %collective-permute-start.19 = (bf16[128,1920]{1,0:T(8,128)(2,1)S(1)}, bf16[128,1920]{1,0:T(8,128)(2,1)S(1)}, u32[]{:S(2)}, u32[]{:S(2)}) collective-permute-start(bf16[128,1920]{1,0:T(8,128)(2,1)S(1)} %copy-done.26), channel_id=1, source_target_pairs={{0,96},{32,0},{64,32},{96,64},{1,97},{33,1},{65,33},{97,65},{2,98}... | collective-permute-start | bytes 1474568 | tf_op jit(solution)/shard_map/ppermute | solution.py:301
  90.8 0.3 collective-permute-start.20
  91.1 6.8 %collective-permute-done.20 = f32[16,2848]{1,0:T(8,128)S(1)} collective-permute-done((f32[16,2848]{1,0:T(8,128)S(1)}, f32[16,2848]{1,0:T(8,128)S(1)}, u32[]{:S(2)}, u32[]{:S(2)}) %collective-permute-start.20) | collective-permute-done | bytes 182304 | tf_op jit(solution)/shard_map/ppermute | solution.py:306
  98.0 0.7 collective-permute-done.16.refs_4_
  98.7 2.2 %collective-permute-start.21 = (bf16[128,1920]{1,0:T(8,128)(2,1)}, bf16[128,1920]{1,0:T(8,128)(2,1)S(1)}, u32[]{:S(2)}, u32[]{:S(2)}) collective-permute-start(bf16[128,1920]{1,0:T(8,128)(2,1)} %get-tuple-element.121), channel_id=1, source_target_pairs={{0,64},{32,96},{64,0},{96,32},{1,65},{33,97},{65,1},{97,33},{2,66}... | collective-permute-start | bytes 1474568 | tf_op jit(solution)/shard_map/ppermute | solution.py:301
  100.9 11.7 %partial_half.2 = (f32[128,928]{1,0:T(8,128)}, bf16[128,1024]{1,0:T(8,128)(2,1)}, bf16[128,1024]{1,0:T(8,128)(2,1)}, bf16[128,1024]{1,0:T(8,128)(2,1)}) custom-call(s32[1]{0:T(128)} %bitcast.base, bf16[128,3840]{1,0:T(8,128)(2,1)} %copy-done.1, bf16[64,3840]{1,0:T(8,128)(2,1)} %copy-done.5, bf16[128,3840]{1,0:T(8,128)(2,1)} %copy-done.4, ...), custom_call_target="tpu_custom_call" | custom-call | flops 1 | bytes 1 | tf_op jit(solution)/shard_map/partial_half/pallas_call | solution.py:213
  112.7 1.7 %collective-permute-start.22 = (bf16[128,1024]{1,0:T(8,128)(2,1)}, bf16[128,1024]{1,0:T(8,128)(2,1)S(1)}, u32[]{:S(2)}, u32[]{:S(2)}) collective-permute-start(bf16[128,1024]{1,0:T(8,128)(2,1)} %get-tuple-element.129), channel_id=1, source_target_pairs={{0,32},{32,64},{64,96},{96,0},{1,33},{33,65},{65,97},{97,1},{2,34}... | collective-permute-start | bytes 786440 | tf_op jit(solution)/shard_map/ppermute | solution.py:301
  114.3 1.6 %collective-permute-start.23 = (bf16[128,1024]{1,0:T(8,128)(2,1)}, bf16[128,1024]{1,0:T(8,128)(2,1)S(1)}, u32[]{:S(2)}, u32[]{:S(2)}) collective-permute-start(bf16[128,1024]{1,0:T(8,128)(2,1)} %get-tuple-element.130), channel_id=1, source_target_pairs={{0,96},{32,0},{64,32},{96,64},{1,97},{33,1},{65,33},{97,65},{2,98}... | collective-permute-start | bytes 786440 | tf_op jit(solution)/shard_map/ppermute | solution.py:301
  116.0 0.5 collective-permute-start.24
  116.5 11.8 %partial_half.3 = (f32[128,928]{1,0:T(8,128)}, bf16[128,1024]{1,0:T(8,128)(2,1)}, bf16[128,1024]{1,0:T(8,128)(2,1)}, bf16[128,1024]{1,0:T(8,128)(2,1)}) custom-call(s32[1]{0:T(128)} %bitcast.base, bf16[128,3840]{1,0:T(8,128)(2,1)} %copy-done.1, bf16[64,3840]{1,0:T(8,128)(2,1)} %copy-done.5, bf16[128,3840]{1,0:T(8,128)(2,1)} %copy-done.4, ...), custom_call_target="tpu_custom_call" | custom-call | flops 1 | bytes 1 | tf_op jit(solution)/shard_map/partial_half/pallas_call | solution.py:213
  128.4 1.0 collective-permute-start.26
  129.5 2.3 %collective-permute-start.27 = (bf16[128,1024]{1,0:T(8,128)(2,1)}, bf16[128,1024]{1,0:T(8,128)(2,1)S(1)}, u32[]{:S(2)}, u32[]{:S(2)}) collective-permute-start(bf16[128,1024]{1,0:T(8,128)(2,1)} %get-tuple-element.135), channel_id=1, source_target_pairs={{0,96},{32,0},{64,32},{96,64},{1,97},{33,1},{65,33},{97,65},{2,98}... | collective-permute-start | bytes 786440 | tf_op jit(solution)/shard_map/ppermute | solution.py:301
  131.7 1.8 %collective-permute-start.28 = (bf16[128,1024]{1,0:T(8,128)(2,1)}, bf16[128,1024]{1,0:T(8,128)(2,1)S(1)}, u32[]{:S(2)}, u32[]{:S(2)}) collective-permute-start(bf16[128,1024]{1,0:T(8,128)(2,1)} %get-tuple-element.136), channel_id=1, source_target_pairs={{0,64},{32,96},{64,0},{96,32},{1,65},{33,97},{65,1},{97,33},{2,66}... | collective-permute-start | bytes 786440 | tf_op jit(solution)/shard_map/ppermute | solution.py:301
  133.5 3.8 %collective-permute-start.29 = (f32[16,2848]{1,0:T(8,128)S(1)}, f32[16,2848]{1,0:T(8,128)S(1)}, u32[]{:S(2)}, u32[]{:S(2)}) collective-permute-start(f32[16,2848]{1,0:T(8,128)S(1)} %add.82), channel_id=1, source_target_pairs={{0,4},{2,6},{4,0},{6,2},{1,5},{3,7},{5,1},{7,3},{8,12},{10,14},{12... | collective-permute-start | bytes 546824 | tf_op jit(solution)/shard_map/ppermute | solution.py:306
  137.3 2.9 %fold.4 = (f32[64,928]{1,0:T(8,128)}, bf16[64,1024]{1,0:T(8,128)(2,1)}) custom-call(s32[1]{0:T(128)} %bitcast.2.swap, f32[128,928]{1,0:T(8,128)} %get-tuple-element.143.own, bf16[128,1024]{1,0:T(8,128)(2,1)} %copy-done.15, bf16[128,1024]{1,0:T(8,128)(2,1)} %copy-done.16, bf16[128,1024]{1,0:T(8,128)(2,1)} %copy-done.17), custom_call_target="tpu_custom_call" | custom-call | flops 1 | bytes 1 | tf_op jit(solution)/shard_map/fold/pallas_call | solution.py:258
  140.3 4.3 %fold.3 = (f32[64,1856]{1,0:T(8,128)}, bf16[64,1920]{1,0:T(8,128)(2,1)}) custom-call(s32[1]{0:T(128)} %bitcast.2.swap, f32[128,1856]{1,0:T(8,128)} %get-tuple-element.137.own, bf16[128,1920]{1,0:T(8,128)(2,1)} %copy-done.12, bf16[128,1920]{1,0:T(8,128)(2,1)} %copy-done.13, bf16[128,1920]{1,0:T(8,128)(2,1)} %copy-done.14), custom_call_target="tpu_custom_call" | custom-call | flops 1 | bytes 1 | tf_op jit(solution)/shard_map/fold/pallas_call | solution.py:258
  144.7 0.6 collective-permute-start.30
  145.5 2.9 %fold.5 = (f32[64,928]{1,0:T(8,128)}, bf16[64,1024]{1,0:T(8,128)(2,1)}) custom-call(s32[1]{0:T(128)} %bitcast.2.swap, f32[128,928]{1,0:T(8,128)} %get-tuple-element.153.own, bf16[128,1024]{1,0:T(8,128)(2,1)} %copy-done.18, bf16[128,1024]{1,0:T(8,128)(2,1)} %copy-done.19, bf16[128,1024]{1,0:T(8,128)(2,1)} %copy-done.20), custom_call_target="tpu_custom_call" | custom-call | flops 1 | bytes 1 | tf_op jit(solution)/shard_map/fold/pallas_call | solution.py:258
  148.4 1.3 collective-permute-start.32
  149.7 0.7 slice.89
  150.5 0.7 collective-permute-start.31
  151.2 0.6 slice_bitcast_fusion
  151.8 3.6 %collective-permute-done.31.got1 = bf16[64,1024]{1,0:T(8,128)(2,1)S(1)} collective-permute-done((bf16[64,1024]{1,0:T(8,128)(2,1)S(1)}, bf16[64,1024]{1,0:T(8,128)(2,1)S(1)}, u32[]{:S(2)}, u32[]{:S(2)}) %collective-permute-start.31) | collective-permute-done | bytes 131104 | tf_op jit(solution)/shard_map/ppermute | solution.py:306
  155.5 0.6 copy-done.25
  156.2 2.9 %finish.1 = bf16[1856,128]{1,0:T(8,128)(2,1)} custom-call(f32[64,1856]{1,0:T(8,128)} %get-tuple-element.150.keep0, bf16[64,1920]{1,0:T(8,128)(2,1)} %copy-done.21, f32[64,928]{1,0:T(8,128)} %get-tuple-element.161.keep1, bf16[64,1024]{1,0:T(8,128)(2,1)} %copy-done.25, f32[64,928]{1,0:T(8,128)} %get-tuple-element.163.keep2, bf16[64,1024]{1,0:T(8,128)(2,1)} %copy-done.24), custom_call_target="tpu_custom_call" | custom-call | tf_op jit(solution)/shard_map/finish/pallas_call | solution.py:289
  (101 shorter events, 1.5 us)
Async XLA Ops:
  0.6 3.0 %copy-start = (bf16[256,928]{0,1:T(8,128)(2,1)S(1)}, bf16[256,928]{0,1:T(8,128)(2,1)}, u32[]{:S(2)}) copy-start(bf16[256,928]{0,1:T(8,128)(2,1)} %param.5) | copy-start | bytes 1425412
  0.7 11.3 %copy-start.2 = (bf16[256,1920]{1,0:T(8,128)(2,1)S(1)}, bf16[256,1920]{1,0:T(8,128)(2,1)}, u32[]{:S(2)}) copy-start(bf16[256,1920]{1,0:T(8,128)(2,1)} %param.6) | copy-start | bytes 2949124
  2.0 2.6 %collective-permute-start = (bf16[128,1920]{1,0:T(8,128)(2,1)S(1)}, bf16[128,1920]{1,0:T(8,128)(2,1)S(1)}, u32[]{:S(2)}, u32[]{:S(2)}) collective-permute-start(bf16[128,1920]{1,0:T(8,128)(2,1)S(1)} %get-tuple-element.170), channel_id=1, source_target_pairs={{0,8},{8,0},{1,9},{9,1},{2,10},{10,2},{3,11},{11,3},{4,12},{12,4},... | collective-permute-start | bytes 1474568 | tf_op jit(solution)/shard_map/ppermute | solution.py:306
  3.6 8.8 %copy-start.9 = (bf16[16,1920]{1,0:T(8,128)(2,1)}, bf16[16,1920]{1,0:T(8,128)(2,1)S(1)}, u32[]{:S(2)}) copy-start(bf16[16,1920]{1,0:T(8,128)(2,1)S(1)} %get-tuple-element.168.refs_10_.refs_8_) | copy-start | bytes 184324
  4.7 15.2 %collective-permute-start.3 = (bf16[64,3840]{1,0:T(8,128)(2,1)S(1)}, bf16[64,3840]{1,0:T(8,128)(2,1)S(1)}, u32[]{:S(2)}, u32[]{:S(2)}) collective-permute-start(bf16[64,3840]{1,0:T(8,128)(2,1)S(1)} %fusion), channel_id=1, source_target_pairs={{0,1},{1,0},{2,3},{3,2},{4,5},{5,4},{6,7},{7,6},{8,9},{9,8},{10,11... | collective-permute-start | bytes 1474568 | tf_op jit(solution)/shard_map/ppermute | solution.py:306
  7.9 14.9 %collective-permute-start.2 = (bf16[64,3840]{1,0:T(8,128)(2,1)S(1)}, bf16[64,3840]{1,0:T(8,128)(2,1)S(1)}, u32[]{:S(2)}, u32[]{:S(2)}) collective-permute-start(bf16[64,3840]{1,0:T(8,128)(2,1)S(1)} %fusion), channel_id=1, source_target_pairs={{0,6},{2,0},{4,2},{6,4},{1,7},{3,1},{5,3},{7,5},{8,14},{10,8},{12,... | collective-permute-start | bytes 1474568 | tf_op jit(solution)/shard_map/ppermute | solution.py:301
  11.9 14.2 %collective-permute-start.1 = (bf16[64,3840]{1,0:T(8,128)(2,1)S(1)}, bf16[64,3840]{1,0:T(8,128)(2,1)S(1)}, u32[]{:S(2)}, u32[]{:S(2)}) collective-permute-start(bf16[64,3840]{1,0:T(8,128)(2,1)S(1)} %fusion), channel_id=1, source_target_pairs={{0,2},{2,4},{4,6},{6,0},{1,3},{3,5},{5,7},{7,1},{8,10},{10,12},{12... | collective-permute-start | bytes 1474568 | tf_op jit(solution)/shard_map/ppermute | solution.py:301
  12.3 1.3 collective-permute-start.4
  12.5 41.2 %copy-start.1 = (bf16[128,3840]{1,0:T(8,128)(2,1)}, bf16[128,3840]{1,0:T(8,128)(2,1)S(1)}, u32[]{:S(2)}) copy-start(bf16[128,3840]{1,0:T(8,128)(2,1)S(1)} %pad_maximum_fusion.refs_0_) | copy-start | bytes 2949124
  19.9 9.6 %copy-start.6 = (bf16[64,3840]{1,0:T(8,128)(2,1)}, bf16[64,3840]{1,0:T(8,128)(2,1)S(1)}, u32[]{:S(2)}) copy-start(bf16[64,3840]{1,0:T(8,128)(2,1)S(1)} %collective-permute-done.3.refs_1_) | copy-start | bytes 1474564
  22.8 6.8 %copy-start.10 = (bf16[64,3840]{1,0:T(8,128)(2,1)}, bf16[64,3840]{1,0:T(8,128)(2,1)S(1)}, u32[]{:S(2)}) copy-start(bf16[64,3840]{1,0:T(8,128)(2,1)S(1)} %collective-permute-done.2.refs_3_) | copy-start | bytes 1474564
  26.2 3.4 %copy-start.11 = (bf16[64,3840]{1,0:T(8,128)(2,1)}, bf16[64,3840]{1,0:T(8,128)(2,1)S(1)}, u32[]{:S(2)}) copy-start(bf16[64,3840]{1,0:T(8,128)(2,1)S(1)} %collective-permute-done.1.refs_2_) | copy-start | bytes 1474564
  26.2 21.8 %collective-permute-start.8 = (bf16[1856,1920]{1,0:T(8,128)(2,1)}, bf16[1856,1920]{1,0:T(8,128)(2,1)}, u32[]{:S(2)}, u32[]{:S(2)}) collective-permute-start(bf16[1856,1920]{1,0:T(8,128)(2,1)} %refs_6_.1), channel_id=1, source_target_pairs={{0,8},{8,0},{1,9},{9,1},{2,10},{10,2},{3,11},{11,3},{4,12},{12,4},... | collective-permute-start | bytes 21381128 | tf_op jit(solution)/shard_map/ppermute | solution.py:306
  27.5 19.2 %collective-permute-start.6 = (bf16[96,3840]{1,0:T(8,128)(2,1)}, bf16[96,3840]{1,0:T(8,128)(2,1)}, u32[]{:S(2)}, u32[]{:S(2)}) collective-permute-start(bf16[96,3840]{1,0:T(8,128)(2,1)} %get-tuple-element.171), channel_id=1, source_target_pairs={{0,6},{2,0},{4,2},{6,4},{1,7},{3,1},{5,3},{7,5},{8,14},{10,8},{12,... | collective-permute-start | bytes 2211848 | tf_op jit(solution)/shard_map/ppermute | solution.py:301
  27.9 20.1 %collective-permute-start.5 = (bf16[96,3840]{1,0:T(8,128)(2,1)}, bf16[96,3840]{1,0:T(8,128)(2,1)}, u32[]{:S(2)}, u32[]{:S(2)}) collective-permute-start(bf16[96,3840]{1,0:T(8,128)(2,1)} %get-tuple-element.172), channel_id=1, source_target_pairs={{0,2},{2,4},{4,6},{6,0},{1,3},{3,5},{5,7},{7,1},{8,10},{10,12},{12... | collective-permute-start | bytes 2211848 | tf_op jit(solution)/shard_map/ppermute | solution.py:301
  29.6 15.0 %collective-permute-start.7 = (bf16[64,3840]{1,0:T(8,128)(2,1)S(1)}, bf16[64,3840]{1,0:T(8,128)(2,1)S(1)}, u32[]{:S(2)}, u32[]{:S(2)}) collective-permute-start(bf16[64,3840]{1,0:T(8,128)(2,1)S(1)} %slice.62), channel_id=1, source_target_pairs={{0,1},{1,0},{2,3},{3,2},{4,5},{5,4},{6,7},{7,6},{8,9},{9,8},{10,11... | collective-permute-start | bytes 1474568 | tf_op jit(solution)/shard_map/ppermute | solution.py:306
  31.1 12.3 %collective-permute-start.9 = (f32[32,256]{1,0:T(8,128)S(1)}, f32[32,256]{1,0:T(8,128)S(1)}, u32[]{:S(2)}, u32[]{:S(2)}) collective-permute-start(f32[32,256]{1,0:T(8,128)S(1)} %add.70), channel_id=1, source_target_pairs={{0,16},{16,0},{1,17},{17,1},{2,18},{18,2},{3,19},{19,3},{4,20},{20... | collective-permute-start | bytes 98312 | tf_op jit(solution)/shard_map/ppermute | solution.py:306
  44.6 10.2 %copy-start.5 = (bf16[64,3840]{1,0:T(8,128)(2,1)}, bf16[64,3840]{1,0:T(8,128)(2,1)S(1)}, u32[]{:S(2)}) copy-start(bf16[64,3840]{1,0:T(8,128)(2,1)S(1)} %collective-permute-done.7.refs_1_) | copy-start | bytes 1474564
  48.0 6.7 %collective-permute-start.12 = (f32[32,256]{1,0:T(8,128)S(1)}, f32[32,256]{1,0:T(8,128)S(1)}, u32[]{:S(2)}, u32[]{:S(2)}) collective-permute-start(f32[32,256]{1,0:T(8,128)S(1)} %add.74), channel_id=1, source_target_pairs={{0,32},{32,0},{64,96},{96,64},{1,33},{33,1},{65,97},{97,65},{2,34}... | collective-permute-start | bytes 98312 | tf_op jit(solution)/shard_map/ppermute | solution.py:306
  51.6 7.0 %collective-permute-start.11 = (bf16[32,3840]{1,0:T(8,128)(2,1)S(1)}, bf16[32,3840]{1,0:T(8,128)(2,1)S(1)}, u32[]{:S(2)}, u32[]{:S(2)}) collective-permute-start(bf16[32,3840]{1,0:T(8,128)(2,1)S(1)} %slice.65), channel_id=1, source_target_pairs={{0,6},{2,0},{4,2},{6,4},{1,7},{3,1},{5,3},{7,5},{8,14},{10,8},{12,... | collective-permute-start | bytes 737288 | tf_op jit(solution)/shard_map/ppermute | solution.py:301
  51.9 8.2 %collective-permute-start.10 = (bf16[32,3840]{1,0:T(8,128)(2,1)S(1)}, bf16[32,3840]{1,0:T(8,128)(2,1)S(1)}, u32[]{:S(2)}, u32[]{:S(2)}) collective-permute-start(bf16[32,3840]{1,0:T(8,128)(2,1)S(1)} %slice.64), channel_id=1, source_target_pairs={{0,2},{2,4},{4,6},{6,0},{1,3},{3,5},{5,7},{7,1},{8,10},{10,12},{12... | collective-permute-start | bytes 737288 | tf_op jit(solution)/shard_map/ppermute | solution.py:301
  58.6 1.5 copy-start.22
  60.1 1.0 copy-start.23
  60.1 23.3 %collective-permute-start.14 = (bf16[128,3840]{1,0:T(8,128)(2,1)}, bf16[128,3840]{1,0:T(8,128)(2,1)S(1)}, u32[]{:S(2)}, u32[]{:S(2)}) collective-permute-start(bf16[128,3840]{1,0:T(8,128)(2,1)} %pad_maximum_fusion.1), channel_id=1, source_target_pairs={{0,6},{2,0},{4,2},{6,4},{1,7},{3,1},{5,3},{7,5},{8,14},{10,8},{12,... | collective-permute-start | bytes 2949128 | tf_op jit(solution)/shard_map/ppermute | solution.py:301
  61.1 23.3 %collective-permute-start.13 = (bf16[128,3840]{1,0:T(8,128)(2,1)}, bf16[128,3840]{1,0:T(8,128)(2,1)S(1)}, u32[]{:S(2)}, u32[]{:S(2)}) collective-permute-start(bf16[128,3840]{1,0:T(8,128)(2,1)} %pad_maximum_fusion.1), channel_id=1, source_target_pairs={{0,2},{2,4},{4,6},{6,0},{1,3},{3,5},{5,7},{7,1},{8,10},{10,12},{12... | collective-permute-start | bytes 2949128 | tf_op jit(solution)/shard_map/ppermute | solution.py:301
  62.1 21.3 %collective-permute-start.15 = (f32[32,256]{1,0:T(8,128)S(1)}, f32[32,256]{1,0:T(8,128)S(1)}, u32[]{:S(2)}, u32[]{:S(2)}) collective-permute-start(f32[32,256]{1,0:T(8,128)S(1)} %add.75), channel_id=1, source_target_pairs={{0,64},{32,96},{64,0},{96,32},{1,65},{33,97},{65,1},{97,33},{2,66}... | collective-permute-start | bytes 98312 | tf_op jit(solution)/shard_map/ppermute | solution.py:306
  83.4 1.6 %copy-start.3 = (bf16[128,3840]{1,0:T(8,128)(2,1)}, bf16[128,3840]{1,0:T(8,128)(2,1)S(1)}, u32[]{:S(2)}) copy-start(bf16[128,3840]{1,0:T(8,128)(2,1)S(1)} %collective-permute-done.14.refs_3_) | copy-start | bytes 2949124
  84.4 0.9 copy-start.4
  84.7 2.8 %copy-start.27 = (bf16[128,1920]{1,0:T(8,128)(2,1)S(1)}, bf16[128,1920]{1,0:T(8,128)(2,1)}, u32[]{:S(2)}) copy-start(bf16[128,1920]{1,0:T(8,128)(2,1)} %get-tuple-element.111) | copy-start | bytes 1474564
  84.7 3.2 %copy-start.26 = (bf16[128,1920]{1,0:T(8,128)(2,1)S(1)}, bf16[128,1920]{1,0:T(8,128)(2,1)}, u32[]{:S(2)}) copy-start(bf16[128,1920]{1,0:T(8,128)(2,1)} %get-tuple-element.112) | copy-start | bytes 1474564
  85.3 12.6 %collective-permute-start.17 = (bf16[64,3840]{1,0:T(8,128)(2,1)S(1)}, bf16[64,3840]{1,0:T(8,128)(2,1)S(1)}, u32[]{:S(2)}, u32[]{:S(2)}) collective-permute-start(bf16[64,3840]{1,0:T(8,128)(2,1)S(1)} %slice.67), channel_id=1, source_target_pairs={{0,6},{2,0},{4,2},{6,4},{1,7},{3,1},{5,3},{7,5},{8,14},{10,8},{12,... | collective-permute-start | bytes 1474568 | tf_op jit(solution)/shard_map/ppermute | solution.py:301
  87.0 11.7 %collective-permute-start.16 = (bf16[64,3840]{1,0:T(8,128)(2,1)S(1)}, bf16[64,3840]{1,0:T(8,128)(2,1)S(1)}, u32[]{:S(2)}, u32[]{:S(2)}) collective-permute-start(bf16[64,3840]{1,0:T(8,128)(2,1)S(1)} %slice.66), channel_id=1, source_target_pairs={{0,2},{2,4},{4,6},{6,0},{1,3},{3,5},{5,7},{7,1},{8,10},{10,12},{12... | collective-permute-start | bytes 1474568 | tf_op jit(solution)/shard_map/ppermute | solution.py:301
  87.4 11.3 %collective-permute-start.18 = (bf16[128,1920]{1,0:T(8,128)(2,1)S(1)}, bf16[128,1920]{1,0:T(8,128)(2,1)S(1)}, u32[]{:S(2)}, u32[]{:S(2)}) collective-permute-start(bf16[128,1920]{1,0:T(8,128)(2,1)S(1)} %copy-done.27), channel_id=1, source_target_pairs={{0,32},{32,64},{64,96},{96,0},{1,33},{33,65},{65,97},{97,1},{2,34}... | collective-permute-start | bytes 1474568 | tf_op jit(solution)/shard_map/ppermute | solution.py:301
  87.9 10.8 %collective-permute-start.19 = (bf16[128,1920]{1,0:T(8,128)(2,1)S(1)}, bf16[128,1920]{1,0:T(8,128)(2,1)S(1)}, u32[]{:S(2)}, u32[]{:S(2)}) collective-permute-start(bf16[128,1920]{1,0:T(8,128)(2,1)S(1)} %copy-done.26), channel_id=1, source_target_pairs={{0,96},{32,0},{64,32},{96,64},{1,97},{33,1},{65,33},{97,65},{2,98}... | collective-permute-start | bytes 1474568 | tf_op jit(solution)/shard_map/ppermute | solution.py:301
  90.8 7.2 %collective-permute-start.20 = (f32[16,2848]{1,0:T(8,128)S(1)}, f32[16,2848]{1,0:T(8,128)S(1)}, u32[]{:S(2)}, u32[]{:S(2)}) collective-permute-start(f32[16,2848]{1,0:T(8,128)S(1)} %pad_maximum_fusion.4), channel_id=1, source_target_pairs={{0,1},{1,0},{2,3},{3,2},{4,5},{5,4},{6,7},{7,6},{8,9},{9,8},{10,11... | collective-permute-start | bytes 546824 | tf_op jit(solution)/shard_map/ppermute | solution.py:306
  98.0 3.0 %copy-start.7 = (bf16[64,3840]{1,0:T(8,128)(2,1)}, bf16[64,3840]{1,0:T(8,128)(2,1)S(1)}, u32[]{:S(2)}) copy-start(bf16[64,3840]{1,0:T(8,128)(2,1)S(1)} %collective-permute-done.17.refs_5_) | copy-start | bytes 1474564
  98.7 2.2 %copy-start.8 = (bf16[64,3840]{1,0:T(8,128)(2,1)}, bf16[64,3840]{1,0:T(8,128)(2,1)S(1)}, u32[]{:S(2)}) copy-start(bf16[64,3840]{1,0:T(8,128)(2,1)S(1)} %collective-permute-done.16.refs_4_) | copy-start | bytes 1474564
  98.7 13.9 %copy-start.12 = (bf16[128,1920]{1,0:T(8,128)(2,1)}, bf16[128,1920]{1,0:T(8,128)(2,1)S(1)}, u32[]{:S(2)}) copy-start(bf16[128,1920]{1,0:T(8,128)(2,1)S(1)} %collective-permute-done.18.a) | copy-start | bytes 1474564
  98.7 13.9 %copy-start.13 = (bf16[128,1920]{1,0:T(8,128)(2,1)}, bf16[128,1920]{1,0:T(8,128)(2,1)S(1)}, u32[]{:S(2)}) copy-start(bf16[128,1920]{1,0:T(8,128)(2,1)S(1)} %collective-permute-done.19.b) | copy-start | bytes 1474564
  98.7 13.9 %collective-permute-start.21 = (bf16[128,1920]{1,0:T(8,128)(2,1)}, bf16[128,1920]{1,0:T(8,128)(2,1)S(1)}, u32[]{:S(2)}, u32[]{:S(2)}) collective-permute-start(bf16[128,1920]{1,0:T(8,128)(2,1)} %get-tuple-element.121), channel_id=1, source_target_pairs={{0,64},{32,96},{64,0},{96,32},{1,65},{33,97},{65,1},{97,33},{2,66}... | collective-permute-start | bytes 1474568 | tf_op jit(solution)/shard_map/ppermute | solution.py:301
  112.7 15.7 %copy-start.14 = (bf16[128,1920]{1,0:T(8,128)(2,1)}, bf16[128,1920]{1,0:T(8,128)(2,1)S(1)}, u32[]{:S(2)}) copy-start(bf16[128,1920]{1,0:T(8,128)(2,1)S(1)} %collective-permute-done.21.c) | copy-start | bytes 1474564
  112.7 15.7 %collective-permute-start.22 = (bf16[128,1024]{1,0:T(8,128)(2,1)}, bf16[128,1024]{1,0:T(8,128)(2,1)S(1)}, u32[]{:S(2)}, u32[]{:S(2)}) collective-permute-start(bf16[128,1024]{1,0:T(8,128)(2,1)} %get-tuple-element.129), channel_id=1, source_target_pairs={{0,32},{32,64},{64,96},{96,0},{1,33},{33,65},{65,97},{97,1},{2,34}... | collective-permute-start | bytes 786440 | tf_op jit(solution)/shard_map/ppermute | solution.py:301
  114.3 14.1 %collective-permute-start.23 = (bf16[128,1024]{1,0:T(8,128)(2,1)}, bf16[128,1024]{1,0:T(8,128)(2,1)S(1)}, u32[]{:S(2)}, u32[]{:S(2)}) collective-permute-start(bf16[128,1024]{1,0:T(8,128)(2,1)} %get-tuple-element.130), channel_id=1, source_target_pairs={{0,96},{32,0},{64,32},{96,64},{1,97},{33,1},{65,33},{97,65},{2,98}... | collective-permute-start | bytes 786440 | tf_op jit(solution)/shard_map/ppermute | solution.py:301
  116.0 12.4 %collective-permute-start.24 = (bf16[128,1024]{1,0:T(8,128)(2,1)}, bf16[128,1024]{1,0:T(8,128)(2,1)S(1)}, u32[]{:S(2)}, u32[]{:S(2)}) collective-permute-start(bf16[128,1024]{1,0:T(8,128)(2,1)} %get-tuple-element.131), channel_id=1, source_target_pairs={{0,64},{32,96},{64,0},{96,32},{1,65},{33,97},{65,1},{97,33},{2,66}... | collective-permute-start | bytes 786440 | tf_op jit(solution)/shard_map/ppermute | solution.py:301
  116.5 11.9 %collective-permute-start.25 = (f32[16,2848]{1,0:T(8,128)S(1)}, f32[16,2848]{1,0:T(8,128)S(1)}, u32[]{:S(2)}, u32[]{:S(2)}) collective-permute-start(f32[16,2848]{1,0:T(8,128)S(1)} %add.81), channel_id=1, source_target_pairs={{0,2},{2,0},{4,6},{6,4},{1,3},{3,1},{5,7},{7,5},{8,10},{10,8},{12,... | collective-permute-start | bytes 546824 | tf_op jit(solution)/shard_map/ppermute | solution.py:306
  128.4 8.9 %copy-start.15 = (bf16[128,1024]{1,0:T(8,128)(2,1)}, bf16[128,1024]{1,0:T(8,128)(2,1)S(1)}, u32[]{:S(2)}) copy-start(bf16[128,1024]{1,0:T(8,128)(2,1)S(1)} %collective-permute-done.22.a) | copy-start | bytes 786436
  128.4 8.9 %copy-start.16 = (bf16[128,1024]{1,0:T(8,128)(2,1)}, bf16[128,1024]{1,0:T(8,128)(2,1)S(1)}, u32[]{:S(2)}) copy-start(bf16[128,1024]{1,0:T(8,128)(2,1)S(1)} %collective-permute-done.23.b) | copy-start | bytes 786436
  128.4 8.9 %copy-start.17 = (bf16[128,1024]{1,0:T(8,128)(2,1)}, bf16[128,1024]{1,0:T(8,128)(2,1)S(1)}, u32[]{:S(2)}) copy-start(bf16[128,1024]{1,0:T(8,128)(2,1)S(1)} %collective-permute-done.24.c) | copy-start | bytes 786436
  128.4 16.2 %collective-permute-start.26 = (bf16[128,1024]{1,0:T(8,128)(2,1)}, bf16[128,1024]{1,0:T(8,128)(2,1)S(1)}, u32[]{:S(2)}, u32[]{:S(2)}) collective-permute-start(bf16[128,1024]{1,0:T(8,128)(2,1)} %get-tuple-element.134), channel_id=1, source_target_pairs={{0,32},{32,64},{64,96},{96,0},{1,33},{33,65},{65,97},{97,1},{2,34}... | collective-permute-start | bytes 786440 | tf_op jit(solution)/shard_map/ppermute | solution.py:301
  129.5 15.2 %collective-permute-start.27 = (bf16[128,1024]{1,0:T(8,128)(2,1)}, bf16[128,1024]{1,0:T(8,128)(2,1)S(1)}, u32[]{:S(2)}, u32[]{:S(2)}) collective-permute-start(bf16[128,1024]{1,0:T(8,128)(2,1)} %get-tuple-element.135), channel_id=1, source_target_pairs={{0,96},{32,0},{64,32},{96,64},{1,97},{33,1},{65,33},{97,65},{2,98}... | collective-permute-start | bytes 786440 | tf_op jit(solution)/shard_map/ppermute | solution.py:301
  131.7 12.9 %collective-permute-start.28 = (bf16[128,1024]{1,0:T(8,128)(2,1)}, bf16[128,1024]{1,0:T(8,128)(2,1)S(1)}, u32[]{:S(2)}, u32[]{:S(2)}) collective-permute-start(bf16[128,1024]{1,0:T(8,128)(2,1)} %get-tuple-element.136), channel_id=1, source_target_pairs={{0,64},{32,96},{64,0},{96,32},{1,65},{33,97},{65,1},{97,33},{2,66}... | collective-permute-start | bytes 786440 | tf_op jit(solution)/shard_map/ppermute | solution.py:301
  133.5 11.1 %collective-permute-start.29 = (f32[16,2848]{1,0:T(8,128)S(1)}, f32[16,2848]{1,0:T(8,128)S(1)}, u32[]{:S(2)}, u32[]{:S(2)}) collective-permute-start(f32[16,2848]{1,0:T(8,128)S(1)} %add.82), channel_id=1, source_target_pairs={{0,4},{2,6},{4,0},{6,2},{1,5},{3,7},{5,1},{7,3},{8,12},{10,14},{12... | collective-permute-start | bytes 546824 | tf_op jit(solution)/shard_map/ppermute | solution.py:306
  140.3 10.2 %copy-start.28 = (bf16[64,1024]{1,0:T(8,128)(2,1)S(1)}, bf16[64,1024]{1,0:T(8,128)(2,1)}, u32[]{:S(2)}) copy-start(bf16[64,1024]{1,0:T(8,128)(2,1)} %get-tuple-element.152) | copy-start | bytes 393220
  144.6 0.7 copy-start.18
  144.6 0.8 copy-start.19
  144.7 0.8 copy-start.20
  144.7 10.8 %collective-permute-start.30 = (bf16[64,1920]{1,0:T(8,128)(2,1)}, bf16[64,1920]{1,0:T(8,128)(2,1)S(1)}, u32[]{:S(2)}, u32[]{:S(2)}) collective-permute-start(bf16[64,1920]{1,0:T(8,128)(2,1)} %get-tuple-element.151), channel_id=1, source_target_pairs={{0,16},{16,0},{1,17},{17,1},{2,18},{18,2},{3,19},{19,3},{4,20},{20... | collective-permute-start | bytes 737288 | tf_op jit(solution)/shard_map/ppermute | solution.py:306
  148.4 7.1 %collective-permute-start.32 = (bf16[64,1024]{1,0:T(8,128)(2,1)}, bf16[64,1024]{1,0:T(8,128)(2,1)S(1)}, u32[]{:S(2)}, u32[]{:S(2)}) collective-permute-start(bf16[64,1024]{1,0:T(8,128)(2,1)} %get-tuple-element.157), channel_id=1, source_target_pairs={{0,16},{16,0},{1,17},{17,1},{2,18},{18,2},{3,19},{19,3},{4,20},{20... | collective-permute-start | bytes 393224 | tf_op jit(solution)/shard_map/ppermute | solution.py:306
  150.5 5.0 %collective-permute-start.31 = (bf16[64,1024]{1,0:T(8,128)(2,1)S(1)}, bf16[64,1024]{1,0:T(8,128)(2,1)S(1)}, u32[]{:S(2)}, u32[]{:S(2)}) collective-permute-start(bf16[64,1024]{1,0:T(8,128)(2,1)S(1)} %copy-done.28), channel_id=1, source_target_pairs={{0,16},{16,0},{1,17},{17,1},{2,18},{18,2},{3,19},{19,3},{4,20},{20... | collective-permute-start | bytes 393224 | tf_op jit(solution)/shard_map/ppermute | solution.py:306
  155.5 0.7 copy-start.25
  155.5 0.7 copy-start.24
  155.5 0.8 copy-start.21

commit v4 on v3

--- a/solution.py
+++ b/solution.py
@@ -327,7 +327,6 @@
     rows = tokens // 2
     p = rows * PARTS[0] // sum(PARTS)
     q = rows - p
-    h = p // 2
     base = jnp.reshape(lax.rem(z - y + 4, 4), (1,)).astype(jnp.int32)
     swap = jnp.reshape(xl ^ xh, (1,)).astype(jnp.int32)
 
@@ -348,45 +347,29 @@
     small = jnp.concatenate([low_part, proj_part], axis=0)
 
     up1, down1 = ahead(block[:p], "z", 1), ahead(block[:p], "z", 3)
-    x0 = across(block[:p], "xh", 1)
-    small_other = across(small, "core", 1)
-    block, weight, up1, down1, x0, small, small_other = phase(block, weight, up1, down1, x0, small, small_other)
-    small = small + small_other
-
-    up2 = ahead(jnp.concatenate([up1[:h], x0], axis=0), "z", 1)
-    down2 = ahead(jnp.concatenate([down1[h:], x0], axis=0), "z", 3)
-    x1 = across(block[p:], "xh", 1)
+    far1 = ahead(block[:p], "z", 2)
+    x0, x1 = across(block[:p], "xh", 1), across(block[p:], "xh", 1)
+    block, weight, up1, down1, far1, x0, x1, small = phase(block, weight, up1, down1, far1, x0, x1, small)
+
+    up2, down2 = ahead(x0, "z", 1), ahead(x0, "z", 3)
+    far2 = across(far1, "xh", 1)
     weight_other = across(weight, "core", 1)
-    small_other = across(small, "xl", 1)
-    block, up2, down2, x1, weight_other, small_other, up_other, down3 = phase(
-        block, up2, down2, x1, weight_other, small_other, up_other, down3
+    pair1 = jnp.concatenate([block[p:], x1], axis=0)
+    small = small + across(small, "core", 1)
+    small = small + across(small, "y", 1)
+    small_other = across(small, "y", 2)
+    block, up2, down2, far2, weight_other, pair1, small, small_other, up_other, down3 = phase(
+        block, up2, down2, far2, weight_other, pair1, small, small_other, up_other, down3
     )
     small = small + small_other
 
-    up3, down3z = ahead(up2[h : 2 * h], "z", 1), ahead(down2[2 * h :], "z", 3)
-    small_other = across(small, "y", 1)
-    pair1 = jnp.concatenate([block[p:], x1], axis=0)
-    pair1, up3, down3z, small_other = phase(pair1, up3, down3z, small_other)
-    small = small + small_other
-
     up4, down4 = ahead(pair1, "z", 1), ahead(pair1, "z", 3)
-    layout0 = [
-        (0, 0, p, 0, 0),
-        (1, 0, p, 0, p),
-        (2, 0, p, 3, 0),
-        (3, 0, p, 1, 0),
-        (4, h, p, 3, p),
-        (5, h, p, 1, p),
-        (4, 0, h, 2, 0),
-        (5, 0, h, 2, h),
-        (6, 0, h, 2, p),
-        (7, 0, h, 2, p + h),
-    ]
+    layout0 = [(i, 0, p, step, i % 2 * p) for i, step in enumerate((0, 0, 3, 3, 1, 1, 2, 2))]
     kept0, a0, b0, c0 = partial(
-        base, (block, x0, up1, down1, up2, down2, up3, down3z), layout0, weight, weight_other, up_own, up_other, down3
+        base, (block, x0, up1, up2, down1, down2, far1, far2), layout0, weight, weight_other, up_own, up_other, down3
     )
-    small_other = across(small, "y", 2)
-    up4, down4, kept0, a0, b0, c0, small_other = phase(up4, down4, kept0, a0, b0, c0, small_other)
+    small_other = across(small, "xl", 1)
+    up4, down4, kept0, a0, b0, c0, small, small_other = phase(up4, down4, kept0, a0, b0, c0, small, small_other)
     small = small + small_other
 
     up5, down5 = ahead(up4[:q], "z", 1), ahead(down4[q:], "z", 3)
@@ -431,15 +414,16 @@
     parts_other = across(parts, "z", 2)
     keep0, send0 = fold(swap, kept0, (a0, c0, b0), width)
     keep1, send1 = fold(swap, kept1, (a1, c1, b1), width // 2)
-    a2, c2, b2, keep0, send0, keep1, send1, parts_other = phase(a2, c2, b2, keep0, send0, keep1, send1, parts_other)
-
-    got0, got1 = across(send0, "xl", 1), across(send1, "xl", 1)
+    got1 = across(send1, "xl", 1)
+    a2, c2, b2, keep0, send0, keep1, got1, parts_other = phase(a2, c2, b2, keep0, send0, keep1, got1, parts_other)
+
+    got0 = across(send0, "xl", 1)
     keep2, send2 = fold(swap, kept2, (a2, c2, b2), width // 2)
     got2 = across(send2, "xl", 1)
     parts = after(parts, send2) + parts_other
     grad_a = parts[:, :width_row_block].T
     grad_b = parts[:, width_row_block:]
-    got0, got1, got2, grad_a, grad_b = phase(got0, got1, got2, grad_a, grad_b)
+    got0, got2, grad_a, grad_b = phase(got0, got2, grad_a, grad_b)
     grad_input = finish(keep0, got0, keep1, got1, keep2, got2).T
     return grad_input, grad_a, grad_b
 

time: 160 us -> 158 us (0.988)
  waiting for transfers between devices: 45.8 us -> 42.1 us
  starting transfers between devices: 43.5 us -> 45.7 us
    ppermute x19 -> x18, waiting for transfers between devices: 16.7 us -> 9.49 us  [ahead(): return lax.ppermute(array, axis, [(i, (i + step) % n) for i in range(n)])]
    ppermute x19 -> x18, starting transfers between devices: 26.6 us -> 32.3 us  [ahead(): return lax.ppermute(array, axis, [(i, (i + step) % n) for i in range(n)])]
    ppermute x14 -> x15, starting transfers between devices: 16.9 us -> 13.4 us  [across(): return lax.ppermute(array, axis, [(i, i ^ bit) for i in range(n)])]
    ppermute x14 -> x15, waiting for transfers between devices: 29.1 us -> 32.6 us  [across(): return lax.ppermute(array, axis, [(i, i ^ bit) for i in range(n)])]
    slice x5 -> x0, local copies, waits for them, and re-layouts: 1.99 us -> none  [the longest x2 1.92 us: on_device(): up3, down3z = (ahead(up2[h:2 * h], 'z', 1), ahead(down2[2 * h:], 'z', 3))]
  transfers between devices with their start and end apart: 33 -> 33, of which waited for: 14 -> 12; matrix products, arithmetic and copies ran while one was open for 6% -> 5% of each run, Pallas kernels for 33% -> 33%
where the time goes in v4:
time: 158 us; the launch traced here: 157 us
  Pallas kernels  54.8 us (35%)
  starting transfers between devices  45.7 us (29%)
  waiting for transfers between devices  42.1 us (27%)
  local copies, waits for them, and re-layouts  7.73 us (5%)
  other arithmetic  4.13 us (3%)
  matrix products  1.86 us (1%)
    ppermute x15, waiting for transfers between devices, across(): return lax.ppermute(array, axis, [(i, i ^ bit) for i in range(n)])  32.6 us
    ppermute x18, starting transfers between devices, ahead(): return lax.ppermute(array, axis, [(i, (i + step) % n) for i in range(n)])  32.3 us
    pallas_call x2, Pallas kernels, partial_half(): pl.pallas_call(functools.partial(half_kernel, which, width, layout, len(p...  23.5 us
    pallas_call x1, Pallas kernels, partial(): pl.pallas_call(functools.partial(partial_kernel, width, layout, len(piece...  18.2 us
    ppermute x15, starting transfers between devices, across(): return lax.ppermute(array, axis, [(i, i ^ bit) for i in range(n)])  13.4 us
    pallas_call x3, Pallas kernels, fold(): pl.pallas_call(functools.partial(fold_kernel, width), in_specs=[pl.BlockS...  10.2 us
    ppermute x18, waiting for transfers between devices, ahead(): return lax.ppermute(array, axis, [(i, (i + step) % n) for i in range(n)])  9.49 us
  transfers between devices with their start and end apart: 33, of which 12 were waited for; matrix products, arithmetic and copies ran while one was open for 5% of the time, Pallas kernels for 33%

profile of v4, /device:TPU:0, one launch (start us, length us, event | category | flops | bytes accessed | tf_op | source)
XLA Modules:
  0.0 157.3 jit_solution(11332477018273732317)
XLA Ops:
  0.7 1.4 constant_dynamic-slice_fusion.3
  2.1 1.5 constant_dynamic-slice_fusion
  3.6 1.0 fusion.4
  4.7 3.2 %collective-permute-start.4 = (bf16[64,3840]{1,0:T(8,128)(2,1)S(1)}, bf16[64,3840]{1,0:T(8,128)(2,1)}, u32[]{:S(2)}, u32[]{:S(2)}) collective-permute-start(bf16[64,3840]{1,0:T(8,128)(2,1)S(1)} %get-tuple-element.168), channel_id=1, source_target_pairs={{0,1},{1,0},{2,3},{3,2},{4,5},{5,4},{6,7},{7,6},{8,9},{9,8},{10,11... | collective-permute-start | bytes 1474568 | tf_op jit(solution)/shard_map/ppermute | solution.py:306
  7.9 3.9 %collective-permute-start.3 = (bf16[64,3840]{1,0:T(8,128)(2,1)S(1)}, bf16[64,3840]{1,0:T(8,128)(2,1)}, u32[]{:S(2)}, u32[]{:S(2)}) collective-permute-start(bf16[64,3840]{1,0:T(8,128)(2,1)S(1)} %get-tuple-element.168), channel_id=1, source_target_pairs={{0,4},{2,6},{4,0},{6,2},{1,5},{3,7},{5,1},{7,3},{8,12},{10,14},{12... | collective-permute-start | bytes 1474568 | tf_op jit(solution)/shard_map/ppermute | solution.py:301
  11.8 0.7 collective-permute-start.2
  12.5 1.3 collective-permute-start.1
  13.8 0.5 collective-permute-start.5
  14.3 0.3 fusion.23
  14.7 1.1 pad_maximum_fusion.refs_0_
  15.9 14.6 %collective-permute-done.5.refs_1_ = bf16[64,3840]{1,0:T(8,128)(2,1)S(1)} collective-permute-done((bf16[64,3840]{1,0:T(8,128)(2,1)S(1)}, bf16[64,3840]{1,0:T(8,128)(2,1)S(1)}, u32[]{:S(2)}, u32[]{:S(2)}) %collective-permute-start.5) | collective-permute-done | bytes 491552 | tf_op jit(solution)/shard_map/ppermute | solution.py:306
  30.5 4.3 %collective-permute-done.2.refs_4_ = bf16[64,3840]{1,0:T(8,128)(2,1)} collective-permute-done((bf16[64,3840]{1,0:T(8,128)(2,1)S(1)}, bf16[64,3840]{1,0:T(8,128)(2,1)}, u32[]{:S(2)}, u32[]{:S(2)}) %collective-permute-start.2) | collective-permute-done | bytes 491552 | tf_op jit(solution)/shard_map/ppermute | solution.py:301
  34.8 0.5 collective-permute-start.10
  35.3 0.9 multiply_bitcast_fusion
  36.2 2.7 %collective-permute-start.7 = (bf16[64,3840]{1,0:T(8,128)(2,1)}, bf16[64,3840]{1,0:T(8,128)(2,1)S(1)}, u32[]{:S(2)}, u32[]{:S(2)}) collective-permute-start(bf16[64,3840]{1,0:T(8,128)(2,1)} %collective-permute-done.4.refs_1_), channel_id=1, source_target_pairs={{0,6},{2,0},{4,2},{6,4},{1,7},{3,1},{5,3},{7,5},{8,14},{10,8},{12,... | collective-permute-start | bytes 1474568 | tf_op jit(solution)/shard_map/ppermute | solution.py:301
  38.9 0.5 collective-permute-start.8
  39.4 1.3 collective-permute-done.10
  40.8 1.6 %collective-permute-start.11 = (f32[32,256]{1,0:T(8,128)S(1)}, f32[32,256]{1,0:T(8,128)S(1)}, u32[]{:S(2)}, u32[]{:S(2)}) collective-permute-start(f32[32,256]{1,0:T(8,128)S(1)} %add.70), channel_id=1, source_target_pairs={{0,32},{32,0},{64,96},{96,64},{1,33},{33,1},{65,97},{97,65},{2,34}... | collective-permute-start | bytes 98312 | tf_op jit(solution)/shard_map/ppermute | solution.py:306
  42.4 0.7 pad_maximum_fusion.3.refs_12_.refs_10_
  43.1 1.6 %collective-permute-done.11 = f32[32,256]{1,0:T(8,128)S(1)} collective-permute-done((f32[32,256]{1,0:T(8,128)S(1)}, f32[32,256]{1,0:T(8,128)S(1)}, u32[]{:S(2)}, u32[]{:S(2)}) %collective-permute-start.11) | collective-permute-done | bytes 32800 | tf_op jit(solution)/shard_map/ppermute | solution.py:306
  44.7 3.2 %collective-permute-start.12 = (f32[32,256]{1,0:T(8,128)S(1)}, f32[32,256]{1,0:T(8,128)S(1)}, u32[]{:S(2)}, u32[]{:S(2)}) collective-permute-start(f32[32,256]{1,0:T(8,128)S(1)} %add.71), channel_id=1, source_target_pairs={{0,64},{32,96},{64,0},{96,32},{1,65},{33,97},{65,1},{97,33},{2,66}... | collective-permute-start | bytes 98312 | tf_op jit(solution)/shard_map/ppermute | solution.py:306
  47.9 1.1 pad_maximum_fusion.1
  48.9 1.2 collective-permute-done.12
  50.1 3.4 %collective-permute-done.8.refs_7_ = bf16[64,3840]{1,0:T(8,128)(2,1)S(1)} collective-permute-done((bf16[64,3840]{1,0:T(8,128)(2,1)}, bf16[64,3840]{1,0:T(8,128)(2,1)S(1)}, u32[]{:S(2)}, u32[]{:S(2)}) %collective-permute-start.8) | collective-permute-done | bytes 491552 | tf_op jit(solution)/shard_map/ppermute | solution.py:306
  53.5 0.8 copy-done.12
  54.3 3.0 %collective-permute-start.14 = (bf16[128,3840]{1,0:T(8,128)(2,1)}, bf16[128,3840]{1,0:T(8,128)(2,1)S(1)}, u32[]{:S(2)}, u32[]{:S(2)}) collective-permute-start(bf16[128,3840]{1,0:T(8,128)(2,1)} %pad_maximum_fusion.1), channel_id=1, source_target_pairs={{0,6},{2,0},{4,2},{6,4},{1,7},{3,1},{5,3},{7,5},{8,14},{10,8},{12,... | collective-permute-start | bytes 2949128 | tf_op jit(solution)/shard_map/ppermute | solution.py:301
  57.3 0.7 collective-permute-start.15
  58.0 18.2 %partial.1 = (f32[128,1856]{1,0:T(8,128)}, bf16[128,1920]{1,0:T(8,128)(2,1)}, bf16[128,1920]{1,0:T(8,128)(2,1)}, bf16[128,1920]{1,0:T(8,128)(2,1)}) custom-call(s32[1]{0:T(128)} %bitcast.base, bf16[128,3840]{1,0:T(8,128)(2,1)} %copy-done.1, bf16[64,3840]{1,0:T(8,128)(2,1)} %collective-permute-done.4.refs_1_, ...), custom_call_target="tpu_custom_call" | custom-call | flops 1 | bytes 1 | tf_op jit(solution)/shard_map/partial/pallas_call | solution.py:135
  76.2 1.1 collective-permute-done.14.refs_3_
  77.3 3.4 %collective-permute-done.13.refs_2_ = bf16[128,3840]{1,0:T(8,128)(2,1)} collective-permute-done((bf16[128,3840]{1,0:T(8,128)(2,1)}, bf16[128,3840]{1,0:T(8,128)(2,1)}, u32[]{:S(2)}, u32[]{:S(2)}) %collective-permute-start.13) | collective-permute-done | bytes 983072 | tf_op jit(solution)/shard_map/ppermute | solution.py:301
  80.7 0.3 fusion.6
  81.0 0.3 fusion.12
  81.4 1.2 slice.51
  82.6 0.3 collective-permute-start.17
  82.8 1.8 %collective-permute-start.16 = (bf16[64,3840]{1,0:T(8,128)(2,1)S(1)}, bf16[64,3840]{1,0:T(8,128)(2,1)S(1)}, u32[]{:S(2)}, u32[]{:S(2)}) collective-permute-start(bf16[64,3840]{1,0:T(8,128)(2,1)S(1)} %slice.51), channel_id=1, source_target_pairs={{0,2},{2,4},{4,6},{6,0},{1,3},{3,5},{5,7},{7,1},{8,10},{10,12},{12... | collective-permute-start | bytes 1474568 | tf_op jit(solution)/shard_map/ppermute | solution.py:301
  84.7 1.6 %collective-permute-start.18 = (bf16[128,1920]{1,0:T(8,128)(2,1)S(1)}, bf16[128,1920]{1,0:T(8,128)(2,1)S(1)}, u32[]{:S(2)}, u32[]{:S(2)}) collective-permute-start(bf16[128,1920]{1,0:T(8,128)(2,1)S(1)} %copy-done.26), channel_id=1, source_target_pairs={{0,32},{32,64},{64,96},{96,0},{1,33},{33,65},{65,97},{97,1},{2,34}... | collective-permute-start | bytes 1474568 | tf_op jit(solution)/shard_map/ppermute | solution.py:301
  86.2 1.7 %collective-permute-start.19 = (bf16[128,1920]{1,0:T(8,128)(2,1)S(1)}, bf16[128,1920]{1,0:T(8,128)(2,1)S(1)}, u32[]{:S(2)}, u32[]{:S(2)}) collective-permute-start(bf16[128,1920]{1,0:T(8,128)(2,1)S(1)} %copy-done.25), channel_id=1, source_target_pairs={{0,96},{32,0},{64,32},{96,64},{1,97},{33,1},{65,33},{97,65},{2,98}... | collective-permute-start | bytes 1474568 | tf_op jit(solution)/shard_map/ppermute | solution.py:301
  88.0 0.6 collective-permute-start.20
  88.6 6.6 %collective-permute-done.20 = f32[16,2848]{1,0:T(8,128)S(1)} collective-permute-done((f32[16,2848]{1,0:T(8,128)S(1)}, f32[16,2848]{1,0:T(8,128)S(1)}, u32[]{:S(2)}, u32[]{:S(2)}) %collective-permute-start.20) | collective-permute-done | bytes 182304 | tf_op jit(solution)/shard_map/ppermute | solution.py:306
  95.2 0.6 collective-permute-done.18.a
  95.8 3.9 %collective-permute-start.21 = (bf16[128,1920]{1,0:T(8,128)(2,1)S(1)}, bf16[128,1920]{1,0:T(8,128)(2,1)S(1)}, u32[]{:S(2)}, u32[]{:S(2)}) collective-permute-start(bf16[128,1920]{1,0:T(8,128)(2,1)S(1)} %copy-done.24), channel_id=1, source_target_pairs={{0,64},{32,96},{64,0},{96,32},{1,65},{33,97},{65,1},{97,33},{2,66}... | collective-permute-start | bytes 1474568 | tf_op jit(solution)/shard_map/ppermute | solution.py:301
  99.7 11.6 %partial_half.2 = (f32[128,928]{1,0:T(8,128)}, bf16[128,1024]{1,0:T(8,128)(2,1)}, bf16[128,1024]{1,0:T(8,128)(2,1)}, bf16[128,1024]{1,0:T(8,128)(2,1)}) custom-call(s32[1]{0:T(128)} %bitcast.base, bf16[128,3840]{1,0:T(8,128)(2,1)} %copy-done.1, bf16[64,3840]{1,0:T(8,128)(2,1)} %copy-done.4, bf16[128,3840]{1,0:T(8,128)(2,1)} %collective-permute-done.13.refs_2_, ...), custom_call_target="tpu_custom_call" | custom-call | flops 1 | bytes 1 | tf_op jit(solution)/shard_map/partial_half/pallas_call | solution.py:213
  111.5 5.3 %collective-permute-start.22 = (bf16[128,1024]{1,0:T(8,128)(2,1)}, bf16[128,1024]{1,0:T(8,128)(2,1)S(1)}, u32[]{:S(2)}, u32[]{:S(2)}) collective-permute-start(bf16[128,1024]{1,0:T(8,128)(2,1)} %get-tuple-element.128), channel_id=1, source_target_pairs={{0,32},{32,64},{64,96},{96,0},{1,33},{33,65},{65,97},{97,1},{2,34}... | collective-permute-start | bytes 786440 | tf_op jit(solution)/shard_map/ppermute | solution.py:301
  116.8 2.1 %collective-permute-start.24 = (bf16[128,1024]{1,0:T(8,128)(2,1)}, bf16[128,1024]{1,0:T(8,128)(2,1)S(1)}, u32[]{:S(2)}, u32[]{:S(2)}) collective-permute-start(bf16[128,1024]{1,0:T(8,128)(2,1)} %get-tuple-element.130), channel_id=1, source_target_pairs={{0,64},{32,96},{64,0},{96,32},{1,65},{33,97},{65,1},{97,33},{2,66}... | collective-permute-start | bytes 786440 | tf_op jit(solution)/shard_map/ppermute | solution.py:301
  118.9 11.8 %partial_half.3 = (f32[128,928]{1,0:T(8,128)}, bf16[128,1024]{1,0:T(8,128)(2,1)}, bf16[128,1024]{1,0:T(8,128)(2,1)}, bf16[128,1024]{1,0:T(8,128)(2,1)}) custom-call(s32[1]{0:T(128)} %bitcast.base, bf16[128,3840]{1,0:T(8,128)(2,1)} %copy-done.1, bf16[64,3840]{1,0:T(8,128)(2,1)} %copy-done.4, bf16[128,3840]{1,0:T(8,128)(2,1)} %collective-permute-done.13.refs_2_, ...), custom_call_target="tpu_custom_call" | custom-call | flops 1 | bytes 1 | tf_op jit(solution)/shard_map/partial_half/pallas_call | solution.py:213
  130.9 0.7 collective-permute-start.26
  131.6 2.6 %collective-permute-start.27 = (bf16[128,1024]{1,0:T(8,128)(2,1)}, bf16[128,1024]{1,0:T(8,128)(2,1)S(1)}, u32[]{:S(2)}, u32[]{:S(2)}) collective-permute-start(bf16[128,1024]{1,0:T(8,128)(2,1)} %get-tuple-element.134), channel_id=1, source_target_pairs={{0,96},{32,0},{64,32},{96,64},{1,97},{33,1},{65,33},{97,65},{2,98}... | collective-permute-start | bytes 786440 | tf_op jit(solution)/shard_map/ppermute | solution.py:301
  134.2 0.8 collective-permute-start.28
  135.0 0.6 collective-permute-start.30
  135.5 2.9 %fold.4 = (f32[64,928]{1,0:T(8,128)}, bf16[64,1024]{1,0:T(8,128)(2,1)}) custom-call(s32[1]{0:T(128)} %bitcast.2.swap, f32[128,928]{1,0:T(8,128)} %get-tuple-element.142.own, bf16[128,1024]{1,0:T(8,128)(2,1)} %copy-done.15, bf16[128,1024]{1,0:T(8,128)(2,1)} %copy-done.16, bf16[128,1024]{1,0:T(8,128)(2,1)} %copy-done.18), custom_call_target="tpu_custom_call" | custom-call | flops 1 | bytes 1 | tf_op jit(solution)/shard_map/fold/pallas_call | solution.py:258
  138.5 0.5 collective-permute-start.29
  139.0 4.3 %fold.3 = (f32[64,1856]{1,0:T(8,128)}, bf16[64,1920]{1,0:T(8,128)(2,1)}) custom-call(s32[1]{0:T(128)} %bitcast.2.swap, f32[128,1856]{1,0:T(8,128)} %get-tuple-element.136.own, bf16[128,1920]{1,0:T(8,128)(2,1)} %copy-done.9, bf16[128,1920]{1,0:T(8,128)(2,1)} %copy-done.10, bf16[128,1920]{1,0:T(8,128)(2,1)} %copy-done.11), custom_call_target="tpu_custom_call" | custom-call | flops 1 | bytes 1 | tf_op jit(solution)/shard_map/fold/pallas_call | solution.py:258
  143.3 1.4 collective-permute-done.29.got1
  144.7 0.2 collective-permute-start.31
  144.9 0.5 copy-done.17
  145.5 0.1 copy-done.20
  145.6 2.9 %fold.5 = (f32[64,928]{1,0:T(8,128)}, bf16[64,1024]{1,0:T(8,128)(2,1)}) custom-call(s32[1]{0:T(128)} %bitcast.2.swap, f32[128,928]{1,0:T(8,128)} %get-tuple-element.151.own, bf16[128,1024]{1,0:T(8,128)(2,1)} %copy-done.17, bf16[128,1024]{1,0:T(8,128)(2,1)} %copy-done.19, bf16[128,1024]{1,0:T(8,128)(2,1)} %copy-done.20), custom_call_target="tpu_custom_call" | custom-call | flops 1 | bytes 1 | tf_op jit(solution)/shard_map/fold/pallas_call | solution.py:258
  148.5 1.2 collective-permute-start.32
  149.8 0.7 slice.76
  150.5 0.6 slice_bitcast_fusion
  151.2 2.5 %collective-permute-done.32.got2 = bf16[64,1024]{1,0:T(8,128)(2,1)S(1)} collective-permute-done((bf16[64,1024]{1,0:T(8,128)(2,1)}, bf16[64,1024]{1,0:T(8,128)(2,1)S(1)}, u32[]{:S(2)}, u32[]{:S(2)}) %collective-permute-start.32) | collective-permute-done | bytes 131104 | tf_op jit(solution)/shard_map/ppermute | solution.py:306
  153.7 0.6 copy-done.23
  154.4 0.1 copy-done.21
  154.5 2.9 %finish.1 = bf16[1856,128]{1,0:T(8,128)(2,1)} custom-call(f32[64,1856]{1,0:T(8,128)} %get-tuple-element.149.keep0, bf16[64,1920]{1,0:T(8,128)(2,1)} %copy-done.21, f32[64,928]{1,0:T(8,128)} %get-tuple-element.159.keep1, bf16[64,1024]{1,0:T(8,128)(2,1)} %copy-done.22, f32[64,928]{1,0:T(8,128)} %get-tuple-element.161.keep2, bf16[64,1024]{1,0:T(8,128)(2,1)} %copy-done.23), custom_call_target="tpu_custom_call" | custom-call | tf_op jit(solution)/shard_map/finish/pallas_call | solution.py:289
  (91 shorter events, 0.8 us)
Async XLA Ops:
  0.6 3.0 %copy-start = (bf16[256,928]{0,1:T(8,128)(2,1)S(1)}, bf16[256,928]{0,1:T(8,128)(2,1)}, u32[]{:S(2)}) copy-start(bf16[256,928]{0,1:T(8,128)(2,1)} %param.5) | copy-start | bytes 1425412
  0.7 13.7 %copy-start.2 = (bf16[256,1920]{1,0:T(8,128)(2,1)S(1)}, bf16[256,1920]{1,0:T(8,128)(2,1)}, u32[]{:S(2)}) copy-start(bf16[256,1920]{1,0:T(8,128)(2,1)} %param.6) | copy-start | bytes 2949124
  2.0 2.6 %collective-permute-start = (bf16[128,1920]{1,0:T(8,128)(2,1)S(1)}, bf16[128,1920]{1,0:T(8,128)(2,1)S(1)}, u32[]{:S(2)}, u32[]{:S(2)}) collective-permute-start(bf16[128,1920]{1,0:T(8,128)(2,1)S(1)} %get-tuple-element.170), channel_id=1, source_target_pairs={{0,8},{8,0},{1,9},{9,1},{2,10},{10,2},{3,11},{11,3},{4,12},{12,4},... | collective-permute-start | bytes 1474568 | tf_op jit(solution)/shard_map/ppermute | solution.py:306
  3.6 12.2 %copy-start.8 = (bf16[16,1920]{1,0:T(8,128)(2,1)}, bf16[16,1920]{1,0:T(8,128)(2,1)S(1)}, u32[]{:S(2)}) copy-start(bf16[16,1920]{1,0:T(8,128)(2,1)S(1)} %get-tuple-element.166.refs_10_.refs_8_) | copy-start | bytes 184324
  4.6 10.0 %copy-start.7 = (bf16[128,1920]{1,0:T(8,128)(2,1)}, bf16[128,1920]{1,0:T(8,128)(2,1)S(1)}, u32[]{:S(2)}) copy-start(bf16[128,1920]{1,0:T(8,128)(2,1)S(1)} %collective-permute-done) | copy-start | bytes 1474564
  4.7 25.7 %collective-permute-start.4 = (bf16[64,3840]{1,0:T(8,128)(2,1)S(1)}, bf16[64,3840]{1,0:T(8,128)(2,1)}, u32[]{:S(2)}, u32[]{:S(2)}) collective-permute-start(bf16[64,3840]{1,0:T(8,128)(2,1)S(1)} %get-tuple-element.168), channel_id=1, source_target_pairs={{0,1},{1,0},{2,3},{3,2},{4,5},{5,4},{6,7},{7,6},{8,9},{9,8},{10,11... | collective-permute-start | bytes 1474568 | tf_op jit(solution)/shard_map/ppermute | solution.py:306
  7.9 22.5 %collective-permute-start.3 = (bf16[64,3840]{1,0:T(8,128)(2,1)S(1)}, bf16[64,3840]{1,0:T(8,128)(2,1)}, u32[]{:S(2)}, u32[]{:S(2)}) collective-permute-start(bf16[64,3840]{1,0:T(8,128)(2,1)S(1)} %get-tuple-element.168), channel_id=1, source_target_pairs={{0,4},{2,6},{4,0},{6,2},{1,5},{3,7},{5,1},{7,3},{8,12},{10,14},{12... | collective-permute-start | bytes 1474568 | tf_op jit(solution)/shard_map/ppermute | solution.py:301
  11.8 23.0 %collective-permute-start.2 = (bf16[64,3840]{1,0:T(8,128)(2,1)S(1)}, bf16[64,3840]{1,0:T(8,128)(2,1)}, u32[]{:S(2)}, u32[]{:S(2)}) collective-permute-start(bf16[64,3840]{1,0:T(8,128)(2,1)S(1)} %get-tuple-element.168), channel_id=1, source_target_pairs={{0,6},{2,0},{4,2},{6,4},{1,7},{3,1},{5,3},{7,5},{8,14},{10,8},{12,... | collective-permute-start | bytes 1474568 | tf_op jit(solution)/shard_map/ppermute | solution.py:301
  12.5 22.3 %collective-permute-start.1 = (bf16[64,3840]{1,0:T(8,128)(2,1)S(1)}, bf16[64,3840]{1,0:T(8,128)(2,1)}, u32[]{:S(2)}, u32[]{:S(2)}) collective-permute-start(bf16[64,3840]{1,0:T(8,128)(2,1)S(1)} %get-tuple-element.168), channel_id=1, source_target_pairs={{0,2},{2,4},{4,6},{6,0},{1,3},{3,5},{5,7},{7,1},{8,10},{10,12},{12... | collective-permute-start | bytes 1474568 | tf_op jit(solution)/shard_map/ppermute | solution.py:301
  13.8 16.6 %collective-permute-start.5 = (bf16[64,3840]{1,0:T(8,128)(2,1)S(1)}, bf16[64,3840]{1,0:T(8,128)(2,1)S(1)}, u32[]{:S(2)}, u32[]{:S(2)}) collective-permute-start(bf16[64,3840]{1,0:T(8,128)(2,1)S(1)} %get-tuple-element.167), channel_id=1, source_target_pairs={{0,1},{1,0},{2,3},{3,2},{4,5},{5,4},{6,7},{7,6},{8,9},{9,8},{10,11... | collective-permute-start | bytes 1474568 | tf_op jit(solution)/shard_map/ppermute | solution.py:306
  15.9 42.1 %copy-start.1 = (bf16[128,3840]{1,0:T(8,128)(2,1)}, bf16[128,3840]{1,0:T(8,128)(2,1)S(1)}, u32[]{:S(2)}) copy-start(bf16[128,3840]{1,0:T(8,128)(2,1)S(1)} %pad_maximum_fusion.refs_0_) | copy-start | bytes 2949124
  30.5 23.1 %copy-start.4 = (bf16[64,3840]{1,0:T(8,128)(2,1)}, bf16[64,3840]{1,0:T(8,128)(2,1)S(1)}, u32[]{:S(2)}) copy-start(bf16[64,3840]{1,0:T(8,128)(2,1)S(1)} %collective-permute-done.5.refs_1_) | copy-start | bytes 1474564
  34.8 18.7 %collective-permute-start.9 = (bf16[1856,1920]{1,0:T(8,128)(2,1)}, bf16[1856,1920]{1,0:T(8,128)(2,1)}, u32[]{:S(2)}, u32[]{:S(2)}) collective-permute-start(bf16[1856,1920]{1,0:T(8,128)(2,1)} %refs_6_.1), channel_id=1, source_target_pairs={{0,8},{8,0},{1,9},{9,1},{2,10},{10,2},{3,11},{11,3},{4,12},{12,4},... | collective-permute-start | bytes 21381128 | tf_op jit(solution)/shard_map/ppermute | solution.py:306
  34.8 6.0 %collective-permute-start.10 = (f32[32,256]{1,0:T(8,128)S(1)}, f32[32,256]{1,0:T(8,128)S(1)}, u32[]{:S(2)}, u32[]{:S(2)}) collective-permute-start(f32[32,256]{1,0:T(8,128)S(1)} %pad_maximum_fusion.4), channel_id=1, source_target_pairs={{0,8},{8,0},{1,9},{9,1},{2,10},{10,2},{3,11},{11,3},{4,12},{12,4},... | collective-permute-start | bytes 98312 | tf_op jit(solution)/shard_map/ppermute | solution.py:306
  36.2 17.2 %collective-permute-start.7 = (bf16[64,3840]{1,0:T(8,128)(2,1)}, bf16[64,3840]{1,0:T(8,128)(2,1)S(1)}, u32[]{:S(2)}, u32[]{:S(2)}) collective-permute-start(bf16[64,3840]{1,0:T(8,128)(2,1)} %collective-permute-done.4.refs_1_), channel_id=1, source_target_pairs={{0,6},{2,0},{4,2},{6,4},{1,7},{3,1},{5,3},{7,5},{8,14},{10,8},{12,... | collective-permute-start | bytes 1474568 | tf_op jit(solution)/shard_map/ppermute | solution.py:301
  38.9 14.6 %collective-permute-start.6 = (bf16[64,3840]{1,0:T(8,128)(2,1)}, bf16[64,3840]{1,0:T(8,128)(2,1)S(1)}, u32[]{:S(2)}, u32[]{:S(2)}) collective-permute-start(bf16[64,3840]{1,0:T(8,128)(2,1)} %collective-permute-done.4.refs_1_), channel_id=1, source_target_pairs={{0,2},{2,4},{4,6},{6,0},{1,3},{3,5},{5,7},{7,1},{8,10},{10,12},{12... | collective-permute-start | bytes 1474568 | tf_op jit(solution)/shard_map/ppermute | solution.py:301
  38.9 14.6 %collective-permute-start.8 = (bf16[64,3840]{1,0:T(8,128)(2,1)}, bf16[64,3840]{1,0:T(8,128)(2,1)S(1)}, u32[]{:S(2)}, u32[]{:S(2)}) collective-permute-start(bf16[64,3840]{1,0:T(8,128)(2,1)} %collective-permute-done.3.refs_6_), channel_id=1, source_target_pairs={{0,1},{1,0},{2,3},{3,2},{4,5},{5,4},{6,7},{7,6},{8,9},{9,8},{10,11... | collective-permute-start | bytes 1474568 | tf_op jit(solution)/shard_map/ppermute | solution.py:306
  40.8 3.9 %collective-permute-start.11 = (f32[32,256]{1,0:T(8,128)S(1)}, f32[32,256]{1,0:T(8,128)S(1)}, u32[]{:S(2)}, u32[]{:S(2)}) collective-permute-start(f32[32,256]{1,0:T(8,128)S(1)} %add.70), channel_id=1, source_target_pairs={{0,32},{32,0},{64,96},{96,64},{1,33},{33,1},{65,97},{97,65},{2,34}... | collective-permute-start | bytes 98312 | tf_op jit(solution)/shard_map/ppermute | solution.py:306
  44.7 5.4 %collective-permute-start.12 = (f32[32,256]{1,0:T(8,128)S(1)}, f32[32,256]{1,0:T(8,128)S(1)}, u32[]{:S(2)}, u32[]{:S(2)}) collective-permute-start(f32[32,256]{1,0:T(8,128)S(1)} %add.71), channel_id=1, source_target_pairs={{0,64},{32,96},{64,0},{96,32},{1,65},{33,97},{65,1},{97,33},{2,66}... | collective-permute-start | bytes 98312 | tf_op jit(solution)/shard_map/ppermute | solution.py:306
  53.5 3.8 %copy-start.14 = (bf16[64,3840]{1,0:T(8,128)(2,1)}, bf16[64,3840]{1,0:T(8,128)(2,1)S(1)}, u32[]{:S(2)}) copy-start(bf16[64,3840]{1,0:T(8,128)(2,1)S(1)} %collective-permute-done.8.refs_7_) | copy-start | bytes 1474564
  53.5 0.8 copy-start.12
  53.5 3.8 %copy-start.13 = (bf16[64,3840]{1,0:T(8,128)(2,1)}, bf16[64,3840]{1,0:T(8,128)(2,1)S(1)}, u32[]{:S(2)}) copy-start(bf16[64,3840]{1,0:T(8,128)(2,1)S(1)} %collective-permute-done.6.refs_3_) | copy-start | bytes 1474564
  54.3 23.0 %collective-permute-start.14 = (bf16[128,3840]{1,0:T(8,128)(2,1)}, bf16[128,3840]{1,0:T(8,128)(2,1)S(1)}, u32[]{:S(2)}, u32[]{:S(2)}) collective-permute-start(bf16[128,3840]{1,0:T(8,128)(2,1)} %pad_maximum_fusion.1), channel_id=1, source_target_pairs={{0,6},{2,0},{4,2},{6,4},{1,7},{3,1},{5,3},{7,5},{8,14},{10,8},{12,... | collective-permute-start | bytes 2949128 | tf_op jit(solution)/shard_map/ppermute | solution.py:301
  57.3 23.4 %collective-permute-start.13 = (bf16[128,3840]{1,0:T(8,128)(2,1)}, bf16[128,3840]{1,0:T(8,128)(2,1)}, u32[]{:S(2)}, u32[]{:S(2)}) collective-permute-start(bf16[128,3840]{1,0:T(8,128)(2,1)} %pad_maximum_fusion.1), channel_id=1, source_target_pairs={{0,2},{2,4},{4,6},{6,0},{1,3},{3,5},{5,7},{7,1},{8,10},{10,12},{12... | collective-permute-start | bytes 2949128 | tf_op jit(solution)/shard_map/ppermute | solution.py:301
  57.3 18.9 %collective-permute-start.15 = (f32[32,256]{1,0:T(8,128)S(1)}, f32[32,256]{1,0:T(8,128)S(1)}, u32[]{:S(2)}, u32[]{:S(2)}) collective-permute-start(f32[32,256]{1,0:T(8,128)S(1)} %add.75), channel_id=1, source_target_pairs={{0,16},{16,0},{1,17},{17,1},{2,18},{18,2},{3,19},{19,3},{4,20},{20... | collective-permute-start | bytes 98312 | tf_op jit(solution)/shard_map/ppermute | solution.py:306
  77.3 5.2 %copy-start.3 = (bf16[128,3840]{1,0:T(8,128)(2,1)}, bf16[128,3840]{1,0:T(8,128)(2,1)S(1)}, u32[]{:S(2)}) copy-start(bf16[128,3840]{1,0:T(8,128)(2,1)S(1)} %collective-permute-done.14.refs_3_) | copy-start | bytes 2949124
  81.0 3.7 %copy-start.26 = (bf16[128,1920]{1,0:T(8,128)(2,1)S(1)}, bf16[128,1920]{1,0:T(8,128)(2,1)}, u32[]{:S(2)}) copy-start(bf16[128,1920]{1,0:T(8,128)(2,1)} %get-tuple-element.109) | copy-start | bytes 1474564
  81.0 5.2 %copy-start.25 = (bf16[128,1920]{1,0:T(8,128)(2,1)S(1)}, bf16[128,1920]{1,0:T(8,128)(2,1)}, u32[]{:S(2)}) copy-start(bf16[128,1920]{1,0:T(8,128)(2,1)} %get-tuple-element.110) | copy-start | bytes 1474564
  81.0 14.8 %copy-start.24 = (bf16[128,1920]{1,0:T(8,128)(2,1)S(1)}, bf16[128,1920]{1,0:T(8,128)(2,1)}, u32[]{:S(2)}) copy-start(bf16[128,1920]{1,0:T(8,128)(2,1)} %get-tuple-element.120) | copy-start | bytes 1474564
  82.6 12.6 %collective-permute-start.17 = (bf16[64,3840]{1,0:T(8,128)(2,1)S(1)}, bf16[64,3840]{1,0:T(8,128)(2,1)S(1)}, u32[]{:S(2)}, u32[]{:S(2)}) collective-permute-start(bf16[64,3840]{1,0:T(8,128)(2,1)S(1)} %slice.52), channel_id=1, source_target_pairs={{0,6},{2,0},{4,2},{6,4},{1,7},{3,1},{5,3},{7,5},{8,14},{10,8},{12,... | collective-permute-start | bytes 1474568 | tf_op jit(solution)/shard_map/ppermute | solution.py:301
  82.8 12.3 %collective-permute-start.16 = (bf16[64,3840]{1,0:T(8,128)(2,1)S(1)}, bf16[64,3840]{1,0:T(8,128)(2,1)S(1)}, u32[]{:S(2)}, u32[]{:S(2)}) collective-permute-start(bf16[64,3840]{1,0:T(8,128)(2,1)S(1)} %slice.51), channel_id=1, source_target_pairs={{0,2},{2,4},{4,6},{6,0},{1,3},{3,5},{5,7},{7,1},{8,10},{10,12},{12... | collective-permute-start | bytes 1474568 | tf_op jit(solution)/shard_map/ppermute | solution.py:301
  84.7 11.2 %collective-permute-start.18 = (bf16[128,1920]{1,0:T(8,128)(2,1)S(1)}, bf16[128,1920]{1,0:T(8,128)(2,1)S(1)}, u32[]{:S(2)}, u32[]{:S(2)}) collective-permute-start(bf16[128,1920]{1,0:T(8,128)(2,1)S(1)} %copy-done.26), channel_id=1, source_target_pairs={{0,32},{32,64},{64,96},{96,0},{1,33},{33,65},{65,97},{97,1},{2,34}... | collective-permute-start | bytes 1474568 | tf_op jit(solution)/shard_map/ppermute | solution.py:301
  86.2 9.6 %collective-permute-start.19 = (bf16[128,1920]{1,0:T(8,128)(2,1)S(1)}, bf16[128,1920]{1,0:T(8,128)(2,1)S(1)}, u32[]{:S(2)}, u32[]{:S(2)}) collective-permute-start(bf16[128,1920]{1,0:T(8,128)(2,1)S(1)} %copy-done.25), channel_id=1, source_target_pairs={{0,96},{32,0},{64,32},{96,64},{1,97},{33,1},{65,33},{97,65},{2,98}... | collective-permute-start | bytes 1474568 | tf_op jit(solution)/shard_map/ppermute | solution.py:301
  88.0 7.2 %collective-permute-start.20 = (f32[16,2848]{1,0:T(8,128)S(1)}, f32[16,2848]{1,0:T(8,128)S(1)}, u32[]{:S(2)}, u32[]{:S(2)}) collective-permute-start(f32[16,2848]{1,0:T(8,128)S(1)} %pad_maximum_fusion.2), channel_id=1, source_target_pairs={{0,1},{1,0},{2,3},{3,2},{4,5},{5,4},{6,7},{7,6},{8,9},{9,8},{10,11... | collective-permute-start | bytes 546824 | tf_op jit(solution)/shard_map/ppermute | solution.py:306
  95.2 4.6 %copy-start.5 = (bf16[64,3840]{1,0:T(8,128)(2,1)}, bf16[64,3840]{1,0:T(8,128)(2,1)S(1)}, u32[]{:S(2)}) copy-start(bf16[64,3840]{1,0:T(8,128)(2,1)S(1)} %collective-permute-done.17.refs_5_) | copy-start | bytes 1474564
  95.2 4.6 %copy-start.6 = (bf16[64,3840]{1,0:T(8,128)(2,1)}, bf16[64,3840]{1,0:T(8,128)(2,1)S(1)}, u32[]{:S(2)}) copy-start(bf16[64,3840]{1,0:T(8,128)(2,1)S(1)} %collective-permute-done.16.refs_4_) | copy-start | bytes 1474564
  95.8 15.6 %copy-start.9 = (bf16[128,1920]{1,0:T(8,128)(2,1)}, bf16[128,1920]{1,0:T(8,128)(2,1)S(1)}, u32[]{:S(2)}) copy-start(bf16[128,1920]{1,0:T(8,128)(2,1)S(1)} %collective-permute-done.18.a) | copy-start | bytes 1474564
  95.8 15.6 %copy-start.10 = (bf16[128,1920]{1,0:T(8,128)(2,1)}, bf16[128,1920]{1,0:T(8,128)(2,1)S(1)}, u32[]{:S(2)}) copy-start(bf16[128,1920]{1,0:T(8,128)(2,1)S(1)} %collective-permute-done.19.b) | copy-start | bytes 1474564
  95.8 15.6 %collective-permute-start.21 = (bf16[128,1920]{1,0:T(8,128)(2,1)S(1)}, bf16[128,1920]{1,0:T(8,128)(2,1)S(1)}, u32[]{:S(2)}, u32[]{:S(2)}) collective-permute-start(bf16[128,1920]{1,0:T(8,128)(2,1)S(1)} %copy-done.24), channel_id=1, source_target_pairs={{0,64},{32,96},{64,0},{96,32},{1,65},{33,97},{65,1},{97,33},{2,66}... | collective-permute-start | bytes 1474568 | tf_op jit(solution)/shard_map/ppermute | solution.py:301
  111.5 19.3 %copy-start.11 = (bf16[128,1920]{1,0:T(8,128)(2,1)}, bf16[128,1920]{1,0:T(8,128)(2,1)S(1)}, u32[]{:S(2)}) copy-start(bf16[128,1920]{1,0:T(8,128)(2,1)S(1)} %collective-permute-done.21.c) | copy-start | bytes 1474564
  111.5 19.3 %collective-permute-start.22 = (bf16[128,1024]{1,0:T(8,128)(2,1)}, bf16[128,1024]{1,0:T(8,128)(2,1)S(1)}, u32[]{:S(2)}, u32[]{:S(2)}) collective-permute-start(bf16[128,1024]{1,0:T(8,128)(2,1)} %get-tuple-element.128), channel_id=1, source_target_pairs={{0,32},{32,64},{64,96},{96,0},{1,33},{33,65},{65,97},{97,1},{2,34}... | collective-permute-start | bytes 786440 | tf_op jit(solution)/shard_map/ppermute | solution.py:301
  116.8 14.0 %collective-permute-start.23 = (bf16[128,1024]{1,0:T(8,128)(2,1)}, bf16[128,1024]{1,0:T(8,128)(2,1)S(1)}, u32[]{:S(2)}, u32[]{:S(2)}) collective-permute-start(bf16[128,1024]{1,0:T(8,128)(2,1)} %get-tuple-element.129), channel_id=1, source_target_pairs={{0,96},{32,0},{64,32},{96,64},{1,97},{33,1},{65,33},{97,65},{2,98}... | collective-permute-start | bytes 786440 | tf_op jit(solution)/shard_map/ppermute | solution.py:301
  116.8 14.1 %collective-permute-start.24 = (bf16[128,1024]{1,0:T(8,128)(2,1)}, bf16[128,1024]{1,0:T(8,128)(2,1)S(1)}, u32[]{:S(2)}, u32[]{:S(2)}) collective-permute-start(bf16[128,1024]{1,0:T(8,128)(2,1)} %get-tuple-element.130), channel_id=1, source_target_pairs={{0,64},{32,96},{64,0},{96,32},{1,65},{33,97},{65,1},{97,33},{2,66}... | collective-permute-start | bytes 786440 | tf_op jit(solution)/shard_map/ppermute | solution.py:301
  118.9 11.9 %collective-permute-start.25 = (f32[16,2848]{1,0:T(8,128)S(1)}, f32[16,2848]{1,0:T(8,128)S(1)}, u32[]{:S(2)}, u32[]{:S(2)}) collective-permute-start(f32[16,2848]{1,0:T(8,128)S(1)} %add.81), channel_id=1, source_target_pairs={{0,2},{2,0},{4,6},{6,4},{1,3},{3,1},{5,7},{7,5},{8,10},{10,8},{12,... | collective-permute-start | bytes 546824 | tf_op jit(solution)/shard_map/ppermute | solution.py:306
  130.8 4.7 %copy-start.15 = (bf16[128,1024]{1,0:T(8,128)(2,1)}, bf16[128,1024]{1,0:T(8,128)(2,1)S(1)}, u32[]{:S(2)}) copy-start(bf16[128,1024]{1,0:T(8,128)(2,1)S(1)} %collective-permute-done.22.a) | copy-start | bytes 786436
  130.8 4.7 %copy-start.16 = (bf16[128,1024]{1,0:T(8,128)(2,1)}, bf16[128,1024]{1,0:T(8,128)(2,1)S(1)}, u32[]{:S(2)}) copy-start(bf16[128,1024]{1,0:T(8,128)(2,1)S(1)} %collective-permute-done.23.b) | copy-start | bytes 786436
  130.8 4.7 %copy-start.18 = (bf16[128,1024]{1,0:T(8,128)(2,1)}, bf16[128,1024]{1,0:T(8,128)(2,1)S(1)}, u32[]{:S(2)}) copy-start(bf16[128,1024]{1,0:T(8,128)(2,1)S(1)} %collective-permute-done.24.c) | copy-start | bytes 786436
  130.9 13.8 %collective-permute-start.26 = (bf16[128,1024]{1,0:T(8,128)(2,1)}, bf16[128,1024]{1,0:T(8,128)(2,1)S(1)}, u32[]{:S(2)}, u32[]{:S(2)}) collective-permute-start(bf16[128,1024]{1,0:T(8,128)(2,1)} %get-tuple-element.133), channel_id=1, source_target_pairs={{0,32},{32,64},{64,96},{96,0},{1,33},{33,65},{65,97},{97,1},{2,34}... | collective-permute-start | bytes 786440 | tf_op jit(solution)/shard_map/ppermute | solution.py:301
  131.6 13.1 %collective-permute-start.27 = (bf16[128,1024]{1,0:T(8,128)(2,1)}, bf16[128,1024]{1,0:T(8,128)(2,1)S(1)}, u32[]{:S(2)}, u32[]{:S(2)}) collective-permute-start(bf16[128,1024]{1,0:T(8,128)(2,1)} %get-tuple-element.134), channel_id=1, source_target_pairs={{0,96},{32,0},{64,32},{96,64},{1,97},{33,1},{65,33},{97,65},{2,98}... | collective-permute-start | bytes 786440 | tf_op jit(solution)/shard_map/ppermute | solution.py:301
  134.2 10.5 %collective-permute-start.28 = (bf16[128,1024]{1,0:T(8,128)(2,1)}, bf16[128,1024]{1,0:T(8,128)(2,1)S(1)}, u32[]{:S(2)}, u32[]{:S(2)}) collective-permute-start(bf16[128,1024]{1,0:T(8,128)(2,1)} %get-tuple-element.135), channel_id=1, source_target_pairs={{0,64},{32,96},{64,0},{96,32},{1,65},{33,97},{65,1},{97,33},{2,66}... | collective-permute-start | bytes 786440 | tf_op jit(solution)/shard_map/ppermute | solution.py:301
  135.0 9.7 %collective-permute-start.30 = (f32[16,2848]{1,0:T(8,128)S(1)}, f32[16,2848]{1,0:T(8,128)S(1)}, u32[]{:S(2)}, u32[]{:S(2)}) collective-permute-start(f32[16,2848]{1,0:T(8,128)S(1)} %add.82), channel_id=1, source_target_pairs={{0,4},{2,6},{4,0},{6,2},{1,5},{3,7},{5,1},{7,3},{8,12},{10,14},{12... | collective-permute-start | bytes 546824 | tf_op jit(solution)/shard_map/ppermute | solution.py:306
  138.5 6.2 %collective-permute-start.29 = (bf16[64,1024]{1,0:T(8,128)(2,1)}, bf16[64,1024]{1,0:T(8,128)(2,1)S(1)}, u32[]{:S(2)}, u32[]{:S(2)}) collective-permute-start(bf16[64,1024]{1,0:T(8,128)(2,1)} %get-tuple-element.147), channel_id=1, source_target_pairs={{0,16},{16,0},{1,17},{17,1},{2,18},{18,2},{3,19},{19,3},{4,20},{20... | collective-permute-start | bytes 393224 | tf_op jit(solution)/shard_map/ppermute | solution.py:306
  144.7 9.1 %copy-start.22 = (bf16[64,1024]{1,0:T(8,128)(2,1)}, bf16[64,1024]{1,0:T(8,128)(2,1)S(1)}, u32[]{:S(2)}) copy-start(bf16[64,1024]{1,0:T(8,128)(2,1)S(1)} %collective-permute-done.29.got1) | copy-start | bytes 393220
  144.7 0.7 copy-start.17
  144.7 0.8 copy-start.19
  144.7 0.9 copy-start.20
  144.7 9.0 %collective-permute-start.31 = (bf16[64,1920]{1,0:T(8,128)(2,1)}, bf16[64,1920]{1,0:T(8,128)(2,1)S(1)}, u32[]{:S(2)}, u32[]{:S(2)}) collective-permute-start(bf16[64,1920]{1,0:T(8,128)(2,1)} %get-tuple-element.150), channel_id=1, source_target_pairs={{0,16},{16,0},{1,17},{17,1},{2,18},{18,2},{3,19},{19,3},{4,20},{20... | collective-permute-start | bytes 737288 | tf_op jit(solution)/shard_map/ppermute | solution.py:306
  148.5 5.2 %collective-permute-start.32 = (bf16[64,1024]{1,0:T(8,128)(2,1)}, bf16[64,1024]{1,0:T(8,128)(2,1)S(1)}, u32[]{:S(2)}, u32[]{:S(2)}) collective-permute-start(bf16[64,1024]{1,0:T(8,128)(2,1)} %get-tuple-element.155), channel_id=1, source_target_pairs={{0,16},{16,0},{1,17},{17,1},{2,18},{18,2},{3,19},{19,3},{4,20},{20... | collective-permute-start | bytes 393224 | tf_op jit(solution)/shard_map/ppermute | solution.py:306
  153.7 0.7 copy-start.23
  153.7 0.7 copy-start.21

commit v5 on v4

--- a/solution.py
+++ b/solution.py
@@ -162,7 +162,8 @@
 
 
 def half_kernel(which, width, layout, n, base, *refs):
-    pieces, (wo, wr, uo, ur, down, own, *outs, held, held_wo, held_wr, low, total, sems, w_sems) = refs[:n], refs[n:]
+    pieces, (wo, wr, *given), refs = refs[:n], refs[n:-12], refs[-12:]
+    down, own, *outs, low, held, held_wo, held_wr, total, sems, w_sems = refs
     rows = own.shape[0]
     half = wo.shape[1]
     always = base[0] >= 0
@@ -181,8 +182,11 @@
     def _():
         for copy in gathers:
             copy.wait()
-        factors = dot_t(held[:, :half], uo[...]) + dot_t(held[:, half:], ur[...])
-        low[...] = jnp.concatenate(split3(factors), axis=1)
+        if len(given) == 1:
+            low[...] = given[0][...]
+        else:
+            factors = dot_t(held[:, :half], given[0][...]) + dot_t(held[:, half:], given[1][...])
+            low[...] = jnp.concatenate(split3(factors), axis=1)
 
     @pl.when(always)
     def _():
@@ -204,7 +208,7 @@
                 put(out, here, coded, scales[d], width)
 
 
-def partial_half(which, base, pieces, layout, wo, wr, uo, ur, down):
+def partial_half(which, base, pieces, layout, wo, wr, given, down):
     width, half = wo.shape[0] // 2, wo.shape[1]
     rows = sum(size for _, _, size, _, _ in layout) // 4
     padded = (width // 128 + 1) * 128
@@ -215,60 +219,67 @@
         grid_spec=pltpu.PrefetchScalarGridSpec(
             num_scalar_prefetch=1,
             grid=(1,),
-            in_specs=[hbm] * (len(pieces) + 2) + [whole(uo), whole(ur), whole(down)],
+            in_specs=[hbm] * (len(pieces) + 2) + [whole(g) for g in given] + [whole(down)],
             out_specs=[pl.BlockSpec((rows, width), lambda j, b: (0, 0))]
-            + [pl.BlockSpec((rows, padded), lambda j, b: (0, 0))] * 3,
+            + [pl.BlockSpec((rows, padded), lambda j, b: (0, 0))] * 3
+            + [pl.BlockSpec((4 * rows, 48), lambda j, b: (0, 0))],
             scratch_shapes=[
                 pltpu.VMEM((4 * rows, 2 * half), jnp.bfloat16),
                 pltpu.VMEM((width, half), jnp.bfloat16),
                 pltpu.VMEM((width, half), jnp.bfloat16),
-                pltpu.VMEM((4 * rows, 48), jnp.bfloat16),
                 pltpu.VMEM((4 * rows, width), jnp.float32),
                 pltpu.SemaphoreType.DMA((len(layout),)),
                 pltpu.SemaphoreType.DMA((2,)),
             ],
         ),
         out_shape=[jax.ShapeDtypeStruct((rows, width), jnp.float32)]
-        + [jax.ShapeDtypeStruct((rows, padded), jnp.bfloat16)] * 3,
+        + [jax.ShapeDtypeStruct((rows, padded), jnp.bfloat16)] * 3
+        + [jax.ShapeDtypeStruct((4 * rows, 48), jnp.bfloat16)],
         compiler_params=pltpu.CompilerParams(vmem_limit_bytes=KERNEL_BYTES),
         cost_estimate=pl.CostEstimate(flops=PRETEND, bytes_accessed=1, transcendentals=0),
         name="partial_half",
-    )(base, *pieces, wo, wr, uo, ur, down)
-
-
-def fold_kernel(width, swap, own, a, b, c, keep, send):
-    rows = keep.shape[0]
-    swapped = swap[0] == 1
-    scales = []
-    for j, here in tiles(width):
-        total = own[:, here]
-        for r in (a, b, c):
-            total = total + decode(r, j, here, width)
-        first, second = total[:rows], total[rows:]
-        keep[:, here] = jnp.where(swapped, second, first)
-        coded, scale = encode(jnp.where(swapped, first, second))
-        scales.append(scale)
-        put(send, here, coded, scales, width)
-
-
-def fold(swap, own, received, width):
-    rows = own.shape[0]
-    padded = received[0].shape[1]
+    )(base, *pieces, wo, wr, *given, down)
+
+
+def fold_kernel(*refs):
+    swapped = refs[0][0] == 1
+    n = (len(refs) - 2) // 5
+    at = 0
+    for i in range(n):
+        own, a, b, c = refs[1 + 4 * i : 5 + 4 * i]
+        keep, send = refs[1 + 4 * n + i], refs[-1].at[:, pl.ds(at, a.shape[1])]
+        at += a.shape[1]
+        rows, width = keep.shape
+        scales = []
+        for j, here in tiles(width):
+            total = own[:, here]
+            for r in (a, b, c):
+                total = total + decode(r, j, here, width)
+            first, second = total[:rows], total[rows:]
+            keep[:, here] = jnp.where(swapped, second, first)
+            coded, scale = encode(jnp.where(swapped, first, second))
+            scales.append(scale)
+            put(send, here, coded, scales, width)
+
+
+def fold(swap, *groups):
     vmem = pl.BlockSpec(memory_space=pltpu.VMEM)
+    rows = groups[0][0].shape[0] // 2
+    out_shape = [jax.ShapeDtypeStruct((rows, group[0].shape[1]), jnp.float32) for group in groups]
+    out_shape.append(jax.ShapeDtypeStruct((rows, sum(group[1].shape[1] for group in groups)), jnp.bfloat16))
     return pl.pallas_call(
-        functools.partial(fold_kernel, width),
-        in_specs=[pl.BlockSpec(memory_space=pltpu.SMEM)] + [vmem] * 4,
-        out_specs=[vmem] * 2,
-        out_shape=[
-            jax.ShapeDtypeStruct((rows // 2, width), jnp.float32),
-            jax.ShapeDtypeStruct((rows // 2, padded), jnp.bfloat16),
-        ],
+        fold_kernel,
+        in_specs=[pl.BlockSpec(memory_space=pltpu.SMEM)] + [vmem] * (4 * len(groups)),
+        out_specs=[vmem] * len(out_shape),
+        out_shape=out_shape,
         cost_estimate=pl.CostEstimate(flops=1, bytes_accessed=1, transcendentals=0),
         name="fold",
-    )(swap, own, *received)
-
-
-def finish_kernel(keep0, got0, keep1, got1, keep2, got2, out, total):
+    )(swap, *(array for group in groups for array in group))
+
+
+def finish_kernel(keep0, keep1, got, keep2, got2, out, total):
+    cut = got.shape[1] - got2.shape[1]
+    got0, got1 = got.at[:, pl.ds(0, cut)], got.at[:, pl.ds(cut, got2.shape[1])]
     rows, width = keep0.shape
     for j, here in tiles(width):
         total[:rows, here] = keep0[:, here] + decode(got0, j, here, width)
@@ -284,11 +295,11 @@
 
 def finish(*keeps_and_gots):
     vmem = pl.BlockSpec(memory_space=pltpu.VMEM)
-    keep0, _, keep1 = keeps_and_gots[:3]
+    keep0, keep1 = keeps_and_gots[:2]
     shape = (keep0.shape[0] + keep1.shape[0], keep0.shape[1])
     return pl.pallas_call(
         finish_kernel,
-        in_specs=[vmem] * 6,
+        in_specs=[vmem] * 5,
         out_specs=vmem,
         out_shape=jax.ShapeDtypeStruct(shape[::-1], jnp.bfloat16),
         scratch_shapes=[pltpu.VMEM(shape, jnp.float32)],
@@ -395,36 +406,34 @@
         (5, 0, q, 2, q),
     ]
 
-    def half_of_sums(which):
+    def half_of_sums(which, *given):
         return partial_half(
-            which, base, (block, x1, up4, down4, up5, down5), layout1, weight, weight_other, up_own, up_other, down3
+            which, base, (block, x1, up4, down4, up5, down5), layout1, weight, weight_other, given, down3
         )
 
     b0 = ahead(b0, "y", 2)
-    kept1, a1, b1, c1 = half_of_sums(0)
-    kept1, a1, b1, c1, b0, parts, block = phase(kept1, a1, b1, c1, b0, parts, block)
+    kept1, a1, b1, c1, factors = half_of_sums(0, up_own, up_other)
+    kept1, a1, b1, c1, b0, parts, block, factors = phase(kept1, a1, b1, c1, b0, parts, block, factors)
 
     a1, c1, b1 = ahead(a1, "y", 1), ahead(c1, "y", 3), ahead(b1, "y", 2)
     parts_other = across(parts, "z", 1)
-    kept2, a2, b2, c2 = half_of_sums(1)
+    kept2, a2, b2, c2, _ = half_of_sums(1, factors)
     kept2, a2, b2, c2, a1, c1, b1, b0, parts_other = phase(kept2, a2, b2, c2, a1, c1, b1, b0, parts_other)
     parts = parts + parts_other
 
     a2, c2, b2 = ahead(a2, "y", 1), ahead(c2, "y", 3), ahead(b2, "y", 2)
     parts_other = across(parts, "z", 2)
-    keep0, send0 = fold(swap, kept0, (a0, c0, b0), width)
-    keep1, send1 = fold(swap, kept1, (a1, c1, b1), width // 2)
+    keep0, keep1, send1 = fold(swap, (kept0, a0, c0, b0), (kept1, a1, c1, b1))
+    a2, c2, b2, keep0, keep1, send1, parts_other = phase(a2, c2, b2, keep0, keep1, send1, parts_other)
+
     got1 = across(send1, "xl", 1)
-    a2, c2, b2, keep0, send0, keep1, got1, parts_other = phase(a2, c2, b2, keep0, send0, keep1, got1, parts_other)
-
-    got0 = across(send0, "xl", 1)
-    keep2, send2 = fold(swap, kept2, (a2, c2, b2), width // 2)
+    keep2, send2 = fold(swap, (kept2, a2, c2, b2))
     got2 = across(send2, "xl", 1)
     parts = after(parts, send2) + parts_other
     grad_a = parts[:, :width_row_block].T
     grad_b = parts[:, width_row_block:]
-    got0, got2, grad_a, grad_b = phase(got0, got2, grad_a, grad_b)
-    grad_input = finish(keep0, got0, keep1, got1, keep2, got2).T
+    got1, got2, grad_a, grad_b = phase(got1, got2, grad_a, grad_b)
+    grad_input = finish(keep0, keep1, got1, keep2, got2).T
     return grad_input, grad_a, grad_b
 
 

time: 158 us -> 155 us (0.981)
  Pallas kernels: 54.8 us -> 51.9 us
    pallas_call x4 -> x3, Pallas kernels: 13 us -> 11.3 us  [the longest x2 8.52 us: fold(): pl.pallas_call(fold_kernel, in_specs=[pl.BlockSpec(memory_space=pltpu.SME...]
    ppermute x15 -> x14, waiting for transfers between devices: 32.6 us -> 32.7 us  [across(): return lax.ppermute(array, axis, [(i, i ^ bit) for i in range(n)])]
    ppermute x15 -> x14, starting transfers between devices: 13.4 us -> 13.2 us  [across(): return lax.ppermute(array, axis, [(i, i ^ bit) for i in range(n)])]
  transfers between devices with their start and end apart: 33 -> 32, of which waited for: 12 -> 12; matrix products, arithmetic and copies ran while one was open for 5% -> 5% of each run, Pallas kernels for 33% -> 32%
where the time goes in v5:
time: 155 us; the launch traced here: 154 us
  Pallas kernels  51.9 us (33%)
  starting transfers between devices  45.5 us (29%)
  waiting for transfers between devices  42.2 us (27%)
  local copies, waits for them, and re-layouts  7.4 us (5%)
  other arithmetic  4.14 us (3%)
  matrix products  1.86 us (1%)
    ppermute x14, waiting for transfers between devices, across(): return lax.ppermute(array, axis, [(i, i ^ bit) for i in range(n)])  32.7 us
    ppermute x18, starting transfers between devices, ahead(): return lax.ppermute(array, axis, [(i, (i + step) % n) for i in range(n)])  32.3 us
    pallas_call x2, Pallas kernels, partial_half(): pl.pallas_call(functools.partial(half_kernel, which, width, layout, len(p...  22.3 us
    pallas_call x1, Pallas kernels, partial(): pl.pallas_call(functools.partial(partial_kernel, width, layout, len(piece...  18.2 us
    ppermute x14, starting transfers between devices, across(): return lax.ppermute(array, axis, [(i, i ^ bit) for i in range(n)])  13.2 us
    ppermute x18, waiting for transfers between devices, ahead(): return lax.ppermute(array, axis, [(i, (i + step) % n) for i in range(n)])  9.5 us
    pallas_call x2, Pallas kernels, fold(): pl.pallas_call(fold_kernel, in_specs=[pl.BlockSpec(memory_space=pltpu.SME...  8.52 us
  transfers between devices with their start and end apart: 32, of which 12 were waited for; matrix products, arithmetic and copies ran while one was open for 5% of the time, Pallas kernels for 32%

profile of v5, /device:TPU:0, one launch (start us, length us, event | category | flops | bytes accessed | tf_op | source)
XLA Modules:
  0.0 154.1 jit_solution(2698300978590426521)
XLA Ops:
  0.7 1.4 constant_dynamic-slice_fusion.3
  2.0 0.1 collective-permute-start
  2.1 1.5 constant_dynamic-slice_fusion
  3.6 1.0 fusion.4
  4.7 3.2 %collective-permute-start.4 = (bf16[64,3840]{1,0:T(8,128)(2,1)S(1)}, bf16[64,3840]{1,0:T(8,128)(2,1)}, u32[]{:S(2)}, u32[]{:S(2)}) collective-permute-start(bf16[64,3840]{1,0:T(8,128)(2,1)S(1)} %get-tuple-element.168), channel_id=1, source_target_pairs={{0,1},{1,0},{2,3},{3,2},{4,5},{5,4},{6,7},{7,6},{8,9},{9,8},{10,11... | collective-permute-start | bytes 1474568 | tf_op jit(solution)/shard_map/ppermute | solution.py:317
  7.9 3.9 %collective-permute-start.3 = (bf16[64,3840]{1,0:T(8,128)(2,1)S(1)}, bf16[64,3840]{1,0:T(8,128)(2,1)}, u32[]{:S(2)}, u32[]{:S(2)}) collective-permute-start(bf16[64,3840]{1,0:T(8,128)(2,1)S(1)} %get-tuple-element.168), channel_id=1, source_target_pairs={{0,4},{2,6},{4,0},{6,2},{1,5},{3,7},{5,1},{7,3},{8,12},{10,14},{12... | collective-permute-start | bytes 1474568 | tf_op jit(solution)/shard_map/ppermute | solution.py:312
  11.8 0.7 collective-permute-start.2
  12.5 1.3 collective-permute-start.1
  13.8 0.5 collective-permute-start.5
  14.3 0.3 fusion.23
  14.7 1.1 pad_maximum_fusion.refs_0_
  15.9 14.6 %collective-permute-done.5.refs_1_ = bf16[64,3840]{1,0:T(8,128)(2,1)S(1)} collective-permute-done((bf16[64,3840]{1,0:T(8,128)(2,1)S(1)}, bf16[64,3840]{1,0:T(8,128)(2,1)S(1)}, u32[]{:S(2)}, u32[]{:S(2)}) %collective-permute-start.5) | collective-permute-done | bytes 491552 | tf_op jit(solution)/shard_map/ppermute | solution.py:317
  30.5 4.3 %collective-permute-done.2.refs_4_ = bf16[64,3840]{1,0:T(8,128)(2,1)} collective-permute-done((bf16[64,3840]{1,0:T(8,128)(2,1)S(1)}, bf16[64,3840]{1,0:T(8,128)(2,1)}, u32[]{:S(2)}, u32[]{:S(2)}) %collective-permute-start.2) | collective-permute-done | bytes 491552 | tf_op jit(solution)/shard_map/ppermute | solution.py:312
  34.8 0.5 collective-permute-start.10
  35.3 0.9 multiply_bitcast_fusion
  36.2 2.7 %collective-permute-start.7 = (bf16[64,3840]{1,0:T(8,128)(2,1)}, bf16[64,3840]{1,0:T(8,128)(2,1)S(1)}, u32[]{:S(2)}, u32[]{:S(2)}) collective-permute-start(bf16[64,3840]{1,0:T(8,128)(2,1)} %collective-permute-done.4.refs_1_), channel_id=1, source_target_pairs={{0,6},{2,0},{4,2},{6,4},{1,7},{3,1},{5,3},{7,5},{8,14},{10,8},{12,... | collective-permute-start | bytes 1474568 | tf_op jit(solution)/shard_map/ppermute | solution.py:312
  38.9 0.5 collective-permute-start.8
  39.4 1.3 collective-permute-done.10
  40.8 1.6 %collective-permute-start.11 = (f32[32,256]{1,0:T(8,128)S(1)}, f32[32,256]{1,0:T(8,128)S(1)}, u32[]{:S(2)}, u32[]{:S(2)}) collective-permute-start(f32[32,256]{1,0:T(8,128)S(1)} %add.70), channel_id=1, source_target_pairs={{0,32},{32,0},{64,96},{96,64},{1,33},{33,1},{65,97},{97,65},{2,34}... | collective-permute-start | bytes 98312 | tf_op jit(solution)/shard_map/ppermute | solution.py:317
  42.4 0.7 pad_maximum_fusion.3.refs_12_.refs_10_.refs_9_
  43.1 1.6 %collective-permute-done.11 = f32[32,256]{1,0:T(8,128)S(1)} collective-permute-done((f32[32,256]{1,0:T(8,128)S(1)}, f32[32,256]{1,0:T(8,128)S(1)}, u32[]{:S(2)}, u32[]{:S(2)}) %collective-permute-start.11) | collective-permute-done | bytes 32800 | tf_op jit(solution)/shard_map/ppermute | solution.py:317
  44.7 3.2 %collective-permute-start.12 = (f32[32,256]{1,0:T(8,128)S(1)}, f32[32,256]{1,0:T(8,128)S(1)}, u32[]{:S(2)}, u32[]{:S(2)}) collective-permute-start(f32[32,256]{1,0:T(8,128)S(1)} %add.71), channel_id=1, source_target_pairs={{0,64},{32,96},{64,0},{96,32},{1,65},{33,97},{65,1},{97,33},{2,66}... | collective-permute-start | bytes 98312 | tf_op jit(solution)/shard_map/ppermute | solution.py:317
  47.9 1.1 pad_maximum_fusion.1
  48.9 1.2 collective-permute-done.12
  50.1 3.4 %collective-permute-done.8.refs_7_ = bf16[64,3840]{1,0:T(8,128)(2,1)S(1)} collective-permute-done((bf16[64,3840]{1,0:T(8,128)(2,1)}, bf16[64,3840]{1,0:T(8,128)(2,1)S(1)}, u32[]{:S(2)}, u32[]{:S(2)}) %collective-permute-start.8) | collective-permute-done | bytes 491552 | tf_op jit(solution)/shard_map/ppermute | solution.py:317
  53.5 0.8 copy-done.12
  54.3 3.0 %collective-permute-start.14 = (bf16[128,3840]{1,0:T(8,128)(2,1)}, bf16[128,3840]{1,0:T(8,128)(2,1)S(1)}, u32[]{:S(2)}, u32[]{:S(2)}) collective-permute-start(bf16[128,3840]{1,0:T(8,128)(2,1)} %pad_maximum_fusion.1), channel_id=1, source_target_pairs={{0,6},{2,0},{4,2},{6,4},{1,7},{3,1},{5,3},{7,5},{8,14},{10,8},{12,... | collective-permute-start | bytes 2949128 | tf_op jit(solution)/shard_map/ppermute | solution.py:312
  57.3 0.7 collective-permute-start.15
  58.0 18.2 %partial.1 = (f32[128,1856]{1,0:T(8,128)}, bf16[128,1920]{1,0:T(8,128)(2,1)}, bf16[128,1920]{1,0:T(8,128)(2,1)}, bf16[128,1920]{1,0:T(8,128)(2,1)}) custom-call(s32[1]{0:T(128)} %bitcast.base, bf16[128,3840]{1,0:T(8,128)(2,1)} %copy-done.1, bf16[64,3840]{1,0:T(8,128)(2,1)} %collective-permute-done.4.refs_1_, ...), custom_call_target="tpu_custom_call" | custom-call | flops 1 | bytes 1 | tf_op jit(solution)/shard_map/partial/pallas_call | solution.py:135
  76.2 1.1 collective-permute-done.14.refs_3_
  77.3 3.4 %collective-permute-done.13.refs_2_ = bf16[128,3840]{1,0:T(8,128)(2,1)} collective-permute-done((bf16[128,3840]{1,0:T(8,128)(2,1)}, bf16[128,3840]{1,0:T(8,128)(2,1)}, u32[]{:S(2)}, u32[]{:S(2)}) %collective-permute-start.13) | collective-permute-done | bytes 983072 | tf_op jit(solution)/shard_map/ppermute | solution.py:312
  80.7 0.3 fusion.6
  81.0 0.3 fusion.12
  81.4 1.2 slice.51
  82.6 0.3 collective-permute-start.17
  82.8 1.8 %collective-permute-start.16 = (bf16[64,3840]{1,0:T(8,128)(2,1)S(1)}, bf16[64,3840]{1,0:T(8,128)(2,1)S(1)}, u32[]{:S(2)}, u32[]{:S(2)}) collective-permute-start(bf16[64,3840]{1,0:T(8,128)(2,1)S(1)} %slice.51), channel_id=1, source_target_pairs={{0,2},{2,4},{4,6},{6,0},{1,3},{3,5},{5,7},{7,1},{8,10},{10,12},{12... | collective-permute-start | bytes 1474568 | tf_op jit(solution)/shard_map/ppermute | solution.py:312
  84.7 1.6 %collective-permute-start.18 = (bf16[128,1920]{1,0:T(8,128)(2,1)S(1)}, bf16[128,1920]{1,0:T(8,128)(2,1)S(1)}, u32[]{:S(2)}, u32[]{:S(2)}) collective-permute-start(bf16[128,1920]{1,0:T(8,128)(2,1)S(1)} %copy-done.25), channel_id=1, source_target_pairs={{0,32},{32,64},{64,96},{96,0},{1,33},{33,65},{65,97},{97,1},{2,34}... | collective-permute-start | bytes 1474568 | tf_op jit(solution)/shard_map/ppermute | solution.py:312
  86.2 1.7 %collective-permute-start.19 = (bf16[128,1920]{1,0:T(8,128)(2,1)S(1)}, bf16[128,1920]{1,0:T(8,128)(2,1)S(1)}, u32[]{:S(2)}, u32[]{:S(2)}) collective-permute-start(bf16[128,1920]{1,0:T(8,128)(2,1)S(1)} %copy-done.24), channel_id=1, source_target_pairs={{0,96},{32,0},{64,32},{96,64},{1,97},{33,1},{65,33},{97,65},{2,98}... | collective-permute-start | bytes 1474568 | tf_op jit(solution)/shard_map/ppermute | solution.py:312
  87.9 0.1 pad_maximum_fusion.2
  88.0 0.6 collective-permute-start.20
  88.6 6.6 %collective-permute-done.20 = f32[16,2848]{1,0:T(8,128)S(1)} collective-permute-done((f32[16,2848]{1,0:T(8,128)S(1)}, f32[16,2848]{1,0:T(8,128)S(1)}, u32[]{:S(2)}, u32[]{:S(2)}) %collective-permute-start.20) | collective-permute-done | bytes 182304 | tf_op jit(solution)/shard_map/ppermute | solution.py:317
  95.2 0.6 collective-permute-done.18.refs_2_
  95.9 3.9 %collective-permute-start.21 = (bf16[128,1920]{1,0:T(8,128)(2,1)S(1)}, bf16[128,1920]{1,0:T(8,128)(2,1)S(1)}, u32[]{:S(2)}, u32[]{:S(2)}) collective-permute-start(bf16[128,1920]{1,0:T(8,128)(2,1)S(1)} %copy-done.23), channel_id=1, source_target_pairs={{0,64},{32,96},{64,0},{96,32},{1,65},{33,97},{65,1},{97,33},{2,66}... | collective-permute-start | bytes 1474568 | tf_op jit(solution)/shard_map/ppermute | solution.py:312
  99.8 11.7 %partial_half.2 = (f32[128,928]{1,0:T(8,128)}, bf16[128,1024]{1,0:T(8,128)(2,1)}, bf16[128,1024]{1,0:T(8,128)(2,1)}, bf16[128,1024]{1,0:T(8,128)(2,1)}, bf16[512,48]{1,0:T(8,128)(2,1)}) custom-call(s32[1]{0:T(128)} %bitcast.base, bf16[128,3840]{1,0:T(8,128)(2,1)} %copy-done.1, bf16[64,3840]{1,0:T(8,128)(2,1)} %copy-done.4, ...), custom_call_target="tpu_custom_call" | custom-call | flops 1 | bytes 1 | tf_op jit(solution)/shard_map/partial_half/pallas_call | solution.py:217
  111.5 5.3 %collective-permute-start.22 = (bf16[128,1024]{1,0:T(8,128)(2,1)}, bf16[128,1024]{1,0:T(8,128)(2,1)S(1)}, u32[]{:S(2)}, u32[]{:S(2)}) collective-permute-start(bf16[128,1024]{1,0:T(8,128)(2,1)} %get-tuple-element.130), channel_id=1, source_target_pairs={{0,32},{32,64},{64,96},{96,0},{1,33},{33,65},{65,97},{97,1},{2,34}... | collective-permute-start | bytes 786440 | tf_op jit(solution)/shard_map/ppermute | solution.py:312
  116.8 2.1 %collective-permute-start.24 = (bf16[128,1024]{1,0:T(8,128)(2,1)}, bf16[128,1024]{1,0:T(8,128)(2,1)S(1)}, u32[]{:S(2)}, u32[]{:S(2)}) collective-permute-start(bf16[128,1024]{1,0:T(8,128)(2,1)} %get-tuple-element.132), channel_id=1, source_target_pairs={{0,64},{32,96},{64,0},{96,32},{1,65},{33,97},{65,1},{97,33},{2,66}... | collective-permute-start | bytes 786440 | tf_op jit(solution)/shard_map/ppermute | solution.py:312
  119.0 10.6 %partial_half.3 = (f32[128,928]{1,0:T(8,128)}, bf16[128,1024]{1,0:T(8,128)(2,1)}, bf16[128,1024]{1,0:T(8,128)(2,1)}, bf16[128,1024]{1,0:T(8,128)(2,1)}, bf16[512,48]{1,0:T(8,128)(2,1)}) custom-call(s32[1]{0:T(128)} %bitcast.base, bf16[128,3840]{1,0:T(8,128)(2,1)} %copy-done.1, bf16[64,3840]{1,0:T(8,128)(2,1)} %copy-done.4, ...), custom_call_target="tpu_custom_call" | custom-call | flops 1 | bytes 1 | tf_op jit(solution)/shard_map/partial_half/pallas_call | solution.py:217
  129.7 0.7 collective-permute-start.26
  130.4 2.6 %collective-permute-start.27 = (bf16[128,1024]{1,0:T(8,128)(2,1)}, bf16[128,1024]{1,0:T(8,128)(2,1)S(1)}, u32[]{:S(2)}, u32[]{:S(2)}) collective-permute-start(bf16[128,1024]{1,0:T(8,128)(2,1)} %get-tuple-element.136), channel_id=1, source_target_pairs={{0,96},{32,0},{64,32},{96,64},{1,97},{33,1},{65,33},{97,65},{2,98}... | collective-permute-start | bytes 786440 | tf_op jit(solution)/shard_map/ppermute | solution.py:312
  133.0 0.8 collective-permute-start.28
  133.8 0.6 collective-permute-start.29
  134.4 5.6 %fold.2 = (f32[64,1856]{1,0:T(8,128)}, f32[64,928]{1,0:T(8,128)}, bf16[64,2944]{1,0:T(8,128)(2,1)}) custom-call(s32[1]{0:T(128)} %bitcast.2.refs_0_, f32[128,1856]{1,0:T(8,128)} %get-tuple-element.138.refs_1_, bf16[128,1920]{1,0:T(8,128)(2,1)} %copy-done.9, bf16[128,1920]{1,0:T(8,128)(2,1)} %copy-done.10, bf16[128,1920]{1,0:T(8,128)(2,1)} %copy-done.11, ...), custom_call_target="tpu_custom_call" | custom-call | flops 1 | bytes 1 | tf_op jit(solution)/shard_map/fold/pallas_call | solution.py:270
  140.0 1.2 collective-permute-done.29
  141.2 0.6 collective-permute-start.30
  141.9 0.1 copy-done.20
  142.1 0.1 copy-done.21
  142.1 2.9 %fold.3 = (f32[64,928]{1,0:T(8,128)}, bf16[64,1024]{1,0:T(8,128)(2,1)}) custom-call(s32[1]{0:T(128)} %bitcast.2.refs_0_, f32[128,928]{1,0:T(8,128)} %get-tuple-element.153.refs_1_, bf16[128,1024]{1,0:T(8,128)(2,1)} %copy-done.19, bf16[128,1024]{1,0:T(8,128)(2,1)} %copy-done.20, bf16[128,1024]{1,0:T(8,128)(2,1)} %copy-done.21), custom_call_target="tpu_custom_call" | custom-call | flops 1 | bytes 1 | tf_op jit(solution)/shard_map/fold/pallas_call | solution.py:270
  145.0 1.2 collective-permute-start.31
  146.3 0.7 slice.76
  147.0 0.6 slice_bitcast_fusion
  147.7 2.9 %collective-permute-done.31.got2 = bf16[64,1024]{1,0:T(8,128)(2,1)S(1)} collective-permute-done((bf16[64,1024]{1,0:T(8,128)(2,1)}, bf16[64,1024]{1,0:T(8,128)(2,1)S(1)}, u32[]{:S(2)}, u32[]{:S(2)}) %collective-permute-start.31) | collective-permute-done | bytes 131104 | tf_op jit(solution)/shard_map/ppermute | solution.py:317
  150.5 0.7 copy-done.22
  151.2 0.1 copy-done.15
  151.3 2.8 %finish.1 = bf16[1856,128]{1,0:T(8,128)(2,1)} custom-call(f32[64,1856]{1,0:T(8,128)} %get-tuple-element.150.keep0, f32[64,928]{1,0:T(8,128)} %get-tuple-element.151.keep1, bf16[64,2944]{1,0:T(8,128)(2,1)} %copy-done.15, f32[64,928]{1,0:T(8,128)} %get-tuple-element.161.keep2, bf16[64,1024]{1,0:T(8,128)(2,1)} %copy-done.22), custom_call_target="tpu_custom_call" | custom-call | tf_op jit(solution)/shard_map/finish/pallas_call | solution.py:300
  (86 shorter events, 0.6 us)
Async XLA Ops:
  0.6 3.0 %copy-start = (bf16[256,928]{0,1:T(8,128)(2,1)S(1)}, bf16[256,928]{0,1:T(8,128)(2,1)}, u32[]{:S(2)}) copy-start(bf16[256,928]{0,1:T(8,128)(2,1)} %param.5) | copy-start | bytes 1425412
  0.7 13.7 %copy-start.2 = (bf16[256,1920]{1,0:T(8,128)(2,1)S(1)}, bf16[256,1920]{1,0:T(8,128)(2,1)}, u32[]{:S(2)}) copy-start(bf16[256,1920]{1,0:T(8,128)(2,1)} %param.6) | copy-start | bytes 2949124
  2.0 2.6 %collective-permute-start = (bf16[128,1920]{1,0:T(8,128)(2,1)S(1)}, bf16[128,1920]{1,0:T(8,128)(2,1)S(1)}, u32[]{:S(2)}, u32[]{:S(2)}) collective-permute-start(bf16[128,1920]{1,0:T(8,128)(2,1)S(1)} %get-tuple-element.170), channel_id=1, source_target_pairs={{0,8},{8,0},{1,9},{9,1},{2,10},{10,2},{3,11},{11,3},{4,12},{12,4},... | collective-permute-start | bytes 1474568 | tf_op jit(solution)/shard_map/ppermute | solution.py:317
  3.6 12.2 %copy-start.8 = (bf16[16,1920]{1,0:T(8,128)(2,1)}, bf16[16,1920]{1,0:T(8,128)(2,1)S(1)}, u32[]{:S(2)}) copy-start(bf16[16,1920]{1,0:T(8,128)(2,1)S(1)} %get-tuple-element.166.refs_10_.refs_8_) | copy-start | bytes 184324
  4.6 10.0 %copy-start.5 = (bf16[128,1920]{1,0:T(8,128)(2,1)}, bf16[128,1920]{1,0:T(8,128)(2,1)S(1)}, u32[]{:S(2)}) copy-start(bf16[128,1920]{1,0:T(8,128)(2,1)S(1)} %collective-permute-done) | copy-start | bytes 1474564
  4.7 25.7 %collective-permute-start.4 = (bf16[64,3840]{1,0:T(8,128)(2,1)S(1)}, bf16[64,3840]{1,0:T(8,128)(2,1)}, u32[]{:S(2)}, u32[]{:S(2)}) collective-permute-start(bf16[64,3840]{1,0:T(8,128)(2,1)S(1)} %get-tuple-element.168), channel_id=1, source_target_pairs={{0,1},{1,0},{2,3},{3,2},{4,5},{5,4},{6,7},{7,6},{8,9},{9,8},{10,11... | collective-permute-start | bytes 1474568 | tf_op jit(solution)/shard_map/ppermute | solution.py:317
  7.9 22.5 %collective-permute-start.3 = (bf16[64,3840]{1,0:T(8,128)(2,1)S(1)}, bf16[64,3840]{1,0:T(8,128)(2,1)}, u32[]{:S(2)}, u32[]{:S(2)}) collective-permute-start(bf16[64,3840]{1,0:T(8,128)(2,1)S(1)} %get-tuple-element.168), channel_id=1, source_target_pairs={{0,4},{2,6},{4,0},{6,2},{1,5},{3,7},{5,1},{7,3},{8,12},{10,14},{12... | collective-permute-start | bytes 1474568 | tf_op jit(solution)/shard_map/ppermute | solution.py:312
  11.8 23.0 %collective-permute-start.2 = (bf16[64,3840]{1,0:T(8,128)(2,1)S(1)}, bf16[64,3840]{1,0:T(8,128)(2,1)}, u32[]{:S(2)}, u32[]{:S(2)}) collective-permute-start(bf16[64,3840]{1,0:T(8,128)(2,1)S(1)} %get-tuple-element.168), channel_id=1, source_target_pairs={{0,6},{2,0},{4,2},{6,4},{1,7},{3,1},{5,3},{7,5},{8,14},{10,8},{12,... | collective-permute-start | bytes 1474568 | tf_op jit(solution)/shard_map/ppermute | solution.py:312
  12.5 22.3 %collective-permute-start.1 = (bf16[64,3840]{1,0:T(8,128)(2,1)S(1)}, bf16[64,3840]{1,0:T(8,128)(2,1)}, u32[]{:S(2)}, u32[]{:S(2)}) collective-permute-start(bf16[64,3840]{1,0:T(8,128)(2,1)S(1)} %get-tuple-element.168), channel_id=1, source_target_pairs={{0,2},{2,4},{4,6},{6,0},{1,3},{3,5},{5,7},{7,1},{8,10},{10,12},{12... | collective-permute-start | bytes 1474568 | tf_op jit(solution)/shard_map/ppermute | solution.py:312
  13.8 16.6 %collective-permute-start.5 = (bf16[64,3840]{1,0:T(8,128)(2,1)S(1)}, bf16[64,3840]{1,0:T(8,128)(2,1)S(1)}, u32[]{:S(2)}, u32[]{:S(2)}) collective-permute-start(bf16[64,3840]{1,0:T(8,128)(2,1)S(1)} %get-tuple-element.167), channel_id=1, source_target_pairs={{0,1},{1,0},{2,3},{3,2},{4,5},{5,4},{6,7},{7,6},{8,9},{9,8},{10,11... | collective-permute-start | bytes 1474568 | tf_op jit(solution)/shard_map/ppermute | solution.py:317
  15.9 42.1 %copy-start.1 = (bf16[128,3840]{1,0:T(8,128)(2,1)}, bf16[128,3840]{1,0:T(8,128)(2,1)S(1)}, u32[]{:S(2)}) copy-start(bf16[128,3840]{1,0:T(8,128)(2,1)S(1)} %pad_maximum_fusion.refs_0_) | copy-start | bytes 2949124
  30.5 23.1 %copy-start.4 = (bf16[64,3840]{1,0:T(8,128)(2,1)}, bf16[64,3840]{1,0:T(8,128)(2,1)S(1)}, u32[]{:S(2)}) copy-start(bf16[64,3840]{1,0:T(8,128)(2,1)S(1)} %collective-permute-done.5.refs_1_) | copy-start | bytes 1474564
  34.8 18.7 %collective-permute-start.9 = (bf16[1856,1920]{1,0:T(8,128)(2,1)}, bf16[1856,1920]{1,0:T(8,128)(2,1)}, u32[]{:S(2)}, u32[]{:S(2)}) collective-permute-start(bf16[1856,1920]{1,0:T(8,128)(2,1)} %refs_6_.1), channel_id=1, source_target_pairs={{0,8},{8,0},{1,9},{9,1},{2,10},{10,2},{3,11},{11,3},{4,12},{12,4},... | collective-permute-start | bytes 21381128 | tf_op jit(solution)/shard_map/ppermute | solution.py:317
  34.8 6.0 %collective-permute-start.10 = (f32[32,256]{1,0:T(8,128)S(1)}, f32[32,256]{1,0:T(8,128)S(1)}, u32[]{:S(2)}, u32[]{:S(2)}) collective-permute-start(f32[32,256]{1,0:T(8,128)S(1)} %pad_maximum_fusion.4), channel_id=1, source_target_pairs={{0,8},{8,0},{1,9},{9,1},{2,10},{10,2},{3,11},{11,3},{4,12},{12,4},... | collective-permute-start | bytes 98312 | tf_op jit(solution)/shard_map/ppermute | solution.py:317
  36.2 17.2 %collective-permute-start.7 = (bf16[64,3840]{1,0:T(8,128)(2,1)}, bf16[64,3840]{1,0:T(8,128)(2,1)S(1)}, u32[]{:S(2)}, u32[]{:S(2)}) collective-permute-start(bf16[64,3840]{1,0:T(8,128)(2,1)} %collective-permute-done.4.refs_1_), channel_id=1, source_target_pairs={{0,6},{2,0},{4,2},{6,4},{1,7},{3,1},{5,3},{7,5},{8,14},{10,8},{12,... | collective-permute-start | bytes 1474568 | tf_op jit(solution)/shard_map/ppermute | solution.py:312
  38.9 14.6 %collective-permute-start.6 = (bf16[64,3840]{1,0:T(8,128)(2,1)}, bf16[64,3840]{1,0:T(8,128)(2,1)S(1)}, u32[]{:S(2)}, u32[]{:S(2)}) collective-permute-start(bf16[64,3840]{1,0:T(8,128)(2,1)} %collective-permute-done.4.refs_1_), channel_id=1, source_target_pairs={{0,2},{2,4},{4,6},{6,0},{1,3},{3,5},{5,7},{7,1},{8,10},{10,12},{12... | collective-permute-start | bytes 1474568 | tf_op jit(solution)/shard_map/ppermute | solution.py:312
  38.9 14.6 %collective-permute-start.8 = (bf16[64,3840]{1,0:T(8,128)(2,1)}, bf16[64,3840]{1,0:T(8,128)(2,1)S(1)}, u32[]{:S(2)}, u32[]{:S(2)}) collective-permute-start(bf16[64,3840]{1,0:T(8,128)(2,1)} %collective-permute-done.3.refs_6_), channel_id=1, source_target_pairs={{0,1},{1,0},{2,3},{3,2},{4,5},{5,4},{6,7},{7,6},{8,9},{9,8},{10,11... | collective-permute-start | bytes 1474568 | tf_op jit(solution)/shard_map/ppermute | solution.py:317
  40.8 3.9 %collective-permute-start.11 = (f32[32,256]{1,0:T(8,128)S(1)}, f32[32,256]{1,0:T(8,128)S(1)}, u32[]{:S(2)}, u32[]{:S(2)}) collective-permute-start(f32[32,256]{1,0:T(8,128)S(1)} %add.70), channel_id=1, source_target_pairs={{0,32},{32,0},{64,96},{96,64},{1,33},{33,1},{65,97},{97,65},{2,34}... | collective-permute-start | bytes 98312 | tf_op jit(solution)/shard_map/ppermute | solution.py:317
  44.7 5.4 %collective-permute-start.12 = (f32[32,256]{1,0:T(8,128)S(1)}, f32[32,256]{1,0:T(8,128)S(1)}, u32[]{:S(2)}, u32[]{:S(2)}) collective-permute-start(f32[32,256]{1,0:T(8,128)S(1)} %add.71), channel_id=1, source_target_pairs={{0,64},{32,96},{64,0},{96,32},{1,65},{33,97},{65,1},{97,33},{2,66}... | collective-permute-start | bytes 98312 | tf_op jit(solution)/shard_map/ppermute | solution.py:317
  53.5 3.8 %copy-start.14 = (bf16[64,3840]{1,0:T(8,128)(2,1)}, bf16[64,3840]{1,0:T(8,128)(2,1)S(1)}, u32[]{:S(2)}) copy-start(bf16[64,3840]{1,0:T(8,128)(2,1)S(1)} %collective-permute-done.8.refs_7_) | copy-start | bytes 1474564
  53.5 0.8 copy-start.12
  53.5 3.8 %copy-start.13 = (bf16[64,3840]{1,0:T(8,128)(2,1)}, bf16[64,3840]{1,0:T(8,128)(2,1)S(1)}, u32[]{:S(2)}) copy-start(bf16[64,3840]{1,0:T(8,128)(2,1)S(1)} %collective-permute-done.6.refs_3_) | copy-start | bytes 1474564
  54.3 23.0 %collective-permute-start.14 = (bf16[128,3840]{1,0:T(8,128)(2,1)}, bf16[128,3840]{1,0:T(8,128)(2,1)S(1)}, u32[]{:S(2)}, u32[]{:S(2)}) collective-permute-start(bf16[128,3840]{1,0:T(8,128)(2,1)} %pad_maximum_fusion.1), channel_id=1, source_target_pairs={{0,6},{2,0},{4,2},{6,4},{1,7},{3,1},{5,3},{7,5},{8,14},{10,8},{12,... | collective-permute-start | bytes 2949128 | tf_op jit(solution)/shard_map/ppermute | solution.py:312
  57.3 23.4 %collective-permute-start.13 = (bf16[128,3840]{1,0:T(8,128)(2,1)}, bf16[128,3840]{1,0:T(8,128)(2,1)}, u32[]{:S(2)}, u32[]{:S(2)}) collective-permute-start(bf16[128,3840]{1,0:T(8,128)(2,1)} %pad_maximum_fusion.1), channel_id=1, source_target_pairs={{0,2},{2,4},{4,6},{6,0},{1,3},{3,5},{5,7},{7,1},{8,10},{10,12},{12... | collective-permute-start | bytes 2949128 | tf_op jit(solution)/shard_map/ppermute | solution.py:312
  57.3 18.9 %collective-permute-start.15 = (f32[32,256]{1,0:T(8,128)S(1)}, f32[32,256]{1,0:T(8,128)S(1)}, u32[]{:S(2)}, u32[]{:S(2)}) collective-permute-start(f32[32,256]{1,0:T(8,128)S(1)} %add.75), channel_id=1, source_target_pairs={{0,16},{16,0},{1,17},{17,1},{2,18},{18,2},{3,19},{19,3},{4,20},{20... | collective-permute-start | bytes 98312 | tf_op jit(solution)/shard_map/ppermute | solution.py:317
  77.3 5.2 %copy-start.3 = (bf16[128,3840]{1,0:T(8,128)(2,1)}, bf16[128,3840]{1,0:T(8,128)(2,1)S(1)}, u32[]{:S(2)}) copy-start(bf16[128,3840]{1,0:T(8,128)(2,1)S(1)} %collective-permute-done.14.refs_3_) | copy-start | bytes 2949124
  81.0 3.7 %copy-start.25 = (bf16[128,1920]{1,0:T(8,128)(2,1)S(1)}, bf16[128,1920]{1,0:T(8,128)(2,1)}, u32[]{:S(2)}) copy-start(bf16[128,1920]{1,0:T(8,128)(2,1)} %get-tuple-element.109) | copy-start | bytes 1474564
  81.0 5.2 %copy-start.24 = (bf16[128,1920]{1,0:T(8,128)(2,1)S(1)}, bf16[128,1920]{1,0:T(8,128)(2,1)}, u32[]{:S(2)}) copy-start(bf16[128,1920]{1,0:T(8,128)(2,1)} %get-tuple-element.110) | copy-start | bytes 1474564
  81.0 14.8 %copy-start.23 = (bf16[128,1920]{1,0:T(8,128)(2,1)S(1)}, bf16[128,1920]{1,0:T(8,128)(2,1)}, u32[]{:S(2)}) copy-start(bf16[128,1920]{1,0:T(8,128)(2,1)} %get-tuple-element.120) | copy-start | bytes 1474564
  82.6 12.6 %collective-permute-start.17 = (bf16[64,3840]{1,0:T(8,128)(2,1)S(1)}, bf16[64,3840]{1,0:T(8,128)(2,1)S(1)}, u32[]{:S(2)}, u32[]{:S(2)}) collective-permute-start(bf16[64,3840]{1,0:T(8,128)(2,1)S(1)} %slice.52), channel_id=1, source_target_pairs={{0,6},{2,0},{4,2},{6,4},{1,7},{3,1},{5,3},{7,5},{8,14},{10,8},{12,... | collective-permute-start | bytes 1474568 | tf_op jit(solution)/shard_map/ppermute | solution.py:312
  82.8 12.3 %collective-permute-start.16 = (bf16[64,3840]{1,0:T(8,128)(2,1)S(1)}, bf16[64,3840]{1,0:T(8,128)(2,1)S(1)}, u32[]{:S(2)}, u32[]{:S(2)}) collective-permute-start(bf16[64,3840]{1,0:T(8,128)(2,1)S(1)} %slice.51), channel_id=1, source_target_pairs={{0,2},{2,4},{4,6},{6,0},{1,3},{3,5},{5,7},{7,1},{8,10},{10,12},{12... | collective-permute-start | bytes 1474568 | tf_op jit(solution)/shard_map/ppermute | solution.py:312
  84.7 11.2 %collective-permute-start.18 = (bf16[128,1920]{1,0:T(8,128)(2,1)S(1)}, bf16[128,1920]{1,0:T(8,128)(2,1)S(1)}, u32[]{:S(2)}, u32[]{:S(2)}) collective-permute-start(bf16[128,1920]{1,0:T(8,128)(2,1)S(1)} %copy-done.25), channel_id=1, source_target_pairs={{0,32},{32,64},{64,96},{96,0},{1,33},{33,65},{65,97},{97,1},{2,34}... | collective-permute-start | bytes 1474568 | tf_op jit(solution)/shard_map/ppermute | solution.py:312
  86.2 9.6 %collective-permute-start.19 = (bf16[128,1920]{1,0:T(8,128)(2,1)S(1)}, bf16[128,1920]{1,0:T(8,128)(2,1)S(1)}, u32[]{:S(2)}, u32[]{:S(2)}) collective-permute-start(bf16[128,1920]{1,0:T(8,128)(2,1)S(1)} %copy-done.24), channel_id=1, source_target_pairs={{0,96},{32,0},{64,32},{96,64},{1,97},{33,1},{65,33},{97,65},{2,98}... | collective-permute-start | bytes 1474568 | tf_op jit(solution)/shard_map/ppermute | solution.py:312
  88.0 7.2 %collective-permute-start.20 = (f32[16,2848]{1,0:T(8,128)S(1)}, f32[16,2848]{1,0:T(8,128)S(1)}, u32[]{:S(2)}, u32[]{:S(2)}) collective-permute-start(f32[16,2848]{1,0:T(8,128)S(1)} %pad_maximum_fusion.2), channel_id=1, source_target_pairs={{0,1},{1,0},{2,3},{3,2},{4,5},{5,4},{6,7},{7,6},{8,9},{9,8},{10,11... | collective-permute-start | bytes 546824 | tf_op jit(solution)/shard_map/ppermute | solution.py:317
  95.2 4.6 %copy-start.6 = (bf16[64,3840]{1,0:T(8,128)(2,1)}, bf16[64,3840]{1,0:T(8,128)(2,1)S(1)}, u32[]{:S(2)}) copy-start(bf16[64,3840]{1,0:T(8,128)(2,1)S(1)} %collective-permute-done.17.refs_5_) | copy-start | bytes 1474564
  95.2 4.6 %copy-start.7 = (bf16[64,3840]{1,0:T(8,128)(2,1)}, bf16[64,3840]{1,0:T(8,128)(2,1)S(1)}, u32[]{:S(2)}) copy-start(bf16[64,3840]{1,0:T(8,128)(2,1)S(1)} %collective-permute-done.16.refs_4_) | copy-start | bytes 1474564
  95.8 15.6 %copy-start.9 = (bf16[128,1920]{1,0:T(8,128)(2,1)}, bf16[128,1920]{1,0:T(8,128)(2,1)S(1)}, u32[]{:S(2)}) copy-start(bf16[128,1920]{1,0:T(8,128)(2,1)S(1)} %collective-permute-done.18.refs_2_) | copy-start | bytes 1474564
  95.9 15.6 %copy-start.10 = (bf16[128,1920]{1,0:T(8,128)(2,1)}, bf16[128,1920]{1,0:T(8,128)(2,1)S(1)}, u32[]{:S(2)}) copy-start(bf16[128,1920]{1,0:T(8,128)(2,1)S(1)} %collective-permute-done.19.refs_3_) | copy-start | bytes 1474564
  95.9 15.6 %collective-permute-start.21 = (bf16[128,1920]{1,0:T(8,128)(2,1)S(1)}, bf16[128,1920]{1,0:T(8,128)(2,1)S(1)}, u32[]{:S(2)}, u32[]{:S(2)}) collective-permute-start(bf16[128,1920]{1,0:T(8,128)(2,1)S(1)} %copy-done.23), channel_id=1, source_target_pairs={{0,64},{32,96},{64,0},{96,32},{1,65},{33,97},{65,1},{97,33},{2,66}... | collective-permute-start | bytes 1474568 | tf_op jit(solution)/shard_map/ppermute | solution.py:312
  111.5 18.1 %copy-start.11 = (bf16[128,1920]{1,0:T(8,128)(2,1)}, bf16[128,1920]{1,0:T(8,128)(2,1)S(1)}, u32[]{:S(2)}) copy-start(bf16[128,1920]{1,0:T(8,128)(2,1)S(1)} %collective-permute-done.21.refs_4_) | copy-start | bytes 1474564
  111.5 18.1 %collective-permute-start.22 = (bf16[128,1024]{1,0:T(8,128)(2,1)}, bf16[128,1024]{1,0:T(8,128)(2,1)S(1)}, u32[]{:S(2)}, u32[]{:S(2)}) collective-permute-start(bf16[128,1024]{1,0:T(8,128)(2,1)} %get-tuple-element.130), channel_id=1, source_target_pairs={{0,32},{32,64},{64,96},{96,0},{1,33},{33,65},{65,97},{97,1},{2,34}... | collective-permute-start | bytes 786440 | tf_op jit(solution)/shard_map/ppermute | solution.py:312
  116.8 12.8 %collective-permute-start.23 = (bf16[128,1024]{1,0:T(8,128)(2,1)}, bf16[128,1024]{1,0:T(8,128)(2,1)S(1)}, u32[]{:S(2)}, u32[]{:S(2)}) collective-permute-start(bf16[128,1024]{1,0:T(8,128)(2,1)} %get-tuple-element.131), channel_id=1, source_target_pairs={{0,96},{32,0},{64,32},{96,64},{1,97},{33,1},{65,33},{97,65},{2,98}... | collective-permute-start | bytes 786440 | tf_op jit(solution)/shard_map/ppermute | solution.py:312
  116.8 12.9 %collective-permute-start.24 = (bf16[128,1024]{1,0:T(8,128)(2,1)}, bf16[128,1024]{1,0:T(8,128)(2,1)S(1)}, u32[]{:S(2)}, u32[]{:S(2)}) collective-permute-start(bf16[128,1024]{1,0:T(8,128)(2,1)} %get-tuple-element.132), channel_id=1, source_target_pairs={{0,64},{32,96},{64,0},{96,32},{1,65},{33,97},{65,1},{97,33},{2,66}... | collective-permute-start | bytes 786440 | tf_op jit(solution)/shard_map/ppermute | solution.py:312
  119.0 10.7 %collective-permute-start.25 = (f32[16,2848]{1,0:T(8,128)S(1)}, f32[16,2848]{1,0:T(8,128)S(1)}, u32[]{:S(2)}, u32[]{:S(2)}) collective-permute-start(f32[16,2848]{1,0:T(8,128)S(1)} %add.81), channel_id=1, source_target_pairs={{0,2},{2,0},{4,6},{6,4},{1,3},{3,1},{5,7},{7,5},{8,10},{10,8},{12,... | collective-permute-start | bytes 546824 | tf_op jit(solution)/shard_map/ppermute | solution.py:317
  129.6 4.7 %copy-start.16 = (bf16[128,1024]{1,0:T(8,128)(2,1)}, bf16[128,1024]{1,0:T(8,128)(2,1)S(1)}, u32[]{:S(2)}) copy-start(bf16[128,1024]{1,0:T(8,128)(2,1)S(1)} %collective-permute-done.22.refs_6_) | copy-start | bytes 786436
  129.7 4.7 %copy-start.17 = (bf16[128,1024]{1,0:T(8,128)(2,1)}, bf16[128,1024]{1,0:T(8,128)(2,1)S(1)}, u32[]{:S(2)}) copy-start(bf16[128,1024]{1,0:T(8,128)(2,1)S(1)} %collective-permute-done.23.refs_7_) | copy-start | bytes 786436
  129.7 4.7 %copy-start.18 = (bf16[128,1024]{1,0:T(8,128)(2,1)}, bf16[128,1024]{1,0:T(8,128)(2,1)S(1)}, u32[]{:S(2)}) copy-start(bf16[128,1024]{1,0:T(8,128)(2,1)S(1)} %collective-permute-done.24.refs_8_) | copy-start | bytes 786436
  129.7 11.5 %collective-permute-start.26 = (bf16[128,1024]{1,0:T(8,128)(2,1)}, bf16[128,1024]{1,0:T(8,128)(2,1)S(1)}, u32[]{:S(2)}, u32[]{:S(2)}) collective-permute-start(bf16[128,1024]{1,0:T(8,128)(2,1)} %get-tuple-element.135), channel_id=1, source_target_pairs={{0,32},{32,64},{64,96},{96,0},{1,33},{33,65},{65,97},{97,1},{2,34}... | collective-permute-start | bytes 786440 | tf_op jit(solution)/shard_map/ppermute | solution.py:312
  130.4 10.8 %collective-permute-start.27 = (bf16[128,1024]{1,0:T(8,128)(2,1)}, bf16[128,1024]{1,0:T(8,128)(2,1)S(1)}, u32[]{:S(2)}, u32[]{:S(2)}) collective-permute-start(bf16[128,1024]{1,0:T(8,128)(2,1)} %get-tuple-element.136), channel_id=1, source_target_pairs={{0,96},{32,0},{64,32},{96,64},{1,97},{33,1},{65,33},{97,65},{2,98}... | collective-permute-start | bytes 786440 | tf_op jit(solution)/shard_map/ppermute | solution.py:312
  133.0 8.2 %collective-permute-start.28 = (bf16[128,1024]{1,0:T(8,128)(2,1)}, bf16[128,1024]{1,0:T(8,128)(2,1)S(1)}, u32[]{:S(2)}, u32[]{:S(2)}) collective-permute-start(bf16[128,1024]{1,0:T(8,128)(2,1)} %get-tuple-element.137), channel_id=1, source_target_pairs={{0,64},{32,96},{64,0},{96,32},{1,65},{33,97},{65,1},{97,33},{2,66}... | collective-permute-start | bytes 786440 | tf_op jit(solution)/shard_map/ppermute | solution.py:312
  133.8 7.4 %collective-permute-start.29 = (f32[16,2848]{1,0:T(8,128)S(1)}, f32[16,2848]{1,0:T(8,128)S(1)}, u32[]{:S(2)}, u32[]{:S(2)}) collective-permute-start(f32[16,2848]{1,0:T(8,128)S(1)} %add.82), channel_id=1, source_target_pairs={{0,4},{2,6},{4,0},{6,2},{1,5},{3,7},{5,1},{7,3},{8,12},{10,14},{12... | collective-permute-start | bytes 546824 | tf_op jit(solution)/shard_map/ppermute | solution.py:317
  141.2 0.7 copy-start.19
  141.2 0.9 copy-start.20
  141.2 0.9 copy-start.21
  141.2 9.3 %collective-permute-start.30 = (bf16[64,2944]{1,0:T(8,128)(2,1)}, bf16[64,2944]{1,0:T(8,128)(2,1)S(1)}, u32[]{:S(2)}, u32[]{:S(2)}) collective-permute-start(bf16[64,2944]{1,0:T(8,128)(2,1)} %get-tuple-element.152), channel_id=1, source_target_pairs={{0,16},{16,0},{1,17},{17,1},{2,18},{18,2},{3,19},{19,3},{4,20},{20... | collective-permute-start | bytes 1130504 | tf_op jit(solution)/shard_map/ppermute | solution.py:317
  145.0 5.5 %collective-permute-start.31 = (bf16[64,1024]{1,0:T(8,128)(2,1)}, bf16[64,1024]{1,0:T(8,128)(2,1)S(1)}, u32[]{:S(2)}, u32[]{:S(2)}) collective-permute-start(bf16[64,1024]{1,0:T(8,128)(2,1)} %get-tuple-element.157), channel_id=1, source_target_pairs={{0,16},{16,0},{1,17},{17,1},{2,18},{18,2},{3,19},{19,3},{4,20},{20... | collective-permute-start | bytes 393224 | tf_op jit(solution)/shard_map/ppermute | solution.py:317
  150.5 0.7 copy-start.22
  150.5 0.8 copy-start.15

commit v6 on v5

--- a/solution.py
+++ b/solution.py
@@ -18,7 +18,7 @@
 SMALLEST = 1e-35
 TILE = 512
 KERNEL_BYTES = 58 << 20
-PRETEND = 1
+ESTIMATED_FLOPS = 3000000000
 
 
 def tiles(width):
@@ -156,7 +156,7 @@
         out_shape=[jax.ShapeDtypeStruct((rows, width), jnp.float32)]
         + [jax.ShapeDtypeStruct((rows, padded), jnp.bfloat16)] * 3,
         compiler_params=pltpu.CompilerParams(vmem_limit_bytes=KERNEL_BYTES),
-        cost_estimate=pl.CostEstimate(flops=PRETEND, bytes_accessed=1, transcendentals=0),
+        cost_estimate=pl.CostEstimate(flops=ESTIMATED_FLOPS, bytes_accessed=1, transcendentals=0),
         name="partial",
     )(base, *pieces, wo, wr, uo, ur, down)
 
@@ -236,7 +236,7 @@
         + [jax.ShapeDtypeStruct((rows, padded), jnp.bfloat16)] * 3
         + [jax.ShapeDtypeStruct((4 * rows, 48), jnp.bfloat16)],
         compiler_params=pltpu.CompilerParams(vmem_limit_bytes=KERNEL_BYTES),
-        cost_estimate=pl.CostEstimate(flops=PRETEND, bytes_accessed=1, transcendentals=0),
+        cost_estimate=pl.CostEstimate(flops=ESTIMATED_FLOPS, bytes_accessed=1, transcendentals=0),
         name="partial_half",
     )(base, *pieces, wo, wr, *given, down)
 

time: 155 us -> 153 us (0.987)
    ppermute x18, starting transfers between devices: 32.3 us -> 29.5 us  [ahead(): return lax.ppermute(array, axis, [(i, (i + step) % n) for i in range(n)])]
    ppermute x14, starting transfers between devices: 13.2 us -> 15.8 us  [across(): return lax.ppermute(array, axis, [(i, i ^ bit) for i in range(n)])]
  transfers between devices with their start and end apart: 32 -> 32, of which waited for: 12 -> 11; matrix products, arithmetic and copies ran while one was open for 5% -> 5% of each run, Pallas kernels for 32% -> 32%
where the time goes in v6:
time: 153 us
  Pallas kernels  51.9 us (34%)
  starting transfers between devices  45.3 us (30%)
  waiting for transfers between devices  41 us (27%)
  local copies, waits for them, and re-layouts  7.33 us (5%)
  other arithmetic  4.16 us (3%)
  matrix products  1.86 us (1%)
    ppermute x14, waiting for transfers between devices, across(): return lax.ppermute(array, axis, [(i, i ^ bit) for i in range(n)])  31.5 us
    ppermute x18, starting transfers between devices, ahead(): return lax.ppermute(array, axis, [(i, (i + step) % n) for i in range(n)])  29.5 us
    pallas_call x2, Pallas kernels, partial_half(): pl.pallas_call(functools.partial(half_kernel, which, width, layout, len(p...  22.3 us
    pallas_call x1, Pallas kernels, partial(): pl.pallas_call(functools.partial(partial_kernel, width, layout, len(piece...  18.2 us
    ppermute x14, starting transfers between devices, across(): return lax.ppermute(array, axis, [(i, i ^ bit) for i in range(n)])  15.8 us
    ppermute x18, waiting for transfers between devices, ahead(): return lax.ppermute(array, axis, [(i, (i + step) % n) for i in range(n)])  9.5 us
    pallas_call x2, Pallas kernels, fold(): pl.pallas_call(fold_kernel, in_specs=[pl.BlockSpec(memory_space=pltpu.SME...  8.52 us
  transfers between devices with their start and end apart: 32, of which 11 were waited for; matrix products, arithmetic and copies ran while one was open for 5% of the time, Pallas kernels for 32%

profile of v6, /device:TPU:0, one launch (start us, length us, event | category | flops | bytes accessed | tf_op | source)
XLA Modules:
  0.0 152.7 jit_solution(11507049119671682959)
XLA Ops:
  0.7 1.4 constant_dynamic-slice_fusion.3
  2.0 0.1 collective-permute-start
  2.1 1.5 constant_dynamic-slice_fusion
  3.6 1.0 fusion.4
  4.7 3.2 %collective-permute-start.4 = (bf16[64,3840]{1,0:T(8,128)(2,1)S(1)}, bf16[64,3840]{1,0:T(8,128)(2,1)}, u32[]{:S(2)}, u32[]{:S(2)}) collective-permute-start(bf16[64,3840]{1,0:T(8,128)(2,1)S(1)} %get-tuple-element.168), channel_id=1, source_target_pairs={{0,1},{1,0},{2,3},{3,2},{4,5},{5,4},{6,7},{7,6},{8,9},{9,8},{10,11... | collective-permute-start | bytes 1474568 | tf_op jit(solution)/shard_map/ppermute | solution.py:317
  7.9 3.9 %collective-permute-start.3 = (bf16[64,3840]{1,0:T(8,128)(2,1)S(1)}, bf16[64,3840]{1,0:T(8,128)(2,1)}, u32[]{:S(2)}, u32[]{:S(2)}) collective-permute-start(bf16[64,3840]{1,0:T(8,128)(2,1)S(1)} %get-tuple-element.168), channel_id=1, source_target_pairs={{0,4},{2,6},{4,0},{6,2},{1,5},{3,7},{5,1},{7,3},{8,12},{10,14},{12... | collective-permute-start | bytes 1474568 | tf_op jit(solution)/shard_map/ppermute | solution.py:312
  11.8 0.7 collective-permute-start.2
  12.5 1.3 collective-permute-start.1
  13.8 0.5 collective-permute-start.5
  14.3 0.3 fusion.23
  14.7 1.1 pad_maximum_fusion.refs_0_
  15.9 14.6 %collective-permute-done.5.refs_1_ = bf16[64,3840]{1,0:T(8,128)(2,1)S(1)} collective-permute-done((bf16[64,3840]{1,0:T(8,128)(2,1)S(1)}, bf16[64,3840]{1,0:T(8,128)(2,1)S(1)}, u32[]{:S(2)}, u32[]{:S(2)}) %collective-permute-start.5) | collective-permute-done | bytes 491552 | tf_op jit(solution)/shard_map/ppermute | solution.py:317
  30.5 4.3 %collective-permute-done.2.refs_4_ = bf16[64,3840]{1,0:T(8,128)(2,1)} collective-permute-done((bf16[64,3840]{1,0:T(8,128)(2,1)S(1)}, bf16[64,3840]{1,0:T(8,128)(2,1)}, u32[]{:S(2)}, u32[]{:S(2)}) %collective-permute-start.2) | collective-permute-done | bytes 491552 | tf_op jit(solution)/shard_map/ppermute | solution.py:312
  34.8 0.5 collective-permute-start.10
  35.3 0.9 multiply_bitcast_fusion
  36.2 2.7 %collective-permute-start.7 = (bf16[64,3840]{1,0:T(8,128)(2,1)}, bf16[64,3840]{1,0:T(8,128)(2,1)S(1)}, u32[]{:S(2)}, u32[]{:S(2)}) collective-permute-start(bf16[64,3840]{1,0:T(8,128)(2,1)} %collective-permute-done.4.refs_1_), channel_id=1, source_target_pairs={{0,6},{2,0},{4,2},{6,4},{1,7},{3,1},{5,3},{7,5},{8,14},{10,8},{12,... | collective-permute-start | bytes 1474568 | tf_op jit(solution)/shard_map/ppermute | solution.py:312
  38.9 0.5 collective-permute-start.8
  39.4 1.3 collective-permute-done.10
  40.8 1.6 %collective-permute-start.11 = (f32[32,256]{1,0:T(8,128)S(1)}, f32[32,256]{1,0:T(8,128)S(1)}, u32[]{:S(2)}, u32[]{:S(2)}) collective-permute-start(f32[32,256]{1,0:T(8,128)S(1)} %add.70), channel_id=1, source_target_pairs={{0,32},{32,0},{64,96},{96,64},{1,33},{33,1},{65,97},{97,65},{2,34}... | collective-permute-start | bytes 98312 | tf_op jit(solution)/shard_map/ppermute | solution.py:317
  42.4 0.7 pad_maximum_fusion.3.refs_12_.refs_10_.refs_9_
  43.1 1.6 %collective-permute-done.11 = f32[32,256]{1,0:T(8,128)S(1)} collective-permute-done((f32[32,256]{1,0:T(8,128)S(1)}, f32[32,256]{1,0:T(8,128)S(1)}, u32[]{:S(2)}, u32[]{:S(2)}) %collective-permute-start.11) | collective-permute-done | bytes 32800 | tf_op jit(solution)/shard_map/ppermute | solution.py:317
  44.7 3.2 %collective-permute-start.12 = (f32[32,256]{1,0:T(8,128)S(1)}, f32[32,256]{1,0:T(8,128)S(1)}, u32[]{:S(2)}, u32[]{:S(2)}) collective-permute-start(f32[32,256]{1,0:T(8,128)S(1)} %add.71), channel_id=1, source_target_pairs={{0,64},{32,96},{64,0},{96,32},{1,65},{33,97},{65,1},{97,33},{2,66}... | collective-permute-start | bytes 98312 | tf_op jit(solution)/shard_map/ppermute | solution.py:317
  47.9 1.1 pad_maximum_fusion.1
  49.0 1.2 collective-permute-done.12
  50.1 3.4 %collective-permute-done.8.refs_7_ = bf16[64,3840]{1,0:T(8,128)(2,1)S(1)} collective-permute-done((bf16[64,3840]{1,0:T(8,128)(2,1)}, bf16[64,3840]{1,0:T(8,128)(2,1)S(1)}, u32[]{:S(2)}, u32[]{:S(2)}) %collective-permute-start.8) | collective-permute-done | bytes 491552 | tf_op jit(solution)/shard_map/ppermute | solution.py:317
  53.5 0.8 copy-done.12
  54.3 3.0 %collective-permute-start.14 = (bf16[128,3840]{1,0:T(8,128)(2,1)}, bf16[128,3840]{1,0:T(8,128)(2,1)S(1)}, u32[]{:S(2)}, u32[]{:S(2)}) collective-permute-start(bf16[128,3840]{1,0:T(8,128)(2,1)} %pad_maximum_fusion.1), channel_id=1, source_target_pairs={{0,6},{2,0},{4,2},{6,4},{1,7},{3,1},{5,3},{7,5},{8,14},{10,8},{12,... | collective-permute-start | bytes 2949128 | tf_op jit(solution)/shard_map/ppermute | solution.py:312
  57.3 0.7 collective-permute-start.15
  58.0 18.2 %partial.1 = (f32[128,1856]{1,0:T(8,128)}, bf16[128,1920]{1,0:T(8,128)(2,1)}, bf16[128,1920]{1,0:T(8,128)(2,1)}, bf16[128,1920]{1,0:T(8,128)(2,1)}) custom-call(s32[1]{0:T(128)} %bitcast.base, bf16[128,3840]{1,0:T(8,128)(2,1)} %copy-done.1, bf16[64,3840]{1,0:T(8,128)(2,1)} %collective-permute-done.4.refs_1_, ...), custom_call_target="tpu_custom_call" | custom-call | flops 3000000000 | bytes 1 | tf_op jit(solution)/shard_map/partial/pallas_call | solution.py:135
  76.2 1.1 collective-permute-done.14.refs_3_
  77.3 3.4 %collective-permute-done.13.refs_2_ = bf16[128,3840]{1,0:T(8,128)(2,1)} collective-permute-done((bf16[128,3840]{1,0:T(8,128)(2,1)}, bf16[128,3840]{1,0:T(8,128)(2,1)}, u32[]{:S(2)}, u32[]{:S(2)}) %collective-permute-start.13) | collective-permute-done | bytes 983072 | tf_op jit(solution)/shard_map/ppermute | solution.py:312
  80.7 0.3 fusion.6
  81.0 0.3 fusion.12
  81.4 1.1 slice.51
  82.5 0.3 collective-permute-start.17
  82.7 1.8 %collective-permute-start.16 = (bf16[64,3840]{1,0:T(8,128)(2,1)S(1)}, bf16[64,3840]{1,0:T(8,128)(2,1)S(1)}, u32[]{:S(2)}, u32[]{:S(2)}) collective-permute-start(bf16[64,3840]{1,0:T(8,128)(2,1)S(1)} %slice.51), channel_id=1, source_target_pairs={{0,2},{2,4},{4,6},{6,0},{1,3},{3,5},{5,7},{7,1},{8,10},{10,12},{12... | collective-permute-start | bytes 1474568 | tf_op jit(solution)/shard_map/ppermute | solution.py:312
  84.6 1.6 %collective-permute-start.18 = (bf16[128,1920]{1,0:T(8,128)(2,1)S(1)}, bf16[128,1920]{1,0:T(8,128)(2,1)S(1)}, u32[]{:S(2)}, u32[]{:S(2)}) collective-permute-start(bf16[128,1920]{1,0:T(8,128)(2,1)S(1)} %copy-done.24), channel_id=1, source_target_pairs={{0,32},{32,64},{64,96},{96,0},{1,33},{33,65},{65,97},{97,1},{2,34}... | collective-permute-start | bytes 1474568 | tf_op jit(solution)/shard_map/ppermute | solution.py:312
  86.2 1.7 %collective-permute-start.19 = (bf16[128,1920]{1,0:T(8,128)(2,1)S(1)}, bf16[128,1920]{1,0:T(8,128)(2,1)S(1)}, u32[]{:S(2)}, u32[]{:S(2)}) collective-permute-start(bf16[128,1920]{1,0:T(8,128)(2,1)S(1)} %copy-done.23), channel_id=1, source_target_pairs={{0,96},{32,0},{64,32},{96,64},{1,97},{33,1},{65,33},{97,65},{2,98}... | collective-permute-start | bytes 1474568 | tf_op jit(solution)/shard_map/ppermute | solution.py:312
  87.8 0.1 pad_maximum_fusion.2
  87.9 0.6 collective-permute-start.20
  88.5 6.6 %collective-permute-done.20 = f32[16,2848]{1,0:T(8,128)S(1)} collective-permute-done((f32[16,2848]{1,0:T(8,128)S(1)}, f32[16,2848]{1,0:T(8,128)S(1)}, u32[]{:S(2)}, u32[]{:S(2)}) %collective-permute-start.20) | collective-permute-done | bytes 182304 | tf_op jit(solution)/shard_map/ppermute | solution.py:317
  95.1 0.6 collective-permute-done.18.refs_2_
  95.8 3.7 %collective-permute-start.21 = (bf16[128,1920]{1,0:T(8,128)(2,1)}, bf16[128,1920]{1,0:T(8,128)(2,1)S(1)}, u32[]{:S(2)}, u32[]{:S(2)}) collective-permute-start(bf16[128,1920]{1,0:T(8,128)(2,1)} %get-tuple-element.120), channel_id=1, source_target_pairs={{0,64},{32,96},{64,0},{96,32},{1,65},{33,97},{65,1},{97,33},{2,66}... | collective-permute-start | bytes 1474568 | tf_op jit(solution)/shard_map/ppermute | solution.py:312
  99.5 11.7 %partial_half.2 = (f32[128,928]{1,0:T(8,128)}, bf16[128,1024]{1,0:T(8,128)(2,1)}, bf16[128,1024]{1,0:T(8,128)(2,1)}, bf16[128,1024]{1,0:T(8,128)(2,1)}, bf16[512,48]{1,0:T(8,128)(2,1)}) custom-call(s32[1]{0:T(128)} %bitcast.base, bf16[128,3840]{1,0:T(8,128)(2,1)} %copy-done.1, bf16[64,3840]{1,0:T(8,128)(2,1)} %copy-done.4, ...), custom_call_target="tpu_custom_call" | custom-call | flops 3000000000 | bytes 1 | tf_op jit(solution)/shard_map/partial_half/pallas_call | solution.py:217
  111.3 0.1 collective-permute-start.25
  111.4 0.5 collective-permute-start.22
  111.8 2.9 %collective-permute-start.23 = (bf16[128,1024]{1,0:T(8,128)(2,1)}, bf16[128,1024]{1,0:T(8,128)(2,1)S(1)}, u32[]{:S(2)}, u32[]{:S(2)}) collective-permute-start(bf16[128,1024]{1,0:T(8,128)(2,1)} %get-tuple-element.131), channel_id=1, source_target_pairs={{0,96},{32,0},{64,32},{96,64},{1,97},{33,1},{65,33},{97,65},{2,98}... | collective-permute-start | bytes 786440 | tf_op jit(solution)/shard_map/ppermute | solution.py:312
  114.7 10.6 %partial_half.3 = (f32[128,928]{1,0:T(8,128)}, bf16[128,1024]{1,0:T(8,128)(2,1)}, bf16[128,1024]{1,0:T(8,128)(2,1)}, bf16[128,1024]{1,0:T(8,128)(2,1)}, bf16[512,48]{1,0:T(8,128)(2,1)}) custom-call(s32[1]{0:T(128)} %bitcast.base, bf16[128,3840]{1,0:T(8,128)(2,1)} %copy-done.1, bf16[64,3840]{1,0:T(8,128)(2,1)} %copy-done.4, ...), custom_call_target="tpu_custom_call" | custom-call | flops 3000000000 | bytes 1 | tf_op jit(solution)/shard_map/partial_half/pallas_call | solution.py:217
  125.4 0.9 collective-permute-start.26
  126.3 2.4 %collective-permute-start.27 = (bf16[128,1024]{1,0:T(8,128)(2,1)}, bf16[128,1024]{1,0:T(8,128)(2,1)S(1)}, u32[]{:S(2)}, u32[]{:S(2)}) collective-permute-start(bf16[128,1024]{1,0:T(8,128)(2,1)} %get-tuple-element.136), channel_id=1, source_target_pairs={{0,96},{32,0},{64,32},{96,64},{1,97},{33,1},{65,33},{97,65},{2,98}... | collective-permute-start | bytes 786440 | tf_op jit(solution)/shard_map/ppermute | solution.py:312
  128.7 2.3 %collective-permute-start.28 = (bf16[128,1024]{1,0:T(8,128)(2,1)}, bf16[128,1024]{1,0:T(8,128)(2,1)S(1)}, u32[]{:S(2)}, u32[]{:S(2)}) collective-permute-start(bf16[128,1024]{1,0:T(8,128)(2,1)} %get-tuple-element.137), channel_id=1, source_target_pairs={{0,64},{32,96},{64,0},{96,32},{1,65},{33,97},{65,1},{97,33},{2,66}... | collective-permute-start | bytes 786440 | tf_op jit(solution)/shard_map/ppermute | solution.py:312
  131.0 3.1 %collective-permute-start.29 = (f32[16,2848]{1,0:T(8,128)S(1)}, f32[16,2848]{1,0:T(8,128)S(1)}, u32[]{:S(2)}, u32[]{:S(2)}) collective-permute-start(f32[16,2848]{1,0:T(8,128)S(1)} %add.82), channel_id=1, source_target_pairs={{0,4},{2,6},{4,0},{6,2},{1,5},{3,7},{5,1},{7,3},{8,12},{10,14},{12... | collective-permute-start | bytes 546824 | tf_op jit(solution)/shard_map/ppermute | solution.py:317
  134.1 5.6 %fold.2 = (f32[64,1856]{1,0:T(8,128)}, f32[64,928]{1,0:T(8,128)}, bf16[64,2944]{1,0:T(8,128)(2,1)}) custom-call(s32[1]{0:T(128)} %bitcast.2.refs_0_, f32[128,1856]{1,0:T(8,128)} %get-tuple-element.138.refs_1_, bf16[128,1920]{1,0:T(8,128)(2,1)} %copy-done.9, bf16[128,1920]{1,0:T(8,128)(2,1)} %copy-done.10, bf16[128,1920]{1,0:T(8,128)(2,1)} %copy-done.11, ...), custom_call_target="tpu_custom_call" | custom-call | flops 1 | bytes 1 | tf_op jit(solution)/shard_map/fold/pallas_call | solution.py:270
  139.8 0.6 collective-permute-start.30
  140.4 0.1 copy-done.20
  140.6 0.1 copy-done.21
  140.6 2.9 %fold.3 = (f32[64,928]{1,0:T(8,128)}, bf16[64,1024]{1,0:T(8,128)(2,1)}) custom-call(s32[1]{0:T(128)} %bitcast.2.refs_0_, f32[128,928]{1,0:T(8,128)} %get-tuple-element.153.refs_1_, bf16[128,1024]{1,0:T(8,128)(2,1)} %copy-done.19, bf16[128,1024]{1,0:T(8,128)(2,1)} %copy-done.20, bf16[128,1024]{1,0:T(8,128)(2,1)} %copy-done.21), custom_call_target="tpu_custom_call" | custom-call | flops 1 | bytes 1 | tf_op jit(solution)/shard_map/fold/pallas_call | solution.py:270
  143.6 1.2 collective-permute-start.31
  144.8 0.7 slice.76
  145.6 0.6 slice_bitcast_fusion
  146.2 2.9 %collective-permute-done.31.got2 = bf16[64,1024]{1,0:T(8,128)(2,1)S(1)} collective-permute-done((bf16[64,1024]{1,0:T(8,128)(2,1)}, bf16[64,1024]{1,0:T(8,128)(2,1)S(1)}, u32[]{:S(2)}, u32[]{:S(2)}) %collective-permute-start.31) | collective-permute-done | bytes 131104 | tf_op jit(solution)/shard_map/ppermute | solution.py:317
  149.1 0.6 copy-done.22
  149.7 0.2 copy-done.15
  149.9 2.8 %finish.1 = bf16[1856,128]{1,0:T(8,128)(2,1)} custom-call(f32[64,1856]{1,0:T(8,128)} %get-tuple-element.150.keep0, f32[64,928]{1,0:T(8,128)} %get-tuple-element.151.keep1, bf16[64,2944]{1,0:T(8,128)(2,1)} %copy-done.15, f32[64,928]{1,0:T(8,128)} %get-tuple-element.161.keep2, bf16[64,1024]{1,0:T(8,128)(2,1)} %copy-done.22), custom_call_target="tpu_custom_call" | custom-call | tf_op jit(solution)/shard_map/finish/pallas_call | solution.py:300
  (84 shorter events, 0.6 us)
Async XLA Ops:
  0.6 3.0 %copy-start = (bf16[256,928]{0,1:T(8,128)(2,1)S(1)}, bf16[256,928]{0,1:T(8,128)(2,1)}, u32[]{:S(2)}) copy-start(bf16[256,928]{0,1:T(8,128)(2,1)} %param.5) | copy-start | bytes 1425412
  0.7 13.7 %copy-start.2 = (bf16[256,1920]{1,0:T(8,128)(2,1)S(1)}, bf16[256,1920]{1,0:T(8,128)(2,1)}, u32[]{:S(2)}) copy-start(bf16[256,1920]{1,0:T(8,128)(2,1)} %param.6) | copy-start | bytes 2949124
  2.0 2.6 %collective-permute-start = (bf16[128,1920]{1,0:T(8,128)(2,1)S(1)}, bf16[128,1920]{1,0:T(8,128)(2,1)S(1)}, u32[]{:S(2)}, u32[]{:S(2)}) collective-permute-start(bf16[128,1920]{1,0:T(8,128)(2,1)S(1)} %get-tuple-element.170), channel_id=1, source_target_pairs={{0,8},{8,0},{1,9},{9,1},{2,10},{10,2},{3,11},{11,3},{4,12},{12,4},... | collective-permute-start | bytes 1474568 | tf_op jit(solution)/shard_map/ppermute | solution.py:317
  3.6 12.2 %copy-start.8 = (bf16[16,1920]{1,0:T(8,128)(2,1)}, bf16[16,1920]{1,0:T(8,128)(2,1)S(1)}, u32[]{:S(2)}) copy-start(bf16[16,1920]{1,0:T(8,128)(2,1)S(1)} %get-tuple-element.166.refs_10_.refs_8_) | copy-start | bytes 184324
  4.6 10.0 %copy-start.5 = (bf16[128,1920]{1,0:T(8,128)(2,1)}, bf16[128,1920]{1,0:T(8,128)(2,1)S(1)}, u32[]{:S(2)}) copy-start(bf16[128,1920]{1,0:T(8,128)(2,1)S(1)} %collective-permute-done) | copy-start | bytes 1474564
  4.7 25.7 %collective-permute-start.4 = (bf16[64,3840]{1,0:T(8,128)(2,1)S(1)}, bf16[64,3840]{1,0:T(8,128)(2,1)}, u32[]{:S(2)}, u32[]{:S(2)}) collective-permute-start(bf16[64,3840]{1,0:T(8,128)(2,1)S(1)} %get-tuple-element.168), channel_id=1, source_target_pairs={{0,1},{1,0},{2,3},{3,2},{4,5},{5,4},{6,7},{7,6},{8,9},{9,8},{10,11... | collective-permute-start | bytes 1474568 | tf_op jit(solution)/shard_map/ppermute | solution.py:317
  7.9 22.5 %collective-permute-start.3 = (bf16[64,3840]{1,0:T(8,128)(2,1)S(1)}, bf16[64,3840]{1,0:T(8,128)(2,1)}, u32[]{:S(2)}, u32[]{:S(2)}) collective-permute-start(bf16[64,3840]{1,0:T(8,128)(2,1)S(1)} %get-tuple-element.168), channel_id=1, source_target_pairs={{0,4},{2,6},{4,0},{6,2},{1,5},{3,7},{5,1},{7,3},{8,12},{10,14},{12... | collective-permute-start | bytes 1474568 | tf_op jit(solution)/shard_map/ppermute | solution.py:312
  11.8 23.0 %collective-permute-start.2 = (bf16[64,3840]{1,0:T(8,128)(2,1)S(1)}, bf16[64,3840]{1,0:T(8,128)(2,1)}, u32[]{:S(2)}, u32[]{:S(2)}) collective-permute-start(bf16[64,3840]{1,0:T(8,128)(2,1)S(1)} %get-tuple-element.168), channel_id=1, source_target_pairs={{0,6},{2,0},{4,2},{6,4},{1,7},{3,1},{5,3},{7,5},{8,14},{10,8},{12,... | collective-permute-start | bytes 1474568 | tf_op jit(solution)/shard_map/ppermute | solution.py:312
  12.5 22.3 %collective-permute-start.1 = (bf16[64,3840]{1,0:T(8,128)(2,1)S(1)}, bf16[64,3840]{1,0:T(8,128)(2,1)}, u32[]{:S(2)}, u32[]{:S(2)}) collective-permute-start(bf16[64,3840]{1,0:T(8,128)(2,1)S(1)} %get-tuple-element.168), channel_id=1, source_target_pairs={{0,2},{2,4},{4,6},{6,0},{1,3},{3,5},{5,7},{7,1},{8,10},{10,12},{12... | collective-permute-start | bytes 1474568 | tf_op jit(solution)/shard_map/ppermute | solution.py:312
  13.8 16.6 %collective-permute-start.5 = (bf16[64,3840]{1,0:T(8,128)(2,1)S(1)}, bf16[64,3840]{1,0:T(8,128)(2,1)S(1)}, u32[]{:S(2)}, u32[]{:S(2)}) collective-permute-start(bf16[64,3840]{1,0:T(8,128)(2,1)S(1)} %get-tuple-element.167), channel_id=1, source_target_pairs={{0,1},{1,0},{2,3},{3,2},{4,5},{5,4},{6,7},{7,6},{8,9},{9,8},{10,11... | collective-permute-start | bytes 1474568 | tf_op jit(solution)/shard_map/ppermute | solution.py:317
  15.9 42.1 %copy-start.1 = (bf16[128,3840]{1,0:T(8,128)(2,1)}, bf16[128,3840]{1,0:T(8,128)(2,1)S(1)}, u32[]{:S(2)}) copy-start(bf16[128,3840]{1,0:T(8,128)(2,1)S(1)} %pad_maximum_fusion.refs_0_) | copy-start | bytes 2949124
  30.5 23.1 %copy-start.4 = (bf16[64,3840]{1,0:T(8,128)(2,1)}, bf16[64,3840]{1,0:T(8,128)(2,1)S(1)}, u32[]{:S(2)}) copy-start(bf16[64,3840]{1,0:T(8,128)(2,1)S(1)} %collective-permute-done.5.refs_1_) | copy-start | bytes 1474564
  34.8 18.7 %collective-permute-start.9 = (bf16[1856,1920]{1,0:T(8,128)(2,1)}, bf16[1856,1920]{1,0:T(8,128)(2,1)}, u32[]{:S(2)}, u32[]{:S(2)}) collective-permute-start(bf16[1856,1920]{1,0:T(8,128)(2,1)} %refs_6_.1), channel_id=1, source_target_pairs={{0,8},{8,0},{1,9},{9,1},{2,10},{10,2},{3,11},{11,3},{4,12},{12,4},... | collective-permute-start | bytes 21381128 | tf_op jit(solution)/shard_map/ppermute | solution.py:317
  34.8 6.0 %collective-permute-start.10 = (f32[32,256]{1,0:T(8,128)S(1)}, f32[32,256]{1,0:T(8,128)S(1)}, u32[]{:S(2)}, u32[]{:S(2)}) collective-permute-start(f32[32,256]{1,0:T(8,128)S(1)} %pad_maximum_fusion.4), channel_id=1, source_target_pairs={{0,8},{8,0},{1,9},{9,1},{2,10},{10,2},{3,11},{11,3},{4,12},{12,4},... | collective-permute-start | bytes 98312 | tf_op jit(solution)/shard_map/ppermute | solution.py:317
  36.2 17.2 %collective-permute-start.7 = (bf16[64,3840]{1,0:T(8,128)(2,1)}, bf16[64,3840]{1,0:T(8,128)(2,1)S(1)}, u32[]{:S(2)}, u32[]{:S(2)}) collective-permute-start(bf16[64,3840]{1,0:T(8,128)(2,1)} %collective-permute-done.4.refs_1_), channel_id=1, source_target_pairs={{0,6},{2,0},{4,2},{6,4},{1,7},{3,1},{5,3},{7,5},{8,14},{10,8},{12,... | collective-permute-start | bytes 1474568 | tf_op jit(solution)/shard_map/ppermute | solution.py:312
  38.9 14.6 %collective-permute-start.6 = (bf16[64,3840]{1,0:T(8,128)(2,1)}, bf16[64,3840]{1,0:T(8,128)(2,1)S(1)}, u32[]{:S(2)}, u32[]{:S(2)}) collective-permute-start(bf16[64,3840]{1,0:T(8,128)(2,1)} %collective-permute-done.4.refs_1_), channel_id=1, source_target_pairs={{0,2},{2,4},{4,6},{6,0},{1,3},{3,5},{5,7},{7,1},{8,10},{10,12},{12... | collective-permute-start | bytes 1474568 | tf_op jit(solution)/shard_map/ppermute | solution.py:312
  38.9 14.6 %collective-permute-start.8 = (bf16[64,3840]{1,0:T(8,128)(2,1)}, bf16[64,3840]{1,0:T(8,128)(2,1)S(1)}, u32[]{:S(2)}, u32[]{:S(2)}) collective-permute-start(bf16[64,3840]{1,0:T(8,128)(2,1)} %collective-permute-done.3.refs_6_), channel_id=1, source_target_pairs={{0,1},{1,0},{2,3},{3,2},{4,5},{5,4},{6,7},{7,6},{8,9},{9,8},{10,11... | collective-permute-start | bytes 1474568 | tf_op jit(solution)/shard_map/ppermute | solution.py:317
  40.8 3.9 %collective-permute-start.11 = (f32[32,256]{1,0:T(8,128)S(1)}, f32[32,256]{1,0:T(8,128)S(1)}, u32[]{:S(2)}, u32[]{:S(2)}) collective-permute-start(f32[32,256]{1,0:T(8,128)S(1)} %add.70), channel_id=1, source_target_pairs={{0,32},{32,0},{64,96},{96,64},{1,33},{33,1},{65,97},{97,65},{2,34}... | collective-permute-start | bytes 98312 | tf_op jit(solution)/shard_map/ppermute | solution.py:317
  44.7 5.4 %collective-permute-start.12 = (f32[32,256]{1,0:T(8,128)S(1)}, f32[32,256]{1,0:T(8,128)S(1)}, u32[]{:S(2)}, u32[]{:S(2)}) collective-permute-start(f32[32,256]{1,0:T(8,128)S(1)} %add.71), channel_id=1, source_target_pairs={{0,64},{32,96},{64,0},{96,32},{1,65},{33,97},{65,1},{97,33},{2,66}... | collective-permute-start | bytes 98312 | tf_op jit(solution)/shard_map/ppermute | solution.py:317
  53.5 3.8 %copy-start.14 = (bf16[64,3840]{1,0:T(8,128)(2,1)}, bf16[64,3840]{1,0:T(8,128)(2,1)S(1)}, u32[]{:S(2)}) copy-start(bf16[64,3840]{1,0:T(8,128)(2,1)S(1)} %collective-permute-done.8.refs_7_) | copy-start | bytes 1474564
  53.5 0.8 copy-start.12
  53.5 3.8 %copy-start.13 = (bf16[64,3840]{1,0:T(8,128)(2,1)}, bf16[64,3840]{1,0:T(8,128)(2,1)S(1)}, u32[]{:S(2)}) copy-start(bf16[64,3840]{1,0:T(8,128)(2,1)S(1)} %collective-permute-done.6.refs_3_) | copy-start | bytes 1474564
  54.3 23.0 %collective-permute-start.14 = (bf16[128,3840]{1,0:T(8,128)(2,1)}, bf16[128,3840]{1,0:T(8,128)(2,1)S(1)}, u32[]{:S(2)}, u32[]{:S(2)}) collective-permute-start(bf16[128,3840]{1,0:T(8,128)(2,1)} %pad_maximum_fusion.1), channel_id=1, source_target_pairs={{0,6},{2,0},{4,2},{6,4},{1,7},{3,1},{5,3},{7,5},{8,14},{10,8},{12,... | collective-permute-start | bytes 2949128 | tf_op jit(solution)/shard_map/ppermute | solution.py:312
  57.3 23.4 %collective-permute-start.13 = (bf16[128,3840]{1,0:T(8,128)(2,1)}, bf16[128,3840]{1,0:T(8,128)(2,1)}, u32[]{:S(2)}, u32[]{:S(2)}) collective-permute-start(bf16[128,3840]{1,0:T(8,128)(2,1)} %pad_maximum_fusion.1), channel_id=1, source_target_pairs={{0,2},{2,4},{4,6},{6,0},{1,3},{3,5},{5,7},{7,1},{8,10},{10,12},{12... | collective-permute-start | bytes 2949128 | tf_op jit(solution)/shard_map/ppermute | solution.py:312
  57.3 18.9 %collective-permute-start.15 = (f32[32,256]{1,0:T(8,128)S(1)}, f32[32,256]{1,0:T(8,128)S(1)}, u32[]{:S(2)}, u32[]{:S(2)}) collective-permute-start(f32[32,256]{1,0:T(8,128)S(1)} %add.75), channel_id=1, source_target_pairs={{0,16},{16,0},{1,17},{17,1},{2,18},{18,2},{3,19},{19,3},{4,20},{20... | collective-permute-start | bytes 98312 | tf_op jit(solution)/shard_map/ppermute | solution.py:317
  77.3 5.1 %copy-start.3 = (bf16[128,3840]{1,0:T(8,128)(2,1)}, bf16[128,3840]{1,0:T(8,128)(2,1)S(1)}, u32[]{:S(2)}) copy-start(bf16[128,3840]{1,0:T(8,128)(2,1)S(1)} %collective-permute-done.14.refs_3_) | copy-start | bytes 2949124
  81.0 3.6 %copy-start.24 = (bf16[128,1920]{1,0:T(8,128)(2,1)S(1)}, bf16[128,1920]{1,0:T(8,128)(2,1)}, u32[]{:S(2)}) copy-start(bf16[128,1920]{1,0:T(8,128)(2,1)} %get-tuple-element.109) | copy-start | bytes 1474564
  81.0 5.1 %copy-start.23 = (bf16[128,1920]{1,0:T(8,128)(2,1)S(1)}, bf16[128,1920]{1,0:T(8,128)(2,1)}, u32[]{:S(2)}) copy-start(bf16[128,1920]{1,0:T(8,128)(2,1)} %get-tuple-element.110) | copy-start | bytes 1474564
  82.5 12.6 %collective-permute-start.17 = (bf16[64,3840]{1,0:T(8,128)(2,1)S(1)}, bf16[64,3840]{1,0:T(8,128)(2,1)S(1)}, u32[]{:S(2)}, u32[]{:S(2)}) collective-permute-start(bf16[64,3840]{1,0:T(8,128)(2,1)S(1)} %slice.52), channel_id=1, source_target_pairs={{0,6},{2,0},{4,2},{6,4},{1,7},{3,1},{5,3},{7,5},{8,14},{10,8},{12,... | collective-permute-start | bytes 1474568 | tf_op jit(solution)/shard_map/ppermute | solution.py:312
  82.7 12.4 %collective-permute-start.16 = (bf16[64,3840]{1,0:T(8,128)(2,1)S(1)}, bf16[64,3840]{1,0:T(8,128)(2,1)S(1)}, u32[]{:S(2)}, u32[]{:S(2)}) collective-permute-start(bf16[64,3840]{1,0:T(8,128)(2,1)S(1)} %slice.51), channel_id=1, source_target_pairs={{0,2},{2,4},{4,6},{6,0},{1,3},{3,5},{5,7},{7,1},{8,10},{10,12},{12... | collective-permute-start | bytes 1474568 | tf_op jit(solution)/shard_map/ppermute | solution.py:312
  84.6 11.2 %collective-permute-start.18 = (bf16[128,1920]{1,0:T(8,128)(2,1)S(1)}, bf16[128,1920]{1,0:T(8,128)(2,1)S(1)}, u32[]{:S(2)}, u32[]{:S(2)}) collective-permute-start(bf16[128,1920]{1,0:T(8,128)(2,1)S(1)} %copy-done.24), channel_id=1, source_target_pairs={{0,32},{32,64},{64,96},{96,0},{1,33},{33,65},{65,97},{97,1},{2,34}... | collective-permute-start | bytes 1474568 | tf_op jit(solution)/shard_map/ppermute | solution.py:312
  86.2 9.6 %collective-permute-start.19 = (bf16[128,1920]{1,0:T(8,128)(2,1)S(1)}, bf16[128,1920]{1,0:T(8,128)(2,1)S(1)}, u32[]{:S(2)}, u32[]{:S(2)}) collective-permute-start(bf16[128,1920]{1,0:T(8,128)(2,1)S(1)} %copy-done.23), channel_id=1, source_target_pairs={{0,96},{32,0},{64,32},{96,64},{1,97},{33,1},{65,33},{97,65},{2,98}... | collective-permute-start | bytes 1474568 | tf_op jit(solution)/shard_map/ppermute | solution.py:312
  87.9 7.2 %collective-permute-start.20 = (f32[16,2848]{1,0:T(8,128)S(1)}, f32[16,2848]{1,0:T(8,128)S(1)}, u32[]{:S(2)}, u32[]{:S(2)}) collective-permute-start(f32[16,2848]{1,0:T(8,128)S(1)} %pad_maximum_fusion.2), channel_id=1, source_target_pairs={{0,1},{1,0},{2,3},{3,2},{4,5},{5,4},{6,7},{7,6},{8,9},{9,8},{10,11... | collective-permute-start | bytes 546824 | tf_op jit(solution)/shard_map/ppermute | solution.py:317
  95.1 4.4 %copy-start.6 = (bf16[64,3840]{1,0:T(8,128)(2,1)}, bf16[64,3840]{1,0:T(8,128)(2,1)S(1)}, u32[]{:S(2)}) copy-start(bf16[64,3840]{1,0:T(8,128)(2,1)S(1)} %collective-permute-done.17.refs_5_) | copy-start | bytes 1474564
  95.1 4.4 %copy-start.7 = (bf16[64,3840]{1,0:T(8,128)(2,1)}, bf16[64,3840]{1,0:T(8,128)(2,1)S(1)}, u32[]{:S(2)}) copy-start(bf16[64,3840]{1,0:T(8,128)(2,1)S(1)} %collective-permute-done.16.refs_4_) | copy-start | bytes 1474564
  95.7 15.5 %copy-start.9 = (bf16[128,1920]{1,0:T(8,128)(2,1)}, bf16[128,1920]{1,0:T(8,128)(2,1)S(1)}, u32[]{:S(2)}) copy-start(bf16[128,1920]{1,0:T(8,128)(2,1)S(1)} %collective-permute-done.18.refs_2_) | copy-start | bytes 1474564
  95.8 15.5 %copy-start.10 = (bf16[128,1920]{1,0:T(8,128)(2,1)}, bf16[128,1920]{1,0:T(8,128)(2,1)S(1)}, u32[]{:S(2)}) copy-start(bf16[128,1920]{1,0:T(8,128)(2,1)S(1)} %collective-permute-done.19.refs_3_) | copy-start | bytes 1474564
  95.8 15.5 %collective-permute-start.21 = (bf16[128,1920]{1,0:T(8,128)(2,1)}, bf16[128,1920]{1,0:T(8,128)(2,1)S(1)}, u32[]{:S(2)}, u32[]{:S(2)}) collective-permute-start(bf16[128,1920]{1,0:T(8,128)(2,1)} %get-tuple-element.120), channel_id=1, source_target_pairs={{0,64},{32,96},{64,0},{96,32},{1,65},{33,97},{65,1},{97,33},{2,66}... | collective-permute-start | bytes 1474568 | tf_op jit(solution)/shard_map/ppermute | solution.py:312
  111.2 14.0 %copy-start.11 = (bf16[128,1920]{1,0:T(8,128)(2,1)}, bf16[128,1920]{1,0:T(8,128)(2,1)S(1)}, u32[]{:S(2)}) copy-start(bf16[128,1920]{1,0:T(8,128)(2,1)S(1)} %collective-permute-done.21.refs_4_) | copy-start | bytes 1474564
  111.3 14.0 %collective-permute-start.25 = (f32[16,2848]{1,0:T(8,128)S(1)}, f32[16,2848]{1,0:T(8,128)S(1)}, u32[]{:S(2)}, u32[]{:S(2)}) collective-permute-start(f32[16,2848]{1,0:T(8,128)S(1)} %add.81), channel_id=1, source_target_pairs={{0,2},{2,0},{4,6},{6,4},{1,3},{3,1},{5,7},{7,5},{8,10},{10,8},{12,... | collective-permute-start | bytes 546824 | tf_op jit(solution)/shard_map/ppermute | solution.py:317
  111.4 14.0 %collective-permute-start.22 = (bf16[128,1024]{1,0:T(8,128)(2,1)}, bf16[128,1024]{1,0:T(8,128)(2,1)S(1)}, u32[]{:S(2)}, u32[]{:S(2)}) collective-permute-start(bf16[128,1024]{1,0:T(8,128)(2,1)} %get-tuple-element.130), channel_id=1, source_target_pairs={{0,32},{32,64},{64,96},{96,0},{1,33},{33,65},{65,97},{97,1},{2,34}... | collective-permute-start | bytes 786440 | tf_op jit(solution)/shard_map/ppermute | solution.py:312
  111.8 13.5 %collective-permute-start.23 = (bf16[128,1024]{1,0:T(8,128)(2,1)}, bf16[128,1024]{1,0:T(8,128)(2,1)S(1)}, u32[]{:S(2)}, u32[]{:S(2)}) collective-permute-start(bf16[128,1024]{1,0:T(8,128)(2,1)} %get-tuple-element.131), channel_id=1, source_target_pairs={{0,96},{32,0},{64,32},{96,64},{1,97},{33,1},{65,33},{97,65},{2,98}... | collective-permute-start | bytes 786440 | tf_op jit(solution)/shard_map/ppermute | solution.py:312
  114.7 10.7 %collective-permute-start.24 = (bf16[128,1024]{1,0:T(8,128)(2,1)}, bf16[128,1024]{1,0:T(8,128)(2,1)S(1)}, u32[]{:S(2)}, u32[]{:S(2)}) collective-permute-start(bf16[128,1024]{1,0:T(8,128)(2,1)} %get-tuple-element.132), channel_id=1, source_target_pairs={{0,64},{32,96},{64,0},{96,32},{1,65},{33,97},{65,1},{97,33},{2,66}... | collective-permute-start | bytes 786440 | tf_op jit(solution)/shard_map/ppermute | solution.py:312
  125.3 8.8 %copy-start.16 = (bf16[128,1024]{1,0:T(8,128)(2,1)}, bf16[128,1024]{1,0:T(8,128)(2,1)S(1)}, u32[]{:S(2)}) copy-start(bf16[128,1024]{1,0:T(8,128)(2,1)S(1)} %collective-permute-done.22.refs_6_) | copy-start | bytes 786436
  125.3 8.8 %copy-start.17 = (bf16[128,1024]{1,0:T(8,128)(2,1)}, bf16[128,1024]{1,0:T(8,128)(2,1)S(1)}, u32[]{:S(2)}) copy-start(bf16[128,1024]{1,0:T(8,128)(2,1)S(1)} %collective-permute-done.23.refs_7_) | copy-start | bytes 786436
  125.4 8.7 %copy-start.18 = (bf16[128,1024]{1,0:T(8,128)(2,1)}, bf16[128,1024]{1,0:T(8,128)(2,1)S(1)}, u32[]{:S(2)}) copy-start(bf16[128,1024]{1,0:T(8,128)(2,1)S(1)} %collective-permute-done.24.refs_8_) | copy-start | bytes 786436
  125.4 14.3 %collective-permute-start.26 = (bf16[128,1024]{1,0:T(8,128)(2,1)}, bf16[128,1024]{1,0:T(8,128)(2,1)S(1)}, u32[]{:S(2)}, u32[]{:S(2)}) collective-permute-start(bf16[128,1024]{1,0:T(8,128)(2,1)} %get-tuple-element.135), channel_id=1, source_target_pairs={{0,32},{32,64},{64,96},{96,0},{1,33},{33,65},{65,97},{97,1},{2,34}... | collective-permute-start | bytes 786440 | tf_op jit(solution)/shard_map/ppermute | solution.py:312
  126.3 13.4 %collective-permute-start.27 = (bf16[128,1024]{1,0:T(8,128)(2,1)}, bf16[128,1024]{1,0:T(8,128)(2,1)S(1)}, u32[]{:S(2)}, u32[]{:S(2)}) collective-permute-start(bf16[128,1024]{1,0:T(8,128)(2,1)} %get-tuple-element.136), channel_id=1, source_target_pairs={{0,96},{32,0},{64,32},{96,64},{1,97},{33,1},{65,33},{97,65},{2,98}... | collective-permute-start | bytes 786440 | tf_op jit(solution)/shard_map/ppermute | solution.py:312
  128.7 11.1 %collective-permute-start.28 = (bf16[128,1024]{1,0:T(8,128)(2,1)}, bf16[128,1024]{1,0:T(8,128)(2,1)S(1)}, u32[]{:S(2)}, u32[]{:S(2)}) collective-permute-start(bf16[128,1024]{1,0:T(8,128)(2,1)} %get-tuple-element.137), channel_id=1, source_target_pairs={{0,64},{32,96},{64,0},{96,32},{1,65},{33,97},{65,1},{97,33},{2,66}... | collective-permute-start | bytes 786440 | tf_op jit(solution)/shard_map/ppermute | solution.py:312
  131.0 8.7 %collective-permute-start.29 = (f32[16,2848]{1,0:T(8,128)S(1)}, f32[16,2848]{1,0:T(8,128)S(1)}, u32[]{:S(2)}, u32[]{:S(2)}) collective-permute-start(f32[16,2848]{1,0:T(8,128)S(1)} %add.82), channel_id=1, source_target_pairs={{0,4},{2,6},{4,0},{6,2},{1,5},{3,7},{5,1},{7,3},{8,12},{10,14},{12... | collective-permute-start | bytes 546824 | tf_op jit(solution)/shard_map/ppermute | solution.py:317
  139.7 0.7 copy-start.19
  139.7 0.8 copy-start.20
  139.8 0.9 copy-start.21
  139.8 9.3 %collective-permute-start.30 = (bf16[64,2944]{1,0:T(8,128)(2,1)}, bf16[64,2944]{1,0:T(8,128)(2,1)S(1)}, u32[]{:S(2)}, u32[]{:S(2)}) collective-permute-start(bf16[64,2944]{1,0:T(8,128)(2,1)} %get-tuple-element.152), channel_id=1, source_target_pairs={{0,16},{16,0},{1,17},{17,1},{2,18},{18,2},{3,19},{19,3},{4,20},{20... | collective-permute-start | bytes 1130504 | tf_op jit(solution)/shard_map/ppermute | solution.py:317
  143.6 5.5 %collective-permute-start.31 = (bf16[64,1024]{1,0:T(8,128)(2,1)}, bf16[64,1024]{1,0:T(8,128)(2,1)S(1)}, u32[]{:S(2)}, u32[]{:S(2)}) collective-permute-start(bf16[64,1024]{1,0:T(8,128)(2,1)} %get-tuple-element.157), channel_id=1, source_target_pairs={{0,16},{16,0},{1,17},{17,1},{2,18},{18,2},{3,19},{19,3},{4,20},{20... | collective-permute-start | bytes 393224 | tf_op jit(solution)/shard_map/ppermute | solution.py:317
  149.1 0.7 copy-start.22
  149.1 0.8 copy-start.15

commit v7 on v6

--- a/solution.py
+++ b/solution.py
@@ -272,7 +272,7 @@
         in_specs=[pl.BlockSpec(memory_space=pltpu.SMEM)] + [vmem] * (4 * len(groups)),
         out_specs=[vmem] * len(out_shape),
         out_shape=out_shape,
-        cost_estimate=pl.CostEstimate(flops=1, bytes_accessed=1, transcendentals=0),
+        cost_estimate=pl.CostEstimate(flops=2000000000, bytes_accessed=1, transcendentals=0),
         name="fold",
     )(swap, *(array for group in groups for array in group))
 

time: 153 us -> 155 us (1.013)
    ppermute x18, starting transfers between devices: 29.5 us -> 32.3 us  [ahead(): return lax.ppermute(array, axis, [(i, (i + step) % n) for i in range(n)])]
    ppermute x14, starting transfers between devices: 15.8 us -> 13.3 us  [across(): return lax.ppermute(array, axis, [(i, i ^ bit) for i in range(n)])]
  transfers between devices with their start and end apart: 32 -> 32, of which waited for: 11 -> 12; matrix products, arithmetic and copies ran while one was open for 5% -> 5% of each run, Pallas kernels for 32% -> 32%
where the time goes in v7:
time: 155 us; the launch traced here: 154 us
  Pallas kernels  51.9 us (33%)
  starting transfers between devices  45.6 us (29%)
  waiting for transfers between devices  42.3 us (27%)
  local copies, waits for them, and re-layouts  7.39 us (5%)
  other arithmetic  4.14 us (3%)
  matrix products  1.86 us (1%)
    ppermute x14, waiting for transfers between devices, across(): return lax.ppermute(array, axis, [(i, i ^ bit) for i in range(n)])  32.8 us
    ppermute x18, starting transfers between devices, ahead(): return lax.ppermute(array, axis, [(i, (i + step) % n) for i in range(n)])  32.3 us
    pallas_call x2, Pallas kernels, partial_half(): pl.pallas_call(functools.partial(half_kernel, which, width, layout, len(p...  22.3 us
    pallas_call x1, Pallas kernels, partial(): pl.pallas_call(functools.partial(partial_kernel, width, layout, len(piece...  18.2 us
    ppermute x14, starting transfers between devices, across(): return lax.ppermute(array, axis, [(i, i ^ bit) for i in range(n)])  13.3 us
    ppermute x18, waiting for transfers between devices, ahead(): return lax.ppermute(array, axis, [(i, (i + step) % n) for i in range(n)])  9.49 us
    pallas_call x2, Pallas kernels, fold(): pl.pallas_call(fold_kernel, in_specs=[pl.BlockSpec(memory_space=pltpu.SME...  8.52 us
  transfers between devices with their start and end apart: 32, of which 12 were waited for; matrix products, arithmetic and copies ran while one was open for 5% of the time, Pallas kernels for 32%

profile of v7, /device:TPU:0, one launch (start us, length us, event | category | flops | bytes accessed | tf_op | source)
XLA Modules:
  0.0 154.3 jit_solution(18278235751424392281)
XLA Ops:
  0.7 1.4 constant_dynamic-slice_fusion.3
  2.0 0.1 collective-permute-start
  2.1 1.5 constant_dynamic-slice_fusion
  3.6 1.0 fusion.4
  4.7 3.2 %collective-permute-start.4 = (bf16[64,3840]{1,0:T(8,128)(2,1)S(1)}, bf16[64,3840]{1,0:T(8,128)(2,1)}, u32[]{:S(2)}, u32[]{:S(2)}) collective-permute-start(bf16[64,3840]{1,0:T(8,128)(2,1)S(1)} %get-tuple-element.168), channel_id=1, source_target_pairs={{0,1},{1,0},{2,3},{3,2},{4,5},{5,4},{6,7},{7,6},{8,9},{9,8},{10,11... | collective-permute-start | bytes 1474568 | tf_op jit(solution)/shard_map/ppermute | solution.py:317
  7.9 3.9 %collective-permute-start.3 = (bf16[64,3840]{1,0:T(8,128)(2,1)S(1)}, bf16[64,3840]{1,0:T(8,128)(2,1)}, u32[]{:S(2)}, u32[]{:S(2)}) collective-permute-start(bf16[64,3840]{1,0:T(8,128)(2,1)S(1)} %get-tuple-element.168), channel_id=1, source_target_pairs={{0,4},{2,6},{4,0},{6,2},{1,5},{3,7},{5,1},{7,3},{8,12},{10,14},{12... | collective-permute-start | bytes 1474568 | tf_op jit(solution)/shard_map/ppermute | solution.py:312
  11.8 0.7 collective-permute-start.2
  12.5 1.3 collective-permute-start.1
  13.8 0.5 collective-permute-start.5
  14.3 0.3 fusion.23
  14.7 1.1 pad_maximum_fusion.refs_0_
  15.9 14.6 %collective-permute-done.5.refs_1_ = bf16[64,3840]{1,0:T(8,128)(2,1)S(1)} collective-permute-done((bf16[64,3840]{1,0:T(8,128)(2,1)S(1)}, bf16[64,3840]{1,0:T(8,128)(2,1)S(1)}, u32[]{:S(2)}, u32[]{:S(2)}) %collective-permute-start.5) | collective-permute-done | bytes 491552 | tf_op jit(solution)/shard_map/ppermute | solution.py:317
  30.5 4.3 %collective-permute-done.2.refs_4_ = bf16[64,3840]{1,0:T(8,128)(2,1)} collective-permute-done((bf16[64,3840]{1,0:T(8,128)(2,1)S(1)}, bf16[64,3840]{1,0:T(8,128)(2,1)}, u32[]{:S(2)}, u32[]{:S(2)}) %collective-permute-start.2) | collective-permute-done | bytes 491552 | tf_op jit(solution)/shard_map/ppermute | solution.py:312
  34.8 0.5 collective-permute-start.10
  35.3 0.9 multiply_bitcast_fusion
  36.2 2.7 %collective-permute-start.7 = (bf16[64,3840]{1,0:T(8,128)(2,1)}, bf16[64,3840]{1,0:T(8,128)(2,1)S(1)}, u32[]{:S(2)}, u32[]{:S(2)}) collective-permute-start(bf16[64,3840]{1,0:T(8,128)(2,1)} %collective-permute-done.4.refs_1_), channel_id=1, source_target_pairs={{0,6},{2,0},{4,2},{6,4},{1,7},{3,1},{5,3},{7,5},{8,14},{10,8},{12,... | collective-permute-start | bytes 1474568 | tf_op jit(solution)/shard_map/ppermute | solution.py:312
  38.9 0.5 collective-permute-start.8
  39.4 1.3 collective-permute-done.10
  40.8 1.6 %collective-permute-start.11 = (f32[32,256]{1,0:T(8,128)S(1)}, f32[32,256]{1,0:T(8,128)S(1)}, u32[]{:S(2)}, u32[]{:S(2)}) collective-permute-start(f32[32,256]{1,0:T(8,128)S(1)} %add.70), channel_id=1, source_target_pairs={{0,32},{32,0},{64,96},{96,64},{1,33},{33,1},{65,97},{97,65},{2,34}... | collective-permute-start | bytes 98312 | tf_op jit(solution)/shard_map/ppermute | solution.py:317
  42.4 0.7 pad_maximum_fusion.3.refs_12_.refs_10_.refs_9_
  43.1 1.6 %collective-permute-done.11 = f32[32,256]{1,0:T(8,128)S(1)} collective-permute-done((f32[32,256]{1,0:T(8,128)S(1)}, f32[32,256]{1,0:T(8,128)S(1)}, u32[]{:S(2)}, u32[]{:S(2)}) %collective-permute-start.11) | collective-permute-done | bytes 32800 | tf_op jit(solution)/shard_map/ppermute | solution.py:317
  44.7 3.2 %collective-permute-start.12 = (f32[32,256]{1,0:T(8,128)S(1)}, f32[32,256]{1,0:T(8,128)S(1)}, u32[]{:S(2)}, u32[]{:S(2)}) collective-permute-start(f32[32,256]{1,0:T(8,128)S(1)} %add.71), channel_id=1, source_target_pairs={{0,64},{32,96},{64,0},{96,32},{1,65},{33,97},{65,1},{97,33},{2,66}... | collective-permute-start | bytes 98312 | tf_op jit(solution)/shard_map/ppermute | solution.py:317
  47.9 1.1 pad_maximum_fusion.1
  48.9 1.2 collective-permute-done.12
  50.1 3.4 %collective-permute-done.8.refs_7_ = bf16[64,3840]{1,0:T(8,128)(2,1)S(1)} collective-permute-done((bf16[64,3840]{1,0:T(8,128)(2,1)}, bf16[64,3840]{1,0:T(8,128)(2,1)S(1)}, u32[]{:S(2)}, u32[]{:S(2)}) %collective-permute-start.8) | collective-permute-done | bytes 491552 | tf_op jit(solution)/shard_map/ppermute | solution.py:317
  53.5 0.8 copy-done.9
  54.3 3.0 %collective-permute-start.14 = (bf16[128,3840]{1,0:T(8,128)(2,1)}, bf16[128,3840]{1,0:T(8,128)(2,1)S(1)}, u32[]{:S(2)}, u32[]{:S(2)}) collective-permute-start(bf16[128,3840]{1,0:T(8,128)(2,1)} %pad_maximum_fusion.1), channel_id=1, source_target_pairs={{0,6},{2,0},{4,2},{6,4},{1,7},{3,1},{5,3},{7,5},{8,14},{10,8},{12,... | collective-permute-start | bytes 2949128 | tf_op jit(solution)/shard_map/ppermute | solution.py:312
  57.3 0.7 collective-permute-start.15
  58.0 18.2 %partial.1 = (f32[128,1856]{1,0:T(8,128)}, bf16[128,1920]{1,0:T(8,128)(2,1)}, bf16[128,1920]{1,0:T(8,128)(2,1)}, bf16[128,1920]{1,0:T(8,128)(2,1)}) custom-call(s32[1]{0:T(128)} %bitcast.base, bf16[128,3840]{1,0:T(8,128)(2,1)} %copy-done.1, bf16[64,3840]{1,0:T(8,128)(2,1)} %collective-permute-done.4.refs_1_, ...), custom_call_target="tpu_custom_call" | custom-call | flops 3000000000 | bytes 1 | tf_op jit(solution)/shard_map/partial/pallas_call | solution.py:135
  76.2 1.1 collective-permute-done.14.refs_3_
  77.3 3.4 %collective-permute-done.13.refs_2_ = bf16[128,3840]{1,0:T(8,128)(2,1)} collective-permute-done((bf16[128,3840]{1,0:T(8,128)(2,1)}, bf16[128,3840]{1,0:T(8,128)(2,1)}, u32[]{:S(2)}, u32[]{:S(2)}) %collective-permute-start.13) | collective-permute-done | bytes 983072 | tf_op jit(solution)/shard_map/ppermute | solution.py:312
  80.7 0.3 fusion.6
  81.0 0.3 fusion.12
  81.4 1.2 slice.51
  82.6 0.3 collective-permute-start.17
  82.8 1.8 %collective-permute-start.16 = (bf16[64,3840]{1,0:T(8,128)(2,1)S(1)}, bf16[64,3840]{1,0:T(8,128)(2,1)S(1)}, u32[]{:S(2)}, u32[]{:S(2)}) collective-permute-start(bf16[64,3840]{1,0:T(8,128)(2,1)S(1)} %slice.51), channel_id=1, source_target_pairs={{0,2},{2,4},{4,6},{6,0},{1,3},{3,5},{5,7},{7,1},{8,10},{10,12},{12... | collective-permute-start | bytes 1474568 | tf_op jit(solution)/shard_map/ppermute | solution.py:312
  84.7 1.6 %collective-permute-start.18 = (bf16[128,1920]{1,0:T(8,128)(2,1)S(1)}, bf16[128,1920]{1,0:T(8,128)(2,1)S(1)}, u32[]{:S(2)}, u32[]{:S(2)}) collective-permute-start(bf16[128,1920]{1,0:T(8,128)(2,1)S(1)} %copy-done.19), channel_id=1, source_target_pairs={{0,32},{32,64},{64,96},{96,0},{1,33},{33,65},{65,97},{97,1},{2,34}... | collective-permute-start | bytes 1474568 | tf_op jit(solution)/shard_map/ppermute | solution.py:312
  86.3 1.7 %collective-permute-start.19 = (bf16[128,1920]{1,0:T(8,128)(2,1)S(1)}, bf16[128,1920]{1,0:T(8,128)(2,1)S(1)}, u32[]{:S(2)}, u32[]{:S(2)}) collective-permute-start(bf16[128,1920]{1,0:T(8,128)(2,1)S(1)} %copy-done.18), channel_id=1, source_target_pairs={{0,96},{32,0},{64,32},{96,64},{1,97},{33,1},{65,33},{97,65},{2,98}... | collective-permute-start | bytes 1474568 | tf_op jit(solution)/shard_map/ppermute | solution.py:312
  87.9 0.1 pad_maximum_fusion.2
  88.0 0.6 collective-permute-start.20
  88.6 6.6 %collective-permute-done.20 = f32[16,2848]{1,0:T(8,128)S(1)} collective-permute-done((f32[16,2848]{1,0:T(8,128)S(1)}, f32[16,2848]{1,0:T(8,128)S(1)}, u32[]{:S(2)}, u32[]{:S(2)}) %collective-permute-start.20) | collective-permute-done | bytes 182304 | tf_op jit(solution)/shard_map/ppermute | solution.py:317
  95.2 0.6 collective-permute-done.18.refs_2_
  95.9 3.9 %collective-permute-start.21 = (bf16[128,1920]{1,0:T(8,128)(2,1)S(1)}, bf16[128,1920]{1,0:T(8,128)(2,1)S(1)}, u32[]{:S(2)}, u32[]{:S(2)}) collective-permute-start(bf16[128,1920]{1,0:T(8,128)(2,1)S(1)} %copy-done.16), channel_id=1, source_target_pairs={{0,64},{32,96},{64,0},{96,32},{1,65},{33,97},{65,1},{97,33},{2,66}... | collective-permute-start | bytes 1474568 | tf_op jit(solution)/shard_map/ppermute | solution.py:312
  99.8 11.7 %partial_half.2 = (f32[128,928]{1,0:T(8,128)}, bf16[128,1024]{1,0:T(8,128)(2,1)}, bf16[128,1024]{1,0:T(8,128)(2,1)}, bf16[128,1024]{1,0:T(8,128)(2,1)}, bf16[512,48]{1,0:T(8,128)(2,1)}) custom-call(s32[1]{0:T(128)} %bitcast.base, bf16[128,3840]{1,0:T(8,128)(2,1)} %copy-done.1, bf16[64,3840]{1,0:T(8,128)(2,1)} %copy-done.4, ...), custom_call_target="tpu_custom_call" | custom-call | flops 3000000000 | bytes 1 | tf_op jit(solution)/shard_map/partial_half/pallas_call | solution.py:217
  111.5 0.1 collective-permute-start.25
  111.6 5.3 %collective-permute-start.22 = (bf16[128,1024]{1,0:T(8,128)(2,1)}, bf16[128,1024]{1,0:T(8,128)(2,1)S(1)}, u32[]{:S(2)}, u32[]{:S(2)}) collective-permute-start(bf16[128,1024]{1,0:T(8,128)(2,1)} %get-tuple-element.130), channel_id=1, source_target_pairs={{0,32},{32,64},{64,96},{96,0},{1,33},{33,65},{65,97},{97,1},{2,34}... | collective-permute-start | bytes 786440 | tf_op jit(solution)/shard_map/ppermute | solution.py:312
  116.9 2.1 %collective-permute-start.24 = (bf16[128,1024]{1,0:T(8,128)(2,1)}, bf16[128,1024]{1,0:T(8,128)(2,1)S(1)}, u32[]{:S(2)}, u32[]{:S(2)}) collective-permute-start(bf16[128,1024]{1,0:T(8,128)(2,1)} %get-tuple-element.132), channel_id=1, source_target_pairs={{0,64},{32,96},{64,0},{96,32},{1,65},{33,97},{65,1},{97,33},{2,66}... | collective-permute-start | bytes 786440 | tf_op jit(solution)/shard_map/ppermute | solution.py:312
  119.1 10.6 %partial_half.3 = (f32[128,928]{1,0:T(8,128)}, bf16[128,1024]{1,0:T(8,128)(2,1)}, bf16[128,1024]{1,0:T(8,128)(2,1)}, bf16[128,1024]{1,0:T(8,128)(2,1)}, bf16[512,48]{1,0:T(8,128)(2,1)}) custom-call(s32[1]{0:T(128)} %bitcast.base, bf16[128,3840]{1,0:T(8,128)(2,1)} %copy-done.1, bf16[64,3840]{1,0:T(8,128)(2,1)} %copy-done.4, ...), custom_call_target="tpu_custom_call" | custom-call | flops 3000000000 | bytes 1 | tf_op jit(solution)/shard_map/partial_half/pallas_call | solution.py:217
  129.8 0.2 collective-permute-start.26
  130.1 3.1 %collective-permute-start.27 = (bf16[128,1024]{1,0:T(8,128)(2,1)}, bf16[128,1024]{1,0:T(8,128)(2,1)S(1)}, u32[]{:S(2)}, u32[]{:S(2)}) collective-permute-start(bf16[128,1024]{1,0:T(8,128)(2,1)} %get-tuple-element.136), channel_id=1, source_target_pairs={{0,96},{32,0},{64,32},{96,64},{1,97},{33,1},{65,33},{97,65},{2,98}... | collective-permute-start | bytes 786440 | tf_op jit(solution)/shard_map/ppermute | solution.py:312
  133.1 0.8 collective-permute-start.28
  133.9 0.5 collective-permute-start.29
  134.4 5.6 %fold.2 = (f32[64,1856]{1,0:T(8,128)}, f32[64,928]{1,0:T(8,128)}, bf16[64,2944]{1,0:T(8,128)(2,1)}) custom-call(s32[1]{0:T(128)} %bitcast.2.refs_0_, f32[128,1856]{1,0:T(8,128)} %get-tuple-element.138.refs_1_, bf16[128,1920]{1,0:T(8,128)(2,1)} %copy-done.14, bf16[128,1920]{1,0:T(8,128)(2,1)} %copy-done.15, bf16[128,1920]{1,0:T(8,128)(2,1)} %copy-done.17, ...), custom_call_target="tpu_custom_call" | custom-call | flops 2000000000 | bytes 1 | tf_op jit(solution)/shard_map/fold/pallas_call | solution.py:270
  140.0 1.3 collective-permute-done.29
  141.3 0.6 collective-permute-start.30
  142.0 0.1 copy-done.24
  142.2 2.9 %fold.3 = (f32[64,928]{1,0:T(8,128)}, bf16[64,1024]{1,0:T(8,128)(2,1)}) custom-call(s32[1]{0:T(128)} %bitcast.2.refs_0_, f32[128,928]{1,0:T(8,128)} %get-tuple-element.153.refs_1_, bf16[128,1024]{1,0:T(8,128)(2,1)} %copy-done.23, bf16[128,1024]{1,0:T(8,128)(2,1)} %copy-done.24, bf16[128,1024]{1,0:T(8,128)(2,1)} %copy-done.25), custom_call_target="tpu_custom_call" | custom-call | flops 2000000000 | bytes 1 | tf_op jit(solution)/shard_map/fold/pallas_call | solution.py:270
  145.2 1.2 collective-permute-start.31
  146.4 0.7 slice.76
  147.2 0.6 slice_bitcast_fusion
  147.8 2.9 %collective-permute-done.31.got2 = bf16[64,1024]{1,0:T(8,128)(2,1)S(1)} collective-permute-done((bf16[64,1024]{1,0:T(8,128)(2,1)}, bf16[64,1024]{1,0:T(8,128)(2,1)S(1)}, u32[]{:S(2)}, u32[]{:S(2)}) %collective-permute-start.31) | collective-permute-done | bytes 131104 | tf_op jit(solution)/shard_map/ppermute | solution.py:317
  150.7 0.7 copy-done.13
  151.3 0.1 copy-done.12
  151.4 2.8 %finish.1 = bf16[1856,128]{1,0:T(8,128)(2,1)} custom-call(f32[64,1856]{1,0:T(8,128)} %get-tuple-element.150.keep0, f32[64,928]{1,0:T(8,128)} %get-tuple-element.151.keep1, bf16[64,2944]{1,0:T(8,128)(2,1)} %copy-done.12, f32[64,928]{1,0:T(8,128)} %get-tuple-element.161.keep2, bf16[64,1024]{1,0:T(8,128)(2,1)} %copy-done.13), custom_call_target="tpu_custom_call" | custom-call | tf_op jit(solution)/shard_map/finish/pallas_call | solution.py:300
  (86 shorter events, 0.7 us)
Async XLA Ops:
  0.6 3.0 %copy-start = (bf16[256,928]{0,1:T(8,128)(2,1)S(1)}, bf16[256,928]{0,1:T(8,128)(2,1)}, u32[]{:S(2)}) copy-start(bf16[256,928]{0,1:T(8,128)(2,1)} %param.5) | copy-start | bytes 1425412
  0.7 13.7 %copy-start.2 = (bf16[256,1920]{1,0:T(8,128)(2,1)S(1)}, bf16[256,1920]{1,0:T(8,128)(2,1)}, u32[]{:S(2)}) copy-start(bf16[256,1920]{1,0:T(8,128)(2,1)} %param.6) | copy-start | bytes 2949124
  2.0 2.6 %collective-permute-start = (bf16[128,1920]{1,0:T(8,128)(2,1)S(1)}, bf16[128,1920]{1,0:T(8,128)(2,1)S(1)}, u32[]{:S(2)}, u32[]{:S(2)}) collective-permute-start(bf16[128,1920]{1,0:T(8,128)(2,1)S(1)} %get-tuple-element.170), channel_id=1, source_target_pairs={{0,8},{8,0},{1,9},{9,1},{2,10},{10,2},{3,11},{11,3},{4,12},{12,4},... | collective-permute-start | bytes 1474568 | tf_op jit(solution)/shard_map/ppermute | solution.py:317
  3.6 12.2 %copy-start.8 = (bf16[16,1920]{1,0:T(8,128)(2,1)}, bf16[16,1920]{1,0:T(8,128)(2,1)S(1)}, u32[]{:S(2)}) copy-start(bf16[16,1920]{1,0:T(8,128)(2,1)S(1)} %get-tuple-element.166.refs_10_.refs_8_) | copy-start | bytes 184324
  4.6 10.0 %copy-start.5 = (bf16[128,1920]{1,0:T(8,128)(2,1)}, bf16[128,1920]{1,0:T(8,128)(2,1)S(1)}, u32[]{:S(2)}) copy-start(bf16[128,1920]{1,0:T(8,128)(2,1)S(1)} %collective-permute-done) | copy-start | bytes 1474564
  4.7 25.7 %collective-permute-start.4 = (bf16[64,3840]{1,0:T(8,128)(2,1)S(1)}, bf16[64,3840]{1,0:T(8,128)(2,1)}, u32[]{:S(2)}, u32[]{:S(2)}) collective-permute-start(bf16[64,3840]{1,0:T(8,128)(2,1)S(1)} %get-tuple-element.168), channel_id=1, source_target_pairs={{0,1},{1,0},{2,3},{3,2},{4,5},{5,4},{6,7},{7,6},{8,9},{9,8},{10,11... | collective-permute-start | bytes 1474568 | tf_op jit(solution)/shard_map/ppermute | solution.py:317
  7.9 22.5 %collective-permute-start.3 = (bf16[64,3840]{1,0:T(8,128)(2,1)S(1)}, bf16[64,3840]{1,0:T(8,128)(2,1)}, u32[]{:S(2)}, u32[]{:S(2)}) collective-permute-start(bf16[64,3840]{1,0:T(8,128)(2,1)S(1)} %get-tuple-element.168), channel_id=1, source_target_pairs={{0,4},{2,6},{4,0},{6,2},{1,5},{3,7},{5,1},{7,3},{8,12},{10,14},{12... | collective-permute-start | bytes 1474568 | tf_op jit(solution)/shard_map/ppermute | solution.py:312
  11.8 23.0 %collective-permute-start.2 = (bf16[64,3840]{1,0:T(8,128)(2,1)S(1)}, bf16[64,3840]{1,0:T(8,128)(2,1)}, u32[]{:S(2)}, u32[]{:S(2)}) collective-permute-start(bf16[64,3840]{1,0:T(8,128)(2,1)S(1)} %get-tuple-element.168), channel_id=1, source_target_pairs={{0,6},{2,0},{4,2},{6,4},{1,7},{3,1},{5,3},{7,5},{8,14},{10,8},{12,... | collective-permute-start | bytes 1474568 | tf_op jit(solution)/shard_map/ppermute | solution.py:312
  12.5 22.3 %collective-permute-start.1 = (bf16[64,3840]{1,0:T(8,128)(2,1)S(1)}, bf16[64,3840]{1,0:T(8,128)(2,1)}, u32[]{:S(2)}, u32[]{:S(2)}) collective-permute-start(bf16[64,3840]{1,0:T(8,128)(2,1)S(1)} %get-tuple-element.168), channel_id=1, source_target_pairs={{0,2},{2,4},{4,6},{6,0},{1,3},{3,5},{5,7},{7,1},{8,10},{10,12},{12... | collective-permute-start | bytes 1474568 | tf_op jit(solution)/shard_map/ppermute | solution.py:312
  13.8 16.6 %collective-permute-start.5 = (bf16[64,3840]{1,0:T(8,128)(2,1)S(1)}, bf16[64,3840]{1,0:T(8,128)(2,1)S(1)}, u32[]{:S(2)}, u32[]{:S(2)}) collective-permute-start(bf16[64,3840]{1,0:T(8,128)(2,1)S(1)} %get-tuple-element.167), channel_id=1, source_target_pairs={{0,1},{1,0},{2,3},{3,2},{4,5},{5,4},{6,7},{7,6},{8,9},{9,8},{10,11... | collective-permute-start | bytes 1474568 | tf_op jit(solution)/shard_map/ppermute | solution.py:317
  15.9 42.1 %copy-start.1 = (bf16[128,3840]{1,0:T(8,128)(2,1)}, bf16[128,3840]{1,0:T(8,128)(2,1)S(1)}, u32[]{:S(2)}) copy-start(bf16[128,3840]{1,0:T(8,128)(2,1)S(1)} %pad_maximum_fusion.refs_0_) | copy-start | bytes 2949124
  30.5 23.1 %copy-start.4 = (bf16[64,3840]{1,0:T(8,128)(2,1)}, bf16[64,3840]{1,0:T(8,128)(2,1)S(1)}, u32[]{:S(2)}) copy-start(bf16[64,3840]{1,0:T(8,128)(2,1)S(1)} %collective-permute-done.5.refs_1_) | copy-start | bytes 1474564
  34.8 18.7 %collective-permute-start.9 = (bf16[1856,1920]{1,0:T(8,128)(2,1)}, bf16[1856,1920]{1,0:T(8,128)(2,1)}, u32[]{:S(2)}, u32[]{:S(2)}) collective-permute-start(bf16[1856,1920]{1,0:T(8,128)(2,1)} %refs_6_.1), channel_id=1, source_target_pairs={{0,8},{8,0},{1,9},{9,1},{2,10},{10,2},{3,11},{11,3},{4,12},{12,4},... | collective-permute-start | bytes 21381128 | tf_op jit(solution)/shard_map/ppermute | solution.py:317
  34.8 6.0 %collective-permute-start.10 = (f32[32,256]{1,0:T(8,128)S(1)}, f32[32,256]{1,0:T(8,128)S(1)}, u32[]{:S(2)}, u32[]{:S(2)}) collective-permute-start(f32[32,256]{1,0:T(8,128)S(1)} %pad_maximum_fusion.4), channel_id=1, source_target_pairs={{0,8},{8,0},{1,9},{9,1},{2,10},{10,2},{3,11},{11,3},{4,12},{12,4},... | collective-permute-start | bytes 98312 | tf_op jit(solution)/shard_map/ppermute | solution.py:317
  36.2 17.2 %collective-permute-start.7 = (bf16[64,3840]{1,0:T(8,128)(2,1)}, bf16[64,3840]{1,0:T(8,128)(2,1)S(1)}, u32[]{:S(2)}, u32[]{:S(2)}) collective-permute-start(bf16[64,3840]{1,0:T(8,128)(2,1)} %collective-permute-done.4.refs_1_), channel_id=1, source_target_pairs={{0,6},{2,0},{4,2},{6,4},{1,7},{3,1},{5,3},{7,5},{8,14},{10,8},{12,... | collective-permute-start | bytes 1474568 | tf_op jit(solution)/shard_map/ppermute | solution.py:312
  38.9 14.6 %collective-permute-start.6 = (bf16[64,3840]{1,0:T(8,128)(2,1)}, bf16[64,3840]{1,0:T(8,128)(2,1)S(1)}, u32[]{:S(2)}, u32[]{:S(2)}) collective-permute-start(bf16[64,3840]{1,0:T(8,128)(2,1)} %collective-permute-done.4.refs_1_), channel_id=1, source_target_pairs={{0,2},{2,4},{4,6},{6,0},{1,3},{3,5},{5,7},{7,1},{8,10},{10,12},{12... | collective-permute-start | bytes 1474568 | tf_op jit(solution)/shard_map/ppermute | solution.py:312
  38.9 14.6 %collective-permute-start.8 = (bf16[64,3840]{1,0:T(8,128)(2,1)}, bf16[64,3840]{1,0:T(8,128)(2,1)S(1)}, u32[]{:S(2)}, u32[]{:S(2)}) collective-permute-start(bf16[64,3840]{1,0:T(8,128)(2,1)} %collective-permute-done.3.refs_6_), channel_id=1, source_target_pairs={{0,1},{1,0},{2,3},{3,2},{4,5},{5,4},{6,7},{7,6},{8,9},{9,8},{10,11... | collective-permute-start | bytes 1474568 | tf_op jit(solution)/shard_map/ppermute | solution.py:317
  40.8 3.9 %collective-permute-start.11 = (f32[32,256]{1,0:T(8,128)S(1)}, f32[32,256]{1,0:T(8,128)S(1)}, u32[]{:S(2)}, u32[]{:S(2)}) collective-permute-start(f32[32,256]{1,0:T(8,128)S(1)} %add.70), channel_id=1, source_target_pairs={{0,32},{32,0},{64,96},{96,64},{1,33},{33,1},{65,97},{97,65},{2,34}... | collective-permute-start | bytes 98312 | tf_op jit(solution)/shard_map/ppermute | solution.py:317
  44.7 5.4 %collective-permute-start.12 = (f32[32,256]{1,0:T(8,128)S(1)}, f32[32,256]{1,0:T(8,128)S(1)}, u32[]{:S(2)}, u32[]{:S(2)}) collective-permute-start(f32[32,256]{1,0:T(8,128)S(1)} %add.71), channel_id=1, source_target_pairs={{0,64},{32,96},{64,0},{96,32},{1,65},{33,97},{65,1},{97,33},{2,66}... | collective-permute-start | bytes 98312 | tf_op jit(solution)/shard_map/ppermute | solution.py:317
  53.5 3.8 %copy-start.11 = (bf16[64,3840]{1,0:T(8,128)(2,1)}, bf16[64,3840]{1,0:T(8,128)(2,1)S(1)}, u32[]{:S(2)}) copy-start(bf16[64,3840]{1,0:T(8,128)(2,1)S(1)} %collective-permute-done.8.refs_7_) | copy-start | bytes 1474564
  53.5 0.8 copy-start.9
  53.5 3.8 %copy-start.10 = (bf16[64,3840]{1,0:T(8,128)(2,1)}, bf16[64,3840]{1,0:T(8,128)(2,1)S(1)}, u32[]{:S(2)}) copy-start(bf16[64,3840]{1,0:T(8,128)(2,1)S(1)} %collective-permute-done.6.refs_3_) | copy-start | bytes 1474564
  54.3 23.0 %collective-permute-start.14 = (bf16[128,3840]{1,0:T(8,128)(2,1)}, bf16[128,3840]{1,0:T(8,128)(2,1)S(1)}, u32[]{:S(2)}, u32[]{:S(2)}) collective-permute-start(bf16[128,3840]{1,0:T(8,128)(2,1)} %pad_maximum_fusion.1), channel_id=1, source_target_pairs={{0,6},{2,0},{4,2},{6,4},{1,7},{3,1},{5,3},{7,5},{8,14},{10,8},{12,... | collective-permute-start | bytes 2949128 | tf_op jit(solution)/shard_map/ppermute | solution.py:312
  57.3 23.4 %collective-permute-start.13 = (bf16[128,3840]{1,0:T(8,128)(2,1)}, bf16[128,3840]{1,0:T(8,128)(2,1)}, u32[]{:S(2)}, u32[]{:S(2)}) collective-permute-start(bf16[128,3840]{1,0:T(8,128)(2,1)} %pad_maximum_fusion.1), channel_id=1, source_target_pairs={{0,2},{2,4},{4,6},{6,0},{1,3},{3,5},{5,7},{7,1},{8,10},{10,12},{12... | collective-permute-start | bytes 2949128 | tf_op jit(solution)/shard_map/ppermute | solution.py:312
  57.3 18.9 %collective-permute-start.15 = (f32[32,256]{1,0:T(8,128)S(1)}, f32[32,256]{1,0:T(8,128)S(1)}, u32[]{:S(2)}, u32[]{:S(2)}) collective-permute-start(f32[32,256]{1,0:T(8,128)S(1)} %add.75), channel_id=1, source_target_pairs={{0,16},{16,0},{1,17},{17,1},{2,18},{18,2},{3,19},{19,3},{4,20},{20... | collective-permute-start | bytes 98312 | tf_op jit(solution)/shard_map/ppermute | solution.py:317
  77.3 5.2 %copy-start.3 = (bf16[128,3840]{1,0:T(8,128)(2,1)}, bf16[128,3840]{1,0:T(8,128)(2,1)S(1)}, u32[]{:S(2)}) copy-start(bf16[128,3840]{1,0:T(8,128)(2,1)S(1)} %collective-permute-done.14.refs_3_) | copy-start | bytes 2949124
  81.0 3.7 %copy-start.19 = (bf16[128,1920]{1,0:T(8,128)(2,1)S(1)}, bf16[128,1920]{1,0:T(8,128)(2,1)}, u32[]{:S(2)}) copy-start(bf16[128,1920]{1,0:T(8,128)(2,1)} %get-tuple-element.109) | copy-start | bytes 1474564
  81.0 5.2 %copy-start.18 = (bf16[128,1920]{1,0:T(8,128)(2,1)S(1)}, bf16[128,1920]{1,0:T(8,128)(2,1)}, u32[]{:S(2)}) copy-start(bf16[128,1920]{1,0:T(8,128)(2,1)} %get-tuple-element.110) | copy-start | bytes 1474564
  81.0 14.8 %copy-start.16 = (bf16[128,1920]{1,0:T(8,128)(2,1)S(1)}, bf16[128,1920]{1,0:T(8,128)(2,1)}, u32[]{:S(2)}) copy-start(bf16[128,1920]{1,0:T(8,128)(2,1)} %get-tuple-element.120) | copy-start | bytes 1474564
  82.6 12.6 %collective-permute-start.17 = (bf16[64,3840]{1,0:T(8,128)(2,1)S(1)}, bf16[64,3840]{1,0:T(8,128)(2,1)S(1)}, u32[]{:S(2)}, u32[]{:S(2)}) collective-permute-start(bf16[64,3840]{1,0:T(8,128)(2,1)S(1)} %slice.52), channel_id=1, source_target_pairs={{0,6},{2,0},{4,2},{6,4},{1,7},{3,1},{5,3},{7,5},{8,14},{10,8},{12,... | collective-permute-start | bytes 1474568 | tf_op jit(solution)/shard_map/ppermute | solution.py:312
  82.8 12.3 %collective-permute-start.16 = (bf16[64,3840]{1,0:T(8,128)(2,1)S(1)}, bf16[64,3840]{1,0:T(8,128)(2,1)S(1)}, u32[]{:S(2)}, u32[]{:S(2)}) collective-permute-start(bf16[64,3840]{1,0:T(8,128)(2,1)S(1)} %slice.51), channel_id=1, source_target_pairs={{0,2},{2,4},{4,6},{6,0},{1,3},{3,5},{5,7},{7,1},{8,10},{10,12},{12... | collective-permute-start | bytes 1474568 | tf_op jit(solution)/shard_map/ppermute | solution.py:312
  84.7 11.2 %collective-permute-start.18 = (bf16[128,1920]{1,0:T(8,128)(2,1)S(1)}, bf16[128,1920]{1,0:T(8,128)(2,1)S(1)}, u32[]{:S(2)}, u32[]{:S(2)}) collective-permute-start(bf16[128,1920]{1,0:T(8,128)(2,1)S(1)} %copy-done.19), channel_id=1, source_target_pairs={{0,32},{32,64},{64,96},{96,0},{1,33},{33,65},{65,97},{97,1},{2,34}... | collective-permute-start | bytes 1474568 | tf_op jit(solution)/shard_map/ppermute | solution.py:312
  86.3 9.6 %collective-permute-start.19 = (bf16[128,1920]{1,0:T(8,128)(2,1)S(1)}, bf16[128,1920]{1,0:T(8,128)(2,1)S(1)}, u32[]{:S(2)}, u32[]{:S(2)}) collective-permute-start(bf16[128,1920]{1,0:T(8,128)(2,1)S(1)} %copy-done.18), channel_id=1, source_target_pairs={{0,96},{32,0},{64,32},{96,64},{1,97},{33,1},{65,33},{97,65},{2,98}... | collective-permute-start | bytes 1474568 | tf_op jit(solution)/shard_map/ppermute | solution.py:312
  88.0 7.2 %collective-permute-start.20 = (f32[16,2848]{1,0:T(8,128)S(1)}, f32[16,2848]{1,0:T(8,128)S(1)}, u32[]{:S(2)}, u32[]{:S(2)}) collective-permute-start(f32[16,2848]{1,0:T(8,128)S(1)} %pad_maximum_fusion.2), channel_id=1, source_target_pairs={{0,1},{1,0},{2,3},{3,2},{4,5},{5,4},{6,7},{7,6},{8,9},{9,8},{10,11... | collective-permute-start | bytes 546824 | tf_op jit(solution)/shard_map/ppermute | solution.py:317
  95.2 4.6 %copy-start.6 = (bf16[64,3840]{1,0:T(8,128)(2,1)}, bf16[64,3840]{1,0:T(8,128)(2,1)S(1)}, u32[]{:S(2)}) copy-start(bf16[64,3840]{1,0:T(8,128)(2,1)S(1)} %collective-permute-done.17.refs_5_) | copy-start | bytes 1474564
  95.2 4.6 %copy-start.7 = (bf16[64,3840]{1,0:T(8,128)(2,1)}, bf16[64,3840]{1,0:T(8,128)(2,1)S(1)}, u32[]{:S(2)}) copy-start(bf16[64,3840]{1,0:T(8,128)(2,1)S(1)} %collective-permute-done.16.refs_4_) | copy-start | bytes 1474564
  95.8 15.7 %copy-start.14 = (bf16[128,1920]{1,0:T(8,128)(2,1)}, bf16[128,1920]{1,0:T(8,128)(2,1)S(1)}, u32[]{:S(2)}) copy-start(bf16[128,1920]{1,0:T(8,128)(2,1)S(1)} %collective-permute-done.18.refs_2_) | copy-start | bytes 1474564
  95.9 15.7 %copy-start.15 = (bf16[128,1920]{1,0:T(8,128)(2,1)}, bf16[128,1920]{1,0:T(8,128)(2,1)S(1)}, u32[]{:S(2)}) copy-start(bf16[128,1920]{1,0:T(8,128)(2,1)S(1)} %collective-permute-done.19.refs_3_) | copy-start | bytes 1474564
  95.9 15.7 %collective-permute-start.21 = (bf16[128,1920]{1,0:T(8,128)(2,1)S(1)}, bf16[128,1920]{1,0:T(8,128)(2,1)S(1)}, u32[]{:S(2)}, u32[]{:S(2)}) collective-permute-start(bf16[128,1920]{1,0:T(8,128)(2,1)S(1)} %copy-done.16), channel_id=1, source_target_pairs={{0,64},{32,96},{64,0},{96,32},{1,65},{33,97},{65,1},{97,33},{2,66}... | collective-permute-start | bytes 1474568 | tf_op jit(solution)/shard_map/ppermute | solution.py:312
  111.5 18.2 %copy-start.17 = (bf16[128,1920]{1,0:T(8,128)(2,1)}, bf16[128,1920]{1,0:T(8,128)(2,1)S(1)}, u32[]{:S(2)}) copy-start(bf16[128,1920]{1,0:T(8,128)(2,1)S(1)} %collective-permute-done.21.refs_4_) | copy-start | bytes 1474564
  111.5 18.2 %collective-permute-start.25 = (f32[16,2848]{1,0:T(8,128)S(1)}, f32[16,2848]{1,0:T(8,128)S(1)}, u32[]{:S(2)}, u32[]{:S(2)}) collective-permute-start(f32[16,2848]{1,0:T(8,128)S(1)} %add.81), channel_id=1, source_target_pairs={{0,2},{2,0},{4,6},{6,4},{1,3},{3,1},{5,7},{7,5},{8,10},{10,8},{12,... | collective-permute-start | bytes 546824 | tf_op jit(solution)/shard_map/ppermute | solution.py:317
  111.6 18.1 %collective-permute-start.22 = (bf16[128,1024]{1,0:T(8,128)(2,1)}, bf16[128,1024]{1,0:T(8,128)(2,1)S(1)}, u32[]{:S(2)}, u32[]{:S(2)}) collective-permute-start(bf16[128,1024]{1,0:T(8,128)(2,1)} %get-tuple-element.130), channel_id=1, source_target_pairs={{0,32},{32,64},{64,96},{96,0},{1,33},{33,65},{65,97},{97,1},{2,34}... | collective-permute-start | bytes 786440 | tf_op jit(solution)/shard_map/ppermute | solution.py:312
  116.9 12.8 %collective-permute-start.23 = (bf16[128,1024]{1,0:T(8,128)(2,1)}, bf16[128,1024]{1,0:T(8,128)(2,1)S(1)}, u32[]{:S(2)}, u32[]{:S(2)}) collective-permute-start(bf16[128,1024]{1,0:T(8,128)(2,1)} %get-tuple-element.131), channel_id=1, source_target_pairs={{0,96},{32,0},{64,32},{96,64},{1,97},{33,1},{65,33},{97,65},{2,98}... | collective-permute-start | bytes 786440 | tf_op jit(solution)/shard_map/ppermute | solution.py:312
  116.9 12.8 %collective-permute-start.24 = (bf16[128,1024]{1,0:T(8,128)(2,1)}, bf16[128,1024]{1,0:T(8,128)(2,1)S(1)}, u32[]{:S(2)}, u32[]{:S(2)}) collective-permute-start(bf16[128,1024]{1,0:T(8,128)(2,1)} %get-tuple-element.132), channel_id=1, source_target_pairs={{0,64},{32,96},{64,0},{96,32},{1,65},{33,97},{65,1},{97,33},{2,66}... | collective-permute-start | bytes 786440 | tf_op jit(solution)/shard_map/ppermute | solution.py:312
  129.8 4.7 %copy-start.20 = (bf16[128,1024]{1,0:T(8,128)(2,1)}, bf16[128,1024]{1,0:T(8,128)(2,1)S(1)}, u32[]{:S(2)}) copy-start(bf16[128,1024]{1,0:T(8,128)(2,1)S(1)} %collective-permute-done.22.refs_6_) | copy-start | bytes 786436
  129.8 4.6 %copy-start.21 = (bf16[128,1024]{1,0:T(8,128)(2,1)}, bf16[128,1024]{1,0:T(8,128)(2,1)S(1)}, u32[]{:S(2)}) copy-start(bf16[128,1024]{1,0:T(8,128)(2,1)S(1)} %collective-permute-done.23.refs_7_) | copy-start | bytes 786436
  129.8 4.6 %copy-start.22 = (bf16[128,1024]{1,0:T(8,128)(2,1)}, bf16[128,1024]{1,0:T(8,128)(2,1)S(1)}, u32[]{:S(2)}) copy-start(bf16[128,1024]{1,0:T(8,128)(2,1)S(1)} %collective-permute-done.24.refs_8_) | copy-start | bytes 786436
  129.8 11.5 %collective-permute-start.26 = (bf16[128,1024]{1,0:T(8,128)(2,1)}, bf16[128,1024]{1,0:T(8,128)(2,1)S(1)}, u32[]{:S(2)}, u32[]{:S(2)}) collective-permute-start(bf16[128,1024]{1,0:T(8,128)(2,1)} %get-tuple-element.135), channel_id=1, source_target_pairs={{0,32},{32,64},{64,96},{96,0},{1,33},{33,65},{65,97},{97,1},{2,34}... | collective-permute-start | bytes 786440 | tf_op jit(solution)/shard_map/ppermute | solution.py:312
  130.1 11.3 %collective-permute-start.27 = (bf16[128,1024]{1,0:T(8,128)(2,1)}, bf16[128,1024]{1,0:T(8,128)(2,1)S(1)}, u32[]{:S(2)}, u32[]{:S(2)}) collective-permute-start(bf16[128,1024]{1,0:T(8,128)(2,1)} %get-tuple-element.136), channel_id=1, source_target_pairs={{0,96},{32,0},{64,32},{96,64},{1,97},{33,1},{65,33},{97,65},{2,98}... | collective-permute-start | bytes 786440 | tf_op jit(solution)/shard_map/ppermute | solution.py:312
  133.1 8.2 %collective-permute-start.28 = (bf16[128,1024]{1,0:T(8,128)(2,1)}, bf16[128,1024]{1,0:T(8,128)(2,1)S(1)}, u32[]{:S(2)}, u32[]{:S(2)}) collective-permute-start(bf16[128,1024]{1,0:T(8,128)(2,1)} %get-tuple-element.137), channel_id=1, source_target_pairs={{0,64},{32,96},{64,0},{96,32},{1,65},{33,97},{65,1},{97,33},{2,66}... | collective-permute-start | bytes 786440 | tf_op jit(solution)/shard_map/ppermute | solution.py:312
  133.9 7.4 %collective-permute-start.29 = (f32[16,2848]{1,0:T(8,128)S(1)}, f32[16,2848]{1,0:T(8,128)S(1)}, u32[]{:S(2)}, u32[]{:S(2)}) collective-permute-start(f32[16,2848]{1,0:T(8,128)S(1)} %add.82), channel_id=1, source_target_pairs={{0,4},{2,6},{4,0},{6,2},{1,5},{3,7},{5,1},{7,3},{8,12},{10,14},{12... | collective-permute-start | bytes 546824 | tf_op jit(solution)/shard_map/ppermute | solution.py:317
  141.3 0.7 copy-start.23
  141.3 0.9 copy-start.24
  141.3 0.9 copy-start.25
  141.3 9.3 %collective-permute-start.30 = (bf16[64,2944]{1,0:T(8,128)(2,1)}, bf16[64,2944]{1,0:T(8,128)(2,1)S(1)}, u32[]{:S(2)}, u32[]{:S(2)}) collective-permute-start(bf16[64,2944]{1,0:T(8,128)(2,1)} %get-tuple-element.152), channel_id=1, source_target_pairs={{0,16},{16,0},{1,17},{17,1},{2,18},{18,2},{3,19},{19,3},{4,20},{20... | collective-permute-start | bytes 1130504 | tf_op jit(solution)/shard_map/ppermute | solution.py:317
  145.2 5.5 %collective-permute-start.31 = (bf16[64,1024]{1,0:T(8,128)(2,1)}, bf16[64,1024]{1,0:T(8,128)(2,1)S(1)}, u32[]{:S(2)}, u32[]{:S(2)}) collective-permute-start(bf16[64,1024]{1,0:T(8,128)(2,1)} %get-tuple-element.157), channel_id=1, source_target_pairs={{0,16},{16,0},{1,17},{17,1},{2,18},{18,2},{3,19},{19,3},{4,20},{20... | collective-permute-start | bytes 393224 | tf_op jit(solution)/shard_map/ppermute | solution.py:317
  150.6 0.7 copy-start.13
  150.7 0.8 copy-start.12
